TPU v7x, 256 devices: a whole 4x4x8 slice. The times are simulated.
256 devices in a mesh: dp: 2 (over core), seq: 128 (over y, x, z).
Axes of the slice: x: 4, y: 4, z: 8, core: 2. Of those that a mesh axis runs over, the one named last changes fastest.
Arguments:
- activations: bfloat16 [4, 8192, 1024], P('dp', 'seq'), may hold values from -28 to 28
- segment_ids: int32 [4, 8192], P('dp', 'seq'), may hold values from 0 to 15, as said below
- interval_bounds: int32 [4, 17], P('dp'), may hold values from 0 to 8192, as said below
- conv_weight: bfloat16 [2, 1024, 1536], replicated, may hold values from -0.109375 to 0.109375
- proj_weight: bfloat16 [2, 1024, 512], replicated, may hold values from -0.25 to 0.25
- gains_in: float32 [2, 1024], replicated, may hold values from 0.25 to 1.75
- biases_in: float32 [2, 1024], replicated, may hold values from -2.5 to 2.5
- gains_mid: float32 [2, 512], replicated, may hold values from 0.25 to 1.75
- biases_mid: float32 [2, 512], replicated, may hold values from -2.5 to 2.5
- cotangent: bfloat16 [4, 8192, 1024], P('dp', 'seq'), may hold values from -24 to 24
Outputs:
- out_acts: bfloat16 [4, 8192, 1024], P('dp', 'seq')
- grad_acts: bfloat16 [4, 8192, 1024], P('dp', 'seq')
- grad_conv: float32 [2, 1024, 1536], P(None, 'seq')
- grad_proj: float32 [2, 1024, 512], P(None, 'seq')
- grad_gains_in: float32 [2, 1024], replicated
- grad_biases_in: float32 [2, 1024], replicated
- grad_gains_mid: float32 [2, 512], replicated
- grad_biases_mid: float32 [2, 512], replicated
Inputs may be any that keep to these rules, and one draw needn't show every extreme that they name: `segment_ids`: never falling along a window; each interval holds 256 to 768 bins, and every window has one of the largest length; bin t lies in interval s exactly when interval_bounds[w, s] <= t < interval_bounds[w, s + 1]. `interval_bounds`: rising in each window, first entry 0 and last entry 8192.
All inputs are finite; a program needn't handle non-finite values.
Results may differ from a plain program's by a relative error of at most 0.02.
Values may be sent and summed in bfloat16 or wider, within the bound.
No kernel may reach another device: no remote copies, remote signals or barrier semaphores. Data moves between devices by JAX's collectives and lax.ppermute only.
A program may use at most 128 MiB of HBM per device.

v0:
```python
import jax
import jax.numpy as jnp
from jax import lax
from jax.sharding import PartitionSpec as P

LAYERS = 2
FIRST_DILATION = 64
SECOND_DILATION = 512


EPSILON = 1e-05


def passed_along(value, axis, steps):
    count = lax.axis_size(axis)
    leading, last = (max(0, -steps), min(count, count - steps))
    return lax.ppermute(value, axis, [(source, source + steps) for source in range(leading, last)])


def gelu_slope(values):
    return jax.jvp(
        lambda argument: jax.nn.gelu(argument, approximate=True),
        (values,),
        (jnp.ones_like(values),),
    )


def normalise(values, norm_gain, norm_bias, count_all):
    middle_tap = lax.psum(jnp.sum(values, axis=0), ("dp", "seq")) / count_all
    shifted = values - middle_tap
    spread = lax.psum(jnp.sum(shifted * shifted, axis=0), ("dp", "seq")) / count_all
    factor = lax.rsqrt(spread + EPSILON)
    normed = shifted * factor
    return (normed, factor, normed * norm_gain + norm_bias)


def normalise_back(upstream, normed, factor, norm_gain, count_all):
    total_sum, cross_sum = lax.psum(
        (jnp.sum(upstream, axis=0), jnp.sum(upstream * normed, axis=0)), ("dp", "seq")
    )
    result = (
        norm_gain * factor * (upstream - total_sum / count_all - normed * cross_sum / count_all)
    )
    return (result, cross_sum, total_sum)


def neighbour_taps(tensor, dilation):
    local_bins = tensor.shape[1]
    extent = min(dilation, local_bins)
    device_hops = -(-dilation // local_bins)
    lower_part = passed_along(tensor, "seq", device_hops)
    upper_part = passed_along(tensor, "seq", -device_hops)
    before = jnp.concatenate([lower_part, tensor[:, : local_bins - extent]], axis=1)
    after_part = jnp.concatenate([tensor[:, extent:], upper_part], axis=1)
    return (before, after_part)


def transposed_product(left_side, right_side):
    return lax.dot_general(
        left_side, right_side, (((1,), (1,)), ((), ())), preferred_element_type=jnp.float32
    )


def column_product(left_side, right_side):
    return lax.dot_general(
        left_side, right_side, (((0,), (0,)), ((), ())), preferred_element_type=jnp.float32
    )


def on_device(
    activations,
    segment_ids,
    interval_bounds,
    conv_weight,
    proj_weight,
    gains_in,
    biases_in,
    gains_mid,
    biases_mid,
    cotangent,
):
    windows, local_bins, channels = activations.shape
    hidden_width = proj_weight.shape[2]
    local_rows = windows * local_bins
    count_all = float(local_rows * lax.axis_size("dp") * lax.axis_size("seq"))
    dilation_list = (FIRST_DILATION, SECOND_DILATION)
    position = lax.axis_index("seq") * local_bins + jnp.arange(local_bins, dtype=jnp.int32)[None, :]
    labels = jnp.arange(interval_bounds.shape[1] - 1, dtype=jnp.int32)
    matches = segment_ids[:, :, None] == labels[None, None, :]
    starts = jnp.sum(jnp.where(matches, interval_bounds[:, None, :-1], 0), axis=2)
    finishes = jnp.sum(jnp.where(matches, interval_bounds[:, None, 1:], 0), axis=2)
    stream = activations
    caches = []
    for layer_index in range(LAYERS):
        dilation = dilation_list[layer_index]
        mask_before = (starts <= position - dilation).astype(jnp.bfloat16)[:, :, None]
        mask_after = (position + dilation < finishes).astype(jnp.bfloat16)[:, :, None]
        kernel = conv_weight[layer_index]
        project = proj_weight[layer_index]
        flattened_rows = stream.reshape(local_rows, channels).astype(jnp.float32)
        normed_in, factor_in, preact_in = normalise(
            flattened_rows, gains_in[layer_index], biases_in[layer_index], count_all
        )
        active_in, slope_in = gelu_slope(preact_in)
        centre_taps = active_in.astype(jnp.bfloat16)
        lower_taps, upper_taps = neighbour_taps(
            centre_taps.reshape(windows, local_bins, channels), dilation
        )
        before_taps = (lower_taps * mask_before).reshape(local_rows, channels)
        after_taps = (upper_taps * mask_after).reshape(local_rows, channels)
        conv_out = jnp.dot(
            before_taps, kernel[:, :hidden_width], preferred_element_type=jnp.float32
        )
        conv_out = conv_out + jnp.dot(
            centre_taps,
            kernel[:, hidden_width : 2 * hidden_width],
            preferred_element_type=jnp.float32,
        )
        conv_out = conv_out + jnp.dot(
            after_taps, kernel[:, 2 * hidden_width :], preferred_element_type=jnp.float32
        )
        normed_mid, factor_mid, preact_mid = normalise(
            conv_out, gains_mid[layer_index], biases_mid[layer_index], count_all
        )
        middle_activation, slope_mid = gelu_slope(preact_mid)
        hidden = middle_activation.astype(jnp.bfloat16)
        branch = transposed_product(hidden, project)
        stream = (
            (flattened_rows + branch).astype(jnp.bfloat16).reshape(windows, local_bins, channels)
        )
        caches.append(
            (
                mask_before,
                mask_after,
                normed_in,
                factor_in,
                slope_in,
                centre_taps,
                before_taps,
                after_taps,
                normed_mid,
                factor_mid,
                slope_mid,
                hidden,
            )
        )
    grad_stream = cotangent
    kernel_grads = []
    project_grads = []
    gain_in_grads = []
    bias_in_grads = []
    gain_mid_grads = []
    bias_mid_grads = []
    for layer_index in range(LAYERS - 1, -1, -1):
        dilation = dilation_list[layer_index]
        (
            mask_before,
            mask_after,
            normed_in,
            factor_in,
            slope_in,
            centre_taps,
            before_taps,
            after_taps,
            normed_mid,
            factor_mid,
            slope_mid,
            hidden,
        ) = caches[layer_index]
        kernel = conv_weight[layer_index]
        project = proj_weight[layer_index]
        upstream = grad_stream.reshape(local_rows, channels)
        grad_hidden = jnp.dot(upstream, project, preferred_element_type=jnp.float32)
        grad_preact_mid = grad_hidden * slope_mid
        grad_conv_f, gain_mid_grad, bias_mid_grad = normalise_back(
            grad_preact_mid, normed_mid, factor_mid, gains_mid[layer_index], count_all
        )
        grad_conv_out = grad_conv_f.astype(jnp.bfloat16)
        lower_grad, upper_grad = neighbour_taps(
            grad_conv_out.reshape(windows, local_bins, hidden_width), dilation
        )
        grad_before = (lower_grad * mask_before).reshape(local_rows, hidden_width)
        grad_after = (upper_grad * mask_after).reshape(local_rows, hidden_width)
        grad_taps = transposed_product(grad_after, kernel[:, :hidden_width])
        grad_taps = grad_taps + transposed_product(
            grad_conv_out, kernel[:, hidden_width : 2 * hidden_width]
        )
        grad_taps = grad_taps + transposed_product(grad_before, kernel[:, 2 * hidden_width :])
        grad_preact_in = grad_taps * slope_in
        grad_branch, gain_in_grad, entry_bias_gradient = normalise_back(
            grad_preact_in, normed_in, factor_in, gains_in[layer_index], count_all
        )

        def grad_term(
            first_row,
            length,
            before_taps=before_taps,
            centre_taps=centre_taps,
            after_taps=after_taps,
            grad_conv_out=grad_conv_out,
            upstream=upstream,
            hidden=hidden,
        ):
            pieces = [
                column_product(before_taps, grad_conv_out),
                column_product(centre_taps, grad_conv_out),
                column_product(after_taps, grad_conv_out),
                column_product(upstream, hidden),
            ]
            return jnp.concatenate(pieces, axis=1)

        row_share = lax.psum_scatter(
            grad_term(jnp.int32(0), lax.axis_size("seq") * (channels // lax.axis_size("seq"))),
            "seq",
            scatter_dimension=0,
            tiled=True,
        )
        row_share = lax.psum(row_share.astype(jnp.bfloat16), "dp").astype(jnp.float32)
        grad_stream = (
            (upstream.astype(jnp.float32) + grad_branch)
            .astype(jnp.bfloat16)
            .reshape(windows, local_bins, channels)
        )
        kernel_grads.append(row_share[:, : 3 * hidden_width])
        project_grads.append(row_share[:, 3 * hidden_width :])
        gain_in_grads.append(gain_in_grad)
        bias_in_grads.append(entry_bias_gradient)
        gain_mid_grads.append(gain_mid_grad)
        bias_mid_grads.append(bias_mid_grad)
    return (
        stream,
        grad_stream,
        jnp.stack(kernel_grads[::-1]),
        jnp.stack(project_grads[::-1]),
        jnp.stack(gain_in_grads[::-1]),
        jnp.stack(bias_in_grads[::-1]),
        jnp.stack(gain_mid_grads[::-1]),
        jnp.stack(bias_mid_grads[::-1]),
    )


def solution(mesh):
    in_specs = (
        P("dp", "seq", None),
        P("dp", "seq"),
        P("dp", None),
        P(),
        P(),
        P(),
        P(),
        P(),
        P(),
        P("dp", "seq", None),
    )
    out_specs = (
        P("dp", "seq", None),
        P("dp", "seq", None),
        P(None, "seq", None),
        P(None, "seq", None),
        P(),
        P(),
        P(),
        P(),
    )
    return jax.shard_map(
        on_device, mesh=mesh, in_specs=in_specs, out_specs=out_specs, check_vma=False
    )
```

profile of v0, /device:TPU:32, one launch (start us, length us, event | category | flops | bytes accessed | tf_op | source)
XLA Modules:
  0.0 2200.2 jit_solution(14623809493235427997)
XLA Ops:
  8.8 1.0 convert_reduce_fusion
  9.8 79.8 %psum.126 = f32[1024]{0:T(1024)S(1)} all-reduce(f32[1024]{0:T(1024)S(1)} %convert_reduce_fusion), channel_id=1, replica_groups=mesh['dp'=2,'seq'=128] {'dp','seq'}, use_global_device_ids=true, to_apply=%region_1.2 | all-reduce | flops 1024 | bytes 8192 | tf_op jit(solution)/shard_map/psum | solution.py:29
  89.6 1.0 multiply_reduce_fusion.3
  90.7 73.3 %psum.127 = f32[1024]{0:T(1024)S(1)} all-reduce(f32[1024]{0:T(1024)S(1)} %multiply_reduce_fusion.3), channel_id=1, replica_groups=mesh['dp'=2,'seq'=128] {'dp','seq'}, use_global_device_ids=true, to_apply=%region_3.4 | all-reduce | flops 1024 | bytes 8192 | tf_op jit(solution)/shard_map/psum | solution.py:31
  164.6 1.9 fusion.64
  166.5 1.9 collective-permute-start.1
  168.4 3.9 collective-permute-start
  172.4 2.0 multiply_add_fusion.1
  174.4 0.8 fusion.103
  175.2 4.9 slice_bitcast_fusion
  180.7 1.0 broadcast_multiply_fusion.2
  182.5 1.0 broadcast_multiply_fusion.3
  184.2 1.0 fusion.104
  185.2 75.9 %psum.128 = f32[512]{0:T(512)S(1)} all-reduce(f32[512]{0:T(512)S(1)} %get-tuple-element.62), channel_id=1, replica_groups=mesh['dp'=2,'seq'=128] {'dp','seq'}, use_global_device_ids=true, to_apply=%region_7.8 | all-reduce | flops 512 | bytes 4096 | tf_op jit(solution)/shard_map/psum | solution.py:29
  261.1 1.0 multiply_reduce_fusion.7
  262.1 75.0 %psum.129 = f32[512]{0:T(512)S(1)} all-reduce(f32[512]{0:T(512)S(1)} %multiply_reduce_fusion.7), channel_id=1, replica_groups=mesh['dp'=2,'seq'=128] {'dp','seq'}, use_global_device_ids=true, to_apply=%region_9.10 | all-reduce | flops 512 | bytes 4096 | tf_op jit(solution)/shard_map/psum | solution.py:31
  337.7 2.6 fusion.105
  340.3 73.4 %psum.130 = f32[1024]{0:T(1024)S(1)} all-reduce(f32[1024]{0:T(1024)S(1)} %get-tuple-element.64), channel_id=1, replica_groups=mesh['dp'=2,'seq'=128] {'dp','seq'}, use_global_device_ids=true, to_apply=%region_11.12 | all-reduce | flops 1024 | bytes 8192 | tf_op jit(solution)/shard_map/psum | solution.py:29
  413.8 1.1 multiply_reduce_fusion.2
  414.9 74.2 %psum.131 = f32[1024]{0:T(1024)S(1)} all-reduce(f32[1024]{0:T(1024)S(1)} %multiply_reduce_fusion.2), channel_id=1, replica_groups=mesh['dp'=2,'seq'=128] {'dp','seq'}, use_global_device_ids=true, to_apply=%region_13.14 | all-reduce | flops 1024 | bytes 8192 | tf_op jit(solution)/shard_map/psum | solution.py:31
  489.7 1.3 multiply_convert_fusion
  491.0 1.3 collective-permute-start.3
  492.3 4.6 collective-permute-start.2
  496.9 1.5 fusion.19
  498.4 2.5 collective-permute-done.3
  501.0 1.6 fusion.15
  503.5 2.2 fusion.106
  505.8 76.6 %psum.132 = f32[512]{0:T(512)S(1)} all-reduce(f32[512]{0:T(512)S(1)} %get-tuple-element.66), channel_id=1, replica_groups=mesh['dp'=2,'seq'=128] {'dp','seq'}, use_global_device_ids=true, to_apply=%region_15.16 | all-reduce | flops 512 | bytes 4096 | tf_op jit(solution)/shard_map/psum | solution.py:29
  582.3 1.0 multiply_reduce_fusion.6
  583.3 73.0 %psum.133 = f32[512]{0:T(512)S(1)} all-reduce(f32[512]{0:T(512)S(1)} %multiply_reduce_fusion.6), channel_id=1, replica_groups=mesh['dp'=2,'seq'=128] {'dp','seq'}, use_global_device_ids=true, to_apply=%region_17.18 | all-reduce | flops 512 | bytes 4096 | tf_op jit(solution)/shard_map/psum | solution.py:31
  657.0 2.5 fusion.98
  659.5 1.8 convolution_bitcast_fusion
  661.3 73.2 %all-reduce.3 = (f32[512]{0:T(512)}, f32[512]{0:T(512)S(1)}) all-reduce(f32[512]{0:T(512)S(1)} %get-tuple-element.23, f32[512]{0:T(512)S(1)} %get-tuple-element.22), channel_id=1, replica_groups=mesh['dp'=2,'seq'=128] {'dp','seq'}, use_global_device_ids=true, to_apply=%region_21.22 | all-reduce | flops 1024 | bytes 8192 | tf_op jit(solution)/shard_map/psum | solution.py:38
  735.1 1.1 multiply_convert_fusion.3
  736.2 1.6 fusion.112
  738.8 3.9 pad_maximum_fusion.1
  742.8 9.2 copy.30
  752.0 3.1 collective-permute-start.5
  755.1 1.7 fusion.17
  756.8 1.3 collective-permute-start.4
  758.9 4.8 collective-permute-done.4
  764.5 1.7 fusion.13
  766.2 2.8 fusion.96
  769.0 77.3 %all-reduce.2 = (f32[1024]{0:T(1024)S(1)}, f32[1024]{0:T(1024)S(1)}) all-reduce(f32[1024]{0:T(1024)S(1)} %get-tuple-element.19, f32[1024]{0:T(1024)S(1)} %get-tuple-element.18), channel_id=1, replica_groups=mesh['dp'=2,'seq'=128] {'dp','seq'}, use_global_device_ids=true, to_apply=%region_25.26 | all-reduce | flops 2048 | bytes 16384 | tf_op jit(solution)/shard_map/psum | solution.py:38
  846.3 1.5 add_convert_fusion.1
  848.5 2.4 fusion.97
  850.9 73.2 %all-reduce.1 = (f32[512]{0:T(512)S(1)}, f32[512]{0:T(512)S(1)}) all-reduce(f32[512]{0:T(512)S(1)} %get-tuple-element.21, f32[512]{0:T(512)S(1)} %get-tuple-element.20), channel_id=1, replica_groups=mesh['dp'=2,'seq'=128] {'dp','seq'}, use_global_device_ids=true, to_apply=%region_29.30 | all-reduce | flops 1024 | bytes 8192 | tf_op jit(solution)/shard_map/psum | solution.py:38
  924.7 1.1 multiply_convert_fusion.2
  925.9 1.5 fusion.109
  928.9 4.0 pad_maximum_fusion
  932.9 9.1 copy.28
  942.8 2.7 fusion.6
  945.5 1.9 collective-permute-start.7
  947.4 3.9 collective-permute-start.6
  953.1 2.1 collective-permute-done.6
  955.9 1.5 fusion.95
  957.4 79.4 %all-reduce = (f32[1024]{0:T(1024)S(1)}, f32[1024]{0:T(1024)S(1)}) all-reduce(f32[1024]{0:T(1024)S(1)} %get-tuple-element.17, f32[1024]{0:T(1024)S(1)} %get-tuple-element.16), channel_id=1, replica_groups=mesh['dp'=2,'seq'=128] {'dp','seq'}, use_global_device_ids=true, to_apply=%region_33.34 | all-reduce | flops 2048 | bytes 16384 | tf_op jit(solution)/shard_map/psum | solution.py:38
  1037.4 2.0 add_convert_fusion
  1039.4 413.6 %reduce-scatter.9.cloned.1.call-done = f32[8,2048]{1,0:T(8,128)} async-done(((f32[1024,2048]{1,0:T(8,128)}), f32[8,2048]{1,0:T(8,128)}) %reduce-scatter.9.cloned.1.call-update) | async-done | bytes 65552
  1453.0 1.8 copy.31
  1454.8 704.6 %reduce-scatter.7.cloned.1.call-done = f32[8,2048]{1,0:T(8,128)} async-done(((f32[1024,2048]{1,0:T(8,128)}), f32[8,2048]{1,0:T(8,128)}) %reduce-scatter.7.cloned.1.call-update) | async-done | bytes 65552
  2159.4 1.8 copy.29
  2161.9 28.4 %all-reduce.7.cloned.1.call-done = (bf16[8,2048]{0,1:T(8,128)(2,1)}, bf16[8,2048]{0,1:T(8,128)(2,1)}) async-done(((bf16[8,2048]{0,1:T(8,128)(2,1)}, bf16[8,2048]{0,1:T(8,128)(2,1)}), (bf16[8,2048]{0,1:T(8,128)(2,1)}, bf16[8,2048]{0,1:T(8,128)(2,1)})) %all-reduce.7.cloned.1.call-update) | async-done | bytes 65552 | tf_op jit(solution)/shard_map/psum | solution.py:218
  2190.3 1.2 convert_element_type.117
  (190 shorter events, 19.1 us)
Async XLA Ops:
  7.2 1445.8 %reduce-scatter.9.cloned.1.call-start = ((), (), s32[]{:S(2)}) async-start(), calls=%async_computation.3 | async-start | bytes 8454144
  8.0 481.7 %copy-start.37 = (f32[1,1024]{1,0:T(1,128)}, f32[1,1024]{1,0:T(1,128)S(1)}, u32[]{:S(2)}) copy-start(f32[1,1024]{1,0:T(1,128)S(1)} %get-tuple-element.42) | copy-start | bytes 12292
  8.8 480.9 %copy-start.20 = (f32[1,1024]{1,0:T(1,128)}, f32[1,1024]{1,0:T(1,128)S(1)}, u32[]{:S(2)}) copy-start(f32[1,1024]{1,0:T(1,128)S(1)} %get-tuple-element.40) | copy-start | bytes 12292
  166.5 14.2 collective-permute-start.1
  168.4 13.7 collective-permute-start
  174.4 6.0 copy-start.16
  175.2 4.9 copy-start.61
  175.2 4.9 copy-start.62
  175.2 5.0 copy-start.63
  180.2 157.5 %copy-start.45 = (f32[1,512]{1,0:T(1,128)}, f32[1,512]{1,0:T(1,128)S(1)}, u32[]{:S(2)}) copy-start(f32[1,512]{1,0:T(1,128)S(1)} %get-tuple-element.51) | copy-start | bytes 6148
  180.2 479.3 %copy-start.44 = (f32[1,512]{1,0:T(1,128)}, f32[1,512]{1,0:T(1,128)S(1)}, u32[]{:S(2)}) copy-start(f32[1,512]{1,0:T(1,128)S(1)} %get-tuple-element.50) | copy-start | bytes 6148
  180.2 157.5 %copy-start.33 = (f32[1,512]{1,0:T(1,128)}, f32[1,512]{1,0:T(1,128)S(1)}, u32[]{:S(2)}) copy-start(f32[1,512]{1,0:T(1,128)S(1)} %get-tuple-element.49) | copy-start | bytes 6148
  180.2 479.2 %copy-start.32 = (f32[1,512]{1,0:T(1,128)}, f32[1,512]{1,0:T(1,128)S(1)}, u32[]{:S(2)}) copy-start(f32[1,512]{1,0:T(1,128)S(1)} %get-tuple-element.48) | copy-start | bytes 6148
  180.3 4.9 copy-start.55
  180.3 320.6 %copy-start.59 = (bf16[2,64]{1,0:T(2,128)(2,1)}, bf16[2,64]{1,0:T(2,128)(2,1)S(1)}, u32[]{:S(2)}) copy-start(bf16[2,64]{1,0:T(2,128)(2,1)S(1)} %get-tuple-element.58) | copy-start | bytes 772
  180.4 4.9 copy-start.57
  180.4 322.3 %copy-start.60 = (bf16[2,64]{1,0:T(2,128)(2,1)}, bf16[2,64]{1,0:T(2,128)(2,1)S(1)}, u32[]{:S(2)}) copy-start(bf16[2,64]{1,0:T(2,128)(2,1)S(1)} %get-tuple-element.56) | copy-start | bytes 772
  180.4 157.3 %copy-start.1 = (bf16[2,64,1024]{2,1,0:T(8,128)(2,1)S(1)}, bf16[2,64,1024]{2,1,0:T(8,128)(2,1)}, u32[]{:S(2)}) copy-start(bf16[2,64,1024]{2,1,0:T(8,128)(2,1)} %param.10) | copy-start | bytes 786436
  261.1 239.9 %copy-start.22 = (f32[512]{0:T(512)}, f32[512]{0:T(512)S(1)}, u32[]{:S(2)}) copy-start(f32[512]{0:T(512)S(1)} %broadcast_multiply_fusion.15) | copy-start | bytes 6148
  337.7 2.6 copy-start.27
  491.0 11.7 copy-start.12
  491.0 9.9 collective-permute-start.3
  492.3 10.4 collective-permute-start.2
  582.3 152.2 %copy-start.25 = (f32[512]{0:T(512)}, f32[512]{0:T(512)S(1)}, u32[]{:S(2)}) copy-start(f32[512]{0:T(512)S(1)} %broadcast_multiply_fusion.14) | copy-start | bytes 6148
  656.4 3.1 copy-start.4
  656.4 3.1 copy-start.11
  657.0 77.6 %copy-start.30 = (f32[512]{0:T(512)}, f32[512]{0:T(512)S(1)}, u32[]{:S(2)}) copy-start(f32[512]{0:T(512)S(1)} %get-tuple-element.55) | copy-start | bytes 6148
  734.5 3.3 copy-start.13
  734.5 3.8 copy-start.8
  736.2 2.6 copy-start
  751.9 1407.4 %reduce-scatter.7.cloned.1.call-start = ((), (), s32[]{:S(2)}) async-start(), calls=%async_computation.2 | async-start | bytes 8454144
  752.0 14.2 copy-start.2
  752.0 14.2 copy-start.21
  752.0 14.2 copy-start.38
  752.0 6.1 collective-permute-start.5
  756.8 6.9 collective-permute-start.4
  764.5 81.9 %copy-start.39 = (f32[1024]{0:T(1024)S(1)}, f32[1024]{0:T(1024)}, u32[]{:S(2)}) copy-start(f32[1024]{0:T(1024)} %get-tuple-element.46) | copy-start | bytes 12292
  766.2 82.3 %copy-start.23 = (f32[512]{0:T(512)S(1)}, f32[512]{0:T(512)}, u32[]{:S(2)}) copy-start(f32[512]{0:T(512)} %copy-done.22) | copy-start | bytes 6148
  766.2 82.3 %copy-start.28 = (f32[512]{0:T(512)S(1)}, f32[512]{0:T(512)}, u32[]{:S(2)}) copy-start(f32[512]{0:T(512)} %copy-done.27) | copy-start | bytes 6148
  766.2 82.3 %copy-start.34 = (f32[1,512]{1,0:T(1,128)S(1)}, f32[1,512]{1,0:T(1,128)}, u32[]{:S(2)}) copy-start(f32[1,512]{1,0:T(1,128)} %copy-done.33) | copy-start | bytes 6148
  766.2 82.3 %copy-start.46 = (f32[1,512]{1,0:T(1,128)S(1)}, f32[1,512]{1,0:T(1,128)}, u32[]{:S(2)}) copy-start(f32[1,512]{1,0:T(1,128)} %copy-done.45) | copy-start | bytes 6148
  846.3 77.8 %copy-start.40 = (f32[1024]{0:T(1024)}, f32[1024]{0:T(1024)S(1)}, u32[]{:S(2)}) copy-start(f32[1024]{0:T(1024)S(1)} %get-tuple-element.30) | copy-start | bytes 12292
  846.3 77.8 %copy-start.42 = (f32[1024]{0:T(1024)}, f32[1024]{0:T(1024)S(1)}, u32[]{:S(2)}) copy-start(f32[1024]{0:T(1024)S(1)} %get-tuple-element.31) | copy-start | bytes 12292
  924.1 4.2 copy-start.49
  924.1 3.3 copy-start.17
  924.1 3.7 copy-start.6
  925.8 2.5 copy-start.3
  925.8 2.5 copy-start.10
  925.8 2.5 copy-start.24
  925.8 2.5 copy-start.29
  925.9 2.5 copy-start.35
  942.1 1248.2 %all-reduce.7.cloned.1.call-start = ((), (), s32[]{:S(2)}) async-start(), calls=%async_computation.4 | async-start | bytes 2097152 | tf_op jit(solution)/shard_map/psum | solution.py:218
  942.8 9.1 copy-start.48
  942.8 9.1 copy-start.50
  942.8 9.7 copy-start.52
  942.8 9.7 copy-start.54
  942.8 10.3 copy-start.58
  942.8 12.5 copy-start.56
  942.8 13.1 copy-start.19
  945.5 7.6 collective-permute-start.7
  947.4 7.9 collective-permute-start.6
  955.4 81.5 %copy-start.41 = (f32[1024]{0:T(1024)S(1)}, f32[1024]{0:T(1024)}, u32[]{:S(2)}) copy-start(f32[1024]{0:T(1024)} %copy-done.40) | copy-start | bytes 12292
  955.4 82.1 %copy-start.36 = (f32[1024]{0:T(1024)S(1)}, f32[1024]{0:T(1024)}, u32[]{:S(2)}) copy-start(f32[1024]{0:T(1024)} %get-tuple-element.44) | copy-start | bytes 12292
  955.9 1205.4 %copy-start.43 = (f32[1024]{0:T(1024)S(1)}, f32[1024]{0:T(1024)}, u32[]{:S(2)}) copy-start(f32[1024]{0:T(1024)} %copy-done.42) | copy-start | bytes 12292
  (11 other events, 10.8 us)
Sparse Core Ops, SparseCore 0:
  752.1 700.8 reduce-scatter.8
  1455.7 703.6 reduce-scatter.6
  2162.0 28.2 all-reduce.6
where the time goes:
time: 2200 us
  waiting for transfers between devices  1160 us (53%)
  blocking collectives  904 us (41%)
  other arithmetic  35.4 us (2%)
  local copies, waits for them, and re-layouts  34.5 us (2%)
  matrix products  33.1 us (2%)
  starting transfers between devices  22 us (1%)
    unnamed x5, waiting for transfers between devices  1120 us
    psum x4, blocking collectives, normalise(): middle_tap = lax.psum(jnp.sum(values, axis=0), ('dp', 'seq')) / count_all  306 us
    psum x4, blocking collectives, normalise_back(): lax.psum((jnp.sum(upstream, axis=0), jnp.sum(upstream * normed, axis=0)),...  303 us
    psum x4, blocking collectives, normalise(): lax.psum(jnp.sum(shifted * shifted, axis=0), ('dp', 'seq')) / count_all  296 us
  transfers between devices with their start and end apart: 11, of which 6 were waited for; matrix products, arithmetic and copies ran while one was open for 2% of the time, Pallas kernels for 0%

commit v1 on v0

v1 whole, which is shorter than its diff:
```python
import jax
import jax.numpy as jnp
from jax import lax
from jax.sharding import Mesh, PartitionSpec as P

LAYERS = 2
FIRST_DILATION = 64
SECOND_DILATION = 512
EPSILON = 1e-05

SIZES = {"dp": 2, "y": 4, "x": 4, "z": 8}
SEQ = ("y", "x", "z")
STAGES = (("dp", "z"), ("y", "x"))
F32 = jnp.float32
BF16 = jnp.bfloat16


def size_of(axes):
    total = 1
    for name in (axes if isinstance(axes, tuple) else (axes,)):
        total *= SIZES[name]
    return total


def shared(value, axes):
    count = size_of(axes)
    return lax.all_to_all(
        jnp.broadcast_to(value[None], (count,) + value.shape), axes, 0, 0, tiled=True
    )


def total_over_all(first, second):
    width = first.shape[0]
    both = jnp.concatenate([first, second])
    for axes in STAGES:
        both = jnp.sum(shared(both, axes), axis=0)
    return both[:width], both[width:]


def moments_over_all(values):
    rows, width = values.shape
    mean = jnp.mean(values, axis=0)
    centred = values - mean
    square = jnp.mean(centred * centred, axis=0)
    for axes in STAGES:
        parts = shared(jnp.concatenate([mean, square]), axes)
        means, squares = parts[:, :width], parts[:, width:]
        mean = jnp.mean(means, axis=0)
        offset = means - mean
        square = jnp.mean(squares + offset * offset, axis=0)
    return mean, square


def gelu_slope(values):
    return jax.jvp(
        lambda argument: jax.nn.gelu(argument, approximate=True),
        (values,),
        (jnp.ones_like(values),),
    )


def normalise(values, norm_gain, norm_bias):
    mean, spread = moments_over_all(values)
    factor = lax.rsqrt(spread + EPSILON)
    normed = (values - mean) * factor
    return (normed, factor, normed * norm_gain + norm_bias)


def normalise_back(upstream, normed, factor, norm_gain, count_all):
    total_sum, cross_sum = total_over_all(
        jnp.sum(upstream, axis=0), jnp.sum(upstream * normed, axis=0)
    )
    result = (
        norm_gain * factor * (upstream - total_sum / count_all - normed * cross_sum / count_all)
    )
    return (result, cross_sum, total_sum)


def passed_along(value, steps):
    count = size_of(SEQ)
    leading, last = (max(0, -steps), min(count, count - steps))
    return lax.ppermute(value, SEQ, [(source, source + steps) for source in range(leading, last)])


def neighbour_taps(tensor, dilation):
    local_bins = tensor.shape[1]
    device_hops = dilation // local_bins
    return passed_along(tensor, device_hops), passed_along(tensor, -device_hops)


def transposed_product(left_side, right_side):
    return lax.dot_general(
        left_side, right_side, (((1,), (1,)), ((), ())), preferred_element_type=F32
    )


def column_product(left_side, right_side):
    return lax.dot_general(
        left_side, right_side, (((0,), (0,)), ((), ())), preferred_element_type=F32
    )


def row_share(left_side, right_side):
    half = right_side.shape[1] // 2
    place = lax.axis_index("dp")
    kept = lax.dynamic_slice_in_dim(right_side, place * half, half, 1)
    given = lax.dynamic_slice_in_dim(right_side, (1 - place) * half, half, 1)
    swap = [(0, 1), (1, 0)]
    arrived = lax.ppermute(column_product(left_side, given).astype(BF16), "dp", swap)
    part = (column_product(left_side, kept) + arrived.astype(F32)).astype(BF16)
    for axes in (("y", "x"), "z"):
        count = size_of(axes)
        part = part.reshape(count, part.shape[0] // count, half)
        part = lax.all_to_all(part, axes, 0, 0, tiled=True)
        part = jnp.sum(part.astype(F32), axis=0)
        if axes != "z":
            part = part.astype(BF16)
    other = lax.ppermute(part, "dp", swap)
    lower = jnp.where(place == 0, part, other)
    upper = jnp.where(place == 0, other, part)
    return jnp.concatenate([lower, upper], axis=1)


def on_device(
    activations,
    segment_ids,
    interval_bounds,
    conv_weight,
    proj_weight,
    gains_in,
    biases_in,
    gains_mid,
    biases_mid,
    cotangent,
):
    windows, local_bins, channels = activations.shape
    hidden_width = proj_weight.shape[2]
    local_rows = windows * local_bins
    count_all = float(local_rows * size_of(("dp",) + SEQ))
    dilation_list = (FIRST_DILATION, SECOND_DILATION)
    position = lax.axis_index(SEQ) * local_bins + jnp.arange(local_bins, dtype=jnp.int32)[None, :]
    labels = jnp.arange(interval_bounds.shape[1] - 1, dtype=jnp.int32)
    matches = segment_ids[:, :, None] == labels[None, None, :]
    starts = jnp.sum(jnp.where(matches, interval_bounds[:, None, :-1], 0), axis=2)
    finishes = jnp.sum(jnp.where(matches, interval_bounds[:, None, 1:], 0), axis=2)
    stream = activations
    caches = []
    for layer_index in range(LAYERS):
        dilation = dilation_list[layer_index]
        mask_before = (starts <= position - dilation).astype(BF16)[:, :, None]
        mask_after = (position + dilation < finishes).astype(BF16)[:, :, None]
        kernel = conv_weight[layer_index]
        project = proj_weight[layer_index]
        flattened_rows = stream.reshape(local_rows, channels).astype(F32)
        normed_in, factor_in, preact_in = normalise(
            flattened_rows, gains_in[layer_index], biases_in[layer_index]
        )
        active_in, slope_in = gelu_slope(preact_in)
        centre_taps = active_in.astype(BF16)
        lower_taps, upper_taps = neighbour_taps(
            centre_taps.reshape(windows, local_bins, channels), dilation
        )
        before_taps = (lower_taps * mask_before).reshape(local_rows, channels)
        after_taps = (upper_taps * mask_after).reshape(local_rows, channels)
        conv_out = jnp.dot(
            centre_taps,
            kernel[:, hidden_width : 2 * hidden_width],
            preferred_element_type=F32,
        )
        conv_out = conv_out + jnp.dot(
            before_taps, kernel[:, :hidden_width], preferred_element_type=F32
        )
        conv_out = conv_out + jnp.dot(
            after_taps, kernel[:, 2 * hidden_width :], preferred_element_type=F32
        )
        normed_mid, factor_mid, preact_mid = normalise(
            conv_out, gains_mid[layer_index], biases_mid[layer_index]
        )
        middle_activation, slope_mid = gelu_slope(preact_mid)
        hidden = middle_activation.astype(BF16)
        branch = transposed_product(hidden, project)
        stream = (flattened_rows + branch).astype(BF16).reshape(windows, local_bins, channels)
        caches.append(
            (
                mask_before,
                mask_after,
                normed_in,
                factor_in,
                slope_in,
                centre_taps,
                normed_mid,
                factor_mid,
                slope_mid,
                hidden,
            )
        )
    grad_stream = cotangent
    kernel_grads = []
    project_grads = []
    gain_in_grads = []
    bias_in_grads = []
    gain_mid_grads = []
    bias_mid_grads = []
    for layer_index in range(LAYERS - 1, -1, -1):
        dilation = dilation_list[layer_index]
        (
            mask_before,
            mask_after,
            normed_in,
            factor_in,
            slope_in,
            centre_taps,
            normed_mid,
            factor_mid,
            slope_mid,
            hidden,
        ) = caches[layer_index]
        kernel = conv_weight[layer_index]
        project = proj_weight[layer_index]
        upstream = grad_stream.reshape(local_rows, channels)
        grad_hidden = jnp.dot(upstream, project, preferred_element_type=F32)
        project_grads.append(row_share(upstream, hidden))
        grad_preact_mid = grad_hidden * slope_mid
        grad_conv_f, gain_mid_grad, bias_mid_grad = normalise_back(
            grad_preact_mid, normed_mid, factor_mid, gains_mid[layer_index], count_all
        )
        grad_conv_out = grad_conv_f.astype(BF16)
        lower_grad, upper_grad = neighbour_taps(
            grad_conv_out.reshape(windows, local_bins, hidden_width), dilation
        )
        grad_before = (lower_grad * mask_before).reshape(local_rows, hidden_width)
        grad_after = (upper_grad * mask_after).reshape(local_rows, hidden_width)
        grad_three = jnp.concatenate([grad_after, grad_conv_out, grad_before], axis=1)
        grad_taps = transposed_product(grad_three, kernel)
        kernel_grads.append(row_share(centre_taps, grad_three))
        grad_preact_in = grad_taps * slope_in
        grad_branch, gain_in_grad, bias_in_grad = normalise_back(
            grad_preact_in, normed_in, factor_in, gains_in[layer_index], count_all
        )
        grad_stream = (
            (upstream.astype(F32) + grad_branch)
            .astype(BF16)
            .reshape(windows, local_bins, channels)
        )
        gain_in_grads.append(gain_in_grad)
        bias_in_grads.append(bias_in_grad)
        gain_mid_grads.append(gain_mid_grad)
        bias_mid_grads.append(bias_mid_grad)
    return (
        stream,
        grad_stream,
        jnp.stack(kernel_grads[::-1]),
        jnp.stack(project_grads[::-1]),
        jnp.stack(gain_in_grads[::-1]),
        jnp.stack(bias_in_grads[::-1]),
        jnp.stack(gain_mid_grads[::-1]),
        jnp.stack(bias_mid_grads[::-1]),
    )


def solution(mesh):
    sizes = tuple(SIZES.values())
    split = Mesh(mesh.devices.reshape(sizes), tuple(SIZES))
    in_specs = (
        P("dp", SEQ, None),
        P("dp", SEQ),
        P("dp", None),
        P(),
        P(),
        P(),
        P(),
        P(),
        P(),
        P("dp", SEQ, None),
    )
    out_specs = (
        P("dp", SEQ, None),
        P("dp", SEQ, None),
        P(None, SEQ, None),
        P(None, SEQ, None),
        P(),
        P(),
        P(),
        P(),
    )
    return jax.shard_map(
        on_device, mesh=split, in_specs=in_specs, out_specs=out_specs, check_vma=False
    )
```

time: 2200 us -> 405 us (0.18)
  waiting for transfers between devices: 1160 us -> 125 us
  blocking collectives: 904 us -> 84.5 us
  starting transfers between devices: 22 us -> 113 us
    unnamed x5 -> x0, waiting for transfers between devices: 1120 us -> none
    psum x12 -> x0, blocking collectives: 904 us -> none  [the longest x4 306 us: normalise(): middle_tap = lax.psum(jnp.sum(values, axis=0), ('dp', 'seq')) / count_all]
    all_to_all x0 -> x17, waiting for transfers between devices: none -> 109 us  [the longest x9 55.2 us: shared(): lax.all_to_all(jnp.broadcast_to(value[None], (count,) + value.shape), axe...]
    all_to_all x0 -> x17, starting transfers between devices: none -> 90.3 us  [the longest x9 58 us: shared(): lax.all_to_all(jnp.broadcast_to(value[None], (count,) + value.shape), axe...]
    all_to_all x0 -> x7, blocking collectives: none -> 84.5 us  [shared(): lax.all_to_all(jnp.broadcast_to(value[None], (count,) + value.shape), axe...]
    psum x1 -> x0, waiting for transfers between devices: 28.4 us -> none  [on_device(): lax.psum(row_share.astype(jnp.bfloat16), 'dp').astype(jnp.float32)]
    unnamed x132 -> x68, local copies, waits for them, and re-layouts: 26.4 us -> 1.02 us
  transfers between devices with their start and end apart: 11 -> 33, of which waited for: 6 -> 22; matrix products, arithmetic and copies ran while one was open for 2% -> 15% of each run, Pallas kernels for 0% -> 0%
where the time goes in v1:
time: 405 us; the launch traced here: 400 us
  waiting for transfers between devices  125 us (31%)
  starting transfers between devices  113 us (28%)
  blocking collectives  84.5 us (21%)
  matrix products  33.2 us (8%)
  other arithmetic  27.7 us (7%)
  local copies, waits for them, and re-layouts  15.1 us (4%)
    all_to_all x7, blocking collectives, shared(): lax.all_to_all(jnp.broadcast_to(value[None], (count,) + value.shape), axe...  84.5 us
    all_to_all x9, starting transfers between devices, shared(): lax.all_to_all(jnp.broadcast_to(value[None], (count,) + value.shape), axe...  58 us
    all_to_all x9, waiting for transfers between devices, shared(): lax.all_to_all(jnp.broadcast_to(value[None], (count,) + value.shape), axe...  55.2 us
    all_to_all x8, waiting for transfers between devices, row_share(): part = lax.all_to_all(part, axes, 0, 0, tiled=True)  53.6 us
    all_to_all x8, starting transfers between devices, row_share(): part = lax.all_to_all(part, axes, 0, 0, tiled=True)  32.4 us
    ppermute x8, starting transfers between devices, passed_along(): lax.ppermute(value, SEQ, [(source, source + steps) for source in range(le...  21.3 us
    dot_general x8, matrix products, column_product(): lax.dot_general(left_side, right_side, (((0,), (0,)), ((), ())), preferre...  15.8 us
    ppermute x8, waiting for transfers between devices, passed_along(): lax.ppermute(value, SEQ, [(source, source + steps) for source in range(le...  14.2 us
  transfers between devices with their start and end apart: 33, of which 22 were waited for; matrix products, arithmetic and copies ran while one was open for 15% of the time, Pallas kernels for 0%

profile of v1, /device:TPU:32, one launch (start us, length us, event | category | flops | bytes accessed | tf_op | source)
XLA Modules:
  0.0 399.8 jit_solution(8958712764797501013)
XLA Ops:
  3.4 8.6 %all-to-all-start = ((f32[16,1,2048]{2,1,0:T(1,128)}), f32[16,1,2048]{2,1,0:T(1,128)S(1)}, u32[]{:S(2)}, u32[]{:S(2)}) async-start(f32[16,1,2048]{2,1,0:T(1,128)} %broadcast_in_dim.58), calls=%async_computation | async-start | bytes 262144 | tf_op jit(solution)/shard_map/all_to_all | solution.py:27
  13.9 5.0 %slice_bitcast_fusion = (bf16[1024,1536]{1,0:T(8,128)(2,1)}, bf16[1024,1536]{1,0:T(8,128)(2,1)S(1)}) fusion(bf16[2,1024,1536]{2,1,0:T(8,128)(2,1)} %param.13), kind=kLoop, calls=%fused_computation.2 | loop fusion | bytes 12582912 | tf_op jit(solution)/shard_map/squeeze | solution.py:152
  21.6 7.0 %all-to-all-start.1 = ((f32[16,1,2048]{2,1,0:T(1,128)}), f32[16,1,2048]{2,1,0:T(1,128)S(1)}, u32[]{:S(2)}, u32[]{:S(2)}) async-start(f32[16,1,2048]{2,1,0:T(1,128)} %broadcast_in_dim.59), calls=%async_computation.1 | async-start | bytes 262144 | tf_op jit(solution)/shard_map/all_to_all | solution.py:27
  29.9 6.7 %all-to-all-done.1 = f32[16,1,2048]{2,1,0:T(1,128)S(1)} async-done(((f32[16,1,2048]{2,1,0:T(1,128)}), f32[16,1,2048]{2,1,0:T(1,128)S(1)}, u32[]{:S(2)}, u32[]{:S(2)}) %all-to-all-start.1) | async-done | bytes 131104 | tf_op jit(solution)/shard_map/all_to_all | solution.py:27
  37.0 2.0 collective-permute-start.1
  39.1 3.8 collective-permute-start
  44.3 3.6 collective-permute-done
  50.3 15.4 %all_to_all.160 = f32[16,1,1024]{2,1,0:T(1,128)S(1)} all-to-all(f32[16,1,1024]{2,1,0:T(1,128)S(1)} %broadcast_in_dim.63), channel_id=1, replica_groups=mesh['dp'=2,'y'=4,'x'=4,'z'=8] {'dp','z'}, dimensions={0} | all-to-all | bytes 131072 | tf_op jit(solution)/shard_map/all_to_all | solution.py:27
  66.4 5.0 %all-to-all-start.3 = ((f32[16,1,1024]{2,1,0:T(1,128)}), f32[16,1,1024]{2,1,0:T(1,128)S(1)}, u32[]{:S(2)}, u32[]{:S(2)}) async-start(f32[16,1,1024]{2,1,0:T(1,128)} %broadcast_in_dim.64), calls=%async_computation.3 | async-start | bytes 131072 | tf_op jit(solution)/shard_map/all_to_all | solution.py:27
  71.4 7.6 %all-to-all-done.3 = f32[16,1,1024]{2,1,0:T(1,128)S(1)} async-done(((f32[16,1,1024]{2,1,0:T(1,128)}), f32[16,1,1024]{2,1,0:T(1,128)S(1)}, u32[]{:S(2)}, u32[]{:S(2)}) %all-to-all-start.3) | async-done | bytes 65568 | tf_op jit(solution)/shard_map/all_to_all | solution.py:27
  80.2 1.7 fusion.135
  82.1 11.9 %all_to_all.161 = f32[16,1,2048]{2,1,0:T(1,128)S(1)} all-to-all(f32[16,1,2048]{2,1,0:T(1,128)S(1)} %broadcast_in_dim.65), channel_id=1, replica_groups=mesh['dp'=2,'y'=4,'x'=4,'z'=8] {'dp','z'}, dimensions={0} | all-to-all | bytes 262144 | tf_op jit(solution)/shard_map/all_to_all | solution.py:27
  94.2 11.1 %all_to_all.162 = f32[16,1,2048]{2,1,0:T(1,128)S(1)} all-to-all(f32[16,1,2048]{2,1,0:T(1,128)S(1)} %broadcast_in_dim.66), channel_id=1, replica_groups=mesh['dp'=2,'y'=4,'x'=4,'z'=8] {'y','x'}, dimensions={0} | all-to-all | bytes 262144 | tf_op jit(solution)/shard_map/all_to_all | solution.py:27
  106.3 1.3 collective-permute-start.3
  107.6 4.6 %collective-permute-start.2 = (bf16[2,64,1024]{2,1,0:T(8,128)(2,1)S(1)}, bf16[2,64,1024]{2,1,0:T(8,128)(2,1)S(1)}, u32[]{:S(2)}, u32[]{:S(2)}) collective-permute-start(bf16[2,64,1024]{2,1,0:T(8,128)(2,1)S(1)} %bitcast.162), channel_id=1, source_target_pairs={{0,8},{1,9},{2,10},{3,11},{4,12},{5,13},{6,14},{7,15},{8,16},{9,17... | collective-permute-start | bytes 786440 | tf_op jit(solution)/shard_map/ppermute | solution.py:82
  112.2 1.5 fusion.6
  113.8 2.3 collective-permute-done.2
  117.1 10.4 %all_to_all.163 = f32[16,1,1024]{2,1,0:T(1,128)S(1)} all-to-all(f32[16,1,1024]{2,1,0:T(1,128)S(1)} %broadcast_in_dim.67), channel_id=1, replica_groups=mesh['dp'=2,'y'=4,'x'=4,'z'=8] {'dp','z'}, dimensions={0} | all-to-all | bytes 131072 | tf_op jit(solution)/shard_map/all_to_all | solution.py:27
  127.6 14.4 %all_to_all.164 = f32[16,1,1024]{2,1,0:T(1,128)S(1)} all-to-all(f32[16,1,1024]{2,1,0:T(1,128)S(1)} %broadcast_in_dim.68), channel_id=1, replica_groups=mesh['dp'=2,'y'=4,'x'=4,'z'=8] {'y','x'}, dimensions={0} | all-to-all | bytes 131072 | tf_op jit(solution)/shard_map/all_to_all | solution.py:27
  142.6 10.5 %all_to_all.165 = f32[16,1,1024]{2,1,0:T(1,128)S(1)} all-to-all(f32[16,1,1024]{2,1,0:T(1,128)S(1)} %broadcast_in_dim.69), channel_id=1, replica_groups=mesh['dp'=2,'y'=4,'x'=4,'z'=8] {'dp','z'}, dimensions={0} | all-to-all | bytes 131072 | tf_op jit(solution)/shard_map/all_to_all | solution.py:27
  153.2 10.8 %all_to_all.166 = f32[16,1,1024]{2,1,0:T(1,128)S(1)} all-to-all(f32[16,1,1024]{2,1,0:T(1,128)S(1)} %broadcast_in_dim.70), channel_id=1, replica_groups=mesh['dp'=2,'y'=4,'x'=4,'z'=8] {'y','x'}, dimensions={0} | all-to-all | bytes 131072 | tf_op jit(solution)/shard_map/all_to_all | solution.py:27
  164.8 2.5 collective-permute-start.5
  169.9 4.3 %collective-permute-done.4 = bf16[2,64,512]{2,1,0:T(8,128)(2,1)S(1)} collective-permute-done((bf16[2,64,512]{2,1,0:T(8,128)(2,1)S(1)}, bf16[2,64,512]{2,1,0:T(8,128)(2,1)S(1)}, u32[]{:S(2)}, u32[]{:S(2)}) %collective-permute-start.4) | collective-permute-done | bytes 131104 | tf_op jit(solution)/shard_map/ppermute | solution.py:82
  174.3 3.2 fusion.124
  178.2 4.4 %all-to-all-start.10 = ((f32[16,1,2048]{2,1,0:T(1,128)}), f32[16,1,2048]{2,1,0:T(1,128)S(1)}, u32[]{:S(2)}, u32[]{:S(2)}) async-start(f32[16,1,2048]{2,1,0:T(1,128)} %broadcast_in_dim.71), calls=%async_computation.10 | async-start | bytes 262144 | tf_op jit(solution)/shard_map/all_to_all | solution.py:27
  183.9 7.0 %all-to-all-done.10 = f32[16,1,2048]{2,1,0:T(1,128)S(1)} async-done(((f32[16,1,2048]{2,1,0:T(1,128)}), f32[16,1,2048]{2,1,0:T(1,128)S(1)}, u32[]{:S(2)}, u32[]{:S(2)}) %all-to-all-start.10) | async-done | bytes 131104 | tf_op jit(solution)/shard_map/all_to_all | solution.py:27
  191.7 7.6 %all-to-all-start.11 = ((f32[16,1,2048]{2,1,0:T(1,128)}), f32[16,1,2048]{2,1,0:T(1,128)S(1)}, u32[]{:S(2)}, u32[]{:S(2)}) async-start(f32[16,1,2048]{2,1,0:T(1,128)} %broadcast_in_dim.72), calls=%async_computation.11 | async-start | bytes 262144 | tf_op jit(solution)/shard_map/all_to_all | solution.py:27
  199.3 7.9 %all-to-all-done.11 = f32[16,1,2048]{2,1,0:T(1,128)S(1)} async-done(((f32[16,1,2048]{2,1,0:T(1,128)}), f32[16,1,2048]{2,1,0:T(1,128)S(1)}, u32[]{:S(2)}, u32[]{:S(2)}) %all-to-all-start.11) | async-done | bytes 131104 | tf_op jit(solution)/shard_map/all_to_all | solution.py:27
  208.2 2.4 fusion.125
  211.2 3.9 all-to-all-start.12
  215.1 1.8 convolution_convert_fusion
  217.0 5.1 %all-to-all-done.12 = f32[16,1,1024]{2,1,0:T(1,128)S(1)} async-done(((f32[16,1,1024]{2,1,0:T(1,128)}), f32[16,1,1024]{2,1,0:T(1,128)S(1)}, u32[]{:S(2)}, u32[]{:S(2)}) %all-to-all-start.12) | async-done | bytes 65568 | tf_op jit(solution)/shard_map/all_to_all | solution.py:27
  222.8 3.5 all-to-all-start.13
  227.5 6.5 %all-to-all-done.13 = f32[16,1,1024]{2,1,0:T(1,128)S(1)} async-done(((f32[16,1,1024]{2,1,0:T(1,128)}), f32[16,1,1024]{2,1,0:T(1,128)S(1)}, u32[]{:S(2)}, u32[]{:S(2)}) %all-to-all-start.13) | async-done | bytes 65568 | tf_op jit(solution)/shard_map/all_to_all | solution.py:27
  235.6 2.5 collective-permute-start.7
  238.2 1.4 add_convert_fusion.2
  240.6 3.6 all-to-all-start.22
  244.1 3.3 collective-permute-start.6
  248.2 2.8 collective-permute-done.6
  251.8 4.1 %fusion.123 = (f32[1024]{0:T(1024)S(1)}, f32[1024]{0:T(1024)S(1)}, f32[128,1024]{1,0:T(8,128)}) fusion(f32[1024]{0:T(1024)S(1)} %add_rsqrt_fusion.1, f32[1024]{0:T(1024)S(1)} %broadcast_multiply_fusion.13, bf16[2,64,1024]{2,1,0:T(8,128)(2,1)S(1)} %copy-done, f32[128,1024]{1,0:T(8,128)} %get-tuple-element.20, bf16[2,1024,1536]{2,1,0:T(8,128)(2,1)} %param.13, ...), kind=kOutput, calls=%fused_computation.276 | convolution fusion | flops 406845440 | bytes 4866048 | tf_op jit(solution)/shard_map/dot_general | solution.py:92
  256.7 9.1 %all-to-all-start.14 = ((f32[16,1,2048]{2,1,0:T(1,128)}), f32[16,1,2048]{2,1,0:T(1,128)S(1)}, u32[]{:S(2)}, u32[]{:S(2)}) async-start(f32[16,1,2048]{2,1,0:T(1,128)} %broadcast_in_dim.75), calls=%async_computation.14 | async-start | bytes 262144 | tf_op jit(solution)/shard_map/all_to_all | solution.py:27
  266.5 7.5 %all-to-all-done.14 = f32[16,1,2048]{2,1,0:T(1,128)S(1)} async-done(((f32[16,1,2048]{2,1,0:T(1,128)}), f32[16,1,2048]{2,1,0:T(1,128)S(1)}, u32[]{:S(2)}, u32[]{:S(2)}) %all-to-all-start.14) | async-done | bytes 131104 | tf_op jit(solution)/shard_map/all_to_all | solution.py:27
  274.0 3.6 all-to-all-start.23
  277.7 6.5 %all-to-all-done.23 = bf16[8,8,256]{2,1,0:T(8,128)(2,1)S(1)} async-done(((bf16[8,8,256]{2,1,0:T(8,128)(2,1)}), bf16[8,8,256]{2,1,0:T(8,128)(2,1)S(1)}, u32[]{:S(2)}, u32[]{:S(2)}) %all-to-all-start.23) | async-done | bytes 32800 | tf_op jit(solution)/shard_map/all_to_all | solution.py:114
  284.9 8.9 %all-to-all-start.15 = ((f32[16,1,2048]{2,1,0:T(1,128)}), f32[16,1,2048]{2,1,0:T(1,128)S(1)}, u32[]{:S(2)}, u32[]{:S(2)}) async-start(f32[16,1,2048]{2,1,0:T(1,128)} %broadcast_in_dim.76), calls=%async_computation.15 | async-start | bytes 262144 | tf_op jit(solution)/shard_map/all_to_all | solution.py:27
  295.0 6.8 %all-to-all-done.15 = f32[16,1,2048]{2,1,0:T(1,128)S(1)} async-done(((f32[16,1,2048]{2,1,0:T(1,128)}), f32[16,1,2048]{2,1,0:T(1,128)S(1)}, u32[]{:S(2)}, u32[]{:S(2)}) %all-to-all-start.15) | async-done | bytes 131104 | tf_op jit(solution)/shard_map/all_to_all | solution.py:27
  301.8 3.6 all-to-all-start.20
  305.4 1.8 pad_maximum_fusion.1
  307.3 3.2 add_convert_fusion
  310.5 5.0 %all-to-all-done.20 = bf16[16,64,256]{2,1,0:T(8,128)(2,1)S(1)} async-done(((bf16[16,64,256]{2,1,0:T(8,128)(2,1)}), bf16[16,64,256]{2,1,0:T(8,128)(2,1)S(1)}, u32[]{:S(2)}, u32[]{:S(2)}) %all-to-all-start.20) | async-done | bytes 524320 | tf_op jit(solution)/shard_map/all_to_all | solution.py:114
  315.5 3.7 all-to-all-start.18
  319.2 2.7 convolution_convert_fusion.1
  322.0 2.4 fusion.3
  324.4 1.3 pad_maximum_fusion.19
  328.9 11.0 %all-to-all-done.18 = bf16[16,64,768]{2,1,0:T(8,128)(2,1)S(1)} async-done(((bf16[16,64,768]{2,1,0:T(8,128)(2,1)}), bf16[16,64,768]{2,1,0:T(8,128)(2,1)S(1)}, u32[]{:S(2)}, u32[]{:S(2)}) %all-to-all-start.18) | async-done | bytes 1572896 | tf_op jit(solution)/shard_map/all_to_all | solution.py:114
  339.9 4.7 %all-to-all-start.21 = ((bf16[8,8,256]{2,1,0:T(8,128)(2,1)}), bf16[8,8,256]{2,1,0:T(8,128)(2,1)S(1)}, u32[]{:S(2)}, u32[]{:S(2)}) async-start(bf16[8,8,256]{2,1,0:T(8,128)(2,1)} %bitcast.42), calls=%async_computation.21 | async-start | bytes 65536 | tf_op jit(solution)/shard_map/all_to_all | solution.py:114
  345.5 5.7 %all-to-all-done.21 = bf16[8,8,256]{2,1,0:T(8,128)(2,1)S(1)} async-done(((bf16[8,8,256]{2,1,0:T(8,128)(2,1)}), bf16[8,8,256]{2,1,0:T(8,128)(2,1)S(1)}, u32[]{:S(2)}, u32[]{:S(2)}) %all-to-all-start.21) | async-done | bytes 32800 | tf_op jit(solution)/shard_map/all_to_all | solution.py:114
  351.2 4.8 %all-to-all-start.19 = ((bf16[8,8,768]{2,1,0:T(8,128)(2,1)}), bf16[8,8,768]{2,1,0:T(8,128)(2,1)S(1)}, u32[]{:S(2)}, u32[]{:S(2)}) async-start(bf16[8,8,768]{2,1,0:T(8,128)(2,1)} %bitcast.39), calls=%async_computation.19 | async-start | bytes 196608 | tf_op jit(solution)/shard_map/all_to_all | solution.py:114
  356.1 3.3 add_convert_fusion.1
  359.4 3.9 all-to-all-done.19
  363.3 3.7 all-to-all-start.16
  370.9 14.1 %all-to-all-done.16 = bf16[16,64,768]{2,1,0:T(8,128)(2,1)S(1)} async-done(((bf16[16,64,768]{2,1,0:T(8,128)(2,1)}), bf16[16,64,768]{2,1,0:T(8,128)(2,1)S(1)}, u32[]{:S(2)}, u32[]{:S(2)}) %all-to-all-start.16) | async-done | bytes 1572896 | tf_op jit(solution)/shard_map/all_to_all | solution.py:114
  385.8 4.7 %all-to-all-start.17 = ((bf16[8,8,768]{2,1,0:T(8,128)(2,1)}), bf16[8,8,768]{2,1,0:T(8,128)(2,1)S(1)}, u32[]{:S(2)}, u32[]{:S(2)}) async-start(bf16[8,8,768]{2,1,0:T(8,128)(2,1)} %bitcast.36), calls=%async_computation.17 | async-start | bytes 196608 | tf_op jit(solution)/shard_map/all_to_all | solution.py:114
  390.5 7.3 %all-to-all-done.17 = bf16[8,8,768]{2,1,0:T(8,128)(2,1)S(1)} async-done(((bf16[8,8,768]{2,1,0:T(8,128)(2,1)}), bf16[8,8,768]{2,1,0:T(8,128)(2,1)S(1)}, u32[]{:S(2)}, u32[]{:S(2)}) %all-to-all-start.17) | async-done | bytes 98336 | tf_op jit(solution)/shard_map/all_to_all | solution.py:114
  (236 shorter events, 45.6 us)
Async XLA Ops:
  3.4 17.3 %all-to-all-start = ((f32[16,1,2048]{2,1,0:T(1,128)}), f32[16,1,2048]{2,1,0:T(1,128)S(1)}, u32[]{:S(2)}, u32[]{:S(2)}) async-start(f32[16,1,2048]{2,1,0:T(1,128)} %broadcast_in_dim.58), calls=%async_computation | async-start | bytes 262144 | tf_op jit(solution)/shard_map/all_to_all | solution.py:27
  13.9 5.0 %copy-start.29 = (s32[2,64]{1,0:T(2,128)S(1)}, s32[2,64]{1,0:T(2,128)}, u32[]{:S(2)}) copy-start(s32[2,64]{1,0:T(2,128)} %param.11) | copy-start | bytes 1540
  13.9 6.3 %copy-start.18 = (f32[2,1024]{1,0:T(2,128)S(1)}, f32[2,1024]{1,0:T(2,128)}, u32[]{:S(2)}) copy-start(f32[2,1024]{1,0:T(2,128)} %param.15) | copy-start | bytes 24580
  13.9 6.3 %copy-start.24 = (f32[2,1024]{1,0:T(2,128)S(1)}, f32[2,1024]{1,0:T(2,128)}, u32[]{:S(2)}) copy-start(f32[2,1024]{1,0:T(2,128)} %param.16) | copy-start | bytes 24580
  13.9 22.9 %copy-start = (bf16[2,64,1024]{2,1,0:T(8,128)(2,1)S(1)}, bf16[2,64,1024]{2,1,0:T(8,128)(2,1)}, u32[]{:S(2)}) copy-start(bf16[2,64,1024]{2,1,0:T(8,128)(2,1)} %param.10) | copy-start | bytes 786436
  21.6 15.0 %all-to-all-start.1 = ((f32[16,1,2048]{2,1,0:T(1,128)}), f32[16,1,2048]{2,1,0:T(1,128)S(1)}, u32[]{:S(2)}, u32[]{:S(2)}) async-start(f32[16,1,2048]{2,1,0:T(1,128)} %broadcast_in_dim.59), calls=%async_computation.1 | async-start | bytes 262144 | tf_op jit(solution)/shard_map/all_to_all | solution.py:27
  36.6 11.3 %copy-start.25 = (bf16[2,64]{1,0:T(2,128)(2,1)S(1)}, bf16[2,64]{1,0:T(2,128)(2,1)}, u32[]{:S(2)}) copy-start(bf16[2,64]{1,0:T(2,128)(2,1)} %get-tuple-element.57) | copy-start | bytes 772
  37.0 11.3 %collective-permute-start.1 = (bf16[2,64,1024]{2,1,0:T(8,128)(2,1)S(1)}, bf16[2,64,1024]{2,1,0:T(8,128)(2,1)S(1)}, u32[]{:S(2)}, u32[]{:S(2)}) collective-permute-start(bf16[2,64,1024]{2,1,0:T(8,128)(2,1)S(1)} %fusion.47), channel_id=1, source_target_pairs={{1,0},{2,1},{3,2},{4,3},{5,4},{6,5},{7,6},{8,7},{9,8},{10,9},{11,1... | collective-permute-start | bytes 786440 | tf_op jit(solution)/shard_map/ppermute | solution.py:82
  39.1 8.8 %collective-permute-start = (bf16[2,64,1024]{2,1,0:T(8,128)(2,1)S(1)}, bf16[2,64,1024]{2,1,0:T(8,128)(2,1)S(1)}, u32[]{:S(2)}, u32[]{:S(2)}) collective-permute-start(bf16[2,64,1024]{2,1,0:T(8,128)(2,1)S(1)} %fusion.47), channel_id=1, source_target_pairs={{0,1},{1,2},{2,3},{3,4},{4,5},{5,6},{6,7},{7,8},{8,9},{9,10},{10,1... | collective-permute-start | bytes 786440 | tf_op jit(solution)/shard_map/ppermute | solution.py:82
  43.9 5.2 %copy-start.5 = (bf16[128,1024]{1,0:T(8,128)(2,1)}, bf16[128,1024]{1,0:T(8,128)(2,1)S(1)}, u32[]{:S(2)}) copy-start(bf16[128,1024]{1,0:T(8,128)(2,1)S(1)} %get-tuple-element.21) | copy-start | bytes 786436
  44.3 27.1 %copy-start.28 = (f32[2,512]{1,0:T(2,128)S(1)}, f32[2,512]{1,0:T(2,128)}, u32[]{:S(2)}) copy-start(f32[2,512]{1,0:T(2,128)} %param.18) | copy-start | bytes 12292
  44.3 27.1 %copy-start.23 = (f32[2,512]{1,0:T(2,128)S(1)}, f32[2,512]{1,0:T(2,128)}, u32[]{:S(2)}) copy-start(f32[2,512]{1,0:T(2,128)} %param.17) | copy-start | bytes 12292
  49.5 0.7 copy-start.2
  49.5 56.0 %copy-start.19 = (f32[2,1024]{1,0:T(2,128)S(1)}, f32[2,1024]{1,0:T(2,128)}, u32[]{:S(2)}) copy-start(f32[2,1024]{1,0:T(2,128)} %param.15) | copy-start | bytes 24580
  49.5 56.6 %copy-start.21 = (f32[1,1024]{1,0:T(1,128)S(1)}, f32[1,1024]{1,0:T(1,128)}, u32[]{:S(2)}) copy-start(f32[1,1024]{1,0:T(1,128)} %get-tuple-element.41) | copy-start | bytes 12292
  66.4 12.6 %all-to-all-start.3 = ((f32[16,1,1024]{2,1,0:T(1,128)}), f32[16,1,1024]{2,1,0:T(1,128)S(1)}, u32[]{:S(2)}, u32[]{:S(2)}) async-start(f32[16,1,1024]{2,1,0:T(1,128)} %broadcast_in_dim.64), calls=%async_computation.3 | async-start | bytes 131072 | tf_op jit(solution)/shard_map/all_to_all | solution.py:27
  80.2 35.8 %copy-start.27 = (bf16[2,64]{1,0:T(2,128)(2,1)S(1)}, bf16[2,64]{1,0:T(2,128)(2,1)}, u32[]{:S(2)}) copy-start(bf16[2,64]{1,0:T(2,128)(2,1)} %get-tuple-element.56) | copy-start | bytes 772
  82.0 34.2 %copy-start.1 = (bf16[1024,1536]{1,0:T(8,128)(2,1)S(1)}, bf16[1024,1536]{1,0:T(8,128)(2,1)}, u32[]{:S(2)}) copy-start(bf16[1024,1536]{1,0:T(8,128)(2,1)} %get-tuple-element.18) | copy-start | bytes 9437188
  94.0 22.5 %copy-start.26 = (bf16[2,64]{1,0:T(2,128)(2,1)S(1)}, bf16[2,64]{1,0:T(2,128)(2,1)}, u32[]{:S(2)}) copy-start(bf16[2,64]{1,0:T(2,128)(2,1)} %get-tuple-element.54) | copy-start | bytes 772
  106.3 10.2 %collective-permute-start.3 = (bf16[2,64,1024]{2,1,0:T(8,128)(2,1)S(1)}, bf16[2,64,1024]{2,1,0:T(8,128)(2,1)S(1)}, u32[]{:S(2)}, u32[]{:S(2)}) collective-permute-start(bf16[2,64,1024]{2,1,0:T(8,128)(2,1)S(1)} %bitcast.161), channel_id=1, source_target_pairs={{8,0},{9,1},{10,2},{11,3},{12,4},{13,5},{14,6},{15,7},{16,8},{17,9... | collective-permute-start | bytes 786440 | tf_op jit(solution)/shard_map/ppermute | solution.py:82
  107.6 8.4 %collective-permute-start.2 = (bf16[2,64,1024]{2,1,0:T(8,128)(2,1)S(1)}, bf16[2,64,1024]{2,1,0:T(8,128)(2,1)S(1)}, u32[]{:S(2)}, u32[]{:S(2)}) collective-permute-start(bf16[2,64,1024]{2,1,0:T(8,128)(2,1)S(1)} %bitcast.162), channel_id=1, source_target_pairs={{0,8},{1,9},{2,10},{3,11},{4,12},{5,13},{6,14},{7,15},{8,16},{9,17... | collective-permute-start | bytes 786440 | tf_op jit(solution)/shard_map/ppermute | solution.py:82
  113.7 28.4 %copy-start.4 = (bf16[2,64,1024]{2,1,0:T(8,128)(2,1)S(1)}, bf16[2,64,1024]{2,1,0:T(8,128)(2,1)}, u32[]{:S(2)}) copy-start(bf16[2,64,1024]{2,1,0:T(8,128)(2,1)} %param.19) | copy-start | bytes 786436
  113.7 28.4 %copy-start.7 = (bf16[2,1024,512]{2,1,0:T(8,128)(2,1)S(1)}, bf16[2,1024,512]{2,1,0:T(8,128)(2,1)}, u32[]{:S(2)}) copy-start(bf16[2,1024,512]{2,1,0:T(8,128)(2,1)} %param.14) | copy-start | bytes 6291460
  164.8 5.0 %collective-permute-start.5 = (bf16[2,64,512]{2,1,0:T(8,128)(2,1)S(1)}, bf16[2,64,512]{2,1,0:T(8,128)(2,1)S(1)}, u32[]{:S(2)}, u32[]{:S(2)}) collective-permute-start(bf16[2,64,512]{2,1,0:T(8,128)(2,1)S(1)} %bitcast.175), channel_id=1, source_target_pairs={{0,8},{1,9},{2,10},{3,11},{4,12},{5,13},{6,14},{7,15},{8,16},{9,17... | collective-permute-start | bytes 393224 | tf_op jit(solution)/shard_map/ppermute | solution.py:82
  167.3 6.9 %collective-permute-start.4 = (bf16[2,64,512]{2,1,0:T(8,128)(2,1)S(1)}, bf16[2,64,512]{2,1,0:T(8,128)(2,1)S(1)}, u32[]{:S(2)}, u32[]{:S(2)}) collective-permute-start(bf16[2,64,512]{2,1,0:T(8,128)(2,1)S(1)} %bitcast.176), channel_id=1, source_target_pairs={{8,0},{9,1},{10,2},{11,3},{12,4},{13,5},{14,6},{15,7},{16,8},{17,9... | collective-permute-start | bytes 393224 | tf_op jit(solution)/shard_map/ppermute | solution.py:82
  177.5 30.7 %copy-start.3 = (f32[128,512]{1,0:T(8,128)S(1)}, f32[128,512]{1,0:T(8,128)}, u32[]{:S(2)}) copy-start(f32[128,512]{1,0:T(8,128)} %copy-done.2) | copy-start | bytes 786436
  178.2 12.6 %all-to-all-start.10 = ((f32[16,1,2048]{2,1,0:T(1,128)}), f32[16,1,2048]{2,1,0:T(1,128)S(1)}, u32[]{:S(2)}, u32[]{:S(2)}) async-start(f32[16,1,2048]{2,1,0:T(1,128)} %broadcast_in_dim.71), calls=%async_computation.10 | async-start | bytes 262144 | tf_op jit(solution)/shard_map/all_to_all | solution.py:27
  183.7 54.4 %collective-permute-start.14 = (bf16[1024,256]{0,1:T(8,128)(2,1)}, bf16[1024,256]{0,1:T(8,128)(2,1)}, u32[]{:S(2)}, u32[]{:S(2)}) collective-permute-start(bf16[1024,256]{0,1:T(8,128)(2,1)} %fusion), channel_id=1, source_target_pairs={{0,128},{128,0},{1,129},{129,1},{2,130},{130,2},{3,131},{131,3},{4... | collective-permute-start | bytes 1572872 | tf_op jit(solution)/shard_map/ppermute | solution.py:109
  191.7 15.6 %all-to-all-start.11 = ((f32[16,1,2048]{2,1,0:T(1,128)}), f32[16,1,2048]{2,1,0:T(1,128)S(1)}, u32[]{:S(2)}, u32[]{:S(2)}) async-start(f32[16,1,2048]{2,1,0:T(1,128)} %broadcast_in_dim.72), calls=%async_computation.11 | async-start | bytes 262144 | tf_op jit(solution)/shard_map/all_to_all | solution.py:27
  199.3 17.5 %copy-start.8 = (bf16[128,1536]{1,0:T(8,128)(2,1)}, bf16[128,1536]{1,0:T(8,128)(2,1)S(1)}, u32[]{:S(2)}) copy-start(bf16[128,1536]{1,0:T(8,128)(2,1)S(1)} %pad_maximum_fusion) | copy-start | bytes 1179652
  211.2 10.9 %all-to-all-start.12 = ((f32[16,1,1024]{2,1,0:T(1,128)}), f32[16,1,1024]{2,1,0:T(1,128)S(1)}, u32[]{:S(2)}, u32[]{:S(2)}) async-start(f32[16,1,1024]{2,1,0:T(1,128)} %broadcast_in_dim.73), calls=%async_computation.12 | async-start | bytes 131072 | tf_op jit(solution)/shard_map/all_to_all | solution.py:27
  216.8 90.5 %collective-permute-start.10 = (bf16[1024,768]{1,0:T(8,128)(2,1)}, bf16[1024,768]{1,0:T(8,128)(2,1)}, u32[]{:S(2)}, u32[]{:S(2)}) collective-permute-start(bf16[1024,768]{1,0:T(8,128)(2,1)} %convolution_convert_fusion), channel_id=1, source_target_pairs={{0,128},{128,0},{1,129},{129,1},{2,130},{130,2},{3,131},{131,3},{4... | collective-permute-start | bytes 4718600 | tf_op jit(solution)/shard_map/ppermute | solution.py:109
  222.8 11.1 %all-to-all-start.13 = ((f32[16,1,1024]{2,1,0:T(1,128)}), f32[16,1,1024]{2,1,0:T(1,128)S(1)}, u32[]{:S(2)}, u32[]{:S(2)}) async-start(f32[16,1,1024]{2,1,0:T(1,128)} %broadcast_in_dim.74), calls=%async_computation.13 | async-start | bytes 131072 | tf_op jit(solution)/shard_map/all_to_all | solution.py:27
  227.5 66.4 %collective-permute-start.12 = (bf16[1024,256]{1,0:T(8,128)(2,1)}, bf16[1024,256]{1,0:T(8,128)(2,1)S(1)}, u32[]{:S(2)}, u32[]{:S(2)}) collective-permute-start(bf16[1024,256]{1,0:T(8,128)(2,1)} %convolution_convert_fusion.3), channel_id=1, source_target_pairs={{0,128},{128,0},{1,129},{129,1},{2,130},{130,2},{3,131},{131,3},{4... | collective-permute-start | bytes 1572872 | tf_op jit(solution)/shard_map/ppermute | solution.py:109
  234.6 1.0 copy-start.17
  235.6 20.3 %copy-start.15 = (bf16[128,512]{1,0:T(8,128)(2,1)}, bf16[128,512]{1,0:T(8,128)(2,1)S(1)}, u32[]{:S(2)}) copy-start(bf16[128,512]{1,0:T(8,128)(2,1)S(1)} %multiply_convert_fusion.2) | copy-start | bytes 393220
  235.6 11.9 %collective-permute-start.7 = (bf16[2,64,512]{2,1,0:T(8,128)(2,1)S(1)}, bf16[2,64,512]{2,1,0:T(8,128)(2,1)S(1)}, u32[]{:S(2)}, u32[]{:S(2)}) collective-permute-start(bf16[2,64,512]{2,1,0:T(8,128)(2,1)S(1)} %bitcast.185), channel_id=1, source_target_pairs={{0,1},{1,2},{2,3},{3,4},{4,5},{5,6},{6,7},{7,8},{8,9},{9,10},{10,1... | collective-permute-start | bytes 393224 | tf_op jit(solution)/shard_map/ppermute | solution.py:82
  240.6 15.4 %all-to-all-start.22 = ((bf16[16,64,256]{2,1,0:T(8,128)(2,1)}), bf16[16,64,256]{2,1,0:T(8,128)(2,1)S(1)}, u32[]{:S(2)}, u32[]{:S(2)}) async-start(bf16[16,64,256]{2,1,0:T(8,128)(2,1)} %bitcast.46), calls=%async_computation.22 | async-start | bytes 1048576 | tf_op jit(solution)/shard_map/all_to_all | solution.py:114
  244.1 6.9 %collective-permute-start.6 = (bf16[2,64,512]{2,1,0:T(8,128)(2,1)S(1)}, bf16[2,64,512]{2,1,0:T(8,128)(2,1)S(1)}, u32[]{:S(2)}, u32[]{:S(2)}) collective-permute-start(bf16[2,64,512]{2,1,0:T(8,128)(2,1)S(1)} %bitcast.186), channel_id=1, source_target_pairs={{1,0},{2,1},{3,2},{4,3},{5,4},{6,5},{7,6},{8,7},{9,8},{10,9},{11,1... | collective-permute-start | bytes 393224 | tf_op jit(solution)/shard_map/ppermute | solution.py:82
  248.2 7.7 %copy-start.12 = (bf16[2,64,512]{2,1,0:T(8,128)(2,1)}, bf16[2,64,512]{2,1,0:T(8,128)(2,1)S(1)}, u32[]{:S(2)}) copy-start(bf16[2,64,512]{2,1,0:T(8,128)(2,1)S(1)} %broadcast_multiply_fusion.4) | copy-start | bytes 393220
  251.8 4.1 %copy-start.13 = (bf16[2,64,512]{2,1,0:T(8,128)(2,1)}, bf16[2,64,512]{2,1,0:T(8,128)(2,1)S(1)}, u32[]{:S(2)}) copy-start(bf16[2,64,512]{2,1,0:T(8,128)(2,1)S(1)} %broadcast_multiply_fusion.5) | copy-start | bytes 393220
  255.9 51.3 %copy-start.9 = (bf16[128,1536]{1,0:T(8,128)(2,1)S(1)}, bf16[128,1536]{1,0:T(8,128)(2,1)}, u32[]{:S(2)}) copy-start(bf16[128,1536]{1,0:T(8,128)(2,1)} %copy-done.8) | copy-start | bytes 1179652
  256.7 17.3 %all-to-all-start.14 = ((f32[16,1,2048]{2,1,0:T(1,128)}), f32[16,1,2048]{2,1,0:T(1,128)S(1)}, u32[]{:S(2)}, u32[]{:S(2)}) async-start(f32[16,1,2048]{2,1,0:T(1,128)} %broadcast_in_dim.75), calls=%async_computation.14 | async-start | bytes 262144 | tf_op jit(solution)/shard_map/all_to_all | solution.py:27
  274.0 10.2 %all-to-all-start.23 = ((bf16[8,8,256]{2,1,0:T(8,128)(2,1)}), bf16[8,8,256]{2,1,0:T(8,128)(2,1)S(1)}, u32[]{:S(2)}, u32[]{:S(2)}) async-start(bf16[8,8,256]{2,1,0:T(8,128)(2,1)} %bitcast.47), calls=%async_computation.23 | async-start | bytes 65536 | tf_op jit(solution)/shard_map/all_to_all | solution.py:114
  284.2 17.7 %copy-start.16 = (bf16[8,8,256]{2,1,0:T(8,128)(2,1)}, bf16[8,8,256]{2,1,0:T(8,128)(2,1)S(1)}, u32[]{:S(2)}) copy-start(bf16[8,8,256]{2,1,0:T(8,128)(2,1)S(1)} %all-to-all-done.23) | copy-start | bytes 98308
  284.9 16.9 %all-to-all-start.15 = ((f32[16,1,2048]{2,1,0:T(1,128)}), f32[16,1,2048]{2,1,0:T(1,128)S(1)}, u32[]{:S(2)}, u32[]{:S(2)}) async-start(f32[16,1,2048]{2,1,0:T(1,128)} %broadcast_in_dim.76), calls=%async_computation.15 | async-start | bytes 262144 | tf_op jit(solution)/shard_map/all_to_all | solution.py:27
  301.8 13.7 %copy-start.10 = (f32[16,1,2048]{2,1,0:T(1,128)}, f32[16,1,2048]{2,1,0:T(1,128)S(1)}, u32[]{:S(2)}) copy-start(f32[16,1,2048]{2,1,0:T(1,128)S(1)} %all-to-all-done.15) | copy-start | bytes 393220
  301.8 13.7 %all-to-all-start.20 = ((bf16[16,64,256]{2,1,0:T(8,128)(2,1)}), bf16[16,64,256]{2,1,0:T(8,128)(2,1)S(1)}, u32[]{:S(2)}, u32[]{:S(2)}) async-start(bf16[16,64,256]{2,1,0:T(8,128)(2,1)} %bitcast.41), calls=%async_computation.20 | async-start | bytes 1048576 | tf_op jit(solution)/shard_map/all_to_all | solution.py:114
  307.3 12.0 %copy-start.6 = (bf16[128,1024]{1,0:T(8,128)(2,1)S(1)}, bf16[128,1024]{1,0:T(8,128)(2,1)}, u32[]{:S(2)}) copy-start(bf16[128,1024]{1,0:T(8,128)(2,1)} %copy-done.5) | copy-start | bytes 786436
  315.5 24.4 %all-to-all-start.18 = ((bf16[16,64,768]{2,1,0:T(8,128)(2,1)}), bf16[16,64,768]{2,1,0:T(8,128)(2,1)S(1)}, u32[]{:S(2)}, u32[]{:S(2)}) async-start(bf16[16,64,768]{2,1,0:T(8,128)(2,1)} %bitcast.157), calls=%async_computation.18 | async-start | bytes 3145728 | tf_op jit(solution)/shard_map/all_to_all | solution.py:114
  322.0 34.1 %collective-permute-start.8 = (bf16[1024,768]{1,0:T(8,128)(2,1)}, bf16[1024,768]{1,0:T(8,128)(2,1)}, u32[]{:S(2)}, u32[]{:S(2)}) collective-permute-start(bf16[1024,768]{1,0:T(8,128)(2,1)} %convolution_convert_fusion.1), channel_id=1, source_target_pairs={{0,128},{128,0},{1,129},{129,1},{2,130},{130,2},{3,131},{131,3},{4... | collective-permute-start | bytes 4718600 | tf_op jit(solution)/shard_map/ppermute | solution.py:109
  326.4 18.2 %collective-permute-start.15 = (f32[8,256]{1,0:T(8,128)S(1)}, f32[8,256]{1,0:T(8,128)S(1)}, u32[]{:S(2)}, u32[]{:S(2)}) collective-permute-start(f32[8,256]{1,0:T(8,128)S(1)} %convert_reduce_fusion.3), channel_id=1, source_target_pairs={{0,128},{128,0},{1,129},{129,1},{2,130},{130,2},{3,131},{131,3},{4... | collective-permute-start | bytes 24584 | tf_op jit(solution)/shard_map/ppermute | solution.py:118
  339.9 11.3 %all-to-all-start.21 = ((bf16[8,8,256]{2,1,0:T(8,128)(2,1)}), bf16[8,8,256]{2,1,0:T(8,128)(2,1)S(1)}, u32[]{:S(2)}, u32[]{:S(2)}) async-start(bf16[8,8,256]{2,1,0:T(8,128)(2,1)} %bitcast.42), calls=%async_computation.21 | async-start | bytes 65536 | tf_op jit(solution)/shard_map/all_to_all | solution.py:114
  351.2 12.1 %all-to-all-start.19 = ((bf16[8,8,768]{2,1,0:T(8,128)(2,1)}), bf16[8,8,768]{2,1,0:T(8,128)(2,1)S(1)}, u32[]{:S(2)}, u32[]{:S(2)}) async-start(bf16[8,8,768]{2,1,0:T(8,128)(2,1)} %bitcast.39), calls=%async_computation.19 | async-start | bytes 196608 | tf_op jit(solution)/shard_map/all_to_all | solution.py:114
  356.0 11.0 %copy-start.11 = (f32[16,1,2048]{2,1,0:T(1,128)S(1)}, f32[16,1,2048]{2,1,0:T(1,128)}, u32[]{:S(2)}) copy-start(f32[16,1,2048]{2,1,0:T(1,128)} %copy-done.10) | copy-start | bytes 393220
  356.0 11.1 %copy-start.22 = (f32[1024]{0:T(1024)S(1)}, f32[1024]{0:T(1024)}, u32[]{:S(2)}) copy-start(f32[1024]{0:T(1024)} %get-tuple-element.35) | copy-start | bytes 12292
  356.0 11.8 %copy-start.14 = (f32[128,1024]{1,0:T(8,128)S(1)}, f32[128,1024]{1,0:T(8,128)}, u32[]{:S(2)}) copy-start(f32[128,1024]{1,0:T(8,128)} %get-tuple-element.69) | copy-start | bytes 1572868
  356.1 11.8 %copy-start.20 = (f32[1,1024]{1,0:T(1,128)S(1)}, f32[1,1024]{1,0:T(1,128)}, u32[]{:S(2)}) copy-start(f32[1,1024]{1,0:T(1,128)} %get-tuple-element.38) | copy-start | bytes 12292
  363.3 21.6 %all-to-all-start.16 = ((bf16[16,64,768]{2,1,0:T(8,128)(2,1)}), bf16[16,64,768]{2,1,0:T(8,128)(2,1)S(1)}, u32[]{:S(2)}, u32[]{:S(2)}) async-start(bf16[16,64,768]{2,1,0:T(8,128)(2,1)} %bitcast.35), calls=%async_computation.16 | async-start | bytes 3145728 | tf_op jit(solution)/shard_map/all_to_all | solution.py:114
  368.7 1.3 collective-permute-start.13
  370.0 20.5 %collective-permute-start.11 = (f32[8,768]{1,0:T(8,128)S(1)}, f32[8,768]{1,0:T(8,128)S(1)}, u32[]{:S(2)}, u32[]{:S(2)}) collective-permute-start(f32[8,768]{1,0:T(8,128)S(1)} %convert_reduce_fusion.1), channel_id=1, source_target_pairs={{0,128},{128,0},{1,129},{129,1},{2,130},{130,2},{3,131},{131,3},{4... | collective-permute-start | bytes 73736 | tf_op jit(solution)/shard_map/ppermute | solution.py:118
  385.8 12.0 %all-to-all-start.17 = ((bf16[8,8,768]{2,1,0:T(8,128)(2,1)}), bf16[8,8,768]{2,1,0:T(8,128)(2,1)S(1)}, u32[]{:S(2)}, u32[]{:S(2)}) async-start(bf16[8,8,768]{2,1,0:T(8,128)(2,1)} %bitcast.36), calls=%async_computation.17 | async-start | bytes 196608 | tf_op jit(solution)/shard_map/all_to_all | solution.py:114
  397.8 1.3 collective-permute-start.9

commit v2 on v1

v2 whole, which is shorter than its diff:
```python
import functools

import jax
import jax.numpy as jnp
from jax import lax
from jax.experimental import pallas as pl
from jax.experimental.pallas import tpu as pltpu
from jax.sharding import Mesh, PartitionSpec as P

FIRST_DILATION = 64
SECOND_DILATION = 512
EPSILON = 1e-05
SIZES = {"dp": 2, "y": 4, "x": 4, "z": 8}
SEQ = ("y", "x", "z")
FIRST_STAGE = ("dp", "z")
SECOND_STAGE = ("y", "x")
GROUP = 16
F32 = jnp.float32
BF16 = jnp.bfloat16
ROWS, CH, HALF = 128, 1024, 512
TOTAL = 32768.0
TANH_SCALE = 0.7978845608028654
CUBE = 0.044715


def gelu(v):
    return 0.5 * v * (1.0 + jnp.tanh(TANH_SCALE * (v + CUBE * (v * v * v))))


def gelu_slope(v):
    square = v * v
    t = jnp.tanh(TANH_SCALE * (v + CUBE * (square * v)))
    half = 0.5 * (1.0 + t)
    slope = half + 0.5 * v * (1.0 - t * t) * (TANH_SCALE * (1.0 + 3.0 * CUBE * square))
    return v * half, slope


def spread_out(out, first, second):
    row = jnp.concatenate([first, second], axis=1)
    for i in range(GROUP):
        out[i] = row


def local_moments(values):
    mean = jnp.sum(values, axis=0, keepdims=True) * (1.0 / ROWS)
    centred = values - mean
    return mean, jnp.sum(centred * centred, axis=0, keepdims=True) * (1.0 / ROWS)


def merged_moments(parts):
    width = parts.shape[2] // 2
    means = [parts[i, :, :width] for i in range(GROUP)]
    mean = sum(means[1:], means[0]) * (1.0 / GROUP)
    square = jnp.zeros_like(mean)
    for i in range(GROUP):
        offset = means[i] - mean
        square = square + (parts[i, :, width:] + offset * offset)
    return mean, square * (1.0 / GROUP)


def merged_sums(parts):
    width = parts.shape[2] // 2
    total = parts[0]
    for i in range(1, GROUP):
        total = total + parts[i]
    return total[:, :width], total[:, width:]


def product(left, right):
    return jnp.dot(left, right, preferred_element_type=F32)


def product_nt(left, right):
    return lax.dot_general(left, right, (((1,), (1,)), ((), ())), preferred_element_type=F32)


def product_tn(left, right):
    return lax.dot_general(left, right, (((0,), (0,)), ((), ())), preferred_element_type=F32)


def k_first(x, out):
    spread_out(out, *local_moments(x[...].astype(F32)))


def k_merge(kind, parts, *rest):
    out = rest[-1]
    merge = merged_moments if kind == "moments" else merged_sums
    spread_out(out, *merge(parts))


def k_entry(layer, parts, x, lower, upper, masks, weight, gains, biases, taps, slope, conv, stat, out):
    mean, spread = merged_moments(parts)
    factor = lax.rsqrt(spread + EPSILON)
    gain, bias = gains[layer : layer + 1], biases[layer : layer + 1]
    active, slope_in = gelu_slope((x[...].astype(F32) - mean) * factor * gain + bias)
    slope[...] = slope_in
    centre = active.astype(BF16)
    taps[...] = centre
    stat[...] = jnp.concatenate([mean, factor], axis=0)

    def side(rows, column):
        values = gelu((rows[...].astype(F32) - mean) * factor * gain + bias)
        mask = masks[:, 2 * layer + column : 2 * layer + column + 1]
        return jnp.where(mask > 0, values, 0.0).astype(BF16)

    result = product(centre, weight[:, HALF : 2 * HALF])
    result = result + product(side(lower, 0), weight[:, :HALF])
    result = result + product(side(upper, 1), weight[:, 2 * HALF :])
    conv[...] = result
    spread_out(out, *local_moments(result))


def middle(layer, parts, conv, gains, biases, project, x):
    mean, spread = merged_moments(parts)
    factor = lax.rsqrt(spread + EPSILON)
    normed = (conv[...] - mean) * factor
    active, slope = gelu_slope(normed * gains[layer : layer + 1] + biases[layer : layer + 1])
    hidden = active.astype(BF16)
    following = (x[...].astype(F32) + product_nt(hidden, project[...])).astype(BF16)
    return factor, normed, slope, hidden, following


def k_middle(parts, conv, gains, biases, project, x, hidden, following, slope, normed, factor, out):
    factor[...], normed[...], slope[...], hidden[...], rows = middle(
        0, parts, conv, gains, biases, project, x
    )
    following[...] = rows
    spread_out(out, *local_moments(rows.astype(F32)))


def begin_backward(upstream, project, slope, normed, grad, pair, out):
    values = product(upstream, project[...]) * slope
    grad[...] = values
    pair[:, :HALF] = values.astype(BF16)
    pair[:, HALF:] = normed.astype(BF16)
    spread_out(
        out,
        jnp.sum(values, axis=0, keepdims=True),
        jnp.sum(values * normed, axis=0, keepdims=True),
    )


def k_turn(parts, conv, gains, biases, project, x, upstream, hidden, following, normed, factor, grad, pair, out):
    factor[...], rows, slope, hidden[...], following[...] = middle(
        1, parts, conv, gains, biases, project, x
    )
    normed[...] = rows
    begin_backward(upstream[...], project, slope, rows, grad, pair, out)


def k_back_middle(
    layer, parts, grad, normed, factor, lower, upper, masks, gains, weight, slope, x, stat, *rest
):
    if layer == 0:
        given_gain, given_bias, three, grad_in, gain_out, bias_out, out = rest
    else:
        three, grad_in, gain_out, bias_out, out = rest
    total, cross = merged_sums(parts)
    gain_out[0:1] = cross
    bias_out[0:1] = total
    if layer == 0:
        gain_out[1:2] = given_gain[...]
        bias_out[1:2] = given_bias[...]
    total, cross = total * (1.0 / TOTAL), cross * (1.0 / TOTAL)
    scale = gains[layer : layer + 1] * factor[...]

    def conv_grad(grads, rows):
        return scale * (grads - total - rows * cross)

    def side(pair, column):
        values = conv_grad(pair[:, :HALF].astype(F32), pair[:, HALF:].astype(F32))
        mask = masks[:, 2 * layer + column : 2 * layer + column + 1]
        return jnp.where(mask > 0, values, 0.0).astype(BF16)

    three[:, :HALF] = side(upper, 1)
    three[:, HALF : 2 * HALF] = conv_grad(grad[...], normed[...]).astype(BF16)
    three[:, 2 * HALF :] = side(lower, 0)
    values = product_nt(three[...], weight[...]) * slope[...]
    grad_in[...] = values
    normed_in = (x[...].astype(F32) - stat[0:1]) * stat[1:2]
    spread_out(
        out,
        jnp.sum(values, axis=0, keepdims=True),
        jnp.sum(values * normed_in, axis=0, keepdims=True),
    )


def back_entry(layer, parts, grad_in, x, stat, gains, upstream):
    total, cross = merged_sums(parts)
    factor = stat[1:2]
    normed = (x[...].astype(F32) - stat[0:1]) * factor
    branch = (gains[layer : layer + 1] * factor) * (
        grad_in[...] - total * (1.0 / TOTAL) - normed * (cross * (1.0 / TOTAL))
    )
    return total, cross, (upstream[...].astype(F32) + branch).astype(BF16)


def k_back_entry(
    parts, grad_in, x, stat, gains, upstream, project, slope, normed, *rest
):
    gain_out, bias_out, stream, grad, pair, out = rest
    bias_out[...], gain_out[...], rows = back_entry(1, parts, grad_in, x, stat, gains, upstream)
    stream[...] = rows
    begin_backward(rows, project, slope[...], normed[...], grad, pair, out)


def k_last(parts, grad_in, x, stat, gains, upstream, given_gain, given_bias, gain_out, bias_out, stream):
    total, cross, stream[...] = back_entry(0, parts, grad_in, x, stat, gains, upstream)
    gain_out[0:1] = cross
    gain_out[1:2] = given_gain[...]
    bias_out[0:1] = total
    bias_out[1:2] = given_bias[...]


def half_of(ref, other):
    half = ref.shape[1] // 2
    place = lax.axis_index("dp")
    place = 1 - place if other else place
    return ref[:, pl.ds(pl.multiple_of(place * half, 128), half)]


def k_give(taps, three, upstream, hidden, out):
    out[:, : 3 * HALF // 2] = product_tn(taps[...], half_of(three, True)).astype(BF16)
    out[:, 3 * HALF // 2 :] = product_tn(upstream[...], half_of(hidden, True)).astype(BF16)


def k_keep(taps, three, upstream, hidden, arrived, out):
    first = arrived[:, : 3 * HALF // 2].astype(F32)
    out[:, : 3 * HALF // 2] = (product_tn(taps[...], half_of(three, False)) + first).astype(BF16)
    second = arrived[:, 3 * HALF // 2 :].astype(F32)
    out[:, 3 * HALF // 2 :] = (product_tn(upstream[...], half_of(hidden, False)) + second).astype(BF16)


def k_gather(parts, out):
    for z in range(8):
        rows = slice(8 * z, 8 * z + 8)
        total = parts[0, rows].astype(F32)
        for i in range(1, GROUP):
            total = total + parts[i, rows].astype(F32)
        total = total.astype(BF16)
        out[z] = total
        out[8 + z] = total


def k_rows(parts_0, parts_1, kernel_out, project_out):
    cut = 3 * HALF // 2
    for layer, parts in enumerate((parts_0, parts_1)):
        for d in range(2):
            total = parts[8 * d].astype(F32)
            for z in range(1, 8):
                total = total + parts[8 * d + z].astype(F32)
            kernel_out[layer, :, d * cut : (d + 1) * cut] = total[:, :cut]
            project_out[layer, :, d * HALF // 2 : (d + 1) * HALF // 2] = total[:, cut:]


def whole(value):
    shape = value.shape
    return pl.BlockSpec(shape, lambda i: (0,) * len(shape))


def layer_of(value, layer):
    return pl.BlockSpec((None,) + value.shape[1:], lambda i: (layer, 0, 0))


def call(kernel, outs, *operands, name, layers=None, waits=(), flops=1 << 22):
    layers = layers or {}
    specs = [
        layer_of(value, layers[i]) if i in layers else whole(value)
        for i, value in enumerate(operands)
    ]
    specs += [pl.BlockSpec(memory_space=pl.ANY)] * len(waits)
    shapes = [jax.ShapeDtypeStruct(shape, dtype) for shape, dtype in outs]
    moved = sum(v.size * v.dtype.itemsize for v in list(operands) + shapes)
    return pl.pallas_call(
        kernel,
        grid=(1,),
        in_specs=specs,
        out_specs=[whole(shape) for shape in shapes],
        out_shape=shapes,
        name=name,
        cost_estimate=pl.CostEstimate(flops=flops, bytes_accessed=moved, transcendentals=0),
        compiler_params=pltpu.CompilerParams(vmem_limit_bytes=48 << 20),
    )(*operands, *waits)


def exchange(value, axes):
    return lax.all_to_all(value, axes, 0, 0, tiled=True)


def over_all(payload, kind, waits=()):
    first = exchange(payload, FIRST_STAGE)
    (merged,) = call(
        functools.partial(k_merge, kind),
        [(payload.shape, F32)],
        first,
        waits=waits,
        name="merge_" + kind,
    )
    return exchange(merged, SECOND_STAGE)


def passed_along(value, steps):
    count = 128
    leading, last = (max(0, -steps), min(count, count - steps))
    return lax.ppermute(value, SEQ, [(source, source + steps) for source in range(leading, last)])


def neighbours(rows, dilation):
    hops = dilation // 64
    return passed_along(rows, hops), passed_along(rows, -hops)


def chip_share(taps, three, upstream, hidden):
    flops = 2 * ROWS * CH * CH
    (given,) = call(
        k_give, [((CH, CH), BF16)], taps, three, upstream, hidden, name="give", flops=flops
    )
    arrived = lax.ppermute(given, "dp", [(0, 1), (1, 0)])
    (share,) = call(
        k_keep, [((CH, CH), BF16)], taps, three, upstream, hidden, arrived, name="keep", flops=flops
    )
    return exchange(share.reshape(GROUP, CH // GROUP, CH), SECOND_STAGE)


def chip_rows(parts):
    (rows,) = call(k_gather, [((GROUP, 8, CH), BF16)], parts, name="gather_rows")
    return exchange(rows, FIRST_STAGE)


def on_device(
    activations,
    segment_ids,
    interval_bounds,
    conv_weight,
    proj_weight,
    gains_in,
    biases_in,
    gains_mid,
    biases_mid,
    cotangent,
):
    windows, local_bins, channels = activations.shape
    position = lax.axis_index(SEQ) * local_bins + jnp.arange(local_bins, dtype=jnp.int32)[None, :]
    labels = jnp.arange(interval_bounds.shape[1] - 1, dtype=jnp.int32)
    matches = segment_ids[:, :, None] == labels[None, None, :]
    starts = jnp.sum(jnp.where(matches, interval_bounds[:, None, :-1], 0), axis=2)
    finishes = jnp.sum(jnp.where(matches, interval_bounds[:, None, 1:], 0), axis=2)
    masks = []
    for dilation in (FIRST_DILATION, SECOND_DILATION):
        masks.append(starts <= position - dilation)
        masks.append(position + dilation < finishes)
    masks = jnp.stack(masks, axis=2).astype(F32).reshape(ROWS, 4)

    wide, narrow = (GROUP, 1, 2 * CH), (GROUP, 1, CH)
    conv_flops = 2 * ROWS * CH * 3 * HALF
    stream_0 = activations.reshape(ROWS, CH)
    grad_2 = cotangent.reshape(ROWS, CH)

    def entry(layer, stream, parts, sides):
        return call(
            functools.partial(k_entry, layer),
            [((ROWS, CH), BF16), ((ROWS, CH), F32), ((ROWS, HALF), F32), ((2, CH), F32), (narrow, F32)],
            parts,
            stream,
            *sides,
            masks,
            conv_weight,
            gains_in,
            biases_in,
            layers={5: layer},
            name="entry",
            flops=conv_flops,
        )

    sides = neighbours(stream_0, FIRST_DILATION)
    (payload,) = call(k_first, [(wide, F32)], stream_0, name="first")
    parts = over_all(payload, "moments", sides)
    taps_0, slope_0, conv_0, stat_0, payload = entry(0, stream_0, parts, sides)
    parts = over_all(payload, "moments")
    hidden_0, stream_1, slope_mid_0, normed_0, factor_0, payload = call(
        k_middle,
        [
            ((ROWS, HALF), BF16),
            ((ROWS, CH), BF16),
            ((ROWS, HALF), F32),
            ((ROWS, HALF), F32),
            ((1, HALF), F32),
            (wide, F32),
        ],
        parts,
        conv_0,
        gains_mid,
        biases_mid,
        proj_weight,
        stream_0,
        layers={4: 0},
        name="middle",
    )
    sides = neighbours(stream_1, SECOND_DILATION)
    parts = over_all(payload, "moments", sides)
    taps_1, slope_1, conv_1, stat_1, payload = entry(1, stream_1, parts, sides)
    parts = over_all(payload, "moments")
    hidden_1, stream_2, normed_1, factor_1, grad, pair, payload = call(
        k_turn,
        [
            ((ROWS, HALF), BF16),
            ((ROWS, CH), BF16),
            ((ROWS, HALF), F32),
            ((1, HALF), F32),
            ((ROWS, HALF), F32),
            ((ROWS, CH), BF16),
            (narrow, F32),
        ],
        parts,
        conv_1,
        gains_mid,
        biases_mid,
        proj_weight,
        stream_1,
        grad_2,
        layers={4: 1},
        name="turn",
    )

    def back_middle(layer, parts, grad, normed, factor, sides, slope, stream, stat, *given):
        rows = 2 - layer
        return call(
            functools.partial(k_back_middle, layer),
            [
                ((ROWS, 3 * HALF), BF16),
                ((ROWS, CH), F32),
                ((rows, HALF), F32),
                ((rows, HALF), F32),
                (wide, F32),
            ],
            parts,
            grad,
            normed,
            factor,
            *sides,
            masks,
            gains_mid,
            conv_weight,
            slope,
            stream,
            stat,
            *given,
            layers={8: layer},
            name="back_middle",
            flops=conv_flops,
        )

    sides = neighbours(pair, SECOND_DILATION)
    parts = over_all(payload, "sums", sides)
    three_1, grad_in, gain_mid, bias_mid, payload = back_middle(
        1, parts, grad, normed_1, factor_1, sides, slope_1, stream_1, stat_1
    )
    parts = over_all(payload, "sums")
    gain_in, bias_in, grad_1, grad, pair, payload = call(
        k_back_entry,
        [
            ((1, CH), F32),
            ((1, CH), F32),
            ((ROWS, CH), BF16),
            ((ROWS, HALF), F32),
            ((ROWS, CH), BF16),
            (narrow, F32),
        ],
        parts,
        grad_in,
        stream_1,
        stat_1,
        gains_in,
        grad_2,
        proj_weight,
        slope_mid_0,
        normed_0,
        layers={6: 0},
        name="back_entry",
    )
    sides = neighbours(pair, FIRST_DILATION)
    chip_1 = chip_share(taps_1, three_1, grad_2, hidden_1)
    parts = over_all(payload, "sums", sides)
    three_0, grad_in, grad_gains_mid, grad_biases_mid, payload = back_middle(
        0, parts, grad, normed_0, factor_0, sides, slope_0, stream_0, stat_0, gain_mid, bias_mid
    )
    rows_1 = chip_rows(chip_1)
    chip_0 = chip_share(taps_0, three_0, grad_1, hidden_0)
    parts = over_all(payload, "sums", (rows_1,))
    grad_gains_in, grad_biases_in, grad_0 = call(
        k_last,
        [((2, CH), F32), ((2, CH), F32), ((ROWS, CH), BF16)],
        parts,
        grad_in,
        stream_0,
        stat_0,
        gains_in,
        grad_1,
        gain_in,
        bias_in,
        name="last",
    )
    grad_conv, grad_proj = call(
        k_rows,
        [((2, 8, 3 * HALF), F32), ((2, 8, HALF), F32)],
        chip_rows(chip_0),
        rows_1,
        name="rows",
    )
    return (
        stream_2.reshape(activations.shape),
        grad_0.reshape(activations.shape),
        grad_conv,
        grad_proj,
        grad_gains_in,
        grad_biases_in,
        grad_gains_mid,
        grad_biases_mid,
    )


def solution(mesh):
    sizes = tuple(SIZES.values())
    split = Mesh(mesh.devices.reshape(sizes), tuple(SIZES))
    bins = P("dp", SEQ, None)
    rows = P(None, SEQ, None)
    in_specs = (bins, P("dp", SEQ), P("dp", None), P(), P(), P(), P(), P(), P(), bins)
    out_specs = (bins, bins, rows, rows, P(), P(), P(), P())
    return jax.shard_map(
        on_device, mesh=split, in_specs=in_specs, out_specs=out_specs, check_vma=False
    )
```

time: 405 us -> 345 us (0.85)
  blocking collectives: 84.5 us -> 128 us
  starting transfers between devices: 113 us -> 69.5 us
  waiting for transfers between devices: 125 us -> 91.3 us
  matrix products: 33.2 us -> 0 us
  Pallas kernels: 0 us -> 30.8 us
  other arithmetic: 27.7 us -> 0.81 us
  local copies, waits for them, and re-layouts: 15.1 us -> 22.1 us
    all_to_all x7 -> x11, blocking collectives: 84.5 us -> 128 us  [exchange(): return lax.all_to_all(value, axes, 0, 0, tiled=True)]
    all_to_all x17 -> x9, starting transfers between devices: 90.3 us -> 50.3 us  [exchange(): return lax.all_to_all(value, axes, 0, 0, tiled=True)]
    dot_general x20 -> x0, matrix products: 33.2 us -> none  [the longest x8 15.8 us: column_product(): lax.dot_general(left_side, right_side, (((0,), (0,)), ((), ())), preferre...]
    pallas_call x0 -> x24, Pallas kernels: none -> 30.8 us  [call(): pl.pallas_call(kernel, grid=(1,), in_specs=specs, out_specs=[whole(shape)...]
    unnamed x68 -> x92, local copies, waits for them, and re-layouts: 1.02 us -> 20.7 us
    all_to_all x17 -> x9, waiting for transfers between devices: 109 us -> 91.3 us  [exchange(): return lax.all_to_all(value, axes, 0, 0, tiled=True)]
    ppermute x8, waiting for transfers between devices: 14.2 us -> 0.02 us  [passed_along(): lax.ppermute(value, SEQ, [(source, source + steps) for source in range(le...]
    reduce_sum x38 -> x1, other arithmetic: 7.69 us -> 0.77 us  [on_device(): jnp.sum(jnp.where(matches, interval_bounds[:, None, :-1], 0), axis=2)]
  transfers between devices with their start and end apart: 33 -> 19, of which waited for: 22 -> 9; matrix products, arithmetic and copies ran while one was open for 15% -> 1% of each run, Pallas kernels for 0% -> 5%
where the time goes in v2:
time: 345 us; the launch traced here: 343 us
  blocking collectives  128 us (37%)
  waiting for transfers between devices  91.3 us (26%)
  starting transfers between devices  69.5 us (20%)
  Pallas kernels  30.8 us (9%)
  local copies, waits for them, and re-layouts  22.1 us (6%)
    all_to_all x11, blocking collectives, exchange(): return lax.all_to_all(value, axes, 0, 0, tiled=True)  128 us
    all_to_all x9, waiting for transfers between devices, exchange(): return lax.all_to_all(value, axes, 0, 0, tiled=True)  91.3 us
    all_to_all x9, starting transfers between devices, exchange(): return lax.all_to_all(value, axes, 0, 0, tiled=True)  50.3 us
    pallas_call x24, Pallas kernels, call(): pl.pallas_call(kernel, grid=(1,), in_specs=specs, out_specs=[whole(shape)...  30.8 us
    unnamed x92, local copies, waits for them, and re-layouts  20.7 us
    ppermute x8, starting transfers between devices, passed_along(): lax.ppermute(value, SEQ, [(source, source + steps) for source in range(le...  19.2 us
  transfers between devices with their start and end apart: 19, of which 9 were waited for; matrix products, arithmetic and copies ran while one was open for 1% of the time, Pallas kernels for 5%

profile of v2, /device:TPU:32, one launch (start us, length us, event | category | flops | bytes accessed | tf_op | source)
XLA Modules:
  0.0 343.2 jit_solution(11070955763368157548)
XLA Ops:
  0.6 3.8 %collective-permute-start = (bf16[128,1024]{1,0:T(8,128)(2,1)}, bf16[128,1024]{1,0:T(8,128)(2,1)S(1)}, u32[]{:S(2)}, u32[]{:S(2)}) collective-permute-start(bf16[128,1024]{1,0:T(8,128)(2,1)} %bitcast.16), channel_id=1, source_target_pairs={{0,1},{1,2},{2,3},{3,4},{4,5},{5,6},{6,7},{7,8},{8,9},{9,10},{10,1... | collective-permute-start | bytes 786440 | tf_op jit(solution)/shard_map/ppermute | solution.py:305
  4.5 2.0 collective-permute-start.1
  6.5 0.9 copy-done.3
  7.5 0.8 first.1
  8.3 9.8 %all-to-all-start = ((f32[16,1,2048]{2,1,0:T(1,128)}), f32[16,1,2048]{2,1,0:T(1,128)S(1)}, u32[]{:S(2)}, u32[]{:S(2)}) async-start(f32[16,1,2048]{2,1,0:T(1,128)} %first.1), calls=%async_computation | async-start | bytes 262144 | tf_op jit(solution)/shard_map/all_to_all | solution.py:287
  18.1 0.8 fusion.4
  20.2 6.1 %all-to-all-done.parts = f32[16,1,2048]{2,1,0:T(1,128)S(1)} async-done(((f32[16,1,2048]{2,1,0:T(1,128)}), f32[16,1,2048]{2,1,0:T(1,128)S(1)}, u32[]{:S(2)}, u32[]{:S(2)}) %all-to-all-start) | async-done | bytes 131104 | tf_op jit(solution)/shard_map/all_to_all | solution.py:287
  27.0 7.0 %all-to-all-start.1 = ((f32[16,1,2048]{2,1,0:T(1,128)}), f32[16,1,2048]{2,1,0:T(1,128)S(1)}, u32[]{:S(2)}, u32[]{:S(2)}) async-start(f32[16,1,2048]{2,1,0:T(1,128)} %merge_moments.4), calls=%async_computation.1 | async-start | bytes 262144 | tf_op jit(solution)/shard_map/all_to_all | solution.py:287
  34.2 7.8 %all-to-all-done.1.parts = f32[16,1,2048]{2,1,0:T(1,128)S(1)} async-done(((f32[16,1,2048]{2,1,0:T(1,128)}), f32[16,1,2048]{2,1,0:T(1,128)S(1)}, u32[]{:S(2)}, u32[]{:S(2)}) %all-to-all-start.1) | async-done | bytes 131104 | tf_op jit(solution)/shard_map/all_to_all | solution.py:287
  42.0 0.9 copy-done.4
  44.4 3.1 entry.2
  47.5 0.8 copy-done.18
  48.3 10.4 %all_to_all.100.parts = f32[16,1,1024]{2,1,0:T(1,128)S(1)} all-to-all(f32[16,1,1024]{2,1,0:T(1,128)S(1)} %get-tuple-element.52), channel_id=1, replica_groups=mesh['dp'=2,'y'=4,'x'=4,'z'=8] {'dp','z'}, dimensions={0} | all-to-all | bytes 131072 | tf_op jit(solution)/shard_map/all_to_all | solution.py:287
  58.7 10.7 %all_to_all.101.parts = f32[16,1,1024]{2,1,0:T(1,128)S(1)} all-to-all(f32[16,1,1024]{2,1,0:T(1,128)S(1)} %merge_moments.5), channel_id=1, replica_groups=mesh['dp'=2,'y'=4,'x'=4,'z'=8] {'y','x'}, dimensions={0} | all-to-all | bytes 131072 | tf_op jit(solution)/shard_map/all_to_all | solution.py:287
  70.1 2.5 collective-permute-start.2
  72.6 1.3 collective-permute-start.3
  73.9 11.7 %all_to_all.102.parts = f32[16,1,2048]{2,1,0:T(1,128)S(1)} all-to-all(f32[16,1,2048]{2,1,0:T(1,128)S(1)} %get-tuple-element.54), channel_id=1, replica_groups=mesh['dp'=2,'y'=4,'x'=4,'z'=8] {'dp','z'}, dimensions={0} | all-to-all | bytes 262144 | tf_op jit(solution)/shard_map/all_to_all | solution.py:287
  85.7 14.5 %all_to_all.103.parts = f32[16,1,2048]{2,1,0:T(1,128)S(1)} all-to-all(f32[16,1,2048]{2,1,0:T(1,128)S(1)} %merge_moments.6), channel_id=1, replica_groups=mesh['dp'=2,'y'=4,'x'=4,'z'=8] {'y','x'}, dimensions={0} | all-to-all | bytes 262144 | tf_op jit(solution)/shard_map/all_to_all | solution.py:287
  100.3 3.1 entry.3
  103.4 10.4 %all_to_all.104.parts = f32[16,1,1024]{2,1,0:T(1,128)S(1)} all-to-all(f32[16,1,1024]{2,1,0:T(1,128)S(1)} %get-tuple-element.56), channel_id=1, replica_groups=mesh['dp'=2,'y'=4,'x'=4,'z'=8] {'dp','z'}, dimensions={0} | all-to-all | bytes 131072 | tf_op jit(solution)/shard_map/all_to_all | solution.py:287
  113.8 10.7 %all_to_all.105.parts = f32[16,1,1024]{2,1,0:T(1,128)S(1)} all-to-all(f32[16,1,1024]{2,1,0:T(1,128)S(1)} %merge_moments.7), channel_id=1, replica_groups=mesh['dp'=2,'y'=4,'x'=4,'z'=8] {'y','x'}, dimensions={0} | all-to-all | bytes 131072 | tf_op jit(solution)/shard_map/all_to_all | solution.py:287
  124.5 1.2 turn.1
  125.8 2.5 collective-permute-start.4
  128.2 1.3 collective-permute-start.5
  129.5 10.5 %all_to_all.106.parts = f32[16,1,1024]{2,1,0:T(1,128)S(1)} all-to-all(f32[16,1,1024]{2,1,0:T(1,128)S(1)} %get-tuple-element.59), channel_id=1, replica_groups=mesh['dp'=2,'y'=4,'x'=4,'z'=8] {'dp','z'}, dimensions={0} | all-to-all | bytes 131072 | tf_op jit(solution)/shard_map/all_to_all | solution.py:287
  140.1 14.2 %all_to_all.107.parts = f32[16,1,1024]{2,1,0:T(1,128)S(1)} all-to-all(f32[16,1,1024]{2,1,0:T(1,128)S(1)} %merge_sums.4), channel_id=1, replica_groups=mesh['dp'=2,'y'=4,'x'=4,'z'=8] {'y','x'}, dimensions={0} | all-to-all | bytes 131072 | tf_op jit(solution)/shard_map/all_to_all | solution.py:287
  154.3 3.1 back_middle.2
  157.4 2.1 give.2
  159.5 11.7 %all_to_all.108.parts = f32[16,1,2048]{2,1,0:T(1,128)S(1)} all-to-all(f32[16,1,2048]{2,1,0:T(1,128)S(1)} %get-tuple-element.66), channel_id=1, replica_groups=mesh['dp'=2,'y'=4,'x'=4,'z'=8] {'dp','z'}, dimensions={0} | all-to-all | bytes 262144 | tf_op jit(solution)/shard_map/all_to_all | solution.py:287
  171.3 11.1 %all_to_all.109.parts = f32[16,1,2048]{2,1,0:T(1,128)S(1)} all-to-all(f32[16,1,2048]{2,1,0:T(1,128)S(1)} %merge_sums.5), channel_id=1, replica_groups=mesh['dp'=2,'y'=4,'x'=4,'z'=8] {'y','x'}, dimensions={0} | all-to-all | bytes 262144 | tf_op jit(solution)/shard_map/all_to_all | solution.py:287
  183.5 2.7 collective-permute-start.6
  186.2 3.2 collective-permute-start.7
  189.4 11.6 %all_to_all.110.parts = f32[16,1,1024]{2,1,0:T(1,128)S(1)} all-to-all(f32[16,1,1024]{2,1,0:T(1,128)S(1)} %get-tuple-element.70), channel_id=1, replica_groups=mesh['dp'=2,'y'=4,'x'=4,'z'=8] {'dp','z'}, dimensions={0} | all-to-all | bytes 131072 | tf_op jit(solution)/shard_map/all_to_all | solution.py:287
  203.0 4.8 %all-to-all-start.13 = ((f32[16,1,1024]{2,1,0:T(1,128)}), f32[16,1,1024]{2,1,0:T(1,128)S(1)}, u32[]{:S(2)}, u32[]{:S(2)}) async-start(f32[16,1,1024]{2,1,0:T(1,128)} %merge_sums.6), calls=%async_computation.13 | async-start | bytes 131072 | tf_op jit(solution)/shard_map/all_to_all | solution.py:287
  207.9 0.9 copy-done.11
  208.8 0.9 copy-done.21
  209.7 2.3 keep.2
  212.1 1.3 copy-done.1
  213.4 2.2 all-to-all-done.13.parts
  215.5 5.2 %all-to-all-start.15 = ((bf16[16,64,1024]{2,1,0:T(8,128)(2,1)}), bf16[16,64,1024]{2,1,0:T(8,128)(2,1)S(1)}, u32[]{:S(2)}, u32[]{:S(2)}) async-start(bf16[16,64,1024]{2,1,0:T(8,128)(2,1)} %bitcast.14), calls=%async_computation.15 | async-start | bytes 4194304 | tf_op jit(solution)/shard_map/all_to_all | solution.py:287
  220.7 0.9 copy-done.13
  221.7 0.9 copy-done.15
  222.6 1.0 copy-done.19
  223.7 0.9 copy-done.28
  227.4 3.6 %back_middle.3 = (bf16[128,1536]{1,0:T(8,128)(2,1)S(1)}, f32[128,1024]{1,0:T(8,128)S(1)}, f32[2,512]{1,0:T(2,128)}, f32[2,512]{1,0:T(2,128)}, f32[16,1,2048]{2,1,0:T(1,128)S(1)}) custom-call(f32[16,1,1024]{2,1,0:T(1,128)S(1)} %all-to-all-done.13.parts, f32[128,512]{1,0:T(8,128)S(1)} %copy-done.28, f32[128,512]{1,0:T(8,128)S(1)} %copy-done.17, ...), custom_call_target="tpu_custom_call" | custom-call | flops 402653184 | bytes 9269248 | tf_op jit(solution)/shard_map/back_middle/pallas_call | solution.py:274
  231.7 2.1 give.3
  233.8 17.1 %all-to-all-done.15.parts = bf16[16,64,1024]{2,1,0:T(8,128)(2,1)S(1)} async-done(((bf16[16,64,1024]{2,1,0:T(8,128)(2,1)}), bf16[16,64,1024]{2,1,0:T(8,128)(2,1)S(1)}, u32[]{:S(2)}, u32[]{:S(2)}) %all-to-all-start.15) | async-done | bytes 2097184 | tf_op jit(solution)/shard_map/all_to_all | solution.py:287
  251.0 4.1 %all-to-all-start.14 = ((f32[16,1,2048]{2,1,0:T(1,128)}), f32[16,1,2048]{2,1,0:T(1,128)S(1)}, u32[]{:S(2)}, u32[]{:S(2)}) async-start(f32[16,1,2048]{2,1,0:T(1,128)} %copy-done.31), calls=%async_computation.14 | async-start | bytes 262144 | tf_op jit(solution)/shard_map/all_to_all | solution.py:287
  255.1 1.0 gather_rows.2
  256.1 7.3 %all-to-all-done.14.parts = f32[16,1,2048]{2,1,0:T(1,128)S(1)} async-done(((f32[16,1,2048]{2,1,0:T(1,128)}), f32[16,1,2048]{2,1,0:T(1,128)S(1)}, u32[]{:S(2)}, u32[]{:S(2)}) %all-to-all-start.14) | async-done | bytes 131104 | tf_op jit(solution)/shard_map/all_to_all | solution.py:287
  263.3 3.7 %all-to-all-start.16 = ((bf16[16,8,1024]{2,1,0:T(8,128)(2,1)}), bf16[16,8,1024]{2,1,0:T(8,128)(2,1)S(1)}, u32[]{:S(2)}, u32[]{:S(2)}) async-start(bf16[16,8,1024]{2,1,0:T(8,128)(2,1)} %gather_rows.2), calls=%async_computation.16 | async-start | bytes 524288 | tf_op jit(solution)/shard_map/all_to_all | solution.py:287
  267.1 0.9 copy-done.9
  268.0 2.3 keep.3
  270.4 1.3 copy-done.2
  271.6 6.4 %all-to-all-done.16.rest_0_.parts_1 = bf16[16,8,1024]{2,1,0:T(8,128)(2,1)S(1)} async-done(((bf16[16,8,1024]{2,1,0:T(8,128)(2,1)}), bf16[16,8,1024]{2,1,0:T(8,128)(2,1)S(1)}, u32[]{:S(2)}, u32[]{:S(2)}) %all-to-all-start.16) | async-done | bytes 262176 | tf_op jit(solution)/shard_map/all_to_all | solution.py:287
  278.1 3.7 %all-to-all-start.18 = ((bf16[16,64,1024]{2,1,0:T(8,128)(2,1)}), bf16[16,64,1024]{2,1,0:T(8,128)(2,1)S(1)}, u32[]{:S(2)}, u32[]{:S(2)}) async-start(bf16[16,64,1024]{2,1,0:T(8,128)(2,1)} %bitcast.15), calls=%async_computation.18 | async-start | bytes 4194304 | tf_op jit(solution)/shard_map/all_to_all | solution.py:287
  281.8 0.9 copy-done.25
  283.4 28.3 %all-to-all-done.18.parts = bf16[16,64,1024]{2,1,0:T(8,128)(2,1)S(1)} async-done(((bf16[16,64,1024]{2,1,0:T(8,128)(2,1)}), bf16[16,64,1024]{2,1,0:T(8,128)(2,1)S(1)}, u32[]{:S(2)}, u32[]{:S(2)}) %all-to-all-start.18) | async-done | bytes 2097184 | tf_op jit(solution)/shard_map/all_to_all | solution.py:287
  311.7 4.2 %all-to-all-start.17 = ((f32[16,1,2048]{2,1,0:T(1,128)}), f32[16,1,2048]{2,1,0:T(1,128)}, u32[]{:S(2)}, u32[]{:S(2)}) async-start(f32[16,1,2048]{2,1,0:T(1,128)} %copy-done.26), calls=%async_computation.17 | async-start | bytes 262144 | tf_op jit(solution)/shard_map/all_to_all | solution.py:287
  315.9 1.0 gather_rows.3
  316.9 7.0 %all-to-all-done.17.parts = f32[16,1,2048]{2,1,0:T(1,128)} async-done(((f32[16,1,2048]{2,1,0:T(1,128)}), f32[16,1,2048]{2,1,0:T(1,128)}, u32[]{:S(2)}, u32[]{:S(2)}) %all-to-all-start.17) | async-done | bytes 131104 | tf_op jit(solution)/shard_map/all_to_all | solution.py:287
  323.9 7.7 %all-to-all-start.19 = ((bf16[16,8,1024]{2,1,0:T(8,128)(2,1)}), bf16[16,8,1024]{2,1,0:T(8,128)(2,1)S(1)}, u32[]{:S(2)}, u32[]{:S(2)}) async-start(bf16[16,8,1024]{2,1,0:T(8,128)(2,1)} %gather_rows.3), calls=%async_computation.19 | async-start | bytes 524288 | tf_op jit(solution)/shard_map/all_to_all | solution.py:287
  331.6 1.8 last.1
  333.4 9.1 %all-to-all-done.19.parts_0 = bf16[16,8,1024]{2,1,0:T(8,128)(2,1)S(1)} async-done(((bf16[16,8,1024]{2,1,0:T(8,128)(2,1)}), bf16[16,8,1024]{2,1,0:T(8,128)(2,1)S(1)}, u32[]{:S(2)}, u32[]{:S(2)}) %all-to-all-start.19) | async-done | bytes 262176 | tf_op jit(solution)/shard_map/all_to_all | solution.py:287
  (120 shorter events, 12.6 us)
Async XLA Ops:
  0.6 25.7 %collective-permute-start = (bf16[128,1024]{1,0:T(8,128)(2,1)}, bf16[128,1024]{1,0:T(8,128)(2,1)S(1)}, u32[]{:S(2)}, u32[]{:S(2)}) collective-permute-start(bf16[128,1024]{1,0:T(8,128)(2,1)} %bitcast.16), channel_id=1, source_target_pairs={{0,1},{1,2},{2,3},{3,4},{4,5},{5,6},{6,7},{7,8},{8,9},{9,10},{10,1... | collective-permute-start | bytes 786440 | tf_op jit(solution)/shard_map/ppermute | solution.py:305
  4.5 21.8 %collective-permute-start.1 = (bf16[128,1024]{1,0:T(8,128)(2,1)}, bf16[128,1024]{1,0:T(8,128)(2,1)S(1)}, u32[]{:S(2)}, u32[]{:S(2)}) collective-permute-start(bf16[128,1024]{1,0:T(8,128)(2,1)} %bitcast.17), channel_id=1, source_target_pairs={{1,0},{2,1},{3,2},{4,3},{5,4},{6,5},{7,6},{8,7},{9,8},{10,9},{11,1... | collective-permute-start | bytes 786440 | tf_op jit(solution)/shard_map/ppermute | solution.py:305
  6.5 1.0 copy-start.3
  8.3 18.0 %all-to-all-start = ((f32[16,1,2048]{2,1,0:T(1,128)}), f32[16,1,2048]{2,1,0:T(1,128)S(1)}, u32[]{:S(2)}, u32[]{:S(2)}) async-start(f32[16,1,2048]{2,1,0:T(1,128)} %first.1), calls=%async_computation | async-start | bytes 262144 | tf_op jit(solution)/shard_map/all_to_all | solution.py:287
  27.0 15.0 %all-to-all-start.1 = ((f32[16,1,2048]{2,1,0:T(1,128)}), f32[16,1,2048]{2,1,0:T(1,128)S(1)}, u32[]{:S(2)}, u32[]{:S(2)}) async-start(f32[16,1,2048]{2,1,0:T(1,128)} %merge_moments.4), calls=%async_computation.1 | async-start | bytes 262144 | tf_op jit(solution)/shard_map/all_to_all | solution.py:287
  34.2 35.2 %copy-start = (bf16[2,1024,512]{2,1,0:T(8,128)(2,1)S(1)}, bf16[2,1024,512]{2,1,0:T(8,128)(2,1)}, u32[]{:S(2)}) copy-start(bf16[2,1024,512]{2,1,0:T(8,128)(2,1)} %project.5) | copy-start | bytes 6291460
  42.0 1.0 copy-start.4
  43.0 0.7 copy-start.29
  43.7 0.7 copy-start.33
  44.4 25.1 %copy-start.5 = (bf16[2,64,1024]{2,1,0:T(8,128)(2,1)S(1)}, bf16[2,64,1024]{2,1,0:T(8,128)(2,1)}, u32[]{:S(2)}) copy-start(bf16[2,64,1024]{2,1,0:T(8,128)(2,1)} %param.10) | copy-start | bytes 786436
  44.4 25.1 %copy-start.32 = (f32[2,512]{1,0:T(2,128)S(1)}, f32[2,512]{1,0:T(2,128)}, u32[]{:S(2)}) copy-start(f32[2,512]{1,0:T(2,128)} %gains.14) | copy-start | bytes 12292
  44.4 25.1 %copy-start.37 = (f32[2,512]{1,0:T(2,128)S(1)}, f32[2,512]{1,0:T(2,128)}, u32[]{:S(2)}) copy-start(f32[2,512]{1,0:T(2,128)} %biases.7) | copy-start | bytes 12292
  47.5 0.8 copy-start.18
  48.3 21.2 %copy-start.7 = (bf16[128,1024]{1,0:T(8,128)(2,1)}, bf16[128,1024]{1,0:T(8,128)(2,1)S(1)}, u32[]{:S(2)}) copy-start(bf16[128,1024]{1,0:T(8,128)(2,1)S(1)} %get-tuple-element.87.taps) | copy-start | bytes 786436
  48.3 51.9 %copy-start.34 = (f32[2,1024]{1,0:T(2,128)}, f32[2,1024]{1,0:T(2,128)S(1)}, u32[]{:S(2)}) copy-start(f32[2,1024]{1,0:T(2,128)S(1)} %get-tuple-element.75.stat) | copy-start | bytes 24580
  70.1 33.2 %copy-start.40 = (f32[1,512]{1,0:T(1,128)}, f32[1,512]{1,0:T(1,128)S(1)}, u32[]{:S(2)}) copy-start(f32[1,512]{1,0:T(1,128)S(1)} %get-tuple-element.73.factor) | copy-start | bytes 6148
  70.1 112.3 %copy-start.16 = (f32[128,512]{1,0:T(8,128)}, f32[128,512]{1,0:T(8,128)S(1)}, u32[]{:S(2)}) copy-start(f32[128,512]{1,0:T(8,128)S(1)} %get-tuple-element.69.normed) | copy-start | bytes 786436
  70.1 15.5 %collective-permute-start.2 = (bf16[128,1024]{1,0:T(8,128)(2,1)S(1)}, bf16[128,1024]{1,0:T(8,128)(2,1)S(1)}, u32[]{:S(2)}, u32[]{:S(2)}) collective-permute-start(bf16[128,1024]{1,0:T(8,128)(2,1)S(1)} %get-tuple-element.55.x), channel_id=1, source_target_pairs={{0,8},{1,9},{2,10},{3,11},{4,12},{5,13},{6,14},{7,15},{8,16},{9,17... | collective-permute-start | bytes 786440 | tf_op jit(solution)/shard_map/ppermute | solution.py:305
  72.6 13.0 %collective-permute-start.3 = (bf16[128,1024]{1,0:T(8,128)(2,1)S(1)}, bf16[128,1024]{1,0:T(8,128)(2,1)S(1)}, u32[]{:S(2)}, u32[]{:S(2)}) collective-permute-start(bf16[128,1024]{1,0:T(8,128)(2,1)S(1)} %get-tuple-element.55.x), channel_id=1, source_target_pairs={{8,0},{9,1},{10,2},{11,3},{12,4},{13,5},{14,6},{15,7},{16,8},{17,9... | collective-permute-start | bytes 786440 | tf_op jit(solution)/shard_map/ppermute | solution.py:305
  100.3 24.3 %copy-start.6 = (bf16[2,64,1024]{2,1,0:T(8,128)(2,1)S(1)}, bf16[2,64,1024]{2,1,0:T(8,128)(2,1)}, u32[]{:S(2)}) copy-start(bf16[2,64,1024]{2,1,0:T(8,128)(2,1)} %param.19) | copy-start | bytes 786436
  103.4 54.0 %copy-start.10 = (bf16[128,1024]{1,0:T(8,128)(2,1)}, bf16[128,1024]{1,0:T(8,128)(2,1)S(1)}, u32[]{:S(2)}) copy-start(bf16[128,1024]{1,0:T(8,128)(2,1)S(1)} %get-tuple-element.79.taps) | copy-start | bytes 786436
  125.8 31.7 %copy-start.20 = (bf16[128,512]{1,0:T(8,128)(2,1)}, bf16[128,512]{1,0:T(8,128)(2,1)S(1)}, u32[]{:S(2)}) copy-start(bf16[128,512]{1,0:T(8,128)(2,1)S(1)} %get-tuple-element.81.hidden) | copy-start | bytes 393220
  125.8 14.3 %collective-permute-start.4 = (bf16[128,1024]{1,0:T(8,128)(2,1)S(1)}, bf16[128,1024]{1,0:T(8,128)(2,1)S(1)}, u32[]{:S(2)}, u32[]{:S(2)}) collective-permute-start(bf16[128,1024]{1,0:T(8,128)(2,1)S(1)} %get-tuple-element.60), channel_id=1, source_target_pairs={{0,8},{1,9},{2,10},{3,11},{4,12},{5,13},{6,14},{7,15},{8,16},{9,17... | collective-permute-start | bytes 786440 | tf_op jit(solution)/shard_map/ppermute | solution.py:305
  128.2 11.8 %collective-permute-start.5 = (bf16[128,1024]{1,0:T(8,128)(2,1)S(1)}, bf16[128,1024]{1,0:T(8,128)(2,1)S(1)}, u32[]{:S(2)}, u32[]{:S(2)}) collective-permute-start(bf16[128,1024]{1,0:T(8,128)(2,1)S(1)} %get-tuple-element.60), channel_id=1, source_target_pairs={{8,0},{9,1},{10,2},{11,3},{12,4},{13,5},{14,6},{15,7},{16,8},{17,9... | collective-permute-start | bytes 786440 | tf_op jit(solution)/shard_map/ppermute | solution.py:305
  157.4 25.0 %copy-start.42 = (f32[1,512]{1,0:T(1,128)}, f32[1,512]{1,0:T(1,128)S(1)}, u32[]{:S(2)}) copy-start(f32[1,512]{1,0:T(1,128)S(1)} %get-tuple-element.76.rest_0_) | copy-start | bytes 6148
  157.4 25.4 %copy-start.44 = (f32[1,512]{1,0:T(1,128)}, f32[1,512]{1,0:T(1,128)S(1)}, u32[]{:S(2)}) copy-start(f32[1,512]{1,0:T(1,128)S(1)} %get-tuple-element.77.rest_1_) | copy-start | bytes 6148
  157.4 25.0 %copy-start.30 = (f32[2,1024]{1,0:T(2,128)S(1)}, f32[2,1024]{1,0:T(2,128)}, u32[]{:S(2)}) copy-start(f32[2,1024]{1,0:T(2,128)} %gains.15) | copy-start | bytes 24580
  159.5 48.4 %collective-permute-start.8 = (bf16[1024,1024]{1,0:T(8,128)(2,1)}, bf16[1024,1024]{1,0:T(8,128)(2,1)}, u32[]{:S(2)}, u32[]{:S(2)}) collective-permute-start(bf16[1024,1024]{1,0:T(8,128)(2,1)} %give.2), channel_id=1, source_target_pairs={{0,128},{128,0},{1,129},{129,1},{2,130},{130,2},{3,131},{131,3},{4... | collective-permute-start | bytes 6291464 | tf_op jit(solution)/shard_map/ppermute | solution.py:318
  182.8 0.7 copy-start.27
  183.5 17.4 %copy-start.38 = (f32[1,1024]{1,0:T(1,128)}, f32[1,1024]{1,0:T(1,128)S(1)}, u32[]{:S(2)}) copy-start(f32[1,1024]{1,0:T(1,128)S(1)} %get-tuple-element.85.given_bias) | copy-start | bytes 12292
  183.5 17.4 %collective-permute-start.6 = (bf16[128,1024]{1,0:T(8,128)(2,1)S(1)}, bf16[128,1024]{1,0:T(8,128)(2,1)S(1)}, u32[]{:S(2)}, u32[]{:S(2)}) collective-permute-start(bf16[128,1024]{1,0:T(8,128)(2,1)S(1)} %get-tuple-element.71), channel_id=1, source_target_pairs={{0,1},{1,2},{2,3},{3,4},{4,5},{5,6},{6,7},{7,8},{8,9},{9,10},{10,1... | collective-permute-start | bytes 786440 | tf_op jit(solution)/shard_map/ppermute | solution.py:305
  186.2 14.8 %collective-permute-start.7 = (bf16[128,1024]{1,0:T(8,128)(2,1)S(1)}, bf16[128,1024]{1,0:T(8,128)(2,1)S(1)}, u32[]{:S(2)}, u32[]{:S(2)}) collective-permute-start(bf16[128,1024]{1,0:T(8,128)(2,1)S(1)} %get-tuple-element.71), channel_id=1, source_target_pairs={{1,0},{2,1},{3,2},{4,3},{5,4},{6,5},{7,6},{8,7},{9,8},{10,9},{11,1... | collective-permute-start | bytes 786440 | tf_op jit(solution)/shard_map/ppermute | solution.py:305
  201.6 0.7 copy-start.12
  202.3 0.7 copy-start.14
  203.0 12.5 %all-to-all-start.13 = ((f32[16,1,1024]{2,1,0:T(1,128)}), f32[16,1,1024]{2,1,0:T(1,128)S(1)}, u32[]{:S(2)}, u32[]{:S(2)}) async-start(f32[16,1,1024]{2,1,0:T(1,128)} %merge_sums.6), calls=%async_computation.13 | async-start | bytes 131072 | tf_op jit(solution)/shard_map/all_to_all | solution.py:287
  207.9 1.0 copy-start.11
  208.8 0.9 copy-start.21
  212.1 1.3 copy-start.1
  215.5 5.2 %copy-start.17 = (f32[128,512]{1,0:T(8,128)S(1)}, f32[128,512]{1,0:T(8,128)}, u32[]{:S(2)}) copy-start(f32[128,512]{1,0:T(8,128)} %copy-done.16) | copy-start | bytes 786436
  215.5 35.4 %all-to-all-start.15 = ((bf16[16,64,1024]{2,1,0:T(8,128)(2,1)}), bf16[16,64,1024]{2,1,0:T(8,128)(2,1)S(1)}, u32[]{:S(2)}, u32[]{:S(2)}) async-start(bf16[16,64,1024]{2,1,0:T(8,128)(2,1)} %bitcast.14), calls=%async_computation.15 | async-start | bytes 4194304 | tf_op jit(solution)/shard_map/all_to_all | solution.py:287
  220.7 1.0 copy-start.13
  221.7 0.9 copy-start.15
  222.6 1.0 copy-start.19
  223.7 0.9 copy-start.28
  224.6 0.7 copy-start.35
  225.3 0.7 copy-start.41
  226.0 0.7 copy-start.43
  226.7 0.7 copy-start.45
  227.4 4.4 %copy-start.8 = (bf16[128,1024]{1,0:T(8,128)(2,1)S(1)}, bf16[128,1024]{1,0:T(8,128)(2,1)}, u32[]{:S(2)}) copy-start(bf16[128,1024]{1,0:T(8,128)(2,1)} %copy-done.7) | copy-start | bytes 786436
  230.9 0.8 copy-start.22
  231.7 2.1 copy-start.31
  233.8 33.2 %collective-permute-start.9 = (bf16[1024,1024]{1,0:T(8,128)(2,1)}, bf16[1024,1024]{1,0:T(8,128)(2,1)}, u32[]{:S(2)}, u32[]{:S(2)}) collective-permute-start(bf16[1024,1024]{1,0:T(8,128)(2,1)} %give.3), channel_id=1, source_target_pairs={{0,128},{128,0},{1,129},{129,1},{2,130},{130,2},{3,131},{131,3},{4... | collective-permute-start | bytes 6291464 | tf_op jit(solution)/shard_map/ppermute | solution.py:318
  251.0 12.4 %all-to-all-start.14 = ((f32[16,1,2048]{2,1,0:T(1,128)}), f32[16,1,2048]{2,1,0:T(1,128)S(1)}, u32[]{:S(2)}, u32[]{:S(2)}) async-start(f32[16,1,2048]{2,1,0:T(1,128)} %copy-done.31), calls=%async_computation.14 | async-start | bytes 262144 | tf_op jit(solution)/shard_map/all_to_all | solution.py:287
  263.3 7.0 %copy-start.24 = (f32[16,1,2048]{2,1,0:T(1,128)}, f32[16,1,2048]{2,1,0:T(1,128)S(1)}, u32[]{:S(2)}) copy-start(f32[16,1,2048]{2,1,0:T(1,128)S(1)} %all-to-all-done.14.parts) | copy-start | bytes 393220
  263.3 14.7 %all-to-all-start.16 = ((bf16[16,8,1024]{2,1,0:T(8,128)(2,1)}), bf16[16,8,1024]{2,1,0:T(8,128)(2,1)S(1)}, u32[]{:S(2)}, u32[]{:S(2)}) async-start(bf16[16,8,1024]{2,1,0:T(8,128)(2,1)} %gather_rows.2), calls=%async_computation.16 | async-start | bytes 524288 | tf_op jit(solution)/shard_map/all_to_all | solution.py:287
  267.1 1.0 copy-start.9
  270.3 1.3 copy-start.2
  278.1 33.6 %all-to-all-start.18 = ((bf16[16,64,1024]{2,1,0:T(8,128)(2,1)}), bf16[16,64,1024]{2,1,0:T(8,128)(2,1)S(1)}, u32[]{:S(2)}, u32[]{:S(2)}) async-start(bf16[16,64,1024]{2,1,0:T(8,128)(2,1)} %bitcast.15), calls=%async_computation.18 | async-start | bytes 4194304 | tf_op jit(solution)/shard_map/all_to_all | solution.py:287
  281.8 0.9 copy-start.25
  282.7 48.9 %copy-start.23 = (f32[128,1024]{1,0:T(8,128)S(1)}, f32[128,1024]{1,0:T(8,128)}, u32[]{:S(2)}) copy-start(f32[128,1024]{1,0:T(8,128)} %copy-done.22) | copy-start | bytes 1572868
  282.7 48.9 %copy-start.36 = (f32[2,1024]{1,0:T(2,128)S(1)}, f32[2,1024]{1,0:T(2,128)}, u32[]{:S(2)}) copy-start(f32[2,1024]{1,0:T(2,128)} %copy-done.34) | copy-start | bytes 24580
  282.7 48.9 %copy-start.39 = (f32[1,1024]{1,0:T(1,128)S(1)}, f32[1,1024]{1,0:T(1,128)}, u32[]{:S(2)}) copy-start(f32[1,1024]{1,0:T(1,128)} %copy-done.38) | copy-start | bytes 12292
  311.7 12.2 %all-to-all-start.17 = ((f32[16,1,2048]{2,1,0:T(1,128)}), f32[16,1,2048]{2,1,0:T(1,128)}, u32[]{:S(2)}, u32[]{:S(2)}) async-start(f32[16,1,2048]{2,1,0:T(1,128)} %copy-done.26), calls=%async_computation.17 | async-start | bytes 262144 | tf_op jit(solution)/shard_map/all_to_all | solution.py:287
  323.9 18.7 %all-to-all-start.19 = ((bf16[16,8,1024]{2,1,0:T(8,128)(2,1)}), bf16[16,8,1024]{2,1,0:T(8,128)(2,1)S(1)}, u32[]{:S(2)}, u32[]{:S(2)}) async-start(bf16[16,8,1024]{2,1,0:T(8,128)(2,1)} %gather_rows.3), calls=%async_computation.19 | async-start | bytes 524288 | tf_op jit(solution)/shard_map/all_to_all | solution.py:287
  (1 other events, 0.7 us)

commit v3 on v2

--- a/solution.py
+++ b/solution.py
@@ -18,6 +18,7 @@
 F32 = jnp.float32
 BF16 = jnp.bfloat16
 ROWS, CH, HALF = 128, 1024, 512
+VMEM_LIMIT = 60 << 20
 TOTAL = 32768.0
 TANH_SCALE = 0.7978845608028654
 CUBE = 0.044715
@@ -85,7 +86,10 @@
 def k_merge(kind, parts, *rest):
     out = rest[-1]
     merge = merged_moments if kind == "moments" else merged_sums
-    spread_out(out, *merge(parts))
+    if out.shape[0] == 1:
+        out[...] = jnp.concatenate(merge(parts), axis=1)
+    else:
+        spread_out(out, *merge(parts))
 
 
 def k_entry(layer, parts, x, lower, upper, masks, weight, gains, biases, taps, slope, conv, stat, out):
@@ -152,7 +156,7 @@
     layer, parts, grad, normed, factor, lower, upper, masks, gains, weight, slope, x, stat, *rest
 ):
     if layer == 0:
-        given_gain, given_bias, three, grad_in, gain_out, bias_out, out = rest
+        given_gain, given_bias, _, three, grad_in, gain_out, bias_out, out = rest
     else:
         three, grad_in, gain_out, bias_out, out = rest
     total, cross = merged_sums(parts)
@@ -186,7 +190,10 @@
 
 
 def back_entry(layer, parts, grad_in, x, stat, gains, upstream):
-    total, cross = merged_sums(parts)
+    if layer == 0:
+        total, cross = parts[:, :CH], parts[:, CH:]
+    else:
+        total, cross = merged_sums(parts)
     factor = stat[1:2]
     normed = (x[...].astype(F32) - stat[0:1]) * factor
     branch = (gains[layer : layer + 1] * factor) * (
@@ -224,14 +231,16 @@
     out[:, 3 * HALF // 2 :] = product_tn(upstream[...], half_of(hidden, True)).astype(BF16)
 
 
-def k_keep(taps, three, upstream, hidden, arrived, out):
+def k_keep(taps, three, upstream, hidden, arrived, *rest):
+    out = rest[-1]
     first = arrived[:, : 3 * HALF // 2].astype(F32)
     out[:, : 3 * HALF // 2] = (product_tn(taps[...], half_of(three, False)) + first).astype(BF16)
     second = arrived[:, 3 * HALF // 2 :].astype(F32)
     out[:, 3 * HALF // 2 :] = (product_tn(upstream[...], half_of(hidden, False)) + second).astype(BF16)
 
 
-def k_gather(parts, out):
+def k_gather(parts, *rest):
+    out = rest[-1]
     for z in range(8):
         rows = slice(8 * z, 8 * z + 8)
         total = parts[0, rows].astype(F32)
@@ -242,15 +251,19 @@
         out[8 + z] = total
 
 
-def k_rows(parts_0, parts_1, kernel_out, project_out):
-    cut = 3 * HALF // 2
-    for layer, parts in enumerate((parts_0, parts_1)):
-        for d in range(2):
-            total = parts[8 * d].astype(F32)
-            for z in range(1, 8):
-                total = total + parts[8 * d + z].astype(F32)
-            kernel_out[layer, :, d * cut : (d + 1) * cut] = total[:, :cut]
-            project_out[layer, :, d * HALF // 2 : (d + 1) * HALF // 2] = total[:, cut:]
+def k_rows(parts_0, own_1, other_1, kernel_out, project_out):
+    cut, width = 3 * HALF // 2, HALF // 2
+    place = lax.axis_index("dp")
+    for d in range(2):
+        total = parts_0[8 * d].astype(F32)
+        for z in range(1, 8):
+            total = total + parts_0[8 * d + z].astype(F32)
+        kernel_out[0, :, d * cut : (d + 1) * cut] = total[:, :cut]
+        project_out[0, :, d * width : (d + 1) * width] = total[:, cut:]
+    for rows, d in ((own_1, place), (other_1, 1 - place)):
+        rows = rows[...].astype(F32)
+        kernel_out[1, :, pl.ds(pl.multiple_of(d * cut, 128), cut)] = rows[:, :cut]
+        project_out[1, :, pl.ds(pl.multiple_of(d * width, 128), width)] = rows[:, cut:]
 
 
 def whole(value):
@@ -279,7 +292,7 @@
         out_shape=shapes,
         name=name,
         cost_estimate=pl.CostEstimate(flops=flops, bytes_accessed=moved, transcendentals=0),
-        compiler_params=pltpu.CompilerParams(vmem_limit_bytes=48 << 20),
+        compiler_params=pltpu.CompilerParams(vmem_limit_bytes=VMEM_LIMIT),
     )(*operands, *waits)
 
 
@@ -310,20 +323,39 @@
     return passed_along(rows, hops), passed_along(rows, -hops)
 
 
-def chip_share(taps, three, upstream, hidden):
+def chip_share(taps, three, upstream, hidden, waits=()):
     flops = 2 * ROWS * CH * CH
     (given,) = call(
         k_give, [((CH, CH), BF16)], taps, three, upstream, hidden, name="give", flops=flops
     )
     arrived = lax.ppermute(given, "dp", [(0, 1), (1, 0)])
     (share,) = call(
-        k_keep, [((CH, CH), BF16)], taps, three, upstream, hidden, arrived, name="keep", flops=flops
-    )
-    return exchange(share.reshape(GROUP, CH // GROUP, CH), SECOND_STAGE)
-
-
-def chip_rows(parts):
-    (rows,) = call(k_gather, [((GROUP, 8, CH), BF16)], parts, name="gather_rows")
+        k_keep,
+        [((CH, CH), BF16)],
+        taps,
+        three,
+        upstream,
+        hidden,
+        arrived,
+        waits=waits,
+        name="keep",
+        flops=flops,
+    )
+    return share
+
+
+def swapped(value, axis, step):
+    pairs = [(i, i ^ step) for i in range(SIZES[axis])]
+    return lax.ppermute(value, axis, pairs)
+
+
+def rows_over(share, axis):
+    return lax.psum_scatter(share, axis, scatter_dimension=0, tiled=True)
+
+
+def rows_at_once(share, waits):
+    parts = exchange(share.reshape(GROUP, CH // GROUP, CH), SECOND_STAGE)
+    (rows,) = call(k_gather, [((GROUP, 8, CH), BF16)], parts, waits=waits, name="gather_rows")
     return exchange(rows, FIRST_STAGE)
 
 
@@ -422,7 +454,9 @@
         name="turn",
     )
 
-    def back_middle(layer, parts, grad, normed, factor, sides, slope, stream, stat, *given):
+    def back_middle(
+        layer, parts, grad, normed, factor, sides, slope, stream, stat, *given, waits=()
+    ):
         rows = 2 - layer
         return call(
             functools.partial(k_back_middle, layer),
@@ -446,6 +480,7 @@
             stat,
             *given,
             layers={8: layer},
+            waits=waits,
             name="back_middle",
             flops=conv_flops,
         )
@@ -479,18 +514,38 @@
         name="back_entry",
     )
     sides = neighbours(pair, FIRST_DILATION)
-    chip_1 = chip_share(taps_1, three_1, grad_2, hidden_1)
+    rows_1 = rows_over(chip_share(taps_1, three_1, grad_2, hidden_1), "y")
     parts = over_all(payload, "sums", sides)
     three_0, grad_in, grad_gains_mid, grad_biases_mid, payload = back_middle(
-        0, parts, grad, normed_0, factor_0, sides, slope_0, stream_0, stat_0, gain_mid, bias_mid
-    )
-    rows_1 = chip_rows(chip_1)
-    chip_0 = chip_share(taps_0, three_0, grad_1, hidden_0)
-    parts = over_all(payload, "sums", (rows_1,))
+        0,
+        parts,
+        grad,
+        normed_0,
+        factor_0,
+        sides,
+        slope_0,
+        stream_0,
+        stat_0,
+        gain_mid,
+        bias_mid,
+        waits=(rows_1,),
+    )
+    rows_1 = rows_over(rows_1, "x")
+    (sums,) = call(
+        functools.partial(k_merge, "sums"),
+        [((1, 2 * CH), F32)],
+        exchange(payload, FIRST_STAGE),
+        name="merge_sums",
+    )
+    chip_0 = chip_share(taps_0, three_0, grad_1, hidden_0, (sums, rows_1))
+    rows_1 = rows_over(rows_1, "z")
+    for axis in ("x", "y"):
+        for step in (1, 2):
+            sums = sums + swapped(sums, axis, step)
     grad_gains_in, grad_biases_in, grad_0 = call(
         k_last,
         [((2, CH), F32), ((2, CH), F32), ((ROWS, CH), BF16)],
-        parts,
+        sums,
         grad_in,
         stream_0,
         stat_0,
@@ -503,8 +558,9 @@
     grad_conv, grad_proj = call(
         k_rows,
         [((2, 8, 3 * HALF), F32), ((2, 8, HALF), F32)],
-        chip_rows(chip_0),
+        rows_at_once(chip_0, (sums, rows_1)),
         rows_1,
+        swapped(rows_1, "dp", 1),
         name="rows",
     )
     return (

time: 345 us -> 377 us (1.093)
  blocking collectives: 128 us -> 161 us
  Pallas kernels: 30.8 us -> 60.6 us
  waiting for transfers between devices: 91.3 us -> 62.9 us
  between operations: 1.11 us -> 14 us
  local copies, waits for them, and re-layouts: 22.1 us -> 13.3 us
  starting transfers between devices: 69.5 us -> 61.6 us
    all_to_all x9 -> x4, waiting for transfers between devices: 91.3 us -> 21.8 us  [exchange(): return lax.all_to_all(value, axes, 0, 0, tiled=True)]
    all_to_all x11 -> x13, blocking collectives: 128 us -> 161 us  [exchange(): return lax.all_to_all(value, axes, 0, 0, tiled=True)]
    ppermute x0 -> x5, waiting for transfers between devices: none -> 31.2 us  [swapped(): return lax.ppermute(value, axis, pairs)]
    pallas_call x24 -> x23, Pallas kernels: 30.8 us -> 60.6 us  [call(): pl.pallas_call(kernel, grid=(1,), in_specs=specs, out_specs=[whole(shape)...]
    all_to_all x9 -> x4, starting transfers between devices: 50.3 us -> 30.2 us  [exchange(): return lax.all_to_all(value, axes, 0, 0, tiled=True)]
    unnamed x92 -> x38, local copies, waits for them, and re-layouts: 20.7 us -> 11.9 us
    ppermute x0 -> x5, starting transfers between devices: none -> 7.95 us  [swapped(): return lax.ppermute(value, axis, pairs)]
    reduce_scatter x0 -> x3, waiting for transfers between devices: none -> 4.83 us  [rows_over(): return lax.psum_scatter(share, axis, scatter_dimension=0, tiled=True)]
  transfers between devices with their start and end apart: 19 -> 22, of which waited for: 9 -> 10; matrix products, arithmetic and copies ran while one was open for 1% -> 1% of each run, Pallas kernels for 5% -> 3%
where the time goes in v3:
time: 377 us; the launch traced here: 375 us
  blocking collectives  161 us (43%)
  waiting for transfers between devices  62.9 us (17%)
  starting transfers between devices  61.6 us (16%)
  Pallas kernels  60.6 us (16%)
  between operations  14 us (4%)
  local copies, waits for them, and re-layouts  13.3 us (4%)
    all_to_all x13, blocking collectives, exchange(): return lax.all_to_all(value, axes, 0, 0, tiled=True)  161 us
    pallas_call x23, Pallas kernels, call(): pl.pallas_call(kernel, grid=(1,), in_specs=specs, out_specs=[whole(shape)...  60.6 us
    ppermute x5, waiting for transfers between devices, swapped(): return lax.ppermute(value, axis, pairs)  31.2 us
    all_to_all x4, starting transfers between devices, exchange(): return lax.all_to_all(value, axes, 0, 0, tiled=True)  30.2 us
    ppermute x8, starting transfers between devices, passed_along(): lax.ppermute(value, SEQ, [(source, source + steps) for source in range(le...  23.4 us
    all_to_all x4, waiting for transfers between devices, exchange(): return lax.all_to_all(value, axes, 0, 0, tiled=True)  21.8 us
    unnamed x38, local copies, waits for them, and re-layouts  11.9 us
    ppermute x5, starting transfers between devices, swapped(): return lax.ppermute(value, axis, pairs)  7.95 us
  transfers between devices with their start and end apart: 22, of which 10 were waited for; matrix products, arithmetic and copies ran while one was open for 1% of the time, Pallas kernels for 3%

profile of v3, /device:TPU:32, one launch (start us, length us, event | category | flops | bytes accessed | tf_op | source)
XLA Modules:
  0.0 375.2 jit_solution(14701614620701024094)
XLA Ops:
  7.2 3.8 %collective-permute-start.1 = (bf16[128,1024]{1,0:T(8,128)(2,1)}, bf16[128,1024]{1,0:T(8,128)(2,1)S(1)}, u32[]{:S(2)}, u32[]{:S(2)}) collective-permute-start(bf16[128,1024]{1,0:T(8,128)(2,1)} %bitcast.14), channel_id=1, source_target_pairs={{1,0},{2,1},{3,2},{4,3},{5,4},{6,5},{7,6},{8,7},{9,8},{10,9},{11,1... | collective-permute-start | bytes 786440 | tf_op jit(solution)/shard_map/ppermute | solution.py:318
  10.9 2.1 collective-permute-start
  13.0 1.8 first.1
  14.8 9.4 %all-to-all-start = ((f32[16,1,2048]{2,1,0:T(1,128)}), f32[16,1,2048]{2,1,0:T(1,128)S(1)}, u32[]{:S(2)}, u32[]{:S(2)}) async-start(f32[16,1,2048]{2,1,0:T(1,128)} %first.1), calls=%async_computation | async-start | bytes 262144 | tf_op jit(solution)/shard_map/all_to_all | solution.py:300
  26.3 6.1 %all-to-all-done.parts = f32[16,1,2048]{2,1,0:T(1,128)S(1)} async-done(((f32[16,1,2048]{2,1,0:T(1,128)}), f32[16,1,2048]{2,1,0:T(1,128)S(1)}, u32[]{:S(2)}, u32[]{:S(2)}) %all-to-all-start) | async-done | bytes 131104 | tf_op jit(solution)/shard_map/all_to_all | solution.py:300
  33.8 1.6 merge_moments.4
  35.4 8.9 %all-to-all-start.1 = ((f32[16,1,2048]{2,1,0:T(1,128)}), f32[16,1,2048]{2,1,0:T(1,128)S(1)}, u32[]{:S(2)}, u32[]{:S(2)}) async-start(f32[16,1,2048]{2,1,0:T(1,128)} %merge_moments.4), calls=%async_computation.1 | async-start | bytes 262144 | tf_op jit(solution)/shard_map/all_to_all | solution.py:300
  45.2 7.1 %all-to-all-done.1.parts = f32[16,1,2048]{2,1,0:T(1,128)S(1)} async-done(((f32[16,1,2048]{2,1,0:T(1,128)}), f32[16,1,2048]{2,1,0:T(1,128)S(1)}, u32[]{:S(2)}, u32[]{:S(2)}) %all-to-all-start.1) | async-done | bytes 131104 | tf_op jit(solution)/shard_map/all_to_all | solution.py:300
  53.0 3.9 %entry.2 = (bf16[128,1024]{1,0:T(8,128)(2,1)}, f32[128,1024]{1,0:T(8,128)}, f32[128,512]{1,0:T(8,128)}, f32[2,1024]{1,0:T(2,128)}, f32[16,1,1024]{2,1,0:T(1,128)}) custom-call(f32[16,1,2048]{2,1,0:T(1,128)} %copy-done.12, bf16[128,1024]{1,0:T(8,128)(2,1)} %bitcast.17, bf16[128,1024]{1,0:T(8,128)(2,1)} %copy-done.4, bf16[128,1024]{1,0:T(8,128)(2,1)} %copy-done.3, ...), custom_call_target="tpu_custom_call" | custom-call | flops 402653184 | bytes 8349696 | tf_op jit(solution)/shard_map/entry/pallas_call | solution.py:287
  56.9 11.3 %all_to_all.85.parts = f32[16,1,1024]{2,1,0:T(1,128)} all-to-all(f32[16,1,1024]{2,1,0:T(1,128)} %get-tuple-element.52), channel_id=1, replica_groups=mesh['dp'=2,'y'=4,'x'=4,'z'=8] {'dp','z'}, dimensions={0} | all-to-all | bytes 131072 | tf_op jit(solution)/shard_map/all_to_all | solution.py:300
  68.3 1.5 merge_moments.5
  69.8 11.8 %all_to_all.86.parts = f32[16,1,1024]{2,1,0:T(1,128)} all-to-all(f32[16,1,1024]{2,1,0:T(1,128)} %merge_moments.5), channel_id=1, replica_groups=mesh['dp'=2,'y'=4,'x'=4,'z'=8] {'y','x'}, dimensions={0} | all-to-all | bytes 131072 | tf_op jit(solution)/shard_map/all_to_all | solution.py:300
  81.6 2.8 middle.1
  84.3 1.3 collective-permute-start.3
  85.6 4.6 %collective-permute-start.2 = (bf16[128,1024]{1,0:T(8,128)(2,1)}, bf16[128,1024]{1,0:T(8,128)(2,1)S(1)}, u32[]{:S(2)}, u32[]{:S(2)}) collective-permute-start(bf16[128,1024]{1,0:T(8,128)(2,1)} %get-tuple-element.55.x), channel_id=1, source_target_pairs={{0,8},{1,9},{2,10},{3,11},{4,12},{5,13},{6,14},{7,15},{8,16},{9,17... | collective-permute-start | bytes 786440 | tf_op jit(solution)/shard_map/ppermute | solution.py:318
  90.2 13.3 %all_to_all.87.parts = f32[16,1,2048]{2,1,0:T(1,128)} all-to-all(f32[16,1,2048]{2,1,0:T(1,128)} %get-tuple-element.54), channel_id=1, replica_groups=mesh['dp'=2,'y'=4,'x'=4,'z'=8] {'dp','z'}, dimensions={0} | all-to-all | bytes 262144 | tf_op jit(solution)/shard_map/all_to_all | solution.py:300
  104.9 1.6 merge_moments.6
  106.5 13.4 %all_to_all.88.parts = f32[16,1,2048]{2,1,0:T(1,128)} all-to-all(f32[16,1,2048]{2,1,0:T(1,128)} %merge_moments.6), channel_id=1, replica_groups=mesh['dp'=2,'y'=4,'x'=4,'z'=8] {'y','x'}, dimensions={0} | all-to-all | bytes 262144 | tf_op jit(solution)/shard_map/all_to_all | solution.py:300
  119.9 3.9 %entry.3 = (bf16[128,1024]{1,0:T(8,128)(2,1)}, f32[128,1024]{1,0:T(8,128)}, f32[128,512]{1,0:T(8,128)}, f32[2,1024]{1,0:T(2,128)}, f32[16,1,1024]{2,1,0:T(1,128)}) custom-call(f32[16,1,2048]{2,1,0:T(1,128)} %all_to_all.88.parts, bf16[128,1024]{1,0:T(8,128)(2,1)} %get-tuple-element.55.x, bf16[128,1024]{1,0:T(8,128)(2,1)} %copy-done.6, ...), custom_call_target="tpu_custom_call" | custom-call | flops 402653184 | bytes 8349696 | tf_op jit(solution)/shard_map/entry/pallas_call | solution.py:287
  123.9 11.4 %all_to_all.89.parts = f32[16,1,1024]{2,1,0:T(1,128)} all-to-all(f32[16,1,1024]{2,1,0:T(1,128)} %get-tuple-element.56), channel_id=1, replica_groups=mesh['dp'=2,'y'=4,'x'=4,'z'=8] {'dp','z'}, dimensions={0} | all-to-all | bytes 131072 | tf_op jit(solution)/shard_map/all_to_all | solution.py:300
  135.3 1.5 merge_moments.7
  136.8 11.8 %all_to_all.90.parts = f32[16,1,1024]{2,1,0:T(1,128)} all-to-all(f32[16,1,1024]{2,1,0:T(1,128)} %merge_moments.7), channel_id=1, replica_groups=mesh['dp'=2,'y'=4,'x'=4,'z'=8] {'y','x'}, dimensions={0} | all-to-all | bytes 131072 | tf_op jit(solution)/shard_map/all_to_all | solution.py:300
  148.6 3.0 turn.1
  151.6 1.3 collective-permute-start.5
  152.9 4.6 %collective-permute-start.4 = (bf16[128,1024]{1,0:T(8,128)(2,1)}, bf16[128,1024]{1,0:T(8,128)(2,1)S(1)}, u32[]{:S(2)}, u32[]{:S(2)}) collective-permute-start(bf16[128,1024]{1,0:T(8,128)(2,1)} %get-tuple-element.60), channel_id=1, source_target_pairs={{0,8},{1,9},{2,10},{3,11},{4,12},{5,13},{6,14},{7,15},{8,16},{9,17... | collective-permute-start | bytes 786440 | tf_op jit(solution)/shard_map/ppermute | solution.py:318
  157.4 12.1 %all_to_all.91.parts = f32[16,1,1024]{2,1,0:T(1,128)} all-to-all(f32[16,1,1024]{2,1,0:T(1,128)} %get-tuple-element.59), channel_id=1, replica_groups=mesh['dp'=2,'y'=4,'x'=4,'z'=8] {'dp','z'}, dimensions={0} | all-to-all | bytes 131072 | tf_op jit(solution)/shard_map/all_to_all | solution.py:300
  170.9 1.5 merge_sums.4
  172.4 13.1 %all_to_all.92.parts = f32[16,1,1024]{2,1,0:T(1,128)} all-to-all(f32[16,1,1024]{2,1,0:T(1,128)} %merge_sums.4), channel_id=1, replica_groups=mesh['dp'=2,'y'=4,'x'=4,'z'=8] {'y','x'}, dimensions={0} | all-to-all | bytes 131072 | tf_op jit(solution)/shard_map/all_to_all | solution.py:300
  185.5 4.5 %back_middle.2 = (bf16[128,1536]{1,0:T(8,128)(2,1)}, f32[128,1024]{1,0:T(8,128)}, f32[1,512]{1,0:T(1,128)}, f32[1,512]{1,0:T(1,128)}, f32[16,1,2048]{2,1,0:T(1,128)}) custom-call(f32[16,1,1024]{2,1,0:T(1,128)} %all_to_all.92.parts, f32[128,512]{1,0:T(8,128)} %get-tuple-element.61.grad, f32[128,512]{1,0:T(8,128)} %get-tuple-element.62.normed, ...), custom_call_target="tpu_custom_call" | custom-call | flops 402653184 | bytes 9261056 | tf_op jit(solution)/shard_map/back_middle/pallas_call | solution.py:287
  190.0 3.2 give.2
  193.3 4.4 %collective-permute-done.8.arrived = bf16[1024,1024]{1,0:T(8,128)(2,1)S(1)} collective-permute-done((bf16[1024,1024]{1,0:T(8,128)(2,1)}, bf16[1024,1024]{1,0:T(8,128)(2,1)S(1)}, u32[]{:S(2)}, u32[]{:S(2)}) %collective-permute-start.8) | collective-permute-done | bytes 2097184 | tf_op jit(solution)/shard_map/ppermute | solution.py:331
  197.6 1.3 copy-done.2
  199.0 4.0 %keep.2 = bf16[1024,1024]{1,0:T(8,128)(2,1)} custom-call(bf16[128,1024]{1,0:T(8,128)(2,1)} %get-tuple-element.78.taps, bf16[128,1536]{1,0:T(8,128)(2,1)} %get-tuple-element.79.three, bf16[128,1024]{1,0:T(8,128)(2,1)} %bitcast.23, bf16[128,512]{1,0:T(8,128)(2,1)} %get-tuple-element.80.hidden, bf16[1024,1024]{1,0:T(8,128)(2,1)} %copy-done.2), custom_call_target="tpu_custom_call" | custom-call | flops 268435456 | bytes 5242880 | tf_op jit(solution)/shard_map/keep/pallas_call | solution.py:287
  203.9 12.4 %all_to_all.93.parts = f32[16,1,2048]{2,1,0:T(1,128)} all-to-all(f32[16,1,2048]{2,1,0:T(1,128)S(1)} %copy-done.14), channel_id=1, replica_groups=mesh['dp'=2,'y'=4,'x'=4,'z'=8] {'dp','z'}, dimensions={0} | all-to-all | bytes 262144 | tf_op jit(solution)/shard_map/all_to_all | solution.py:300
  216.3 1.6 merge_sums.5
  217.9 12.2 %all_to_all.94.parts = f32[16,1,2048]{2,1,0:T(1,128)} all-to-all(f32[16,1,2048]{2,1,0:T(1,128)} %merge_sums.5), channel_id=1, replica_groups=mesh['dp'=2,'y'=4,'x'=4,'z'=8] {'y','x'}, dimensions={0} | all-to-all | bytes 262144 | tf_op jit(solution)/shard_map/all_to_all | solution.py:300
  230.0 2.9 back_entry.1
  233.0 2.3 collective-permute-start.7
  235.3 3.5 collective-permute-start.6
  238.8 12.4 %all_to_all.95.parts = f32[16,1,1024]{2,1,0:T(1,128)} all-to-all(f32[16,1,1024]{2,1,0:T(1,128)} %get-tuple-element.70), channel_id=1, replica_groups=mesh['dp'=2,'y'=4,'x'=4,'z'=8] {'dp','z'}, dimensions={0} | all-to-all | bytes 131072 | tf_op jit(solution)/shard_map/all_to_all | solution.py:300
  252.7 1.5 merge_sums.6
  254.1 13.1 %all_to_all.96.parts = f32[16,1,1024]{2,1,0:T(1,128)} all-to-all(f32[16,1,1024]{2,1,0:T(1,128)} %merge_sums.6), channel_id=1, replica_groups=mesh['dp'=2,'y'=4,'x'=4,'z'=8] {'y','x'}, dimensions={0} | all-to-all | bytes 131072 | tf_op jit(solution)/shard_map/all_to_all | solution.py:300
  267.3 4.5 %back_middle.3 = (bf16[128,1536]{1,0:T(8,128)(2,1)}, f32[128,1024]{1,0:T(8,128)}, f32[2,512]{1,0:T(2,128)}, f32[2,512]{1,0:T(2,128)}, f32[16,1,2048]{2,1,0:T(1,128)}) custom-call(f32[16,1,1024]{2,1,0:T(1,128)} %all_to_all.96.parts, f32[128,512]{1,0:T(8,128)} %get-tuple-element.72.grad, f32[128,512]{1,0:T(8,128)} %get-tuple-element.69.normed, ...), custom_call_target="tpu_custom_call" | custom-call | flops 402653184 | bytes 9269248 | tf_op jit(solution)/shard_map/back_middle/pallas_call | solution.py:287
  271.7 3.3 give.3
  275.1 12.4 %all_to_all.97.parts = f32[16,1,2048]{2,1,0:T(1,128)} all-to-all(f32[16,1,2048]{2,1,0:T(1,128)S(1)} %copy-done.15), channel_id=1, replica_groups=mesh['dp'=2,'y'=4,'x'=4,'z'=8] {'dp','z'}, dimensions={0} | all-to-all | bytes 262144 | tf_op jit(solution)/shard_map/all_to_all | solution.py:300
  287.5 1.5 merge_sums.7.rest_0_
  289.0 3.9 %reduce-scatter.6.cloned.1.call-done.rest_1_ = bf16[64,1024]{1,0:T(8,128)(2,1)} async-done(((bf16[256,1024]{1,0:T(8,128)(2,1)}), bf16[64,1024]{1,0:T(8,128)(2,1)}) %reduce-scatter.6.cloned.1.call-update) | async-done | bytes 131088 | tf_op jit(solution)/shard_map/reduce_scatter | solution.py:353
  293.0 1.3 copy-done.1
  294.3 4.0 %keep.3 = bf16[1024,1024]{1,0:T(8,128)(2,1)} custom-call(bf16[128,1024]{1,0:T(8,128)(2,1)} %get-tuple-element.87.taps, bf16[128,1536]{1,0:T(8,128)(2,1)} %get-tuple-element.88.three, bf16[128,1024]{1,0:T(8,128)(2,1)} %get-tuple-element.83.upstream, bf16[128,512]{1,0:T(8,128)(2,1)} %get-tuple-element.89.hidden, bf16[1024,1024]{1,0:T(8,128)(2,1)} %copy-done.1, ...), custom_call_target="tpu_custom_call" | custom-call | flops 268435456 | bytes 5242880 | tf_op jit(solution)/shard_map/keep/pallas_call | solution.py:287
  298.3 5.4 %all-to-all-start.15 = ((bf16[16,64,1024]{2,1,0:T(8,128)(2,1)}), bf16[16,64,1024]{2,1,0:T(8,128)(2,1)S(1)}, u32[]{:S(2)}, u32[]{:S(2)}) async-start(bf16[16,64,1024]{2,1,0:T(8,128)(2,1)} %bitcast.13), calls=%async_computation.17 | async-start | bytes 4194304 | tf_op jit(solution)/shard_map/all_to_all | solution.py:300
  304.5 2.0 collective-permute-start.9
  306.5 22.7 %collective-permute-done.9 = f32[1,2048]{1,0:T(1,128)S(1)} collective-permute-done((f32[1,2048]{1,0:T(1,128)S(1)}, f32[1,2048]{1,0:T(1,128)S(1)}, u32[]{:S(2)}, u32[]{:S(2)}) %collective-permute-start.9) | collective-permute-done | bytes 8224 | tf_op jit(solution)/shard_map/ppermute | solution.py:349
  329.2 1.9 collective-permute-start.10
  331.1 3.3 collective-permute-done.10
  334.5 0.9 collective-permute-start.11
  335.4 2.8 collective-permute-done.11
  338.2 2.9 collective-permute-start.12
  341.1 2.4 collective-permute-done.12
  344.9 1.3 copy-done
  346.3 2.6 gather_rows.1
  348.8 6.5 %all-to-all-start.16 = ((bf16[16,8,1024]{2,1,0:T(8,128)(2,1)}), bf16[16,8,1024]{2,1,0:T(8,128)(2,1)S(1)}, u32[]{:S(2)}, u32[]{:S(2)}) async-start(bf16[16,8,1024]{2,1,0:T(8,128)(2,1)} %gather_rows.1), calls=%async_computation.19 | async-start | bytes 524288 | tf_op jit(solution)/shard_map/all_to_all | solution.py:300
  355.6 2.1 last.1
  357.7 8.6 %all-to-all-done.16.parts_0 = bf16[16,8,1024]{2,1,0:T(8,128)(2,1)S(1)} async-done(((bf16[16,8,1024]{2,1,0:T(8,128)(2,1)}), bf16[16,8,1024]{2,1,0:T(8,128)(2,1)S(1)}, u32[]{:S(2)}, u32[]{:S(2)}) %all-to-all-start.16) | async-done | bytes 262176 | tf_op jit(solution)/shard_map/all_to_all | solution.py:300
  367.0 1.7 rows.1
  (80 shorter events, 13.4 us)
Async XLA Ops:
  7.2 25.2 %collective-permute-start.1 = (bf16[128,1024]{1,0:T(8,128)(2,1)}, bf16[128,1024]{1,0:T(8,128)(2,1)S(1)}, u32[]{:S(2)}, u32[]{:S(2)}) collective-permute-start(bf16[128,1024]{1,0:T(8,128)(2,1)} %bitcast.14), channel_id=1, source_target_pairs={{1,0},{2,1},{3,2},{4,3},{5,4},{6,5},{7,6},{8,7},{9,8},{10,9},{11,1... | collective-permute-start | bytes 786440 | tf_op jit(solution)/shard_map/ppermute | solution.py:318
  10.9 21.5 %collective-permute-start = (bf16[128,1024]{1,0:T(8,128)(2,1)}, bf16[128,1024]{1,0:T(8,128)(2,1)S(1)}, u32[]{:S(2)}, u32[]{:S(2)}) collective-permute-start(bf16[128,1024]{1,0:T(8,128)(2,1)} %bitcast.15), channel_id=1, source_target_pairs={{0,1},{1,2},{2,3},{3,4},{4,5},{5,6},{6,7},{7,8},{8,9},{9,10},{10,1... | collective-permute-start | bytes 786440 | tf_op jit(solution)/shard_map/ppermute | solution.py:318
  14.8 17.6 %all-to-all-start = ((f32[16,1,2048]{2,1,0:T(1,128)}), f32[16,1,2048]{2,1,0:T(1,128)S(1)}, u32[]{:S(2)}, u32[]{:S(2)}) async-start(f32[16,1,2048]{2,1,0:T(1,128)} %first.1), calls=%async_computation | async-start | bytes 262144 | tf_op jit(solution)/shard_map/all_to_all | solution.py:300
  32.4 0.6 copy-start.13
  32.4 0.7 copy-start.3
  33.1 0.7 copy-start.4
  35.4 16.9 %all-to-all-start.1 = ((f32[16,1,2048]{2,1,0:T(1,128)}), f32[16,1,2048]{2,1,0:T(1,128)S(1)}, u32[]{:S(2)}, u32[]{:S(2)}) async-start(f32[16,1,2048]{2,1,0:T(1,128)} %merge_moments.4), calls=%async_computation.1 | async-start | bytes 262144 | tf_op jit(solution)/shard_map/all_to_all | solution.py:300
  44.3 222.9 %reduce-scatter.4.cloned.1.call-start = ((), (), s32[]{:S(2)}) async-start(), calls=%async_computation.20 | async-start | bytes 2621440 | tf_op jit(solution)/shard_map/reduce_scatter | solution.py:353
  52.3 0.7 copy-start.12
  84.3 19.2 %collective-permute-start.3 = (bf16[128,1024]{1,0:T(8,128)(2,1)}, bf16[128,1024]{1,0:T(8,128)(2,1)S(1)}, u32[]{:S(2)}, u32[]{:S(2)}) collective-permute-start(bf16[128,1024]{1,0:T(8,128)(2,1)} %get-tuple-element.55.x), channel_id=1, source_target_pairs={{8,0},{9,1},{10,2},{11,3},{12,4},{13,5},{14,6},{15,7},{16,8},{17,9... | collective-permute-start | bytes 786440 | tf_op jit(solution)/shard_map/ppermute | solution.py:318
  85.6 17.9 %collective-permute-start.2 = (bf16[128,1024]{1,0:T(8,128)(2,1)}, bf16[128,1024]{1,0:T(8,128)(2,1)S(1)}, u32[]{:S(2)}, u32[]{:S(2)}) collective-permute-start(bf16[128,1024]{1,0:T(8,128)(2,1)} %get-tuple-element.55.x), channel_id=1, source_target_pairs={{0,8},{1,9},{2,10},{3,11},{4,12},{5,13},{6,14},{7,15},{8,16},{9,17... | collective-permute-start | bytes 786440 | tf_op jit(solution)/shard_map/ppermute | solution.py:318
  103.5 0.7 copy-start.5
  104.2 0.7 copy-start.6
  151.6 17.9 %collective-permute-start.5 = (bf16[128,1024]{1,0:T(8,128)(2,1)}, bf16[128,1024]{1,0:T(8,128)(2,1)S(1)}, u32[]{:S(2)}, u32[]{:S(2)}) collective-permute-start(bf16[128,1024]{1,0:T(8,128)(2,1)} %get-tuple-element.60), channel_id=1, source_target_pairs={{8,0},{9,1},{10,2},{11,3},{12,4},{13,5},{14,6},{15,7},{16,8},{17,9... | collective-permute-start | bytes 786440 | tf_op jit(solution)/shard_map/ppermute | solution.py:318
  152.9 16.6 %collective-permute-start.4 = (bf16[128,1024]{1,0:T(8,128)(2,1)}, bf16[128,1024]{1,0:T(8,128)(2,1)S(1)}, u32[]{:S(2)}, u32[]{:S(2)}) collective-permute-start(bf16[128,1024]{1,0:T(8,128)(2,1)} %get-tuple-element.60), channel_id=1, source_target_pairs={{0,8},{1,9},{2,10},{3,11},{4,12},{5,13},{6,14},{7,15},{8,16},{9,17... | collective-permute-start | bytes 786440 | tf_op jit(solution)/shard_map/ppermute | solution.py:318
  169.5 0.7 copy-start.9
  170.2 0.7 copy-start.10
  193.3 4.4 %collective-permute-start.8 = (bf16[1024,1024]{1,0:T(8,128)(2,1)}, bf16[1024,1024]{1,0:T(8,128)(2,1)S(1)}, u32[]{:S(2)}, u32[]{:S(2)}) collective-permute-start(bf16[1024,1024]{1,0:T(8,128)(2,1)} %give.2), channel_id=1, source_target_pairs={{0,128},{128,0},{1,129},{129,1},{2,130},{130,2},{3,131},{131,3},{4... | collective-permute-start | bytes 6291464 | tf_op jit(solution)/shard_map/ppermute | solution.py:331
  197.6 1.3 copy-start.2
  203.0 0.9 copy-start.14
  203.0 89.9 %reduce-scatter.6.cloned.1.call-start = ((), (), s32[]{:S(2)}) async-start(), calls=%async_computation.21 | async-start | bytes 655360 | tf_op jit(solution)/shard_map/reduce_scatter | solution.py:353
  233.0 18.3 %collective-permute-start.7 = (bf16[128,1024]{1,0:T(8,128)(2,1)}, bf16[128,1024]{1,0:T(8,128)(2,1)S(1)}, u32[]{:S(2)}, u32[]{:S(2)}) collective-permute-start(bf16[128,1024]{1,0:T(8,128)(2,1)} %get-tuple-element.71), channel_id=1, source_target_pairs={{1,0},{2,1},{3,2},{4,3},{5,4},{6,5},{7,6},{8,7},{9,8},{10,9},{11,1... | collective-permute-start | bytes 786440 | tf_op jit(solution)/shard_map/ppermute | solution.py:318
  235.3 16.0 %collective-permute-start.6 = (bf16[128,1024]{1,0:T(8,128)(2,1)}, bf16[128,1024]{1,0:T(8,128)(2,1)S(1)}, u32[]{:S(2)}, u32[]{:S(2)}) collective-permute-start(bf16[128,1024]{1,0:T(8,128)(2,1)} %get-tuple-element.71), channel_id=1, source_target_pairs={{0,1},{1,2},{2,3},{3,4},{4,5},{5,6},{6,7},{7,8},{8,9},{9,10},{10,1... | collective-permute-start | bytes 786440 | tf_op jit(solution)/shard_map/ppermute | solution.py:318
  251.3 0.7 copy-start.7
  252.0 0.7 copy-start.8
  271.7 3.3 copy-start.15
  275.0 17.9 %collective-permute-start.13 = (bf16[1024,1024]{1,0:T(8,128)(2,1)}, bf16[1024,1024]{1,0:T(8,128)(2,1)S(1)}, u32[]{:S(2)}, u32[]{:S(2)}) collective-permute-start(bf16[1024,1024]{1,0:T(8,128)(2,1)} %give.3), channel_id=1, source_target_pairs={{0,128},{128,0},{1,129},{129,1},{2,130},{130,2},{3,131},{131,3},{4... | collective-permute-start | bytes 6291464 | tf_op jit(solution)/shard_map/ppermute | solution.py:331
  293.0 1.3 copy-start.1
  298.3 6.2 %copy-start.16 = (f32[1,2048]{1,0:T(1,128)S(1)}, f32[1,2048]{1,0:T(1,128)}, u32[]{:S(2)}) copy-start(f32[1,2048]{1,0:T(1,128)} %merge_sums.7.rest_0_) | copy-start | bytes 24580
  298.3 46.6 %all-to-all-start.15 = ((bf16[16,64,1024]{2,1,0:T(8,128)(2,1)}), bf16[16,64,1024]{2,1,0:T(8,128)(2,1)S(1)}, u32[]{:S(2)}, u32[]{:S(2)}) async-start(bf16[16,64,1024]{2,1,0:T(8,128)(2,1)} %bitcast.13), calls=%async_computation.17 | async-start | bytes 4194304 | tf_op jit(solution)/shard_map/all_to_all | solution.py:300
  303.8 41.2 %reduce-scatter.8.cloned.1.call-start = ((), (), s32[]{:S(2)}) async-start(), calls=%async_computation.22 | async-start | bytes 147456 | tf_op jit(solution)/shard_map/reduce_scatter | solution.py:353
  304.5 24.7 %collective-permute-start.9 = (f32[1,2048]{1,0:T(1,128)S(1)}, f32[1,2048]{1,0:T(1,128)S(1)}, u32[]{:S(2)}, u32[]{:S(2)}) collective-permute-start(f32[1,2048]{1,0:T(1,128)S(1)} %copy-done.16), channel_id=1, source_target_pairs={{0,8},{8,0},{16,24},{24,16},{1,9},{9,1},{17,25},{25,17},{2,10},{10... | collective-permute-start | bytes 24584 | tf_op jit(solution)/shard_map/ppermute | solution.py:349
  329.2 5.2 %collective-permute-start.10 = (f32[1,2048]{1,0:T(1,128)S(1)}, f32[1,2048]{1,0:T(1,128)S(1)}, u32[]{:S(2)}, u32[]{:S(2)}) collective-permute-start(f32[1,2048]{1,0:T(1,128)S(1)} %add.78), channel_id=1, source_target_pairs={{0,16},{8,24},{16,0},{24,8},{1,17},{9,25},{17,1},{25,9},{2,18},{10... | collective-permute-start | bytes 24584 | tf_op jit(solution)/shard_map/ppermute | solution.py:349
  334.5 3.7 collective-permute-start.11
  338.2 5.2 %collective-permute-start.12 = (f32[1,2048]{1,0:T(1,128)S(1)}, f32[1,2048]{1,0:T(1,128)S(1)}, u32[]{:S(2)}, u32[]{:S(2)}) collective-permute-start(f32[1,2048]{1,0:T(1,128)S(1)} %add.80), channel_id=1, source_target_pairs={{0,64},{32,96},{64,0},{96,32},{1,65},{33,97},{65,1},{97,33},{2,66}... | collective-permute-start | bytes 24584 | tf_op jit(solution)/shard_map/ppermute | solution.py:349
  344.9 10.5 %copy-start.17 = (bf16[8,1024]{1,0:T(8,128)(2,1)S(1)}, bf16[8,1024]{1,0:T(8,128)(2,1)}, u32[]{:S(2)}) copy-start(bf16[8,1024]{1,0:T(8,128)(2,1)} %reduce-scatter.8.cloned.1.call-done.rest_1_.own_1) | copy-start | bytes 49156
  344.9 1.3 copy-start
  348.8 17.5 %all-to-all-start.16 = ((bf16[16,8,1024]{2,1,0:T(8,128)(2,1)}), bf16[16,8,1024]{2,1,0:T(8,128)(2,1)S(1)}, u32[]{:S(2)}, u32[]{:S(2)}) async-start(bf16[16,8,1024]{2,1,0:T(8,128)(2,1)} %gather_rows.1), calls=%async_computation.19 | async-start | bytes 524288 | tf_op jit(solution)/shard_map/all_to_all | solution.py:300
  355.4 2.3 collective-permute-start.14
  357.7 8.6 %copy-start.18 = (bf16[8,1024]{1,0:T(8,128)(2,1)}, bf16[8,1024]{1,0:T(8,128)(2,1)S(1)}, u32[]{:S(2)}) copy-start(bf16[8,1024]{1,0:T(8,128)(2,1)S(1)} %collective-permute-done.14.other_1) | copy-start | bytes 49156
  366.3 0.7 copy-start.11
Sparse Core Ops, SparseCore 0:
  203.1 27.0 reduce-scatter.3
  275.2 17.7 reduce-scatter.5
  307.3 37.6 reduce-scatter.7

commit v4 on v3

--- a/solution.py
+++ b/solution.py
@@ -18,7 +18,7 @@
 F32 = jnp.float32
 BF16 = jnp.bfloat16
 ROWS, CH, HALF = 128, 1024, 512
-VMEM_LIMIT = 60 << 20
+VMEM_LIMIT = 32 << 20
 TOTAL = 32768.0
 TANH_SCALE = 0.7978845608028654
 CUBE = 0.044715
@@ -124,11 +124,14 @@
     return factor, normed, slope, hidden, following
 
 
-def k_middle(parts, conv, gains, biases, project, x, hidden, following, slope, normed, factor, out):
+def k_middle(
+    parts, conv, gains, biases, project, x, hidden, following, kept, slope, normed, factor, out
+):
     factor[...], normed[...], slope[...], hidden[...], rows = middle(
         0, parts, conv, gains, biases, project, x
     )
     following[...] = rows
+    kept[...] = rows
     spread_out(out, *local_moments(rows.astype(F32)))
 
 
@@ -156,7 +159,7 @@
     layer, parts, grad, normed, factor, lower, upper, masks, gains, weight, slope, x, stat, *rest
 ):
     if layer == 0:
-        given_gain, given_bias, _, three, grad_in, gain_out, bias_out, out = rest
+        given_gain, given_bias, three, grad_in, gain_out, bias_out, out = rest
     else:
         three, grad_in, gain_out, bias_out, out = rest
     total, cross = merged_sums(parts)
@@ -226,44 +229,51 @@
     return ref[:, pl.ds(pl.multiple_of(place * half, 128), half)]
 
 
-def k_give(taps, three, upstream, hidden, out):
-    out[:, : 3 * HALF // 2] = product_tn(taps[...], half_of(three, True)).astype(BF16)
-    out[:, 3 * HALF // 2 :] = product_tn(upstream[...], half_of(hidden, True)).astype(BF16)
-
-
-def k_keep(taps, three, upstream, hidden, arrived, *rest):
-    out = rest[-1]
-    first = arrived[:, : 3 * HALF // 2].astype(F32)
-    out[:, : 3 * HALF // 2] = (product_tn(taps[...], half_of(three, False)) + first).astype(BF16)
-    second = arrived[:, 3 * HALF // 2 :].astype(F32)
-    out[:, 3 * HALF // 2 :] = (product_tn(upstream[...], half_of(hidden, False)) + second).astype(BF16)
-
-
-def k_gather(parts, *rest):
+def k_give(*refs):
+    out, first = refs[-1], 0
+    for left, right in zip(refs[0:-1:2], refs[1:-1:2]):
+        width = right.shape[1] // 2
+        out[:, first : first + width] = product_tn(left[...], half_of(right, True)).astype(BF16)
+        first += width
+
+
+def k_keep(pairs, arrived, *refs):
+    out, first = refs[-1], 0
+    for i in range(pairs):
+        left, right = refs[2 * i], refs[2 * i + 1]
+        width = right.shape[1] // 2
+        other = arrived[:, first : first + width].astype(F32)
+        mine = product_tn(left[...], half_of(right, False))
+        out[:, first : first + width] = (mine + other).astype(BF16)
+        first += width
+
+
+def k_gather(parts, other, *rest):
     out = rest[-1]
     for z in range(8):
         rows = slice(8 * z, 8 * z + 8)
         total = parts[0, rows].astype(F32)
         for i in range(1, GROUP):
             total = total + parts[i, rows].astype(F32)
-        total = total.astype(BF16)
-        out[z] = total
-        out[8 + z] = total
-
-
-def k_rows(parts_0, own_1, other_1, kernel_out, project_out):
+        whole_row = jnp.concatenate([total.astype(BF16), other[rows, :]], axis=1)
+        out[z] = whole_row
+        out[8 + z] = whole_row
+
+
+def k_rows(parts, kernel_out, project_out):
     cut, width = 3 * HALF // 2, HALF // 2
-    place = lax.axis_index("dp")
     for d in range(2):
-        total = parts_0[8 * d].astype(F32)
+        total = parts[8 * d].astype(F32)
         for z in range(1, 8):
-            total = total + parts_0[8 * d + z].astype(F32)
-        kernel_out[0, :, d * cut : (d + 1) * cut] = total[:, :cut]
-        project_out[0, :, d * width : (d + 1) * width] = total[:, cut:]
-    for rows, d in ((own_1, place), (other_1, 1 - place)):
-        rows = rows[...].astype(F32)
-        kernel_out[1, :, pl.ds(pl.multiple_of(d * cut, 128), cut)] = rows[:, :cut]
-        project_out[1, :, pl.ds(pl.multiple_of(d * width, 128), width)] = rows[:, cut:]
+            total = total + parts[8 * d + z].astype(F32)
+        for layer in range(2):
+            first = layer * CH
+            kernel_out[layer, :, d * cut : (d + 1) * cut] = total[:, first : first + cut]
+            project_out[layer, :, d * width : (d + 1) * width] = total[:, first + cut : first + CH]
+
+
+def k_pass(value, out):
+    out[...] = value[...]
 
 
 def whole(value):
@@ -271,45 +281,92 @@
     return pl.BlockSpec(shape, lambda i: (0,) * len(shape))
 
 
-def layer_of(value, layer):
-    return pl.BlockSpec((None,) + value.shape[1:], lambda i: (layer, 0, 0))
-
-
-def call(kernel, outs, *operands, name, layers=None, waits=(), flops=1 << 22):
+def in_memory(value):
+    return pltpu.with_memory_space_constraint(value, pltpu.HBM)
+
+
+def staged(kernel, counts, loaded, stored):
+    n_in, n_waits, n_out = counts
+
+    def body(*refs):
+        ins, outs = list(refs[:n_in]), list(refs[n_in + n_waits : n_in + n_waits + n_out])
+        scratch = list(refs[n_in + n_waits + n_out :])
+        sems, copies, results = scratch.pop(), [], []
+        for place, (i, layer) in enumerate(loaded):
+            source = ins[i] if layer is None else ins[i].at[layer]
+            ins[i] = scratch.pop(0)
+            copies.append(pltpu.make_async_copy(source, ins[i], sems.at[place]))
+            copies[-1].start()
+        for place, i in enumerate(stored):
+            target, outs[i] = outs[i], scratch.pop(0)
+            results.append(
+                pltpu.make_async_copy(outs[i], target, sems.at[len(loaded) + place])
+            )
+        for copy in copies:
+            copy.wait()
+        kernel(*ins, *outs)
+        for copy in results:
+            copy.start()
+        for copy in results:
+            copy.wait()
+
+    return body
+
+
+def call(kernel, outs, *operands, name, loaded=(), stored=(), layers=None, waits=(), held=(), flops=1 << 22):
     layers = layers or {}
-    specs = [
-        layer_of(value, layers[i]) if i in layers else whole(value)
-        for i, value in enumerate(operands)
-    ]
-    specs += [pl.BlockSpec(memory_space=pl.ANY)] * len(waits)
+    in_hbm = pl.BlockSpec(memory_space=pltpu.HBM)
+    specs = [in_hbm if i in loaded else whole(value) for i, value in enumerate(operands)]
+    specs += [pl.BlockSpec(memory_space=pl.ANY)] * len(waits) + [in_hbm] * len(held)
     shapes = [jax.ShapeDtypeStruct(shape, dtype) for shape, dtype in outs]
     moved = sum(v.size * v.dtype.itemsize for v in list(operands) + shapes)
+    scratch = []
+    for i in loaded:
+        shape = operands[i].shape
+        scratch.append(pltpu.VMEM(shape[1:] if i in layers else shape, operands[i].dtype))
+    scratch += [pltpu.VMEM(*outs[i]) for i in stored]
+    scratch.append(pltpu.SemaphoreType.DMA((max(1, len(loaded) + len(stored)),)))
+    body = staged(
+        kernel,
+        (len(operands), len(waits) + len(held), len(outs)),
+        [(i, layers.get(i)) for i in loaded],
+        stored,
+    )
     return pl.pallas_call(
-        kernel,
+        body,
         grid=(1,),
         in_specs=specs,
-        out_specs=[whole(shape) for shape in shapes],
-        out_shape=shapes,
+        out_specs=[in_hbm if i in stored else whole(shape) for i, shape in enumerate(shapes)],
+        out_shape=[
+            pltpu.HBM(shape.shape, shape.dtype) if i in stored else shape
+            for i, shape in enumerate(shapes)
+        ],
+        scratch_shapes=scratch,
         name=name,
         cost_estimate=pl.CostEstimate(flops=flops, bytes_accessed=moved, transcendentals=0),
         compiler_params=pltpu.CompilerParams(vmem_limit_bytes=VMEM_LIMIT),
-    )(*operands, *waits)
+    )(
+        *[in_memory(value) if i in loaded else value for i, value in enumerate(operands)],
+        *waits,
+        *[in_memory(value) for value in held],
+    )
 
 
 def exchange(value, axes):
     return lax.all_to_all(value, axes, 0, 0, tiled=True)
 
 
-def over_all(payload, kind, waits=()):
+def over_all(payload, kind, waits=(), held=()):
     first = exchange(payload, FIRST_STAGE)
     (merged,) = call(
         functools.partial(k_merge, kind),
         [(payload.shape, F32)],
         first,
         waits=waits,
+        held=held,
         name="merge_" + kind,
     )
-    return exchange(merged, SECOND_STAGE)
+    return exchange(merged, SECOND_STAGE), merged
 
 
 def passed_along(value, steps):
@@ -323,21 +380,31 @@
     return passed_along(rows, hops), passed_along(rows, -hops)
 
 
-def chip_share(taps, three, upstream, hidden, waits=()):
-    flops = 2 * ROWS * CH * CH
+def chip_share(*pairs, waits=(), waits_first=(), held=()):
+    operands = [value for pair in pairs for value in pair]
+    width = sum(right.shape[1] for _, right in pairs) // 2
+    shape = [((CH, width), BF16)]
+    flops = 2 * ROWS * CH * width
+    count = len(operands)
     (given,) = call(
-        k_give, [((CH, CH), BF16)], taps, three, upstream, hidden, name="give", flops=flops
-    )
-    arrived = lax.ppermute(given, "dp", [(0, 1), (1, 0)])
+        k_give,
+        shape,
+        *operands,
+        loaded=tuple(range(count)),
+        waits=waits_first,
+        name="give",
+        flops=flops,
+    )
+    arrived = swapped(given, "dp", 1)
     (share,) = call(
-        k_keep,
-        [((CH, CH), BF16)],
-        taps,
-        three,
-        upstream,
-        hidden,
+        functools.partial(k_keep, len(pairs)),
+        shape,
         arrived,
+        *operands,
+        loaded=tuple(range(1, count + 1)),
+        stored=(0,),
         waits=waits,
+        held=held,
         name="keep",
         flops=flops,
     )
@@ -351,12 +418,6 @@
 
 def rows_over(share, axis):
     return lax.psum_scatter(share, axis, scatter_dimension=0, tiled=True)
-
-
-def rows_at_once(share, waits):
-    parts = exchange(share.reshape(GROUP, CH // GROUP, CH), SECOND_STAGE)
-    (rows,) = call(k_gather, [((GROUP, 8, CH), BF16)], parts, waits=waits, name="gather_rows")
-    return exchange(rows, FIRST_STAGE)
 
 
 def on_device(
@@ -399,20 +460,23 @@
             conv_weight,
             gains_in,
             biases_in,
+            loaded=(5, 6, 7) if layer else (1, 5, 6, 7),
+            stored=(0, 1, 3),
             layers={5: layer},
             name="entry",
             flops=conv_flops,
         )
 
     sides = neighbours(stream_0, FIRST_DILATION)
-    (payload,) = call(k_first, [(wide, F32)], stream_0, name="first")
-    parts = over_all(payload, "moments", sides)
+    (payload,) = call(k_first, [(wide, F32)], stream_0, loaded=(0,), name="first")
+    parts, _ = over_all(payload, "moments", sides)
     taps_0, slope_0, conv_0, stat_0, payload = entry(0, stream_0, parts, sides)
-    parts = over_all(payload, "moments")
-    hidden_0, stream_1, slope_mid_0, normed_0, factor_0, payload = call(
+    parts, _ = over_all(payload, "moments")
+    hidden_0, stream_1, kept_1, slope_mid_0, normed_0, factor_0, payload = call(
         k_middle,
         [
             ((ROWS, HALF), BF16),
+            ((ROWS, CH), BF16),
             ((ROWS, CH), BF16),
             ((ROWS, HALF), F32),
             ((ROWS, HALF), F32),
@@ -425,13 +489,15 @@
         biases_mid,
         proj_weight,
         stream_0,
+        loaded=(2, 3, 4, 5),
+        stored=(0, 2, 3, 4, 5),
         layers={4: 0},
         name="middle",
     )
     sides = neighbours(stream_1, SECOND_DILATION)
-    parts = over_all(payload, "moments", sides)
+    parts, _ = over_all(payload, "moments", sides)
     taps_1, slope_1, conv_1, stat_1, payload = entry(1, stream_1, parts, sides)
-    parts = over_all(payload, "moments")
+    parts, _ = over_all(payload, "moments")
     hidden_1, stream_2, normed_1, factor_1, grad, pair, payload = call(
         k_turn,
         [
@@ -448,14 +514,16 @@
         gains_mid,
         biases_mid,
         proj_weight,
-        stream_1,
+        kept_1,
         grad_2,
+        loaded=(2, 3, 4, 5, 6),
+        stored=(0, 1),
         layers={4: 1},
         name="turn",
     )
 
     def back_middle(
-        layer, parts, grad, normed, factor, sides, slope, stream, stat, *given, waits=()
+        layer, parts, grad, normed, factor, sides, slope, stream, stat, *given, held=()
     ):
         rows = 2 - layer
         return call(
@@ -479,18 +547,21 @@
             stream,
             stat,
             *given,
+            loaded=(7, 8, 9, 10, 11) if layer else (2, 3, 7, 8, 9, 10, 11, 12, 13),
+            stored=(0, 2, 3),
             layers={8: layer},
-            waits=waits,
+            held=held,
             name="back_middle",
             flops=conv_flops,
         )
 
     sides = neighbours(pair, SECOND_DILATION)
-    parts = over_all(payload, "sums", sides)
+    parts, _ = over_all(payload, "sums", sides)
     three_1, grad_in, gain_mid, bias_mid, payload = back_middle(
-        1, parts, grad, normed_1, factor_1, sides, slope_1, stream_1, stat_1
-    )
-    parts = over_all(payload, "sums")
+        1, parts, grad, normed_1, factor_1, sides, slope_1, kept_1, stat_1
+    )
+    parts, merged = over_all(payload, "sums")
+    share_1 = chip_share((taps_1, three_1), (grad_2, hidden_1), waits_first=(merged,))
     gain_in, bias_in, grad_1, grad, pair, payload = call(
         k_back_entry,
         [
@@ -503,19 +574,21 @@
         ],
         parts,
         grad_in,
-        stream_1,
+        kept_1,
         stat_1,
         gains_in,
         grad_2,
         proj_weight,
         slope_mid_0,
         normed_0,
+        loaded=(2, 3, 4, 5, 6, 7, 8),
+        stored=(0, 1, 2),
         layers={6: 0},
         name="back_entry",
     )
     sides = neighbours(pair, FIRST_DILATION)
-    rows_1 = rows_over(chip_share(taps_1, three_1, grad_2, hidden_1), "y")
-    parts = over_all(payload, "sums", sides)
+    parts, _ = over_all(payload, "sums", sides, (share_1,))
+    rows_1 = rows_over(share_1, "y")
     three_0, grad_in, grad_gains_mid, grad_biases_mid, payload = back_middle(
         0,
         parts,
@@ -528,17 +601,25 @@
         stat_0,
         gain_mid,
         bias_mid,
-        waits=(rows_1,),
-    )
-    rows_1 = rows_over(rows_1, "x")
+    )
     (sums,) = call(
         functools.partial(k_merge, "sums"),
         [((1, 2 * CH), F32)],
         exchange(payload, FIRST_STAGE),
         name="merge_sums",
     )
-    chip_0 = chip_share(taps_0, three_0, grad_1, hidden_0, (sums, rows_1))
-    rows_1 = rows_over(rows_1, "z")
+    (rows_1,) = call(
+        k_pass,
+        [(rows_1.shape, BF16)],
+        rows_1,
+        loaded=(0,),
+        stored=(0,),
+        waits=(sums,),
+        name="pass",
+    )
+    share_0 = chip_share((taps_0, three_0), (grad_1, hidden_0), held=(rows_1,))
+    rows_1 = rows_over(rows_1, "x")
+    share_0 = exchange(share_0.reshape(GROUP, CH // GROUP, CH), SECOND_STAGE)
     for axis in ("x", "y"):
         for step in (1, 2):
             sums = sums + swapped(sums, axis, step)
@@ -553,14 +634,24 @@
         grad_1,
         gain_in,
         bias_in,
+        loaded=(2, 3, 4, 5, 6, 7),
+        stored=(0, 1, 2),
         name="last",
+    )
+    (rows,) = call(
+        k_gather,
+        [((GROUP, 8, 2 * CH), BF16)],
+        share_0,
+        rows_1,
+        loaded=(1,),
+        waits=(sums,),
+        name="gather_rows",
     )
     grad_conv, grad_proj = call(
         k_rows,
         [((2, 8, 3 * HALF), F32), ((2, 8, HALF), F32)],
-        rows_at_once(chip_0, (sums, rows_1)),
-        rows_1,
-        swapped(rows_1, "dp", 1),
+        exchange(rows, FIRST_STAGE),
+        stored=(0, 1),
         name="rows",
     )
     return (

time: 377 us -> 340 us (0.902)
  Pallas kernels: 60.6 us -> 44.7 us
  local copies, waits for them, and re-layouts: 13.3 us -> 1.47 us
  blocking collectives: 161 us -> 150 us
  waiting for transfers between devices: 62.9 us -> 67 us
    pallas_call x23 -> x24, Pallas kernels: 60.6 us -> 44.7 us  [call(): pl.pallas_call(body, grid=(1,), in_specs=specs, out_specs=[in_hbm if i in...]
    unnamed x38 -> x0, local copies, waits for them, and re-layouts: 11.9 us -> none
    all_to_all x13, blocking collectives: 161 us -> 150 us  [exchange(): return lax.all_to_all(value, axes, 0, 0, tiled=True)]
    ppermute x5 -> x6, waiting for transfers between devices: 31.2 us -> 38 us  [swapped(): return lax.ppermute(value, axis, pairs)]
    all_to_all x4, waiting for transfers between devices: 21.8 us -> 28.2 us  [exchange(): return lax.all_to_all(value, axes, 0, 0, tiled=True)]
    reduce_scatter x3 -> x2, waiting for transfers between devices: 4.83 us -> 0.04 us  [rows_over(): return lax.psum_scatter(share, axis, scatter_dimension=0, tiled=True)]
    ppermute x2 -> x0, waiting for transfers between devices: 4.37 us -> none  [chip_share(): arrived = lax.ppermute(given, 'dp', [(0, 1), (1, 0)])]
    ppermute x5 -> x6, starting transfers between devices: 7.95 us -> 9.19 us  [swapped(): return lax.ppermute(value, axis, pairs)]
  transfers between devices with their start and end apart: 22 -> 20, of which waited for: 10 -> 8; matrix products, arithmetic and copies ran while one was open for 1% -> 1% of each run, Pallas kernels for 3% -> 4%
where the time goes in v4:
time: 340 us; the launch traced here: 339 us
  blocking collectives  150 us (44%)
  waiting for transfers between devices  67 us (20%)
  starting transfers between devices  61 us (18%)
  Pallas kernels  44.7 us (13%)
  between operations  14.4 us (4%)
    all_to_all x13, blocking collectives, exchange(): return lax.all_to_all(value, axes, 0, 0, tiled=True)  150 us
    pallas_call x24, Pallas kernels, call(): pl.pallas_call(body, grid=(1,), in_specs=specs, out_specs=[in_hbm if i in...  44.7 us
    ppermute x6, waiting for transfers between devices, swapped(): return lax.ppermute(value, axis, pairs)  38 us
    all_to_all x4, starting transfers between devices, exchange(): return lax.all_to_all(value, axes, 0, 0, tiled=True)  28.3 us
    all_to_all x4, waiting for transfers between devices, exchange(): return lax.all_to_all(value, axes, 0, 0, tiled=True)  28.2 us
    ppermute x8, starting transfers between devices, passed_along(): lax.ppermute(value, SEQ, [(source, source + steps) for source in range(le...  23.4 us
    ppermute x6, starting transfers between devices, swapped(): return lax.ppermute(value, axis, pairs)  9.19 us
  transfers between devices with their start and end apart: 20, of which 8 were waited for; matrix products, arithmetic and copies ran while one was open for 1% of the time, Pallas kernels for 4%

profile of v4, /device:TPU:32, one launch (start us, length us, event | category | flops | bytes accessed | tf_op | source)
XLA Modules:
  0.0 339.0 jit_solution(5552786534590274499)
XLA Ops:
  7.2 3.8 %collective-permute-start.1 = (bf16[128,1024]{1,0:T(8,128)(2,1)}, bf16[128,1024]{1,0:T(8,128)(2,1)S(1)}, u32[]{:S(2)}, u32[]{:S(2)}) collective-permute-start(bf16[128,1024]{1,0:T(8,128)(2,1)} %bitcast.14), channel_id=1, source_target_pairs={{1,0},{2,1},{3,2},{4,3},{5,4},{6,5},{7,6},{8,7},{9,8},{10,9},{11,1... | collective-permute-start | bytes 786440 | tf_op jit(solution)/shard_map/ppermute | solution.py:375
  10.9 2.1 collective-permute-start
  13.0 1.8 first.1
  14.8 9.4 %all-to-all-start = ((f32[16,1,2048]{2,1,0:T(1,128)}), f32[16,1,2048]{2,1,0:T(1,128)S(1)}, u32[]{:S(2)}, u32[]{:S(2)}) async-start(f32[16,1,2048]{2,1,0:T(1,128)} %first.1), calls=%async_computation | async-start | bytes 262144 | tf_op jit(solution)/shard_map/all_to_all | solution.py:356
  24.2 0.8 fusion.4
  25.0 0.8 select_reduce_fusion.1
  25.8 0.1 lt.37
  25.9 0.1 lt.40
  26.0 0.1 le.40
  26.1 0.1 le.37
  26.3 6.1 %all-to-all-done.refs_0_ = f32[16,1,2048]{2,1,0:T(1,128)S(1)} async-done(((f32[16,1,2048]{2,1,0:T(1,128)}), f32[16,1,2048]{2,1,0:T(1,128)S(1)}, u32[]{:S(2)}, u32[]{:S(2)}) %all-to-all-start) | async-done | bytes 131104 | tf_op jit(solution)/shard_map/all_to_all | solution.py:356
  32.4 0.7 merge_moments.4
  33.1 8.9 %all-to-all-start.1 = ((f32[16,1,2048]{2,1,0:T(1,128)}), f32[16,1,2048]{2,1,0:T(1,128)S(1)}, u32[]{:S(2)}, u32[]{:S(2)}) async-start(f32[16,1,2048]{2,1,0:T(1,128)} %merge_moments.4), calls=%async_computation.1 | async-start | bytes 262144 | tf_op jit(solution)/shard_map/all_to_all | solution.py:356
  42.1 0.1 copy.27
  42.3 7.8 %all-to-all-done.1.refs_0_ = f32[16,1,2048]{2,1,0:T(1,128)S(1)} async-done(((f32[16,1,2048]{2,1,0:T(1,128)}), f32[16,1,2048]{2,1,0:T(1,128)S(1)}, u32[]{:S(2)}, u32[]{:S(2)}) %all-to-all-start.1) | async-done | bytes 131104 | tf_op jit(solution)/shard_map/all_to_all | solution.py:356
  50.0 3.8 %entry.2 = (bf16[128,1024]{1,0:T(8,128)(2,1)}, f32[128,1024]{1,0:T(8,128)}, f32[128,512]{1,0:T(8,128)S(1)}, f32[2,1024]{1,0:T(2,128)}, f32[16,1,1024]{2,1,0:T(1,128)S(1)}) custom-call(f32[16,1,2048]{2,1,0:T(1,128)S(1)} %all-to-all-done.1.refs_0_, bf16[128,1024]{1,0:T(8,128)(2,1)} %bitcast.17, bf16[128,1024]{1,0:T(8,128)(2,1)S(1)} %collective-permute-done.refs_1_.refs_2_, ...), custom_call_target="tpu_custom_call" | custom-call | flops 402653184 | bytes 8349696 | tf_op jit(solution)/shard_map/entry/pallas_call | solution.py:335
  53.8 10.4 %all_to_all.85.refs_0_ = f32[16,1,1024]{2,1,0:T(1,128)S(1)} all-to-all(f32[16,1,1024]{2,1,0:T(1,128)S(1)} %get-tuple-element.53), channel_id=1, replica_groups=mesh['dp'=2,'y'=4,'x'=4,'z'=8] {'dp','z'}, dimensions={0} | all-to-all | bytes 131072 | tf_op jit(solution)/shard_map/all_to_all | solution.py:356
  64.2 10.7 %all_to_all.86.refs_0_ = f32[16,1,1024]{2,1,0:T(1,128)S(1)} all-to-all(f32[16,1,1024]{2,1,0:T(1,128)S(1)} %merge_moments.5), channel_id=1, replica_groups=mesh['dp'=2,'y'=4,'x'=4,'z'=8] {'y','x'}, dimensions={0} | all-to-all | bytes 131072 | tf_op jit(solution)/shard_map/all_to_all | solution.py:356
  75.0 2.8 middle.1
  77.8 1.3 collective-permute-start.3
  79.1 4.6 %collective-permute-start.2 = (bf16[128,1024]{1,0:T(8,128)(2,1)S(1)}, bf16[128,1024]{1,0:T(8,128)(2,1)S(1)}, u32[]{:S(2)}, u32[]{:S(2)}) collective-permute-start(bf16[128,1024]{1,0:T(8,128)(2,1)S(1)} %get-tuple-element.56.refs_1_), channel_id=1, source_target_pairs={{0,8},{1,9},{2,10},{3,11},{4,12},{5,13},{6,14},{7,15},{8,16},{9,17... | collective-permute-start | bytes 786440 | tf_op jit(solution)/shard_map/ppermute | solution.py:375
  83.6 11.7 %all_to_all.87.refs_0_ = f32[16,1,2048]{2,1,0:T(1,128)S(1)} all-to-all(f32[16,1,2048]{2,1,0:T(1,128)S(1)} %get-tuple-element.55), channel_id=1, replica_groups=mesh['dp'=2,'y'=4,'x'=4,'z'=8] {'dp','z'}, dimensions={0} | all-to-all | bytes 262144 | tf_op jit(solution)/shard_map/all_to_all | solution.py:356
  95.5 13.1 %all_to_all.88.refs_0_ = f32[16,1,2048]{2,1,0:T(1,128)S(1)} all-to-all(f32[16,1,2048]{2,1,0:T(1,128)S(1)} %merge_moments.6), channel_id=1, replica_groups=mesh['dp'=2,'y'=4,'x'=4,'z'=8] {'y','x'}, dimensions={0} | all-to-all | bytes 262144 | tf_op jit(solution)/shard_map/all_to_all | solution.py:356
  108.5 3.7 %entry.3 = (bf16[128,1024]{1,0:T(8,128)(2,1)}, f32[128,1024]{1,0:T(8,128)}, f32[128,512]{1,0:T(8,128)S(1)}, f32[2,1024]{1,0:T(2,128)}, f32[16,1,1024]{2,1,0:T(1,128)S(1)}) custom-call(f32[16,1,2048]{2,1,0:T(1,128)S(1)} %all_to_all.88.refs_0_, bf16[128,1024]{1,0:T(8,128)(2,1)S(1)} %get-tuple-element.56.refs_1_, ...), custom_call_target="tpu_custom_call" | custom-call | flops 402653184 | bytes 8349696 | tf_op jit(solution)/shard_map/entry/pallas_call | solution.py:335
  112.2 10.4 %all_to_all.89.refs_0_ = f32[16,1,1024]{2,1,0:T(1,128)S(1)} all-to-all(f32[16,1,1024]{2,1,0:T(1,128)S(1)} %get-tuple-element.57), channel_id=1, replica_groups=mesh['dp'=2,'y'=4,'x'=4,'z'=8] {'dp','z'}, dimensions={0} | all-to-all | bytes 131072 | tf_op jit(solution)/shard_map/all_to_all | solution.py:356
  122.6 10.7 %all_to_all.90.refs_0_ = f32[16,1,1024]{2,1,0:T(1,128)S(1)} all-to-all(f32[16,1,1024]{2,1,0:T(1,128)S(1)} %merge_moments.7), channel_id=1, replica_groups=mesh['dp'=2,'y'=4,'x'=4,'z'=8] {'y','x'}, dimensions={0} | all-to-all | bytes 131072 | tf_op jit(solution)/shard_map/all_to_all | solution.py:356
  133.4 2.7 turn.1
  136.1 1.3 collective-permute-start.5
  137.4 4.6 %collective-permute-start.4 = (bf16[128,1024]{1,0:T(8,128)(2,1)S(1)}, bf16[128,1024]{1,0:T(8,128)(2,1)S(1)}, u32[]{:S(2)}, u32[]{:S(2)}) collective-permute-start(bf16[128,1024]{1,0:T(8,128)(2,1)S(1)} %get-tuple-element.62), channel_id=1, source_target_pairs={{0,8},{1,9},{2,10},{3,11},{4,12},{5,13},{6,14},{7,15},{8,16},{9,17... | collective-permute-start | bytes 786440 | tf_op jit(solution)/shard_map/ppermute | solution.py:375
  141.9 10.5 %all_to_all.91.refs_0_ = f32[16,1,1024]{2,1,0:T(1,128)S(1)} all-to-all(f32[16,1,1024]{2,1,0:T(1,128)S(1)} %get-tuple-element.61), channel_id=1, replica_groups=mesh['dp'=2,'y'=4,'x'=4,'z'=8] {'dp','z'}, dimensions={0} | all-to-all | bytes 131072 | tf_op jit(solution)/shard_map/all_to_all | solution.py:356
  152.5 12.8 %all_to_all.92.refs_0_ = f32[16,1,1024]{2,1,0:T(1,128)S(1)} all-to-all(f32[16,1,1024]{2,1,0:T(1,128)S(1)} %merge_sums.4), channel_id=1, replica_groups=mesh['dp'=2,'y'=4,'x'=4,'z'=8] {'y','x'}, dimensions={0} | all-to-all | bytes 131072 | tf_op jit(solution)/shard_map/all_to_all | solution.py:356
  165.3 3.7 %back_middle.2 = (bf16[128,1536]{1,0:T(8,128)(2,1)}, f32[128,1024]{1,0:T(8,128)S(1)}, f32[1,512]{1,0:T(1,128)}, f32[1,512]{1,0:T(1,128)}, f32[16,1,2048]{2,1,0:T(1,128)S(1)}) custom-call(f32[16,1,1024]{2,1,0:T(1,128)S(1)} %all_to_all.92.refs_0_, f32[128,512]{1,0:T(8,128)S(1)} %get-tuple-element.63.refs_1_, f32[128,512]{1,0:T(8,128)S(1)} %get-tuple-element.64.refs_2_, ...), custom_call_target="tpu_custom_call" | custom-call | flops 402653184 | bytes 9261056 | tf_op jit(solution)/shard_map/back_middle/pallas_call | solution.py:335
  169.0 11.7 %all_to_all.93.refs_0_ = f32[16,1,2048]{2,1,0:T(1,128)S(1)} all-to-all(f32[16,1,2048]{2,1,0:T(1,128)S(1)} %get-tuple-element.68), channel_id=1, replica_groups=mesh['dp'=2,'y'=4,'x'=4,'z'=8] {'dp','z'}, dimensions={0} | all-to-all | bytes 262144 | tf_op jit(solution)/shard_map/all_to_all | solution.py:356
  180.8 1.9 give.2
  182.7 0.1 collective-permute-start.8
  182.8 4.1 %collective-permute-done.8.refs_0_ = bf16[1024,1024]{1,0:T(8,128)(2,1)S(1)} collective-permute-done((bf16[1024,1024]{1,0:T(8,128)(2,1)S(1)}, bf16[1024,1024]{1,0:T(8,128)(2,1)S(1)}, u32[]{:S(2)}, u32[]{:S(2)}) %collective-permute-start.8) | collective-permute-done | bytes 2097184 | tf_op jit(solution)/shard_map/ppermute | solution.py:416
  187.0 3.3 keep.2.refs_3_
  190.3 11.1 %all_to_all.94.refs_0_ = f32[16,1,2048]{2,1,0:T(1,128)S(1)} all-to-all(f32[16,1,2048]{2,1,0:T(1,128)S(1)} %merge_sums.5.refs_4_), channel_id=1, replica_groups=mesh['dp'=2,'y'=4,'x'=4,'z'=8] {'y','x'}, dimensions={0} | all-to-all | bytes 262144 | tf_op jit(solution)/shard_map/all_to_all | solution.py:356
  201.4 2.6 back_entry.1
  204.0 2.3 collective-permute-start.7
  206.3 3.5 %collective-permute-start.6 = (bf16[128,1024]{1,0:T(8,128)(2,1)S(1)}, bf16[128,1024]{1,0:T(8,128)(2,1)S(1)}, u32[]{:S(2)}, u32[]{:S(2)}) collective-permute-start(bf16[128,1024]{1,0:T(8,128)(2,1)S(1)} %get-tuple-element.73), channel_id=1, source_target_pairs={{0,1},{1,2},{2,3},{3,4},{4,5},{5,6},{6,7},{7,8},{8,9},{9,10},{10,1... | collective-permute-start | bytes 786440 | tf_op jit(solution)/shard_map/ppermute | solution.py:375
  209.9 12.1 %all_to_all.95.refs_0_ = f32[16,1,1024]{2,1,0:T(1,128)S(1)} all-to-all(f32[16,1,1024]{2,1,0:T(1,128)S(1)} %get-tuple-element.72), channel_id=1, replica_groups=mesh['dp'=2,'y'=4,'x'=4,'z'=8] {'dp','z'}, dimensions={0} | all-to-all | bytes 131072 | tf_op jit(solution)/shard_map/all_to_all | solution.py:356
  222.0 12.6 %all_to_all.96.refs_0_ = f32[16,1,1024]{2,1,0:T(1,128)S(1)} all-to-all(f32[16,1,1024]{2,1,0:T(1,128)S(1)} %merge_sums.6), channel_id=1, replica_groups=mesh['dp'=2,'y'=4,'x'=4,'z'=8] {'y','x'}, dimensions={0} | all-to-all | bytes 131072 | tf_op jit(solution)/shard_map/all_to_all | solution.py:356
  234.6 3.9 %back_middle.3 = (bf16[128,1536]{1,0:T(8,128)(2,1)}, f32[128,1024]{1,0:T(8,128)S(1)}, f32[2,512]{1,0:T(2,128)}, f32[2,512]{1,0:T(2,128)}, f32[16,1,2048]{2,1,0:T(1,128)S(1)}) custom-call(f32[16,1,1024]{2,1,0:T(1,128)S(1)} %all_to_all.96.refs_0_, f32[128,512]{1,0:T(8,128)S(1)} %get-tuple-element.77.refs_1_, f32[128,512]{1,0:T(8,128)} %get-tuple-element.71.refs_8_.refs_2_, ...), custom_call_target="tpu_custom_call" | custom-call | flops 402653184 | bytes 9269248 | tf_op jit(solution)/shard_map/back_middle/pallas_call | solution.py:335
  238.5 2.0 give.3
  240.5 0.1 collective-permute-start.13
  240.6 11.7 %all_to_all.97.refs_0_ = f32[16,1,2048]{2,1,0:T(1,128)S(1)} all-to-all(f32[16,1,2048]{2,1,0:T(1,128)S(1)} %get-tuple-element.83), channel_id=1, replica_groups=mesh['dp'=2,'y'=4,'x'=4,'z'=8] {'dp','z'}, dimensions={0} | all-to-all | bytes 262144 | tf_op jit(solution)/shard_map/all_to_all | solution.py:356
  252.4 1.9 pass.1.refs_5_
  254.3 4.9 %keep.3 = bf16[1024,1024]{1,0:T(8,128)(2,1)} custom-call(bf16[1024,1024]{1,0:T(8,128)(2,1)} %collective-permute-done.13.refs_0_, bf16[128,1024]{1,0:T(8,128)(2,1)} %get-tuple-element.89.refs_0_.refs_1_, bf16[128,1536]{1,0:T(8,128)(2,1)} %get-tuple-element.90.refs_1_.refs_2_, bf16[128,1024]{1,0:T(8,128)(2,1)} %get-tuple-element.85.refs_5_.refs_2_.refs_3_, ...), custom_call_target="tpu_custom_call" | custom-call | flops 268435456 | bytes 5242880 | tf_op jit(solution)/shard_map/keep/pallas_call | solution.py:335
  259.2 3.7 %all-to-all-start.15 = ((bf16[16,64,1024]{2,1,0:T(8,128)(2,1)}), bf16[16,64,1024]{2,1,0:T(8,128)(2,1)S(1)}, u32[]{:S(2)}, u32[]{:S(2)}) async-start(bf16[16,64,1024]{2,1,0:T(8,128)(2,1)} %bitcast.13), calls=%async_computation.16 | async-start | bytes 4194304 | tf_op jit(solution)/shard_map/all_to_all | solution.py:356
  263.0 0.7 reduce-scatter.5.cloned.1.call-update
  263.7 1.9 collective-permute-start.9
  265.6 26.8 %collective-permute-done.9 = f32[1,2048]{1,0:T(1,128)S(1)} collective-permute-done((f32[1,2048]{1,0:T(1,128)S(1)}, f32[1,2048]{1,0:T(1,128)S(1)}, u32[]{:S(2)}, u32[]{:S(2)}) %collective-permute-start.9) | collective-permute-done | bytes 8224 | tf_op jit(solution)/shard_map/ppermute | solution.py:416
  292.4 3.0 collective-permute-start.10
  295.3 2.3 collective-permute-done.10
  297.6 1.0 collective-permute-start.11
  298.7 2.7 collective-permute-done.11
  301.4 3.1 collective-permute-start.12
  304.5 2.1 collective-permute-done.12
  306.7 2.0 gather_rows.1
  308.7 6.3 %all-to-all-start.16 = ((bf16[16,8,2048]{2,1,0:T(8,128)(2,1)}), bf16[16,8,2048]{2,1,0:T(8,128)(2,1)S(1)}, u32[]{:S(2)}, u32[]{:S(2)}) async-start(bf16[16,8,2048]{2,1,0:T(8,128)(2,1)} %gather_rows.1), calls=%async_computation.18 | async-start | bytes 1048576 | tf_op jit(solution)/shard_map/all_to_all | solution.py:356
  315.0 2.0 last.1
  317.0 14.4 %all-to-all-done.16.refs_0_ = bf16[16,8,2048]{2,1,0:T(8,128)(2,1)S(1)} async-done(((bf16[16,8,2048]{2,1,0:T(8,128)(2,1)}), bf16[16,8,2048]{2,1,0:T(8,128)(2,1)S(1)}, u32[]{:S(2)}, u32[]{:S(2)}) %all-to-all-start.16) | async-done | bytes 524320 | tf_op jit(solution)/shard_map/all_to_all | solution.py:356
  331.4 0.7 rows.1
  (38 shorter events, 0.8 us)
Async XLA Ops:
  7.2 25.2 %collective-permute-start.1 = (bf16[128,1024]{1,0:T(8,128)(2,1)}, bf16[128,1024]{1,0:T(8,128)(2,1)S(1)}, u32[]{:S(2)}, u32[]{:S(2)}) collective-permute-start(bf16[128,1024]{1,0:T(8,128)(2,1)} %bitcast.14), channel_id=1, source_target_pairs={{1,0},{2,1},{3,2},{4,3},{5,4},{6,5},{7,6},{8,7},{9,8},{10,9},{11,1... | collective-permute-start | bytes 786440 | tf_op jit(solution)/shard_map/ppermute | solution.py:375
  10.9 21.5 %collective-permute-start = (bf16[128,1024]{1,0:T(8,128)(2,1)}, bf16[128,1024]{1,0:T(8,128)(2,1)S(1)}, u32[]{:S(2)}, u32[]{:S(2)}) collective-permute-start(bf16[128,1024]{1,0:T(8,128)(2,1)} %bitcast.15), channel_id=1, source_target_pairs={{0,1},{1,2},{2,3},{3,4},{4,5},{5,6},{6,7},{7,8},{8,9},{9,10},{10,1... | collective-permute-start | bytes 786440 | tf_op jit(solution)/shard_map/ppermute | solution.py:375
  14.8 17.6 %all-to-all-start = ((f32[16,1,2048]{2,1,0:T(1,128)}), f32[16,1,2048]{2,1,0:T(1,128)S(1)}, u32[]{:S(2)}, u32[]{:S(2)}) async-start(f32[16,1,2048]{2,1,0:T(1,128)} %first.1), calls=%async_computation | async-start | bytes 262144 | tf_op jit(solution)/shard_map/all_to_all | solution.py:356
  33.1 16.9 %all-to-all-start.1 = ((f32[16,1,2048]{2,1,0:T(1,128)}), f32[16,1,2048]{2,1,0:T(1,128)S(1)}, u32[]{:S(2)}, u32[]{:S(2)}) async-start(f32[16,1,2048]{2,1,0:T(1,128)} %merge_moments.4), calls=%async_computation.1 | async-start | bytes 262144 | tf_op jit(solution)/shard_map/all_to_all | solution.py:356
  42.0 210.3 %reduce-scatter.3.cloned.1.call-start = ((), (), s32[]{:S(2)}) async-start(), calls=%async_computation.19 | async-start | bytes 2621440 | tf_op jit(solution)/shard_map/reduce_scatter | solution.py:420
  77.8 17.6 %collective-permute-start.3 = (bf16[128,1024]{1,0:T(8,128)(2,1)S(1)}, bf16[128,1024]{1,0:T(8,128)(2,1)S(1)}, u32[]{:S(2)}, u32[]{:S(2)}) collective-permute-start(bf16[128,1024]{1,0:T(8,128)(2,1)S(1)} %get-tuple-element.56.refs_1_), channel_id=1, source_target_pairs={{8,0},{9,1},{10,2},{11,3},{12,4},{13,5},{14,6},{15,7},{16,8},{17,9... | collective-permute-start | bytes 786440 | tf_op jit(solution)/shard_map/ppermute | solution.py:375
  79.1 16.3 %collective-permute-start.2 = (bf16[128,1024]{1,0:T(8,128)(2,1)S(1)}, bf16[128,1024]{1,0:T(8,128)(2,1)S(1)}, u32[]{:S(2)}, u32[]{:S(2)}) collective-permute-start(bf16[128,1024]{1,0:T(8,128)(2,1)S(1)} %get-tuple-element.56.refs_1_), channel_id=1, source_target_pairs={{0,8},{1,9},{2,10},{3,11},{4,12},{5,13},{6,14},{7,15},{8,16},{9,17... | collective-permute-start | bytes 786440 | tf_op jit(solution)/shard_map/ppermute | solution.py:375
  136.1 16.4 %collective-permute-start.5 = (bf16[128,1024]{1,0:T(8,128)(2,1)S(1)}, bf16[128,1024]{1,0:T(8,128)(2,1)S(1)}, u32[]{:S(2)}, u32[]{:S(2)}) collective-permute-start(bf16[128,1024]{1,0:T(8,128)(2,1)S(1)} %get-tuple-element.62), channel_id=1, source_target_pairs={{8,0},{9,1},{10,2},{11,3},{12,4},{13,5},{14,6},{15,7},{16,8},{17,9... | collective-permute-start | bytes 786440 | tf_op jit(solution)/shard_map/ppermute | solution.py:375
  137.4 15.1 %collective-permute-start.4 = (bf16[128,1024]{1,0:T(8,128)(2,1)S(1)}, bf16[128,1024]{1,0:T(8,128)(2,1)S(1)}, u32[]{:S(2)}, u32[]{:S(2)}) collective-permute-start(bf16[128,1024]{1,0:T(8,128)(2,1)S(1)} %get-tuple-element.62), channel_id=1, source_target_pairs={{0,8},{1,9},{2,10},{3,11},{4,12},{5,13},{6,14},{7,15},{8,16},{9,17... | collective-permute-start | bytes 786440 | tf_op jit(solution)/shard_map/ppermute | solution.py:375
  182.7 4.2 %collective-permute-start.8 = (bf16[1024,1024]{1,0:T(8,128)(2,1)S(1)}, bf16[1024,1024]{1,0:T(8,128)(2,1)S(1)}, u32[]{:S(2)}, u32[]{:S(2)}) collective-permute-start(bf16[1024,1024]{1,0:T(8,128)(2,1)S(1)} %give.2), channel_id=1, source_target_pairs={{0,128},{128,0},{1,129},{129,1},{2,130},{130,2},{3,131},{131,3},{4... | collective-permute-start | bytes 6291464 | tf_op jit(solution)/shard_map/ppermute | solution.py:416
  204.0 17.9 %collective-permute-start.7 = (bf16[128,1024]{1,0:T(8,128)(2,1)S(1)}, bf16[128,1024]{1,0:T(8,128)(2,1)S(1)}, u32[]{:S(2)}, u32[]{:S(2)}) collective-permute-start(bf16[128,1024]{1,0:T(8,128)(2,1)S(1)} %get-tuple-element.73), channel_id=1, source_target_pairs={{1,0},{2,1},{3,2},{4,3},{5,4},{6,5},{7,6},{8,7},{9,8},{10,9},{11,1... | collective-permute-start | bytes 786440 | tf_op jit(solution)/shard_map/ppermute | solution.py:375
  206.3 15.6 %collective-permute-start.6 = (bf16[128,1024]{1,0:T(8,128)(2,1)S(1)}, bf16[128,1024]{1,0:T(8,128)(2,1)S(1)}, u32[]{:S(2)}, u32[]{:S(2)}) collective-permute-start(bf16[128,1024]{1,0:T(8,128)(2,1)S(1)} %get-tuple-element.73), channel_id=1, source_target_pairs={{0,1},{1,2},{2,3},{3,4},{4,5},{5,6},{6,7},{7,8},{8,9},{9,10},{10,1... | collective-permute-start | bytes 786440 | tf_op jit(solution)/shard_map/ppermute | solution.py:375
  240.5 13.8 %collective-permute-start.13 = (bf16[1024,1024]{1,0:T(8,128)(2,1)S(1)}, bf16[1024,1024]{1,0:T(8,128)(2,1)}, u32[]{:S(2)}, u32[]{:S(2)}) collective-permute-start(bf16[1024,1024]{1,0:T(8,128)(2,1)S(1)} %give.3), channel_id=1, source_target_pairs={{0,128},{128,0},{1,129},{129,1},{2,130},{130,2},{3,131},{131,3},{4... | collective-permute-start | bytes 6291464 | tf_op jit(solution)/shard_map/ppermute | solution.py:416
  259.2 47.5 %all-to-all-start.15 = ((bf16[16,64,1024]{2,1,0:T(8,128)(2,1)}), bf16[16,64,1024]{2,1,0:T(8,128)(2,1)S(1)}, u32[]{:S(2)}, u32[]{:S(2)}) async-start(bf16[16,64,1024]{2,1,0:T(8,128)(2,1)} %bitcast.13), calls=%async_computation.16 | async-start | bytes 4194304 | tf_op jit(solution)/shard_map/all_to_all | solution.py:356
  262.9 43.7 %reduce-scatter.5.cloned.1.call-start = ((), (), s32[]{:S(2)}) async-start(), calls=%async_computation.20 | async-start | bytes 655360 | tf_op jit(solution)/shard_map/reduce_scatter | solution.py:420
  263.7 28.7 %collective-permute-start.9 = (f32[1,2048]{1,0:T(1,128)S(1)}, f32[1,2048]{1,0:T(1,128)S(1)}, u32[]{:S(2)}, u32[]{:S(2)}) collective-permute-start(f32[1,2048]{1,0:T(1,128)S(1)} %merge_sums.7.refs_1_), channel_id=1, source_target_pairs={{0,8},{8,0},{16,24},{24,16},{1,9},{9,1},{17,25},{25,17},{2,10},{10... | collective-permute-start | bytes 24584 | tf_op jit(solution)/shard_map/ppermute | solution.py:416
  292.4 5.2 %collective-permute-start.10 = (f32[1,2048]{1,0:T(1,128)S(1)}, f32[1,2048]{1,0:T(1,128)S(1)}, u32[]{:S(2)}, u32[]{:S(2)}) collective-permute-start(f32[1,2048]{1,0:T(1,128)S(1)} %add.76), channel_id=1, source_target_pairs={{0,16},{8,24},{16,0},{24,8},{1,17},{9,25},{17,1},{25,9},{2,18},{10... | collective-permute-start | bytes 24584 | tf_op jit(solution)/shard_map/ppermute | solution.py:416
  297.6 3.7 %collective-permute-start.11 = (f32[1,2048]{1,0:T(1,128)S(1)}, f32[1,2048]{1,0:T(1,128)S(1)}, u32[]{:S(2)}, u32[]{:S(2)}) collective-permute-start(f32[1,2048]{1,0:T(1,128)S(1)} %add.77), channel_id=1, source_target_pairs={{0,32},{32,0},{64,96},{96,64},{1,33},{33,1},{65,97},{97,65},{2,34}... | collective-permute-start | bytes 24584 | tf_op jit(solution)/shard_map/ppermute | solution.py:416
  301.4 5.2 %collective-permute-start.12 = (f32[1,2048]{1,0:T(1,128)S(1)}, f32[1,2048]{1,0:T(1,128)S(1)}, u32[]{:S(2)}, u32[]{:S(2)}) collective-permute-start(f32[1,2048]{1,0:T(1,128)S(1)} %add.78), channel_id=1, source_target_pairs={{0,64},{32,96},{64,0},{96,32},{1,65},{33,97},{65,1},{97,33},{2,66}... | collective-permute-start | bytes 24584 | tf_op jit(solution)/shard_map/ppermute | solution.py:416
  308.7 22.7 %all-to-all-start.16 = ((bf16[16,8,2048]{2,1,0:T(8,128)(2,1)}), bf16[16,8,2048]{2,1,0:T(8,128)(2,1)S(1)}, u32[]{:S(2)}, u32[]{:S(2)}) async-start(bf16[16,8,2048]{2,1,0:T(8,128)(2,1)} %gather_rows.1), calls=%async_computation.18 | async-start | bytes 1048576 | tf_op jit(solution)/shard_map/all_to_all | solution.py:356
Sparse Core Ops, SparseCore 0:
  190.4 27.1 reduce-scatter.2
  266.5 24.9 reduce-scatter.4

commit v5 on v4

--- a/solution.py
+++ b/solution.py
@@ -248,8 +248,7 @@
         first += width
 
 
-def k_gather(parts, other, *rest):
-    out = rest[-1]
+def k_gather(parts, other, out):
     for z in range(8):
         rows = slice(8 * z, 8 * z + 8)
         total = parts[0, rows].astype(F32)
@@ -272,10 +271,6 @@
             project_out[layer, :, d * width : (d + 1) * width] = total[:, first + cut : first + CH]
 
 
-def k_pass(value, out):
-    out[...] = value[...]
-
-
 def whole(value):
     shape = value.shape
     return pl.BlockSpec(shape, lambda i: (0,) * len(shape))
@@ -285,30 +280,62 @@
     return pltpu.with_memory_space_constraint(value, pltpu.HBM)
 
 
+class Loaded:
+    def __init__(self, copy, ref):
+        self.copy, self.ref, self.shape = copy, ref, ref.shape
+        copy.start()
+
+    def finish(self):
+        if self.copy is not None:
+            self.copy.wait()
+            self.copy = None
+
+    def __getitem__(self, place):
+        self.finish()
+        return self.ref[place]
+
+
+class Stored:
+    def __init__(self, copy, ref):
+        self.copy, self.ref, self.shape, self.started = copy, ref, ref.shape, False
+
+    def start(self):
+        if not self.started:
+            self.copy.start()
+            self.started = True
+
+    def __getitem__(self, place):
+        return self.ref[place]
+
+    def __setitem__(self, place, value):
+        self.ref[place] = value
+        if place is Ellipsis:
+            self.start()
+
+
 def staged(kernel, counts, loaded, stored):
     n_in, n_waits, n_out = counts
 
     def body(*refs):
         ins, outs = list(refs[:n_in]), list(refs[n_in + n_waits : n_in + n_waits + n_out])
         scratch = list(refs[n_in + n_waits + n_out :])
-        sems, copies, results = scratch.pop(), [], []
+        sems, late, results = scratch.pop(), [], []
         for place, (i, layer) in enumerate(loaded):
             source = ins[i] if layer is None else ins[i].at[layer]
-            ins[i] = scratch.pop(0)
-            copies.append(pltpu.make_async_copy(source, ins[i], sems.at[place]))
-            copies[-1].start()
-        for place, i in enumerate(stored):
-            target, outs[i] = outs[i], scratch.pop(0)
-            results.append(
-                pltpu.make_async_copy(outs[i], target, sems.at[len(loaded) + place])
-            )
-        for copy in copies:
-            copy.wait()
+            buffer = scratch.pop(0)
+            ins[i] = Loaded(pltpu.make_async_copy(source, buffer, sems.at[place]), buffer)
+            late.append(ins[i])
+        for place, i in enumerate(stored, len(loaded)):
+            buffer = scratch.pop(0)
+            outs[i] = Stored(pltpu.make_async_copy(buffer, outs[i], sems.at[place]), buffer)
+            results.append(outs[i])
         kernel(*ins, *outs)
-        for copy in results:
-            copy.start()
-        for copy in results:
-            copy.wait()
+        for value in late:
+            value.finish()
+        for value in results:
+            value.start()
+        for value in results:
+            value.copy.wait()
 
     return body
 
@@ -562,6 +589,7 @@
     )
     parts, merged = over_all(payload, "sums")
     share_1 = chip_share((taps_1, three_1), (grad_2, hidden_1), waits_first=(merged,))
+    rows_1 = rows_over(share_1, SECOND_STAGE)
     gain_in, bias_in, grad_1, grad, pair, payload = call(
         k_back_entry,
         [
@@ -587,8 +615,7 @@
         name="back_entry",
     )
     sides = neighbours(pair, FIRST_DILATION)
-    parts, _ = over_all(payload, "sums", sides, (share_1,))
-    rows_1 = rows_over(share_1, "y")
+    parts, _ = over_all(payload, "sums", sides)
     three_0, grad_in, grad_gains_mid, grad_biases_mid, payload = back_middle(
         0,
         parts,
@@ -608,17 +635,7 @@
         exchange(payload, FIRST_STAGE),
         name="merge_sums",
     )
-    (rows_1,) = call(
-        k_pass,
-        [(rows_1.shape, BF16)],
-        rows_1,
-        loaded=(0,),
-        stored=(0,),
-        waits=(sums,),
-        name="pass",
-    )
-    share_0 = chip_share((taps_0, three_0), (grad_1, hidden_0), held=(rows_1,))
-    rows_1 = rows_over(rows_1, "x")
+    share_0 = chip_share((taps_0, three_0), (grad_1, hidden_0), waits=(sums,))
     share_0 = exchange(share_0.reshape(GROUP, CH // GROUP, CH), SECOND_STAGE)
     for axis in ("x", "y"):
         for step in (1, 2):
@@ -644,7 +661,6 @@
         share_0,
         rows_1,
         loaded=(1,),
-        waits=(sums,),
         name="gather_rows",
     )
     grad_conv, grad_proj = call(

time: 340 us -> 350 us (1.029)
  blocking collectives: 150 us -> 174 us
  waiting for transfers between devices: 67 us -> 57.2 us
  starting transfers between devices: 61 us -> 56.5 us
    reduce_scatter x2 -> x1, waiting for transfers between devices: 0.04 us -> 29.1 us  [rows_over(): return lax.psum_scatter(share, axis, scatter_dimension=0, tiled=True)]
    ppermute x6, waiting for transfers between devices: 38 us -> 10.3 us  [swapped(): return lax.ppermute(value, axis, pairs)]
    all_to_all x13, blocking collectives: 150 us -> 174 us  [exchange(): return lax.all_to_all(value, axes, 0, 0, tiled=True)]
    all_to_all x4, waiting for transfers between devices: 28.2 us -> 17.8 us  [exchange(): return lax.all_to_all(value, axes, 0, 0, tiled=True)]
    ppermute x8, starting transfers between devices: 23.4 us -> 19.3 us  [passed_along(): lax.ppermute(value, SEQ, [(source, source + steps) for source in range(le...]
    pallas_call x24 -> x23, Pallas kernels: 44.7 us -> 43.4 us  [call(): pl.pallas_call(body, grid=(1,), in_specs=specs, out_specs=[in_hbm if i in...]
  transfers between devices with their start and end apart: 20 -> 19, of which waited for: 8 -> 8; matrix products, arithmetic and copies ran while one was open for 1% -> 1% of each run, Pallas kernels for 4% -> 6%
where the time goes in v5:
time: 350 us; the launch traced here: 348 us
  blocking collectives  174 us (50%)
  waiting for transfers between devices  57.2 us (16%)
  starting transfers between devices  56.5 us (16%)
  Pallas kernels  43.4 us (12%)
  between operations  14.4 us (4%)
    all_to_all x13, blocking collectives, exchange(): return lax.all_to_all(value, axes, 0, 0, tiled=True)  174 us
    pallas_call x23, Pallas kernels, call(): pl.pallas_call(body, grid=(1,), in_specs=specs, out_specs=[in_hbm if i in...  43.4 us
    all_to_all x4, starting transfers between devices, exchange(): return lax.all_to_all(value, axes, 0, 0, tiled=True)  29.5 us
    reduce_scatter x1, waiting for transfers between devices, rows_over(): return lax.psum_scatter(share, axis, scatter_dimension=0, tiled=True)  29.1 us
    ppermute x8, starting transfers between devices, passed_along(): lax.ppermute(value, SEQ, [(source, source + steps) for source in range(le...  19.3 us
    all_to_all x4, waiting for transfers between devices, exchange(): return lax.all_to_all(value, axes, 0, 0, tiled=True)  17.8 us
    ppermute x6, waiting for transfers between devices, swapped(): return lax.ppermute(value, axis, pairs)  10.3 us
    ppermute x6, starting transfers between devices, swapped(): return lax.ppermute(value, axis, pairs)  7.76 us
  transfers between devices with their start and end apart: 19, of which 8 were waited for; matrix products, arithmetic and copies ran while one was open for 1% of the time, Pallas kernels for 6%

profile of v5, /device:TPU:32, one launch (start us, length us, event | category | flops | bytes accessed | tf_op | source)
XLA Modules:
  0.0 348.3 jit_solution(11127491815014116177)
XLA Ops:
  7.2 3.8 %collective-permute-start = (bf16[128,1024]{1,0:T(8,128)(2,1)}, bf16[128,1024]{1,0:T(8,128)(2,1)S(1)}, u32[]{:S(2)}, u32[]{:S(2)}) collective-permute-start(bf16[128,1024]{1,0:T(8,128)(2,1)} %bitcast.14), channel_id=1, source_target_pairs={{0,1},{1,2},{2,3},{3,4},{4,5},{5,6},{6,7},{7,8},{8,9},{9,10},{10,1... | collective-permute-start | bytes 786440 | tf_op jit(solution)/shard_map/ppermute | solution.py:402
  11.0 2.0 collective-permute-start.1
  13.0 1.8 first.1
  14.8 9.8 %all-to-all-start = ((f32[16,1,2048]{2,1,0:T(1,128)}), f32[16,1,2048]{2,1,0:T(1,128)S(1)}, u32[]{:S(2)}, u32[]{:S(2)}) async-start(f32[16,1,2048]{2,1,0:T(1,128)} %first.1), calls=%async_computation | async-start | bytes 262144 | tf_op jit(solution)/shard_map/all_to_all | solution.py:383
  24.6 0.8 fusion.4
  25.5 0.8 select_reduce_fusion.1
  26.2 0.1 lt.37
  26.3 0.1 reduce_sum.25
  26.4 0.1 lt.40
  26.6 0.1 le.37
  26.7 0.1 le.40
  26.8 6.1 %all-to-all-done.refs_0_ = f32[16,1,2048]{2,1,0:T(1,128)S(1)} async-done(((f32[16,1,2048]{2,1,0:T(1,128)}), f32[16,1,2048]{2,1,0:T(1,128)S(1)}, u32[]{:S(2)}, u32[]{:S(2)}) %all-to-all-start) | async-done | bytes 131104 | tf_op jit(solution)/shard_map/all_to_all | solution.py:383
  32.8 0.7 merge_moments.4
  33.6 7.0 %all-to-all-start.1 = ((f32[16,1,2048]{2,1,0:T(1,128)}), f32[16,1,2048]{2,1,0:T(1,128)S(1)}, u32[]{:S(2)}, u32[]{:S(2)}) async-start(f32[16,1,2048]{2,1,0:T(1,128)} %merge_moments.4), calls=%async_computation.1 | async-start | bytes 262144 | tf_op jit(solution)/shard_map/all_to_all | solution.py:383
  40.7 0.1 copy.27
  40.8 7.8 %all-to-all-done.1.refs_0_ = f32[16,1,2048]{2,1,0:T(1,128)S(1)} async-done(((f32[16,1,2048]{2,1,0:T(1,128)}), f32[16,1,2048]{2,1,0:T(1,128)S(1)}, u32[]{:S(2)}, u32[]{:S(2)}) %all-to-all-start.1) | async-done | bytes 131104 | tf_op jit(solution)/shard_map/all_to_all | solution.py:383
  48.6 3.2 entry.2
  51.8 10.4 %all_to_all.85.refs_0_ = f32[16,1,1024]{2,1,0:T(1,128)S(1)} all-to-all(f32[16,1,1024]{2,1,0:T(1,128)S(1)} %get-tuple-element.53), channel_id=1, replica_groups=mesh['dp'=2,'y'=4,'x'=4,'z'=8] {'dp','z'}, dimensions={0} | all-to-all | bytes 131072 | tf_op jit(solution)/shard_map/all_to_all | solution.py:383
  62.2 10.7 %all_to_all.86.refs_0_ = f32[16,1,1024]{2,1,0:T(1,128)S(1)} all-to-all(f32[16,1,1024]{2,1,0:T(1,128)S(1)} %merge_moments.5), channel_id=1, replica_groups=mesh['dp'=2,'y'=4,'x'=4,'z'=8] {'y','x'}, dimensions={0} | all-to-all | bytes 131072 | tf_op jit(solution)/shard_map/all_to_all | solution.py:383
  72.9 2.8 middle.1
  75.8 2.5 collective-permute-start.2
  78.3 1.3 collective-permute-start.3
  79.6 11.8 %all_to_all.87.refs_0_ = f32[16,1,2048]{2,1,0:T(1,128)S(1)} all-to-all(f32[16,1,2048]{2,1,0:T(1,128)S(1)} %get-tuple-element.55), channel_id=1, replica_groups=mesh['dp'=2,'y'=4,'x'=4,'z'=8] {'dp','z'}, dimensions={0} | all-to-all | bytes 262144 | tf_op jit(solution)/shard_map/all_to_all | solution.py:383
  91.4 14.5 %all_to_all.88.refs_0_ = f32[16,1,2048]{2,1,0:T(1,128)S(1)} all-to-all(f32[16,1,2048]{2,1,0:T(1,128)S(1)} %merge_moments.6), channel_id=1, replica_groups=mesh['dp'=2,'y'=4,'x'=4,'z'=8] {'y','x'}, dimensions={0} | all-to-all | bytes 262144 | tf_op jit(solution)/shard_map/all_to_all | solution.py:383
  105.9 3.0 entry.3
  108.9 10.4 %all_to_all.89.refs_0_ = f32[16,1,1024]{2,1,0:T(1,128)S(1)} all-to-all(f32[16,1,1024]{2,1,0:T(1,128)S(1)} %get-tuple-element.57), channel_id=1, replica_groups=mesh['dp'=2,'y'=4,'x'=4,'z'=8] {'dp','z'}, dimensions={0} | all-to-all | bytes 131072 | tf_op jit(solution)/shard_map/all_to_all | solution.py:383
  119.3 10.7 %all_to_all.90.refs_0_ = f32[16,1,1024]{2,1,0:T(1,128)S(1)} all-to-all(f32[16,1,1024]{2,1,0:T(1,128)S(1)} %merge_moments.7), channel_id=1, replica_groups=mesh['dp'=2,'y'=4,'x'=4,'z'=8] {'y','x'}, dimensions={0} | all-to-all | bytes 131072 | tf_op jit(solution)/shard_map/all_to_all | solution.py:383
  130.1 2.6 turn.1
  132.7 2.5 collective-permute-start.4
  135.2 1.3 collective-permute-start.5
  136.5 10.5 %all_to_all.91.refs_0_ = f32[16,1,1024]{2,1,0:T(1,128)S(1)} all-to-all(f32[16,1,1024]{2,1,0:T(1,128)S(1)} %get-tuple-element.61), channel_id=1, replica_groups=mesh['dp'=2,'y'=4,'x'=4,'z'=8] {'dp','z'}, dimensions={0} | all-to-all | bytes 131072 | tf_op jit(solution)/shard_map/all_to_all | solution.py:383
  147.0 14.2 %all_to_all.92.refs_0_ = f32[16,1,1024]{2,1,0:T(1,128)S(1)} all-to-all(f32[16,1,1024]{2,1,0:T(1,128)S(1)} %merge_sums.4), channel_id=1, replica_groups=mesh['dp'=2,'y'=4,'x'=4,'z'=8] {'y','x'}, dimensions={0} | all-to-all | bytes 131072 | tf_op jit(solution)/shard_map/all_to_all | solution.py:383
  161.2 4.0 %back_middle.2 = (bf16[128,1536]{1,0:T(8,128)(2,1)}, f32[128,1024]{1,0:T(8,128)S(1)}, f32[1,512]{1,0:T(1,128)}, f32[1,512]{1,0:T(1,128)}, f32[16,1,2048]{2,1,0:T(1,128)S(1)}) custom-call(f32[16,1,1024]{2,1,0:T(1,128)S(1)} %all_to_all.92.refs_0_, f32[128,512]{1,0:T(8,128)S(1)} %get-tuple-element.63.refs_1_, f32[128,512]{1,0:T(8,128)S(1)} %get-tuple-element.64.refs_2_, ...), custom_call_target="tpu_custom_call" | custom-call | flops 402653184 | bytes 9261056 | tf_op jit(solution)/shard_map/back_middle/pallas_call | solution.py:362
  165.2 11.7 %all_to_all.93.refs_0_ = f32[16,1,2048]{2,1,0:T(1,128)S(1)} all-to-all(f32[16,1,2048]{2,1,0:T(1,128)S(1)} %get-tuple-element.68), channel_id=1, replica_groups=mesh['dp'=2,'y'=4,'x'=4,'z'=8] {'dp','z'}, dimensions={0} | all-to-all | bytes 262144 | tf_op jit(solution)/shard_map/all_to_all | solution.py:383
  177.0 3.6 %give.3 = bf16[1024,1024]{1,0:T(8,128)(2,1)} custom-call(bf16[128,1024]{1,0:T(8,128)(2,1)} %get-tuple-element.89.refs_0_.refs_1_, bf16[128,1536]{1,0:T(8,128)(2,1)} %get-tuple-element.90.refs_1_.refs_2_, bf16[128,1024]{1,0:T(8,128)(2,1)} %bitcast.22, bf16[128,512]{1,0:T(8,128)(2,1)} %get-tuple-element.91.refs_3_.refs_4_, f32[16,1,2048]{2,1,0:T(1,128)S(1)} %merge_sums.5.refs_4_), custom_call_target="tpu_custom_call" | custom-call | flops 268435456 | bytes 3145728 | tf_op jit(solution)/shard_map/give/pallas_call | solution.py:362
  180.6 0.1 collective-permute-start.13
  180.7 11.1 %all_to_all.94.refs_0_ = f32[16,1,2048]{2,1,0:T(1,128)S(1)} all-to-all(f32[16,1,2048]{2,1,0:T(1,128)S(1)} %merge_sums.5.refs_4_), channel_id=1, replica_groups=mesh['dp'=2,'y'=4,'x'=4,'z'=8] {'y','x'}, dimensions={0} | all-to-all | bytes 262144 | tf_op jit(solution)/shard_map/all_to_all | solution.py:383
  191.9 2.0 back_entry.1
  193.9 2.7 collective-permute-start.6
  196.6 3.2 collective-permute-start.7
  199.8 11.6 %all_to_all.95.refs_0_ = f32[16,1,1024]{2,1,0:T(1,128)S(1)} all-to-all(f32[16,1,1024]{2,1,0:T(1,128)S(1)} %get-tuple-element.72), channel_id=1, replica_groups=mesh['dp'=2,'y'=4,'x'=4,'z'=8] {'dp','z'}, dimensions={0} | all-to-all | bytes 131072 | tf_op jit(solution)/shard_map/all_to_all | solution.py:383
  211.3 0.7 merge_sums.6
  212.0 5.1 %all-to-all-start.13 = ((f32[16,1,1024]{2,1,0:T(1,128)}), f32[16,1,1024]{2,1,0:T(1,128)S(1)}, u32[]{:S(2)}, u32[]{:S(2)}) async-start(f32[16,1,1024]{2,1,0:T(1,128)} %merge_sums.6), calls=%async_computation.13 | async-start | bytes 131072 | tf_op jit(solution)/shard_map/all_to_all | solution.py:383
  217.2 3.7 %keep.3 = bf16[1024,1024]{1,0:T(8,128)(2,1)} custom-call(bf16[1024,1024]{1,0:T(8,128)(2,1)S(1)} %collective-permute-done.13.refs_0_, bf16[128,1024]{1,0:T(8,128)(2,1)} %get-tuple-element.89.refs_0_.refs_1_, bf16[128,1536]{1,0:T(8,128)(2,1)} %get-tuple-element.90.refs_1_.refs_2_, bf16[128,1024]{1,0:T(8,128)(2,1)} %bitcast.24, ...), custom_call_target="tpu_custom_call" | custom-call | flops 268435456 | bytes 5242880 | tf_op jit(solution)/shard_map/keep/pallas_call | solution.py:362
  220.9 3.9 %all-to-all-done.13.refs_0_ = f32[16,1,1024]{2,1,0:T(1,128)S(1)} async-done(((f32[16,1,1024]{2,1,0:T(1,128)}), f32[16,1,1024]{2,1,0:T(1,128)S(1)}, u32[]{:S(2)}, u32[]{:S(2)}) %all-to-all-start.13) | async-done | bytes 65568 | tf_op jit(solution)/shard_map/all_to_all | solution.py:383
  224.8 4.4 %back_middle.3 = (bf16[128,1536]{1,0:T(8,128)(2,1)}, f32[128,1024]{1,0:T(8,128)S(1)}, f32[2,512]{1,0:T(2,128)}, f32[2,512]{1,0:T(2,128)}, f32[16,1,2048]{2,1,0:T(1,128)S(1)}) custom-call(f32[16,1,1024]{2,1,0:T(1,128)S(1)} %all-to-all-done.13.refs_0_, f32[128,512]{1,0:T(8,128)S(1)} %get-tuple-element.74.refs_1_, ...), custom_call_target="tpu_custom_call" | custom-call | flops 402653184 | bytes 9269248 | tf_op jit(solution)/shard_map/back_middle/pallas_call | solution.py:362
  229.2 2.3 give.2
  231.5 0.1 collective-permute-start.12
  231.6 12.0 %all_to_all.96.refs_0_ = f32[16,1,2048]{2,1,0:T(1,128)S(1)} all-to-all(f32[16,1,2048]{2,1,0:T(1,128)S(1)} %get-tuple-element.80), channel_id=1, replica_groups=mesh['dp'=2,'y'=4,'x'=4,'z'=8] {'dp','z'}, dimensions={0} | all-to-all | bytes 262144 | tf_op jit(solution)/shard_map/all_to_all | solution.py:383
  243.7 3.7 %keep.2 = bf16[1024,1024]{1,0:T(8,128)(2,1)} custom-call(bf16[1024,1024]{1,0:T(8,128)(2,1)S(1)} %collective-permute-done.12.refs_0_, bf16[128,1024]{1,0:T(8,128)(2,1)} %get-tuple-element.86.refs_0_.refs_1_, bf16[128,1536]{1,0:T(8,128)(2,1)} %get-tuple-element.87.refs_1_.refs_2_, bf16[128,1024]{1,0:T(8,128)(2,1)} %get-tuple-element.82.refs_5_.refs_2_.refs_3_, ...), custom_call_target="tpu_custom_call" | custom-call | flops 268435456 | bytes 5242880 | tf_op jit(solution)/shard_map/keep/pallas_call | solution.py:362
  247.3 34.9 %all_to_all.97.refs_0_ = bf16[16,64,1024]{2,1,0:T(8,128)(2,1)S(1)} all-to-all(bf16[16,64,1024]{2,1,0:T(8,128)(2,1)} %bitcast.13), channel_id=1, replica_groups=mesh['dp'=2,'y'=4,'x'=4,'z'=8] {'y','x'}, dimensions={0} | all-to-all | bytes 4194304 | tf_op jit(solution)/shard_map/all_to_all | solution.py:383
  282.2 29.1 %reduce-scatter.2.cloned.1.call-done.refs_1_ = bf16[64,1024]{1,0:T(8,128)(2,1)} async-done(((bf16[1024,1024]{1,0:T(8,128)(2,1)}), bf16[64,1024]{1,0:T(8,128)(2,1)}) %reduce-scatter.2.cloned.1.call-update) | async-done | bytes 131088 | tf_op jit(solution)/shard_map/reduce_scatter | solution.py:447
  311.3 2.0 gather_rows.1
  313.3 7.5 %all-to-all-start.16 = ((bf16[16,8,2048]{2,1,0:T(8,128)(2,1)}), bf16[16,8,2048]{2,1,0:T(8,128)(2,1)S(1)}, u32[]{:S(2)}, u32[]{:S(2)}) async-start(bf16[16,8,2048]{2,1,0:T(8,128)(2,1)} %gather_rows.1), calls=%async_computation.17 | async-start | bytes 1048576 | tf_op jit(solution)/shard_map/all_to_all | solution.py:383
  320.8 1.1 collective-permute-start.8
  321.9 2.5 collective-permute-done.8
  324.5 2.6 collective-permute-start.9
  327.1 2.6 collective-permute-done.9
  329.7 1.2 collective-permute-start.10
  330.9 2.5 collective-permute-done.10
  333.5 2.6 collective-permute-start.11
  336.1 2.6 collective-permute-done.11
  338.7 2.0 last.1
  340.8 0.7 rows.1
  (34 shorter events, 0.6 us)
Async XLA Ops:
  7.2 25.7 %collective-permute-start = (bf16[128,1024]{1,0:T(8,128)(2,1)}, bf16[128,1024]{1,0:T(8,128)(2,1)S(1)}, u32[]{:S(2)}, u32[]{:S(2)}) collective-permute-start(bf16[128,1024]{1,0:T(8,128)(2,1)} %bitcast.14), channel_id=1, source_target_pairs={{0,1},{1,2},{2,3},{3,4},{4,5},{5,6},{6,7},{7,8},{8,9},{9,10},{10,1... | collective-permute-start | bytes 786440 | tf_op jit(solution)/shard_map/ppermute | solution.py:402
  11.0 21.8 %collective-permute-start.1 = (bf16[128,1024]{1,0:T(8,128)(2,1)}, bf16[128,1024]{1,0:T(8,128)(2,1)S(1)}, u32[]{:S(2)}, u32[]{:S(2)}) collective-permute-start(bf16[128,1024]{1,0:T(8,128)(2,1)} %bitcast.15), channel_id=1, source_target_pairs={{1,0},{2,1},{3,2},{4,3},{5,4},{6,5},{7,6},{8,7},{9,8},{10,9},{11,1... | collective-permute-start | bytes 786440 | tf_op jit(solution)/shard_map/ppermute | solution.py:402
  14.8 18.0 %all-to-all-start = ((f32[16,1,2048]{2,1,0:T(1,128)}), f32[16,1,2048]{2,1,0:T(1,128)S(1)}, u32[]{:S(2)}, u32[]{:S(2)}) async-start(f32[16,1,2048]{2,1,0:T(1,128)} %first.1), calls=%async_computation | async-start | bytes 262144 | tf_op jit(solution)/shard_map/all_to_all | solution.py:383
  33.6 15.0 %all-to-all-start.1 = ((f32[16,1,2048]{2,1,0:T(1,128)}), f32[16,1,2048]{2,1,0:T(1,128)S(1)}, u32[]{:S(2)}, u32[]{:S(2)}) async-start(f32[16,1,2048]{2,1,0:T(1,128)} %merge_moments.4), calls=%async_computation.1 | async-start | bytes 262144 | tf_op jit(solution)/shard_map/all_to_all | solution.py:383
  75.8 15.5 %collective-permute-start.2 = (bf16[128,1024]{1,0:T(8,128)(2,1)S(1)}, bf16[128,1024]{1,0:T(8,128)(2,1)S(1)}, u32[]{:S(2)}, u32[]{:S(2)}) collective-permute-start(bf16[128,1024]{1,0:T(8,128)(2,1)S(1)} %get-tuple-element.56.refs_1_), channel_id=1, source_target_pairs={{0,8},{1,9},{2,10},{3,11},{4,12},{5,13},{6,14},{7,15},{8,16},{9,17... | collective-permute-start | bytes 786440 | tf_op jit(solution)/shard_map/ppermute | solution.py:402
  78.3 13.1 %collective-permute-start.3 = (bf16[128,1024]{1,0:T(8,128)(2,1)S(1)}, bf16[128,1024]{1,0:T(8,128)(2,1)S(1)}, u32[]{:S(2)}, u32[]{:S(2)}) collective-permute-start(bf16[128,1024]{1,0:T(8,128)(2,1)S(1)} %get-tuple-element.56.refs_1_), channel_id=1, source_target_pairs={{8,0},{9,1},{10,2},{11,3},{12,4},{13,5},{14,6},{15,7},{16,8},{17,9... | collective-permute-start | bytes 786440 | tf_op jit(solution)/shard_map/ppermute | solution.py:402
  132.7 14.3 %collective-permute-start.4 = (bf16[128,1024]{1,0:T(8,128)(2,1)S(1)}, bf16[128,1024]{1,0:T(8,128)(2,1)S(1)}, u32[]{:S(2)}, u32[]{:S(2)}) collective-permute-start(bf16[128,1024]{1,0:T(8,128)(2,1)S(1)} %get-tuple-element.62), channel_id=1, source_target_pairs={{0,8},{1,9},{2,10},{3,11},{4,12},{5,13},{6,14},{7,15},{8,16},{9,17... | collective-permute-start | bytes 786440 | tf_op jit(solution)/shard_map/ppermute | solution.py:402
  135.2 11.8 %collective-permute-start.5 = (bf16[128,1024]{1,0:T(8,128)(2,1)S(1)}, bf16[128,1024]{1,0:T(8,128)(2,1)S(1)}, u32[]{:S(2)}, u32[]{:S(2)}) collective-permute-start(bf16[128,1024]{1,0:T(8,128)(2,1)S(1)} %get-tuple-element.62), channel_id=1, source_target_pairs={{8,0},{9,1},{10,2},{11,3},{12,4},{13,5},{14,6},{15,7},{16,8},{17,9... | collective-permute-start | bytes 786440 | tf_op jit(solution)/shard_map/ppermute | solution.py:402
  180.6 36.6 %collective-permute-start.13 = (bf16[1024,1024]{1,0:T(8,128)(2,1)}, bf16[1024,1024]{1,0:T(8,128)(2,1)S(1)}, u32[]{:S(2)}, u32[]{:S(2)}) collective-permute-start(bf16[1024,1024]{1,0:T(8,128)(2,1)} %give.3), channel_id=1, source_target_pairs={{0,128},{128,0},{1,129},{129,1},{2,130},{130,2},{3,131},{131,3},{4... | collective-permute-start | bytes 6291464 | tf_op jit(solution)/shard_map/ppermute | solution.py:443
  193.9 17.4 %collective-permute-start.6 = (bf16[128,1024]{1,0:T(8,128)(2,1)S(1)}, bf16[128,1024]{1,0:T(8,128)(2,1)S(1)}, u32[]{:S(2)}, u32[]{:S(2)}) collective-permute-start(bf16[128,1024]{1,0:T(8,128)(2,1)S(1)} %get-tuple-element.73), channel_id=1, source_target_pairs={{0,1},{1,2},{2,3},{3,4},{4,5},{5,6},{6,7},{7,8},{8,9},{9,10},{10,1... | collective-permute-start | bytes 786440 | tf_op jit(solution)/shard_map/ppermute | solution.py:402
  196.6 14.8 %collective-permute-start.7 = (bf16[128,1024]{1,0:T(8,128)(2,1)S(1)}, bf16[128,1024]{1,0:T(8,128)(2,1)S(1)}, u32[]{:S(2)}, u32[]{:S(2)}) collective-permute-start(bf16[128,1024]{1,0:T(8,128)(2,1)S(1)} %get-tuple-element.73), channel_id=1, source_target_pairs={{1,0},{2,1},{3,2},{4,3},{5,4},{6,5},{7,6},{8,7},{9,8},{10,9},{11,1... | collective-permute-start | bytes 786440 | tf_op jit(solution)/shard_map/ppermute | solution.py:402
  212.0 12.8 %all-to-all-start.13 = ((f32[16,1,1024]{2,1,0:T(1,128)}), f32[16,1,1024]{2,1,0:T(1,128)S(1)}, u32[]{:S(2)}, u32[]{:S(2)}) async-start(f32[16,1,1024]{2,1,0:T(1,128)} %merge_sums.6), calls=%async_computation.13 | async-start | bytes 131072 | tf_op jit(solution)/shard_map/all_to_all | solution.py:383
  217.1 94.2 %reduce-scatter.2.cloned.1.call-start = ((), (), s32[]{:S(2)}) async-start(), calls=%async_computation.18 | async-start | bytes 2228224 | tf_op jit(solution)/shard_map/reduce_scatter | solution.py:447
  231.5 12.1 %collective-permute-start.12 = (bf16[1024,1024]{1,0:T(8,128)(2,1)S(1)}, bf16[1024,1024]{1,0:T(8,128)(2,1)S(1)}, u32[]{:S(2)}, u32[]{:S(2)}) collective-permute-start(bf16[1024,1024]{1,0:T(8,128)(2,1)S(1)} %give.2), channel_id=1, source_target_pairs={{0,128},{128,0},{1,129},{129,1},{2,130},{130,2},{3,131},{131,3},{4... | collective-permute-start | bytes 6291464 | tf_op jit(solution)/shard_map/ppermute | solution.py:443
  313.3 27.5 %all-to-all-start.16 = ((bf16[16,8,2048]{2,1,0:T(8,128)(2,1)}), bf16[16,8,2048]{2,1,0:T(8,128)(2,1)S(1)}, u32[]{:S(2)}, u32[]{:S(2)}) async-start(bf16[16,8,2048]{2,1,0:T(8,128)(2,1)} %gather_rows.1), calls=%async_computation.17 | async-start | bytes 1048576 | tf_op jit(solution)/shard_map/all_to_all | solution.py:383
  320.8 3.7 %collective-permute-start.8 = (f32[1,2048]{1,0:T(1,128)S(1)}, f32[1,2048]{1,0:T(1,128)S(1)}, u32[]{:S(2)}, u32[]{:S(2)}) collective-permute-start(f32[1,2048]{1,0:T(1,128)S(1)} %merge_sums.7.refs_5_), channel_id=1, source_target_pairs={{0,8},{8,0},{16,24},{24,16},{1,9},{9,1},{17,25},{25,17},{2,10},{10... | collective-permute-start | bytes 24584 | tf_op jit(solution)/shard_map/ppermute | solution.py:443
  324.5 5.2 %collective-permute-start.9 = (f32[1,2048]{1,0:T(1,128)S(1)}, f32[1,2048]{1,0:T(1,128)S(1)}, u32[]{:S(2)}, u32[]{:S(2)}) collective-permute-start(f32[1,2048]{1,0:T(1,128)S(1)} %add.74), channel_id=1, source_target_pairs={{0,16},{8,24},{16,0},{24,8},{1,17},{9,25},{17,1},{25,9},{2,18},{10... | collective-permute-start | bytes 24584 | tf_op jit(solution)/shard_map/ppermute | solution.py:443
  329.7 3.7 %collective-permute-start.10 = (f32[1,2048]{1,0:T(1,128)S(1)}, f32[1,2048]{1,0:T(1,128)S(1)}, u32[]{:S(2)}, u32[]{:S(2)}) collective-permute-start(f32[1,2048]{1,0:T(1,128)S(1)} %add.75), channel_id=1, source_target_pairs={{0,32},{32,0},{64,96},{96,64},{1,33},{33,1},{65,97},{97,65},{2,34}... | collective-permute-start | bytes 24584 | tf_op jit(solution)/shard_map/ppermute | solution.py:443
  333.5 5.2 %collective-permute-start.11 = (f32[1,2048]{1,0:T(1,128)S(1)}, f32[1,2048]{1,0:T(1,128)S(1)}, u32[]{:S(2)}, u32[]{:S(2)}) collective-permute-start(f32[1,2048]{1,0:T(1,128)S(1)} %add.76), channel_id=1, source_target_pairs={{0,64},{32,96},{64,0},{96,32},{1,65},{33,97},{65,1},{97,33},{2,66}... | collective-permute-start | bytes 24584 | tf_op jit(solution)/shard_map/ppermute | solution.py:443
Sparse Core Ops, SparseCore 0:
  221.5 89.7 reduce-scatter.1

commit v6 on v5

--- a/solution.py
+++ b/solution.py
@@ -269,6 +269,10 @@
             first = layer * CH
             kernel_out[layer, :, d * cut : (d + 1) * cut] = total[:, first : first + cut]
             project_out[layer, :, d * width : (d + 1) * width] = total[:, first + cut : first + CH]
+
+
+def k_pass(value, out):
+    out[...] = value[...]
 
 
 def whole(value):
@@ -340,10 +344,13 @@
     return body
 
 
-def call(kernel, outs, *operands, name, loaded=(), stored=(), layers=None, waits=(), held=(), flops=1 << 22):
+def call(kernel, outs, *operands, name, loaded=(), free=(), stored=(), layers=None, waits=(), held=(), flops=1 << 22):
     layers = layers or {}
     in_hbm = pl.BlockSpec(memory_space=pltpu.HBM)
-    specs = [in_hbm if i in loaded else whole(value) for i, value in enumerate(operands)]
+    specs = [
+        pl.BlockSpec(memory_space=pl.ANY) if i in free else in_hbm if i in loaded else whole(value)
+        for i, value in enumerate(operands)
+    ]
     specs += [pl.BlockSpec(memory_space=pl.ANY)] * len(waits) + [in_hbm] * len(held)
     shapes = [jax.ShapeDtypeStruct(shape, dtype) for shape, dtype in outs]
     moved = sum(v.size * v.dtype.itemsize for v in list(operands) + shapes)
@@ -373,7 +380,7 @@
         cost_estimate=pl.CostEstimate(flops=flops, bytes_accessed=moved, transcendentals=0),
         compiler_params=pltpu.CompilerParams(vmem_limit_bytes=VMEM_LIMIT),
     )(
-        *[in_memory(value) if i in loaded else value for i, value in enumerate(operands)],
+        *[in_memory(v) if i in loaded and i not in free else v for i, v in enumerate(operands)],
         *waits,
         *[in_memory(value) for value in held],
     )
@@ -488,6 +495,7 @@
             gains_in,
             biases_in,
             loaded=(5, 6, 7) if layer else (1, 5, 6, 7),
+            free=(6, 7) if layer else (),
             stored=(0, 1, 3),
             layers={5: layer},
             name="entry",
@@ -517,6 +525,7 @@
         proj_weight,
         stream_0,
         loaded=(2, 3, 4, 5),
+        free=(2, 3, 4, 5),
         stored=(0, 2, 3, 4, 5),
         layers={4: 0},
         name="middle",
@@ -544,6 +553,7 @@
         kept_1,
         grad_2,
         loaded=(2, 3, 4, 5, 6),
+        free=(2, 3, 4, 5, 6),
         stored=(0, 1),
         layers={4: 1},
         name="turn",
@@ -575,6 +585,7 @@
             stat,
             *given,
             loaded=(7, 8, 9, 10, 11) if layer else (2, 3, 7, 8, 9, 10, 11, 12, 13),
+            free=(7, 9, 10, 11) if layer else (2, 3, 7, 9, 10, 11, 12, 13),
             stored=(0, 2, 3),
             layers={8: layer},
             held=held,
@@ -587,9 +598,7 @@
     three_1, grad_in, gain_mid, bias_mid, payload = back_middle(
         1, parts, grad, normed_1, factor_1, sides, slope_1, kept_1, stat_1
     )
-    parts, merged = over_all(payload, "sums")
-    share_1 = chip_share((taps_1, three_1), (grad_2, hidden_1), waits_first=(merged,))
-    rows_1 = rows_over(share_1, SECOND_STAGE)
+    parts, merged_1 = over_all(payload, "sums")
     gain_in, bias_in, grad_1, grad, pair, payload = call(
         k_back_entry,
         [
@@ -610,12 +619,17 @@
         slope_mid_0,
         normed_0,
         loaded=(2, 3, 4, 5, 6, 7, 8),
+        free=(2, 3, 4, 5, 6, 7, 8),
         stored=(0, 1, 2),
         layers={6: 0},
         name="back_entry",
     )
     sides = neighbours(pair, FIRST_DILATION)
-    parts, _ = over_all(payload, "sums", sides)
+    parts, merged_0 = over_all(payload, "sums", sides)
+    share_1 = chip_share(
+        (taps_1, three_1), (grad_2, hidden_1), waits_first=(merged_1,), waits=(merged_0,)
+    )
+    rows_1 = rows_over(share_1, "y")
     three_0, grad_in, grad_gains_mid, grad_biases_mid, payload = back_middle(
         0,
         parts,
@@ -636,6 +650,16 @@
         name="merge_sums",
     )
     share_0 = chip_share((taps_0, three_0), (grad_1, hidden_0), waits=(sums,))
+    (rows_1,) = call(
+        k_pass,
+        [(rows_1.shape, BF16)],
+        rows_1,
+        loaded=(0,),
+        stored=(0,),
+        held=(share_0,),
+        name="pass",
+    )
+    rows_1 = rows_over(rows_1, "x")
     share_0 = exchange(share_0.reshape(GROUP, CH // GROUP, CH), SECOND_STAGE)
     for axis in ("x", "y"):
         for step in (1, 2):
@@ -652,6 +676,7 @@
         gain_in,
         bias_in,
         loaded=(2, 3, 4, 5, 6, 7),
+        free=(2, 3, 4, 5, 6, 7),
         stored=(0, 1, 2),
         name="last",
     )

time: 350 us -> 319 us (0.911)
  blocking collectives: 174 us -> 152 us
  starting transfers between devices: 56.5 us -> 48.1 us
  Pallas kernels: 43.4 us -> 39.8 us
    reduce_scatter x1 -> x2, waiting for transfers between devices: 29.1 us -> 0.02 us  [rows_over(): return lax.psum_scatter(share, axis, scatter_dimension=0, tiled=True)]
    all_to_all x4, waiting for transfers between devices: 17.8 us -> 44.1 us  [exchange(): return lax.all_to_all(value, axes, 0, 0, tiled=True)]
    all_to_all x13, blocking collectives: 174 us -> 152 us  [exchange(): return lax.all_to_all(value, axes, 0, 0, tiled=True)]
    ppermute x6, starting transfers between devices: 7.76 us -> 2.21 us  [swapped(): return lax.ppermute(value, axis, pairs)]
    ppermute x6, waiting for transfers between devices: 10.3 us -> 15.8 us  [swapped(): return lax.ppermute(value, axis, pairs)]
    pallas_call x23 -> x24, Pallas kernels: 43.4 us -> 39.8 us  [call(): pl.pallas_call(body, grid=(1,), in_specs=specs, out_specs=[in_hbm if i in...]
  transfers between devices with their start and end apart: 19 -> 20, of which waited for: 8 -> 7; matrix products, arithmetic and copies ran while one was open for 1% -> 1% of each run, Pallas kernels for 6% -> 5%
where the time goes in v6:
time: 319 us; the launch traced here: 317 us
  blocking collectives  152 us (48%)
  waiting for transfers between devices  60 us (19%)
  starting transfers between devices  48.1 us (15%)
  Pallas kernels  39.8 us (12%)
  between operations  14.6 us (5%)
    all_to_all x13, blocking collectives, exchange(): return lax.all_to_all(value, axes, 0, 0, tiled=True)  152 us
    all_to_all x4, waiting for transfers between devices, exchange(): return lax.all_to_all(value, axes, 0, 0, tiled=True)  44.1 us
    pallas_call x24, Pallas kernels, call(): pl.pallas_call(body, grid=(1,), in_specs=specs, out_specs=[in_hbm if i in...  39.8 us
    all_to_all x4, starting transfers between devices, exchange(): return lax.all_to_all(value, axes, 0, 0, tiled=True)  26.3 us
    ppermute x8, starting transfers between devices, passed_along(): lax.ppermute(value, SEQ, [(source, source + steps) for source in range(le...  19.5 us
    ppermute x6, waiting for transfers between devices, swapped(): return lax.ppermute(value, axis, pairs)  15.8 us
  transfers between devices with their start and end apart: 20, of which 7 were waited for; matrix products, arithmetic and copies ran while one was open for 1% of the time, Pallas kernels for 5%

profile of v6, /device:TPU:32, one launch (start us, length us, event | category | flops | bytes accessed | tf_op | source)
XLA Modules:
  0.0 317.3 jit_solution(14865902207162905617)
XLA Ops:
  7.2 3.8 %collective-permute-start = (bf16[128,1024]{1,0:T(8,128)(2,1)}, bf16[128,1024]{1,0:T(8,128)(2,1)S(1)}, u32[]{:S(2)}, u32[]{:S(2)}) collective-permute-start(bf16[128,1024]{1,0:T(8,128)(2,1)} %bitcast.13), channel_id=1, source_target_pairs={{0,1},{1,2},{2,3},{3,4},{4,5},{5,6},{6,7},{7,8},{8,9},{9,10},{10,1... | collective-permute-start | bytes 786440 | tf_op jit(solution)/shard_map/ppermute | solution.py:409
  11.0 2.0 collective-permute-start.1
  13.0 1.8 first.1
  14.8 9.8 %all-to-all-start = ((f32[16,1,2048]{2,1,0:T(1,128)}), f32[16,1,2048]{2,1,0:T(1,128)S(1)}, u32[]{:S(2)}, u32[]{:S(2)}) async-start(f32[16,1,2048]{2,1,0:T(1,128)} %first.1), calls=%async_computation | async-start | bytes 262144 | tf_op jit(solution)/shard_map/all_to_all | solution.py:390
  24.6 0.8 fusion.4
  25.5 0.8 select_reduce_fusion.1
  26.2 0.1 le.37
  26.3 0.1 le.40
  26.4 0.1 reduce_sum.23
  26.5 0.1 lt.37
  26.6 0.1 lt.40
  26.7 0.1 reduce_sum.25
  26.8 6.1 %all-to-all-done.refs_0_ = f32[16,1,2048]{2,1,0:T(1,128)S(1)} async-done(((f32[16,1,2048]{2,1,0:T(1,128)}), f32[16,1,2048]{2,1,0:T(1,128)S(1)}, u32[]{:S(2)}, u32[]{:S(2)}) %all-to-all-start) | async-done | bytes 131104 | tf_op jit(solution)/shard_map/all_to_all | solution.py:390
  32.8 0.7 merge_moments.4
  33.6 7.0 %all-to-all-start.1 = ((f32[16,1,2048]{2,1,0:T(1,128)}), f32[16,1,2048]{2,1,0:T(1,128)S(1)}, u32[]{:S(2)}, u32[]{:S(2)}) async-start(f32[16,1,2048]{2,1,0:T(1,128)} %merge_moments.4), calls=%async_computation.1 | async-start | bytes 262144 | tf_op jit(solution)/shard_map/all_to_all | solution.py:390
  40.7 0.1 copy.27
  40.9 7.7 %all-to-all-done.1.refs_0_ = f32[16,1,2048]{2,1,0:T(1,128)S(1)} async-done(((f32[16,1,2048]{2,1,0:T(1,128)}), f32[16,1,2048]{2,1,0:T(1,128)S(1)}, u32[]{:S(2)}, u32[]{:S(2)}) %all-to-all-start.1) | async-done | bytes 131104 | tf_op jit(solution)/shard_map/all_to_all | solution.py:390
  48.6 3.2 entry.2
  51.8 10.4 %all_to_all.85.refs_0_ = f32[16,1,1024]{2,1,0:T(1,128)S(1)} all-to-all(f32[16,1,1024]{2,1,0:T(1,128)S(1)} %get-tuple-element.53), channel_id=1, replica_groups=mesh['dp'=2,'y'=4,'x'=4,'z'=8] {'dp','z'}, dimensions={0} | all-to-all | bytes 131072 | tf_op jit(solution)/shard_map/all_to_all | solution.py:390
  62.2 10.7 %all_to_all.86.refs_0_ = f32[16,1,1024]{2,1,0:T(1,128)S(1)} all-to-all(f32[16,1,1024]{2,1,0:T(1,128)S(1)} %merge_moments.5), channel_id=1, replica_groups=mesh['dp'=2,'y'=4,'x'=4,'z'=8] {'y','x'}, dimensions={0} | all-to-all | bytes 131072 | tf_op jit(solution)/shard_map/all_to_all | solution.py:390
  73.0 2.0 middle.1
  75.0 2.5 collective-permute-start.2
  77.5 1.3 collective-permute-start.3
  78.8 11.7 %all_to_all.87.refs_0_ = f32[16,1,2048]{2,1,0:T(1,128)S(1)} all-to-all(f32[16,1,2048]{2,1,0:T(1,128)S(1)} %get-tuple-element.55), channel_id=1, replica_groups=mesh['dp'=2,'y'=4,'x'=4,'z'=8] {'dp','z'}, dimensions={0} | all-to-all | bytes 262144 | tf_op jit(solution)/shard_map/all_to_all | solution.py:390
  90.5 0.1 merge_moments.6
  90.6 14.5 %all_to_all.88.refs_0_ = f32[16,1,2048]{2,1,0:T(1,128)S(1)} all-to-all(f32[16,1,2048]{2,1,0:T(1,128)S(1)} %merge_moments.6), channel_id=1, replica_groups=mesh['dp'=2,'y'=4,'x'=4,'z'=8] {'y','x'}, dimensions={0} | all-to-all | bytes 262144 | tf_op jit(solution)/shard_map/all_to_all | solution.py:390
  105.1 3.1 entry.3
  108.2 10.4 %all_to_all.89.refs_0_ = f32[16,1,1024]{2,1,0:T(1,128)S(1)} all-to-all(f32[16,1,1024]{2,1,0:T(1,128)S(1)} %get-tuple-element.57), channel_id=1, replica_groups=mesh['dp'=2,'y'=4,'x'=4,'z'=8] {'dp','z'}, dimensions={0} | all-to-all | bytes 131072 | tf_op jit(solution)/shard_map/all_to_all | solution.py:390
  118.7 10.9 %all_to_all.90.refs_0_ = f32[16,1,1024]{2,1,0:T(1,128)S(1)} all-to-all(f32[16,1,1024]{2,1,0:T(1,128)S(1)} %merge_moments.7), channel_id=1, replica_groups=mesh['dp'=2,'y'=4,'x'=4,'z'=8] {'y','x'}, dimensions={0} | all-to-all | bytes 131072 | tf_op jit(solution)/shard_map/all_to_all | solution.py:390
  129.5 1.7 turn.1
  131.3 2.5 collective-permute-start.4
  133.8 1.3 collective-permute-start.5
  135.1 10.5 %all_to_all.91.refs_0_ = f32[16,1,1024]{2,1,0:T(1,128)S(1)} all-to-all(f32[16,1,1024]{2,1,0:T(1,128)S(1)} %get-tuple-element.61), channel_id=1, replica_groups=mesh['dp'=2,'y'=4,'x'=4,'z'=8] {'dp','z'}, dimensions={0} | all-to-all | bytes 131072 | tf_op jit(solution)/shard_map/all_to_all | solution.py:390
  145.6 14.2 %all_to_all.92.refs_0_ = f32[16,1,1024]{2,1,0:T(1,128)S(1)} all-to-all(f32[16,1,1024]{2,1,0:T(1,128)S(1)} %merge_sums.4), channel_id=1, replica_groups=mesh['dp'=2,'y'=4,'x'=4,'z'=8] {'y','x'}, dimensions={0} | all-to-all | bytes 131072 | tf_op jit(solution)/shard_map/all_to_all | solution.py:390
  159.8 4.0 %back_middle.2 = (bf16[128,1536]{1,0:T(8,128)(2,1)}, f32[128,1024]{1,0:T(8,128)S(1)}, f32[1,512]{1,0:T(1,128)}, f32[1,512]{1,0:T(1,128)}, f32[16,1,2048]{2,1,0:T(1,128)S(1)}) custom-call(f32[16,1,1024]{2,1,0:T(1,128)S(1)} %all_to_all.92.refs_0_, f32[128,512]{1,0:T(8,128)S(1)} %get-tuple-element.63.refs_1_, f32[128,512]{1,0:T(8,128)S(1)} %get-tuple-element.64.refs_2_, ...), custom_call_target="tpu_custom_call" | custom-call | flops 402653184 | bytes 9261056 | tf_op jit(solution)/shard_map/back_middle/pallas_call | solution.py:369
  163.9 11.8 %all_to_all.93.refs_0_ = f32[16,1,2048]{2,1,0:T(1,128)S(1)} all-to-all(f32[16,1,2048]{2,1,0:T(1,128)S(1)} %get-tuple-element.68), channel_id=1, replica_groups=mesh['dp'=2,'y'=4,'x'=4,'z'=8] {'dp','z'}, dimensions={0} | all-to-all | bytes 262144 | tf_op jit(solution)/shard_map/all_to_all | solution.py:390
  175.8 2.3 give.3
  178.1 0.1 collective-permute-start.13
  178.2 11.1 %all_to_all.94.refs_0_ = f32[16,1,2048]{2,1,0:T(1,128)S(1)} all-to-all(f32[16,1,2048]{2,1,0:T(1,128)S(1)} %merge_sums.5.refs_4_), channel_id=1, replica_groups=mesh['dp'=2,'y'=4,'x'=4,'z'=8] {'y','x'}, dimensions={0} | all-to-all | bytes 262144 | tf_op jit(solution)/shard_map/all_to_all | solution.py:390
  189.3 1.3 back_entry.1
  190.6 2.7 collective-permute-start.6
  193.3 3.4 %collective-permute-start.7 = (bf16[128,1024]{1,0:T(8,128)(2,1)S(1)}, bf16[128,1024]{1,0:T(8,128)(2,1)S(1)}, u32[]{:S(2)}, u32[]{:S(2)}) collective-permute-start(bf16[128,1024]{1,0:T(8,128)(2,1)S(1)} %get-tuple-element.73), channel_id=1, source_target_pairs={{1,0},{2,1},{3,2},{4,3},{5,4},{6,5},{7,6},{8,7},{9,8},{10,9},{11,1... | collective-permute-start | bytes 786440 | tf_op jit(solution)/shard_map/ppermute | solution.py:409
  196.6 11.6 %all_to_all.95.refs_0_ = f32[16,1,1024]{2,1,0:T(1,128)S(1)} all-to-all(f32[16,1,1024]{2,1,0:T(1,128)S(1)} %get-tuple-element.72), channel_id=1, replica_groups=mesh['dp'=2,'y'=4,'x'=4,'z'=8] {'dp','z'}, dimensions={0} | all-to-all | bytes 131072 | tf_op jit(solution)/shard_map/all_to_all | solution.py:390
  208.3 3.7 %keep.3 = bf16[1024,1024]{1,0:T(8,128)(2,1)} custom-call(bf16[1024,1024]{1,0:T(8,128)(2,1)S(1)} %collective-permute-done.13.refs_0_, bf16[128,1024]{1,0:T(8,128)(2,1)} %get-tuple-element.89.refs_0_.refs_1_, bf16[128,1536]{1,0:T(8,128)(2,1)} %get-tuple-element.90.refs_1_.refs_2_, bf16[128,1024]{1,0:T(8,128)(2,1)} %bitcast.21, ...), custom_call_target="tpu_custom_call" | custom-call | flops 268435456 | bytes 5242880 | tf_op jit(solution)/shard_map/keep/pallas_call | solution.py:369
  212.0 12.5 %all_to_all.96.refs_0_ = f32[16,1,1024]{2,1,0:T(1,128)S(1)} all-to-all(f32[16,1,1024]{2,1,0:T(1,128)S(1)} %merge_sums.6.refs_5_), channel_id=1, replica_groups=mesh['dp'=2,'y'=4,'x'=4,'z'=8] {'y','x'}, dimensions={0} | all-to-all | bytes 131072 | tf_op jit(solution)/shard_map/all_to_all | solution.py:390
  224.6 4.1 %back_middle.3 = (bf16[128,1536]{1,0:T(8,128)(2,1)}, f32[128,1024]{1,0:T(8,128)S(1)}, f32[2,512]{1,0:T(2,128)}, f32[2,512]{1,0:T(2,128)}, f32[16,1,2048]{2,1,0:T(1,128)S(1)}) custom-call(f32[16,1,1024]{2,1,0:T(1,128)S(1)} %all_to_all.96.refs_0_, f32[128,512]{1,0:T(8,128)S(1)} %get-tuple-element.74.refs_1_, f32[128,512]{1,0:T(8,128)S(1)} %copy-done.6, ...), custom_call_target="tpu_custom_call" | custom-call | flops 402653184 | bytes 9269248 | tf_op jit(solution)/shard_map/back_middle/pallas_call | solution.py:369
  228.7 2.3 give.2
  231.0 0.1 collective-permute-start.12
  231.1 12.0 %all_to_all.97.refs_0_ = f32[16,1,2048]{2,1,0:T(1,128)S(1)} all-to-all(f32[16,1,2048]{2,1,0:T(1,128)S(1)} %get-tuple-element.80), channel_id=1, replica_groups=mesh['dp'=2,'y'=4,'x'=4,'z'=8] {'dp','z'}, dimensions={0} | all-to-all | bytes 262144 | tf_op jit(solution)/shard_map/all_to_all | solution.py:390
  243.1 3.7 %keep.2.refs_1_ = bf16[1024,1024]{1,0:T(8,128)(2,1)} custom-call(bf16[1024,1024]{1,0:T(8,128)(2,1)S(1)} %collective-permute-done.12.refs_0_, bf16[128,1024]{1,0:T(8,128)(2,1)} %get-tuple-element.86.refs_0_.refs_1_, bf16[128,1536]{1,0:T(8,128)(2,1)} %get-tuple-element.87.refs_1_.refs_2_, bf16[128,1024]{1,0:T(8,128)(2,1)} %get-tuple-element.82.refs_5_.refs_2_.refs_3_, ...), custom_call_target="tpu_custom_call" | custom-call | flops 268435456 | bytes 5242880 | tf_op jit(solution)/shard_map/keep/pallas_call | solution.py:369
  246.8 3.7 %all-to-all-start.15 = ((bf16[16,64,1024]{2,1,0:T(8,128)(2,1)}), bf16[16,64,1024]{2,1,0:T(8,128)(2,1)S(1)}, u32[]{:S(2)}, u32[]{:S(2)}) async-start(bf16[16,64,1024]{2,1,0:T(8,128)(2,1)} %bitcast.24), calls=%async_computation.15 | async-start | bytes 4194304 | tf_op jit(solution)/shard_map/all_to_all | solution.py:390
  250.6 1.9 pass.1
  252.6 30.3 %all-to-all-done.15.refs_0_ = bf16[16,64,1024]{2,1,0:T(8,128)(2,1)S(1)} async-done(((bf16[16,64,1024]{2,1,0:T(8,128)(2,1)}), bf16[16,64,1024]{2,1,0:T(8,128)(2,1)S(1)}, u32[]{:S(2)}, u32[]{:S(2)}) %all-to-all-start.15) | async-done | bytes 2097184 | tf_op jit(solution)/shard_map/all_to_all | solution.py:390
  282.9 2.0 gather_rows.1
  284.9 5.8 %all-to-all-start.16 = ((bf16[16,8,2048]{2,1,0:T(8,128)(2,1)}), bf16[16,8,2048]{2,1,0:T(8,128)(2,1)S(1)}, u32[]{:S(2)}, u32[]{:S(2)}) async-start(bf16[16,8,2048]{2,1,0:T(8,128)(2,1)} %gather_rows.1), calls=%async_computation.18 | async-start | bytes 1048576 | tf_op jit(solution)/shard_map/all_to_all | solution.py:390
  290.7 3.6 %collective-permute-done.8 = f32[1,2048]{1,0:T(1,128)S(1)} collective-permute-done((f32[1,2048]{1,0:T(1,128)S(1)}, f32[1,2048]{1,0:T(1,128)S(1)}, u32[]{:S(2)}, u32[]{:S(2)}) %collective-permute-start.8) | collective-permute-done | bytes 8224 | tf_op jit(solution)/shard_map/ppermute | solution.py:450
  294.3 0.1 collective-permute-start.9
  294.4 5.1 %collective-permute-done.9 = f32[1,2048]{1,0:T(1,128)S(1)} collective-permute-done((f32[1,2048]{1,0:T(1,128)S(1)}, f32[1,2048]{1,0:T(1,128)S(1)}, u32[]{:S(2)}, u32[]{:S(2)}) %collective-permute-start.9) | collective-permute-done | bytes 8224 | tf_op jit(solution)/shard_map/ppermute | solution.py:450
  299.6 0.6 collective-permute-start.10
  300.2 3.1 collective-permute-done.10
  303.3 1.3 collective-permute-start.11
  304.7 3.9 %collective-permute-done.11 = f32[1,2048]{1,0:T(1,128)S(1)} collective-permute-done((f32[1,2048]{1,0:T(1,128)S(1)}, f32[1,2048]{1,0:T(1,128)S(1)}, u32[]{:S(2)}, u32[]{:S(2)}) %collective-permute-start.11) | collective-permute-done | bytes 8224 | tf_op jit(solution)/shard_map/ppermute | solution.py:450
  308.6 1.1 last.1
  309.8 0.7 rows.1
  (80 shorter events, 0.7 us)
Async XLA Ops:
  7.2 25.7 %collective-permute-start = (bf16[128,1024]{1,0:T(8,128)(2,1)}, bf16[128,1024]{1,0:T(8,128)(2,1)S(1)}, u32[]{:S(2)}, u32[]{:S(2)}) collective-permute-start(bf16[128,1024]{1,0:T(8,128)(2,1)} %bitcast.13), channel_id=1, source_target_pairs={{0,1},{1,2},{2,3},{3,4},{4,5},{5,6},{6,7},{7,8},{8,9},{9,10},{10,1... | collective-permute-start | bytes 786440 | tf_op jit(solution)/shard_map/ppermute | solution.py:409
  11.0 21.8 %collective-permute-start.1 = (bf16[128,1024]{1,0:T(8,128)(2,1)}, bf16[128,1024]{1,0:T(8,128)(2,1)S(1)}, u32[]{:S(2)}, u32[]{:S(2)}) collective-permute-start(bf16[128,1024]{1,0:T(8,128)(2,1)} %bitcast.14), channel_id=1, source_target_pairs={{1,0},{2,1},{3,2},{4,3},{5,4},{6,5},{7,6},{8,7},{9,8},{10,9},{11,1... | collective-permute-start | bytes 786440 | tf_op jit(solution)/shard_map/ppermute | solution.py:409
  14.8 18.0 %all-to-all-start = ((f32[16,1,2048]{2,1,0:T(1,128)}), f32[16,1,2048]{2,1,0:T(1,128)S(1)}, u32[]{:S(2)}, u32[]{:S(2)}) async-start(f32[16,1,2048]{2,1,0:T(1,128)} %first.1), calls=%async_computation | async-start | bytes 262144 | tf_op jit(solution)/shard_map/all_to_all | solution.py:390
  33.6 15.0 %all-to-all-start.1 = ((f32[16,1,2048]{2,1,0:T(1,128)}), f32[16,1,2048]{2,1,0:T(1,128)S(1)}, u32[]{:S(2)}, u32[]{:S(2)}) async-start(f32[16,1,2048]{2,1,0:T(1,128)} %merge_moments.4), calls=%async_computation.1 | async-start | bytes 262144 | tf_op jit(solution)/shard_map/all_to_all | solution.py:390
  40.6 210.0 %reduce-scatter.3.cloned.1.call-start = ((), (), s32[]{:S(2)}) async-start(), calls=%async_computation.19 | async-start | bytes 2621440 | tf_op jit(solution)/shard_map/reduce_scatter | solution.py:454
  40.9 32.1 %copy-start = (bf16[2,1024,512]{2,1,0:T(8,128)(2,1)S(1)}, bf16[2,1024,512]{2,1,0:T(8,128)(2,1)}, u32[]{:S(2)}) copy-start(bf16[2,1024,512]{2,1,0:T(8,128)(2,1)} %refs_6_.5) | copy-start | bytes 6291460
  40.9 32.1 %copy-start.1 = (bf16[2,64,1024]{2,1,0:T(8,128)(2,1)S(1)}, bf16[2,64,1024]{2,1,0:T(8,128)(2,1)}, u32[]{:S(2)}) copy-start(bf16[2,64,1024]{2,1,0:T(8,128)(2,1)} %param.10) | copy-start | bytes 786436
  40.9 32.1 %copy-start.11 = (f32[2,512]{1,0:T(2,128)S(1)}, f32[2,512]{1,0:T(2,128)}, u32[]{:S(2)}) copy-start(f32[2,512]{1,0:T(2,128)} %refs_7_.7) | copy-start | bytes 12292
  40.9 32.1 %copy-start.15 = (f32[2,512]{1,0:T(2,128)S(1)}, f32[2,512]{1,0:T(2,128)}, u32[]{:S(2)}) copy-start(f32[2,512]{1,0:T(2,128)} %refs_3_.3) | copy-start | bytes 12292
  62.2 42.9 %copy-start.10 = (f32[2,1024]{1,0:T(2,128)S(1)}, f32[2,1024]{1,0:T(2,128)}, u32[]{:S(2)}) copy-start(f32[2,1024]{1,0:T(2,128)} %refs_4_.7) | copy-start | bytes 24580
  62.2 42.9 %copy-start.12 = (f32[2,1024]{1,0:T(2,128)S(1)}, f32[2,1024]{1,0:T(2,128)}, u32[]{:S(2)}) copy-start(f32[2,1024]{1,0:T(2,128)} %refs_7_.5) | copy-start | bytes 24580
  75.0 15.5 %collective-permute-start.2 = (bf16[128,1024]{1,0:T(8,128)(2,1)S(1)}, bf16[128,1024]{1,0:T(8,128)(2,1)S(1)}, u32[]{:S(2)}, u32[]{:S(2)}) collective-permute-start(bf16[128,1024]{1,0:T(8,128)(2,1)S(1)} %get-tuple-element.56.refs_1_), channel_id=1, source_target_pairs={{0,8},{1,9},{2,10},{3,11},{4,12},{5,13},{6,14},{7,15},{8,16},{9,17... | collective-permute-start | bytes 786440 | tf_op jit(solution)/shard_map/ppermute | solution.py:409
  77.5 13.0 %collective-permute-start.3 = (bf16[128,1024]{1,0:T(8,128)(2,1)S(1)}, bf16[128,1024]{1,0:T(8,128)(2,1)S(1)}, u32[]{:S(2)}, u32[]{:S(2)}) collective-permute-start(bf16[128,1024]{1,0:T(8,128)(2,1)S(1)} %get-tuple-element.56.refs_1_), channel_id=1, source_target_pairs={{8,0},{9,1},{10,2},{11,3},{12,4},{13,5},{14,6},{15,7},{16,8},{17,9... | collective-permute-start | bytes 786440 | tf_op jit(solution)/shard_map/ppermute | solution.py:409
  105.1 24.4 %copy-start.2 = (bf16[2,64,1024]{2,1,0:T(8,128)(2,1)S(1)}, bf16[2,64,1024]{2,1,0:T(8,128)(2,1)}, u32[]{:S(2)}) copy-start(bf16[2,64,1024]{2,1,0:T(8,128)(2,1)} %param.19) | copy-start | bytes 786436
  105.1 24.4 %copy-start.5 = (bf16[128,1024]{1,0:T(8,128)(2,1)S(1)}, bf16[128,1024]{1,0:T(8,128)(2,1)}, u32[]{:S(2)}) copy-start(bf16[128,1024]{1,0:T(8,128)(2,1)} %get-tuple-element.59.refs_5_.refs_10_.refs_2_) | copy-start | bytes 786436
  118.6 41.2 %copy-start.8 = (f32[128,1024]{1,0:T(8,128)S(1)}, f32[128,1024]{1,0:T(8,128)}, u32[]{:S(2)}) copy-start(f32[128,1024]{1,0:T(8,128)} %get-tuple-element.66.refs_9_) | copy-start | bytes 1572868
  118.6 41.2 %copy-start.14 = (f32[2,1024]{1,0:T(2,128)S(1)}, f32[2,1024]{1,0:T(2,128)}, u32[]{:S(2)}) copy-start(f32[2,1024]{1,0:T(2,128)} %get-tuple-element.67.refs_11_.refs_3_) | copy-start | bytes 24580
  131.3 14.3 %collective-permute-start.4 = (bf16[128,1024]{1,0:T(8,128)(2,1)S(1)}, bf16[128,1024]{1,0:T(8,128)(2,1)S(1)}, u32[]{:S(2)}, u32[]{:S(2)}) collective-permute-start(bf16[128,1024]{1,0:T(8,128)(2,1)S(1)} %get-tuple-element.62), channel_id=1, source_target_pairs={{0,8},{1,9},{2,10},{3,11},{4,12},{5,13},{6,14},{7,15},{8,16},{9,17... | collective-permute-start | bytes 786440 | tf_op jit(solution)/shard_map/ppermute | solution.py:409
  133.8 11.8 %collective-permute-start.5 = (bf16[128,1024]{1,0:T(8,128)(2,1)S(1)}, bf16[128,1024]{1,0:T(8,128)(2,1)S(1)}, u32[]{:S(2)}, u32[]{:S(2)}) collective-permute-start(bf16[128,1024]{1,0:T(8,128)(2,1)S(1)} %get-tuple-element.62), channel_id=1, source_target_pairs={{8,0},{9,1},{10,2},{11,3},{12,4},{13,5},{14,6},{15,7},{16,8},{17,9... | collective-permute-start | bytes 786440 | tf_op jit(solution)/shard_map/ppermute | solution.py:409
  163.8 25.5 %copy-start.3 = (bf16[2,64,1024]{2,1,0:T(8,128)(2,1)S(1)}, bf16[2,64,1024]{2,1,0:T(8,128)(2,1)}, u32[]{:S(2)}) copy-start(bf16[2,64,1024]{2,1,0:T(8,128)(2,1)} %param.19) | copy-start | bytes 786436
  163.8 25.5 %copy-start.6 = (f32[128,512]{1,0:T(8,128)S(1)}, f32[128,512]{1,0:T(8,128)}, u32[]{:S(2)}) copy-start(f32[128,512]{1,0:T(8,128)} %get-tuple-element.71.refs_8_.refs_2_) | copy-start | bytes 786436
  163.9 25.4 %copy-start.9 = (f32[128,512]{1,0:T(8,128)S(1)}, f32[128,512]{1,0:T(8,128)}, u32[]{:S(2)}) copy-start(f32[128,512]{1,0:T(8,128)} %get-tuple-element.70.refs_7_) | copy-start | bytes 786436
  178.1 30.2 %collective-permute-start.13 = (bf16[1024,1024]{1,0:T(8,128)(2,1)S(1)}, bf16[1024,1024]{1,0:T(8,128)(2,1)S(1)}, u32[]{:S(2)}, u32[]{:S(2)}) collective-permute-start(bf16[1024,1024]{1,0:T(8,128)(2,1)S(1)} %give.3), channel_id=1, source_target_pairs={{0,128},{128,0},{1,129},{129,1},{2,130},{130,2},{3,131},{131,3},{4... | collective-permute-start | bytes 6291464 | tf_op jit(solution)/shard_map/ppermute | solution.py:450
  190.6 17.6 %collective-permute-start.6 = (bf16[128,1024]{1,0:T(8,128)(2,1)S(1)}, bf16[128,1024]{1,0:T(8,128)(2,1)S(1)}, u32[]{:S(2)}, u32[]{:S(2)}) collective-permute-start(bf16[128,1024]{1,0:T(8,128)(2,1)S(1)} %get-tuple-element.73), channel_id=1, source_target_pairs={{0,1},{1,2},{2,3},{3,4},{4,5},{5,6},{6,7},{7,8},{8,9},{9,10},{10,1... | collective-permute-start | bytes 786440 | tf_op jit(solution)/shard_map/ppermute | solution.py:409
  193.3 14.9 %collective-permute-start.7 = (bf16[128,1024]{1,0:T(8,128)(2,1)S(1)}, bf16[128,1024]{1,0:T(8,128)(2,1)S(1)}, u32[]{:S(2)}, u32[]{:S(2)}) collective-permute-start(bf16[128,1024]{1,0:T(8,128)(2,1)S(1)} %get-tuple-element.73), channel_id=1, source_target_pairs={{1,0},{2,1},{3,2},{4,3},{5,4},{6,5},{7,6},{8,7},{9,8},{10,9},{11,1... | collective-permute-start | bytes 786440 | tf_op jit(solution)/shard_map/ppermute | solution.py:409
  211.9 12.6 %copy-start.7 = (f32[128,1024]{1,0:T(8,128)S(1)}, f32[128,1024]{1,0:T(8,128)}, u32[]{:S(2)}) copy-start(f32[128,1024]{1,0:T(8,128)} %get-tuple-element.76.refs_9_) | copy-start | bytes 1572868
  212.0 12.6 %copy-start.13 = (f32[2,1024]{1,0:T(2,128)S(1)}, f32[2,1024]{1,0:T(2,128)}, u32[]{:S(2)}) copy-start(f32[2,1024]{1,0:T(2,128)} %get-tuple-element.77.refs_11_.refs_3_) | copy-start | bytes 24580
  212.0 12.6 %copy-start.18 = (f32[1,512]{1,0:T(1,128)S(1)}, f32[1,512]{1,0:T(1,128)}, u32[]{:S(2)}) copy-start(f32[1,512]{1,0:T(1,128)} %get-tuple-element.75.refs_3_) | copy-start | bytes 6148
  212.0 12.6 %copy-start.19 = (f32[1,512]{1,0:T(1,128)S(1)}, f32[1,512]{1,0:T(1,128)}, u32[]{:S(2)}) copy-start(f32[1,512]{1,0:T(1,128)} %get-tuple-element.78.refs_12_) | copy-start | bytes 6148
  212.0 12.6 %copy-start.20 = (f32[1,512]{1,0:T(1,128)S(1)}, f32[1,512]{1,0:T(1,128)}, u32[]{:S(2)}) copy-start(f32[1,512]{1,0:T(1,128)} %get-tuple-element.79.refs_13_) | copy-start | bytes 6148
  231.0 12.1 %collective-permute-start.12 = (bf16[1024,1024]{1,0:T(8,128)(2,1)S(1)}, bf16[1024,1024]{1,0:T(8,128)(2,1)S(1)}, u32[]{:S(2)}, u32[]{:S(2)}) collective-permute-start(bf16[1024,1024]{1,0:T(8,128)(2,1)S(1)} %give.2), channel_id=1, source_target_pairs={{0,128},{128,0},{1,129},{129,1},{2,130},{130,2},{3,131},{131,3},{4... | collective-permute-start | bytes 6291464 | tf_op jit(solution)/shard_map/ppermute | solution.py:450
  246.8 36.1 %all-to-all-start.15 = ((bf16[16,64,1024]{2,1,0:T(8,128)(2,1)}), bf16[16,64,1024]{2,1,0:T(8,128)(2,1)S(1)}, u32[]{:S(2)}, u32[]{:S(2)}) async-start(bf16[16,64,1024]{2,1,0:T(8,128)(2,1)} %bitcast.24), calls=%async_computation.15 | async-start | bytes 4194304 | tf_op jit(solution)/shard_map/all_to_all | solution.py:390
  250.5 32.4 %reduce-scatter.5.cloned.1.call-start = ((), (), s32[]{:S(2)}) async-start(), calls=%async_computation.20 | async-start | bytes 655360 | tf_op jit(solution)/shard_map/reduce_scatter | solution.py:454
  252.5 56.1 %copy-start.4 = (bf16[128,1024]{1,0:T(8,128)(2,1)S(1)}, bf16[128,1024]{1,0:T(8,128)(2,1)}, u32[]{:S(2)}) copy-start(bf16[128,1024]{1,0:T(8,128)(2,1)} %get-tuple-element.82.refs_5_.refs_2_.refs_3_) | copy-start | bytes 786436
  252.5 56.1 %copy-start.16 = (f32[1,1024]{1,0:T(1,128)S(1)}, f32[1,1024]{1,0:T(1,128)}, u32[]{:S(2)}) copy-start(f32[1,1024]{1,0:T(1,128)} %get-tuple-element.83.refs_6_) | copy-start | bytes 12292
  252.5 56.1 %copy-start.17 = (f32[1,1024]{1,0:T(1,128)S(1)}, f32[1,1024]{1,0:T(1,128)}, u32[]{:S(2)}) copy-start(f32[1,1024]{1,0:T(1,128)} %get-tuple-element.84.refs_7_) | copy-start | bytes 12292
  284.9 24.9 %all-to-all-start.16 = ((bf16[16,8,2048]{2,1,0:T(8,128)(2,1)}), bf16[16,8,2048]{2,1,0:T(8,128)(2,1)S(1)}, u32[]{:S(2)}, u32[]{:S(2)}) async-start(bf16[16,8,2048]{2,1,0:T(8,128)(2,1)} %gather_rows.1), calls=%async_computation.18 | async-start | bytes 1048576 | tf_op jit(solution)/shard_map/all_to_all | solution.py:390
  290.6 3.7 %collective-permute-start.8 = (f32[1,2048]{1,0:T(1,128)S(1)}, f32[1,2048]{1,0:T(1,128)S(1)}, u32[]{:S(2)}, u32[]{:S(2)}) collective-permute-start(f32[1,2048]{1,0:T(1,128)S(1)} %merge_sums.7.refs_5_), channel_id=1, source_target_pairs={{0,8},{8,0},{16,24},{24,16},{1,9},{9,1},{17,25},{25,17},{2,10},{10... | collective-permute-start | bytes 24584 | tf_op jit(solution)/shard_map/ppermute | solution.py:450
  294.3 5.2 %collective-permute-start.9 = (f32[1,2048]{1,0:T(1,128)S(1)}, f32[1,2048]{1,0:T(1,128)S(1)}, u32[]{:S(2)}, u32[]{:S(2)}) collective-permute-start(f32[1,2048]{1,0:T(1,128)S(1)} %add.76), channel_id=1, source_target_pairs={{0,16},{8,24},{16,0},{24,8},{1,17},{9,25},{17,1},{25,9},{2,18},{10... | collective-permute-start | bytes 24584 | tf_op jit(solution)/shard_map/ppermute | solution.py:450
  299.6 3.7 %collective-permute-start.10 = (f32[1,2048]{1,0:T(1,128)S(1)}, f32[1,2048]{1,0:T(1,128)S(1)}, u32[]{:S(2)}, u32[]{:S(2)}) collective-permute-start(f32[1,2048]{1,0:T(1,128)S(1)} %add.77), channel_id=1, source_target_pairs={{0,32},{32,0},{64,96},{96,64},{1,33},{33,1},{65,97},{97,65},{2,34}... | collective-permute-start | bytes 24584 | tf_op jit(solution)/shard_map/ppermute | solution.py:450
  303.3 5.2 %collective-permute-start.11 = (f32[1,2048]{1,0:T(1,128)S(1)}, f32[1,2048]{1,0:T(1,128)S(1)}, u32[]{:S(2)}, u32[]{:S(2)}) collective-permute-start(f32[1,2048]{1,0:T(1,128)S(1)} %add.78), channel_id=1, source_target_pairs={{0,64},{32,96},{64,0},{96,32},{1,65},{33,97},{65,1},{97,33},{2,66}... | collective-permute-start | bytes 24584 | tf_op jit(solution)/shard_map/ppermute | solution.py:450
Sparse Core Ops, SparseCore 0:
  212.2 28.4 reduce-scatter.2
  254.1 24.8 reduce-scatter.4

commit v7 on v6

--- a/solution.py
+++ b/solution.py
@@ -38,7 +38,7 @@
 
 def spread_out(out, first, second):
     row = jnp.concatenate([first, second], axis=1)
-    for i in range(GROUP):
+    for i in range(out.shape[0]):
         out[i] = row
 
 
@@ -83,13 +83,9 @@
     spread_out(out, *local_moments(x[...].astype(F32)))
 
 
-def k_merge(kind, parts, *rest):
-    out = rest[-1]
+def k_merge(kind, parts, out):
     merge = merged_moments if kind == "moments" else merged_sums
-    if out.shape[0] == 1:
-        out[...] = jnp.concatenate(merge(parts), axis=1)
-    else:
-        spread_out(out, *merge(parts))
+    spread_out(out, *merge(parts))
 
 
 def k_entry(layer, parts, x, lower, upper, masks, weight, gains, biases, taps, slope, conv, stat, out):
@@ -194,7 +190,7 @@
 
 def back_entry(layer, parts, grad_in, x, stat, gains, upstream):
     if layer == 0:
-        total, cross = parts[:, :CH], parts[:, CH:]
+        total, cross = parts[0, :, :CH], parts[0, :, CH:]
     else:
         total, cross = merged_sums(parts)
     factor = stat[1:2]
@@ -269,6 +265,11 @@
             first = layer * CH
             kernel_out[layer, :, d * cut : (d + 1) * cut] = total[:, first : first + cut]
             project_out[layer, :, d * width : (d + 1) * width] = total[:, first + cut : first + CH]
+
+
+def k_merge_first(parts, x, out, sent):
+    sent[...] = x[...]
+    spread_out(out, *merged_moments(parts))
 
 
 def k_pass(value, out):
@@ -502,9 +503,18 @@
             flops=conv_flops,
         )
 
-    sides = neighbours(stream_0, FIRST_DILATION)
     (payload,) = call(k_first, [(wide, F32)], stream_0, loaded=(0,), name="first")
-    parts, _ = over_all(payload, "moments", sides)
+    merged, sent = call(
+        k_merge_first,
+        [(wide, F32), ((ROWS, CH), BF16)],
+        exchange(payload, FIRST_STAGE),
+        stream_0,
+        loaded=(1,),
+        free=(1,),
+        name="merge_moments",
+    )
+    sides = neighbours(sent, FIRST_DILATION)
+    parts = exchange(merged, SECOND_STAGE)
     taps_0, slope_0, conv_0, stat_0, payload = entry(0, stream_0, parts, sides)
     parts, _ = over_all(payload, "moments")
     hidden_0, stream_1, kept_1, slope_mid_0, normed_0, factor_0, payload = call(
@@ -570,7 +580,7 @@
                 ((ROWS, CH), F32),
                 ((rows, HALF), F32),
                 ((rows, HALF), F32),
-                (wide, F32),
+                (wide if layer else (1, 1, 2 * CH), F32),
             ],
             parts,
             grad,
@@ -643,13 +653,13 @@
         gain_mid,
         bias_mid,
     )
-    (sums,) = call(
-        functools.partial(k_merge, "sums"),
-        [((1, 2 * CH), F32)],
-        exchange(payload, FIRST_STAGE),
-        name="merge_sums",
-    )
-    share_0 = chip_share((taps_0, three_0), (grad_1, hidden_0), waits=(sums,))
+    share_0 = chip_share((taps_0, three_0), (grad_1, hidden_0))
+    (sums,) = call(k_pass, [(payload.shape, F32)], payload, held=(share_0,), name="pass_sums")
+    for axis, step in (("dp", 1), ("z", 1), ("z", 2), ("z", 4)):
+        sums = sums + swapped(sums, axis, step)
+    near = sums
+    for axis, step in (("x", 1), ("x", 2), ("y", 1), ("y", 2)):
+        sums = sums + swapped(sums, axis, step)
     (rows_1,) = call(
         k_pass,
         [(rows_1.shape, BF16)],
@@ -661,9 +671,6 @@
     )
     rows_1 = rows_over(rows_1, "x")
     share_0 = exchange(share_0.reshape(GROUP, CH // GROUP, CH), SECOND_STAGE)
-    for axis in ("x", "y"):
-        for step in (1, 2):
-            sums = sums + swapped(sums, axis, step)
     grad_gains_in, grad_biases_in, grad_0 = call(
         k_last,
         [((2, CH), F32), ((2, CH), F32), ((ROWS, CH), BF16)],
@@ -686,6 +693,7 @@
         share_0,
         rows_1,
         loaded=(1,),
+        waits=(near,),
         name="gather_rows",
     )
     grad_conv, grad_proj = call(

time: 319 us -> 314 us (0.984)
  blocking collectives: 152 us -> 142 us
    ppermute x6 -> x10, waiting for transfers between devices: 15.8 us -> 33 us  [swapped(): return lax.ppermute(value, axis, pairs)]
    all_to_all x4, waiting for transfers between devices: 44.1 us -> 28.9 us  [exchange(): return lax.all_to_all(value, axes, 0, 0, tiled=True)]
    all_to_all x13 -> x12, blocking collectives: 152 us -> 142 us  [exchange(): return lax.all_to_all(value, axes, 0, 0, tiled=True)]
    ppermute x6 -> x10, starting transfers between devices: 2.21 us -> 6.46 us  [swapped(): return lax.ppermute(value, axis, pairs)]
  transfers between devices with their start and end apart: 20 -> 24, of which waited for: 7 -> 12; matrix products, arithmetic and copies ran while one was open for 1% -> 1% of each run, Pallas kernels for 5% -> 5%
where the time goes in v7:
time: 314 us; the launch traced here: 312 us
  blocking collectives  142 us (45%)
  waiting for transfers between devices  62 us (20%)
  starting transfers between devices  50.4 us (16%)
  Pallas kernels  39.8 us (13%)
  between operations  14.7 us (5%)
    all_to_all x12, blocking collectives, exchange(): return lax.all_to_all(value, axes, 0, 0, tiled=True)  142 us
    pallas_call x24, Pallas kernels, call(): pl.pallas_call(body, grid=(1,), in_specs=specs, out_specs=[in_hbm if i in...  39.8 us
    ppermute x10, waiting for transfers between devices, swapped(): return lax.ppermute(value, axis, pairs)  33 us
    all_to_all x4, waiting for transfers between devices, exchange(): return lax.all_to_all(value, axes, 0, 0, tiled=True)  28.9 us
    all_to_all x4, starting transfers between devices, exchange(): return lax.all_to_all(value, axes, 0, 0, tiled=True)  24.4 us
    ppermute x8, starting transfers between devices, passed_along(): lax.ppermute(value, SEQ, [(source, source + steps) for source in range(le...  19.4 us
    ppermute x10, starting transfers between devices, swapped(): return lax.ppermute(value, axis, pairs)  6.46 us
  transfers between devices with their start and end apart: 24, of which 12 were waited for; matrix products, arithmetic and copies ran while one was open for 1% of the time, Pallas kernels for 5%

profile of v7, /device:TPU:32, one launch (start us, length us, event | category | flops | bytes accessed | tf_op | source)
XLA Modules:
  0.0 312.1 jit_solution(15087073892326774356)
XLA Ops:
  7.2 1.8 first.1
  8.9 8.6 %all-to-all-start = ((f32[16,1,2048]{2,1,0:T(1,128)}), f32[16,1,2048]{2,1,0:T(1,128)S(1)}, u32[]{:S(2)}, u32[]{:S(2)}) async-start(f32[16,1,2048]{2,1,0:T(1,128)} %first.1), calls=%async_computation | async-start | bytes 262144 | tf_op jit(solution)/shard_map/all_to_all | solution.py:391
  17.5 0.8 fusion.4
  18.4 0.8 select_reduce_fusion.1
  19.7 6.1 %all-to-all-done.refs_0_ = f32[16,1,2048]{2,1,0:T(1,128)S(1)} async-done(((f32[16,1,2048]{2,1,0:T(1,128)}), f32[16,1,2048]{2,1,0:T(1,128)S(1)}, u32[]{:S(2)}, u32[]{:S(2)}) %all-to-all-start) | async-done | bytes 131104 | tf_op jit(solution)/shard_map/all_to_all | solution.py:391
  25.8 0.9 copy-done.1
  26.7 0.7 merge_moments.4
  27.4 2.7 collective-permute-start
  30.1 3.2 %collective-permute-start.1 = (bf16[128,1024]{1,0:T(8,128)(2,1)S(1)}, bf16[128,1024]{1,0:T(8,128)(2,1)S(1)}, u32[]{:S(2)}, u32[]{:S(2)}) collective-permute-start(bf16[128,1024]{1,0:T(8,128)(2,1)S(1)} %get-tuple-element.56), channel_id=1, source_target_pairs={{1,0},{2,1},{3,2},{4,3},{5,4},{6,5},{7,6},{8,7},{9,8},{10,9},{11,1... | collective-permute-start | bytes 786440 | tf_op jit(solution)/shard_map/ppermute | solution.py:410
  33.3 7.0 %all-to-all-start.1 = ((f32[16,1,2048]{2,1,0:T(1,128)}), f32[16,1,2048]{2,1,0:T(1,128)S(1)}, u32[]{:S(2)}, u32[]{:S(2)}) async-start(f32[16,1,2048]{2,1,0:T(1,128)} %get-tuple-element.55), calls=%async_computation.1 | async-start | bytes 262144 | tf_op jit(solution)/shard_map/all_to_all | solution.py:391
  40.4 0.1 copy.27
  40.6 7.7 %all-to-all-done.1.refs_0_ = f32[16,1,2048]{2,1,0:T(1,128)S(1)} async-done(((f32[16,1,2048]{2,1,0:T(1,128)}), f32[16,1,2048]{2,1,0:T(1,128)S(1)}, u32[]{:S(2)}, u32[]{:S(2)}) %all-to-all-start.1) | async-done | bytes 131104 | tf_op jit(solution)/shard_map/all_to_all | solution.py:391
  48.4 3.2 %entry.2 = (bf16[128,1024]{1,0:T(8,128)(2,1)}, f32[128,1024]{1,0:T(8,128)}, f32[128,512]{1,0:T(8,128)S(1)}, f32[2,1024]{1,0:T(2,128)}, f32[16,1,1024]{2,1,0:T(1,128)S(1)}) custom-call(f32[16,1,2048]{2,1,0:T(1,128)S(1)} %all-to-all-done.1.refs_0_, bf16[128,1024]{1,0:T(8,128)(2,1)} %bitcast.14, bf16[128,1024]{1,0:T(8,128)(2,1)S(1)} %collective-permute-done.refs_2_, ...), custom_call_target="tpu_custom_call" | custom-call | flops 402653184 | bytes 8349696 | tf_op jit(solution)/shard_map/entry/pallas_call | solution.py:370
  51.5 11.9 %all_to_all.80.refs_0_ = f32[16,1,1024]{2,1,0:T(1,128)S(1)} all-to-all(f32[16,1,1024]{2,1,0:T(1,128)S(1)} %get-tuple-element.57), channel_id=1, replica_groups=mesh['dp'=2,'y'=4,'x'=4,'z'=8] {'dp','z'}, dimensions={0} | all-to-all | bytes 131072 | tf_op jit(solution)/shard_map/all_to_all | solution.py:391
  63.5 10.7 %all_to_all.81.refs_0_ = f32[16,1,1024]{2,1,0:T(1,128)S(1)} all-to-all(f32[16,1,1024]{2,1,0:T(1,128)S(1)} %merge_moments.5), channel_id=1, replica_groups=mesh['dp'=2,'y'=4,'x'=4,'z'=8] {'y','x'}, dimensions={0} | all-to-all | bytes 131072 | tf_op jit(solution)/shard_map/all_to_all | solution.py:391
  74.3 2.0 middle.1
  76.2 2.5 collective-permute-start.2
  78.7 1.3 collective-permute-start.3
  80.0 11.7 %all_to_all.82.refs_0_ = f32[16,1,2048]{2,1,0:T(1,128)S(1)} all-to-all(f32[16,1,2048]{2,1,0:T(1,128)S(1)} %get-tuple-element.59), channel_id=1, replica_groups=mesh['dp'=2,'y'=4,'x'=4,'z'=8] {'dp','z'}, dimensions={0} | all-to-all | bytes 262144 | tf_op jit(solution)/shard_map/all_to_all | solution.py:391
  91.8 14.5 %all_to_all.83.refs_0_ = f32[16,1,2048]{2,1,0:T(1,128)S(1)} all-to-all(f32[16,1,2048]{2,1,0:T(1,128)S(1)} %merge_moments.6), channel_id=1, replica_groups=mesh['dp'=2,'y'=4,'x'=4,'z'=8] {'y','x'}, dimensions={0} | all-to-all | bytes 262144 | tf_op jit(solution)/shard_map/all_to_all | solution.py:391
  106.4 3.1 entry.3
  109.5 10.4 %all_to_all.84.refs_0_ = f32[16,1,1024]{2,1,0:T(1,128)S(1)} all-to-all(f32[16,1,1024]{2,1,0:T(1,128)S(1)} %get-tuple-element.61), channel_id=1, replica_groups=mesh['dp'=2,'y'=4,'x'=4,'z'=8] {'dp','z'}, dimensions={0} | all-to-all | bytes 131072 | tf_op jit(solution)/shard_map/all_to_all | solution.py:391
  119.9 10.9 %all_to_all.85.refs_0_ = f32[16,1,1024]{2,1,0:T(1,128)S(1)} all-to-all(f32[16,1,1024]{2,1,0:T(1,128)S(1)} %merge_moments.7), channel_id=1, replica_groups=mesh['dp'=2,'y'=4,'x'=4,'z'=8] {'y','x'}, dimensions={0} | all-to-all | bytes 131072 | tf_op jit(solution)/shard_map/all_to_all | solution.py:391
  130.8 1.7 turn.1
  132.5 2.5 collective-permute-start.4
  135.0 1.3 collective-permute-start.5
  136.3 10.5 %all_to_all.86.refs_0_ = f32[16,1,1024]{2,1,0:T(1,128)S(1)} all-to-all(f32[16,1,1024]{2,1,0:T(1,128)S(1)} %get-tuple-element.65), channel_id=1, replica_groups=mesh['dp'=2,'y'=4,'x'=4,'z'=8] {'dp','z'}, dimensions={0} | all-to-all | bytes 131072 | tf_op jit(solution)/shard_map/all_to_all | solution.py:391
  146.9 14.2 %all_to_all.87.refs_0_ = f32[16,1,1024]{2,1,0:T(1,128)S(1)} all-to-all(f32[16,1,1024]{2,1,0:T(1,128)S(1)} %merge_sums.3), channel_id=1, replica_groups=mesh['dp'=2,'y'=4,'x'=4,'z'=8] {'y','x'}, dimensions={0} | all-to-all | bytes 131072 | tf_op jit(solution)/shard_map/all_to_all | solution.py:391
  161.1 4.0 %back_middle.2 = (bf16[128,1536]{1,0:T(8,128)(2,1)}, f32[128,1024]{1,0:T(8,128)S(1)}, f32[1,512]{1,0:T(1,128)}, f32[1,512]{1,0:T(1,128)}, f32[16,1,2048]{2,1,0:T(1,128)S(1)}) custom-call(f32[16,1,1024]{2,1,0:T(1,128)S(1)} %all_to_all.87.refs_0_, f32[128,512]{1,0:T(8,128)S(1)} %get-tuple-element.67.refs_1_, f32[128,512]{1,0:T(8,128)S(1)} %get-tuple-element.68.refs_2_, ...), custom_call_target="tpu_custom_call" | custom-call | flops 402653184 | bytes 9261056 | tf_op jit(solution)/shard_map/back_middle/pallas_call | solution.py:370
  165.1 11.9 %all_to_all.88.refs_0_ = f32[16,1,2048]{2,1,0:T(1,128)S(1)} all-to-all(f32[16,1,2048]{2,1,0:T(1,128)S(1)} %get-tuple-element.72), channel_id=1, replica_groups=mesh['dp'=2,'y'=4,'x'=4,'z'=8] {'dp','z'}, dimensions={0} | all-to-all | bytes 262144 | tf_op jit(solution)/shard_map/all_to_all | solution.py:391
  177.0 2.3 give.3
  179.3 0.1 collective-permute-start.17
  179.4 11.1 %all_to_all.89.refs_0_ = f32[16,1,2048]{2,1,0:T(1,128)S(1)} all-to-all(f32[16,1,2048]{2,1,0:T(1,128)S(1)} %merge_sums.4.refs_4_), channel_id=1, replica_groups=mesh['dp'=2,'y'=4,'x'=4,'z'=8] {'y','x'}, dimensions={0} | all-to-all | bytes 262144 | tf_op jit(solution)/shard_map/all_to_all | solution.py:391
  190.5 1.3 back_entry.1
  191.8 2.9 collective-permute-start.6
  194.7 3.2 %collective-permute-start.7 = (bf16[128,1024]{1,0:T(8,128)(2,1)S(1)}, bf16[128,1024]{1,0:T(8,128)(2,1)S(1)}, u32[]{:S(2)}, u32[]{:S(2)}) collective-permute-start(bf16[128,1024]{1,0:T(8,128)(2,1)S(1)} %get-tuple-element.77), channel_id=1, source_target_pairs={{1,0},{2,1},{3,2},{4,3},{5,4},{6,5},{7,6},{8,7},{9,8},{10,9},{11,1... | collective-permute-start | bytes 786440 | tf_op jit(solution)/shard_map/ppermute | solution.py:410
  197.9 11.6 %all_to_all.90.refs_0_ = f32[16,1,1024]{2,1,0:T(1,128)S(1)} all-to-all(f32[16,1,1024]{2,1,0:T(1,128)S(1)} %get-tuple-element.76), channel_id=1, replica_groups=mesh['dp'=2,'y'=4,'x'=4,'z'=8] {'dp','z'}, dimensions={0} | all-to-all | bytes 131072 | tf_op jit(solution)/shard_map/all_to_all | solution.py:391
  209.5 3.7 %keep.3 = bf16[1024,1024]{1,0:T(8,128)(2,1)} custom-call(bf16[1024,1024]{1,0:T(8,128)(2,1)S(1)} %collective-permute-done.17.refs_0_, bf16[128,1024]{1,0:T(8,128)(2,1)} %get-tuple-element.93.refs_0_.refs_1_, bf16[128,1536]{1,0:T(8,128)(2,1)} %get-tuple-element.94.refs_1_.refs_2_, bf16[128,1024]{1,0:T(8,128)(2,1)} %bitcast.20, ...), custom_call_target="tpu_custom_call" | custom-call | flops 268435456 | bytes 5242880 | tf_op jit(solution)/shard_map/keep/pallas_call | solution.py:370
  213.3 12.5 %all_to_all.91.refs_0_ = f32[16,1,1024]{2,1,0:T(1,128)S(1)} all-to-all(f32[16,1,1024]{2,1,0:T(1,128)S(1)} %merge_sums.5.refs_5_), channel_id=1, replica_groups=mesh['dp'=2,'y'=4,'x'=4,'z'=8] {'y','x'}, dimensions={0} | all-to-all | bytes 131072 | tf_op jit(solution)/shard_map/all_to_all | solution.py:391
  225.8 4.1 %back_middle.3 = (bf16[128,1536]{1,0:T(8,128)(2,1)}, f32[128,1024]{1,0:T(8,128)S(1)}, f32[2,512]{1,0:T(2,128)}, f32[2,512]{1,0:T(2,128)}, f32[1,1,2048]{2,1,0:T(1,128)S(1)}) custom-call(f32[16,1,1024]{2,1,0:T(1,128)S(1)} %all_to_all.91.refs_0_, f32[128,512]{1,0:T(8,128)S(1)} %get-tuple-element.78.refs_1_, f32[128,512]{1,0:T(8,128)S(1)} %copy-done.7, ...), custom_call_target="tpu_custom_call" | custom-call | flops 402653184 | bytes 9146368 | tf_op jit(solution)/shard_map/back_middle/pallas_call | solution.py:370
  229.9 2.3 give.2
  232.3 4.1 %collective-permute-done.8.refs_0_ = bf16[1024,1024]{1,0:T(8,128)(2,1)S(1)} collective-permute-done((bf16[1024,1024]{1,0:T(8,128)(2,1)S(1)}, bf16[1024,1024]{1,0:T(8,128)(2,1)S(1)}, u32[]{:S(2)}, u32[]{:S(2)}) %collective-permute-start.8) | collective-permute-done | bytes 2097184 | tf_op jit(solution)/shard_map/ppermute | solution.py:451
  236.5 3.7 %keep.2.refs_1_ = bf16[1024,1024]{1,0:T(8,128)(2,1)} custom-call(bf16[1024,1024]{1,0:T(8,128)(2,1)S(1)} %collective-permute-done.8.refs_0_, bf16[128,1024]{1,0:T(8,128)(2,1)} %get-tuple-element.85.refs_0_.refs_1_, bf16[128,1536]{1,0:T(8,128)(2,1)} %get-tuple-element.86.refs_1_.refs_2_, bf16[128,1024]{1,0:T(8,128)(2,1)} %get-tuple-element.87.refs_2_.refs_3_.refs_5_, ...), custom_call_target="tpu_custom_call" | custom-call | flops 268435456 | bytes 5242880 | tf_op jit(solution)/shard_map/keep/pallas_call | solution.py:370
  240.2 3.7 %all-to-all-start.14 = ((bf16[16,64,1024]{2,1,0:T(8,128)(2,1)}), bf16[16,64,1024]{2,1,0:T(8,128)(2,1)S(1)}, u32[]{:S(2)}, u32[]{:S(2)}) async-start(bf16[16,64,1024]{2,1,0:T(8,128)(2,1)} %bitcast.23), calls=%async_computation.14 | async-start | bytes 4194304 | tf_op jit(solution)/shard_map/all_to_all | solution.py:391
  244.0 1.9 pass.1
  246.0 0.2 collective-permute-start.9
  246.2 1.0 collective-permute-done.9
  247.3 1.1 collective-permute-start.10
  248.4 2.6 collective-permute-done.10
  251.0 0.8 collective-permute-start.11
  251.8 3.9 %collective-permute-done.11 = f32[1,1,2048]{2,1,0:T(1,128)S(1)} collective-permute-done((f32[1,1,2048]{2,1,0:T(1,128)S(1)}, f32[1,1,2048]{2,1,0:T(1,128)S(1)}, u32[]{:S(2)}, u32[]{:S(2)}) %collective-permute-start.11) | collective-permute-done | bytes 8224 | tf_op jit(solution)/shard_map/ppermute | solution.py:451
  255.7 2.4 collective-permute-start.12
  258.1 5.2 %collective-permute-done.12 = f32[1,1,2048]{2,1,0:T(1,128)S(1)} collective-permute-done((f32[1,1,2048]{2,1,0:T(1,128)S(1)}, f32[1,1,2048]{2,1,0:T(1,128)S(1)}, u32[]{:S(2)}, u32[]{:S(2)}) %collective-permute-start.12) | collective-permute-done | bytes 8224 | tf_op jit(solution)/shard_map/ppermute | solution.py:451
  263.3 15.1 %all-to-all-done.14.refs_0_ = bf16[16,64,1024]{2,1,0:T(8,128)(2,1)S(1)} async-done(((bf16[16,64,1024]{2,1,0:T(8,128)(2,1)}), bf16[16,64,1024]{2,1,0:T(8,128)(2,1)S(1)}, u32[]{:S(2)}, u32[]{:S(2)}) %all-to-all-start.14) | async-done | bytes 2097184 | tf_op jit(solution)/shard_map/all_to_all | solution.py:391
  278.4 2.0 gather_rows.1
  280.4 5.0 %all-to-all-start.15 = ((bf16[16,8,2048]{2,1,0:T(8,128)(2,1)}), bf16[16,8,2048]{2,1,0:T(8,128)(2,1)S(1)}, u32[]{:S(2)}, u32[]{:S(2)}) async-start(bf16[16,8,2048]{2,1,0:T(8,128)(2,1)} %gather_rows.1), calls=%async_computation.17 | async-start | bytes 1048576 | tf_op jit(solution)/shard_map/all_to_all | solution.py:391
  285.4 3.6 %collective-permute-done.13 = f32[1,1,2048]{2,1,0:T(1,128)S(1)} collective-permute-done((f32[1,1,2048]{2,1,0:T(1,128)S(1)}, f32[1,1,2048]{2,1,0:T(1,128)S(1)}, u32[]{:S(2)}, u32[]{:S(2)}) %collective-permute-start.13) | collective-permute-done | bytes 8224 | tf_op jit(solution)/shard_map/ppermute | solution.py:451
  289.2 5.1 %collective-permute-done.14 = f32[1,1,2048]{2,1,0:T(1,128)S(1)} collective-permute-done((f32[1,1,2048]{2,1,0:T(1,128)S(1)}, f32[1,1,2048]{2,1,0:T(1,128)S(1)}, u32[]{:S(2)}, u32[]{:S(2)}) %collective-permute-start.14) | collective-permute-done | bytes 8224 | tf_op jit(solution)/shard_map/ppermute | solution.py:451
  294.3 0.5 collective-permute-start.15
  294.9 3.2 %collective-permute-done.15 = f32[1,1,2048]{2,1,0:T(1,128)S(1)} collective-permute-done((f32[1,1,2048]{2,1,0:T(1,128)S(1)}, f32[1,1,2048]{2,1,0:T(1,128)S(1)}, u32[]{:S(2)}, u32[]{:S(2)}) %collective-permute-start.15) | collective-permute-done | bytes 8224 | tf_op jit(solution)/shard_map/ppermute | solution.py:451
  298.1 1.1 collective-permute-start.16
  299.2 4.1 %collective-permute-done.16 = f32[1,1,2048]{2,1,0:T(1,128)S(1)} collective-permute-done((f32[1,1,2048]{2,1,0:T(1,128)S(1)}, f32[1,1,2048]{2,1,0:T(1,128)S(1)}, u32[]{:S(2)}, u32[]{:S(2)}) %collective-permute-start.16) | collective-permute-done | bytes 8224 | tf_op jit(solution)/shard_map/ppermute | solution.py:451
  303.4 1.1 last.1
  304.5 0.7 rows.1
  (93 shorter events, 1.4 us)
Async XLA Ops:
  8.9 16.8 %all-to-all-start = ((f32[16,1,2048]{2,1,0:T(1,128)}), f32[16,1,2048]{2,1,0:T(1,128)S(1)}, u32[]{:S(2)}, u32[]{:S(2)}) async-start(f32[16,1,2048]{2,1,0:T(1,128)} %first.1), calls=%async_computation | async-start | bytes 262144 | tf_op jit(solution)/shard_map/all_to_all | solution.py:391
  25.8 1.0 copy-start.1
  27.4 20.9 %collective-permute-start = (bf16[128,1024]{1,0:T(8,128)(2,1)S(1)}, bf16[128,1024]{1,0:T(8,128)(2,1)S(1)}, u32[]{:S(2)}, u32[]{:S(2)}) collective-permute-start(bf16[128,1024]{1,0:T(8,128)(2,1)S(1)} %get-tuple-element.56), channel_id=1, source_target_pairs={{0,1},{1,2},{2,3},{3,4},{4,5},{5,6},{6,7},{7,8},{8,9},{9,10},{10,1... | collective-permute-start | bytes 786440 | tf_op jit(solution)/shard_map/ppermute | solution.py:410
  30.1 18.2 %collective-permute-start.1 = (bf16[128,1024]{1,0:T(8,128)(2,1)S(1)}, bf16[128,1024]{1,0:T(8,128)(2,1)S(1)}, u32[]{:S(2)}, u32[]{:S(2)}) collective-permute-start(bf16[128,1024]{1,0:T(8,128)(2,1)S(1)} %get-tuple-element.56), channel_id=1, source_target_pairs={{1,0},{2,1},{3,2},{4,3},{5,4},{6,5},{7,6},{8,7},{9,8},{10,9},{11,1... | collective-permute-start | bytes 786440 | tf_op jit(solution)/shard_map/ppermute | solution.py:410
  33.3 15.0 %all-to-all-start.1 = ((f32[16,1,2048]{2,1,0:T(1,128)}), f32[16,1,2048]{2,1,0:T(1,128)S(1)}, u32[]{:S(2)}, u32[]{:S(2)}) async-start(f32[16,1,2048]{2,1,0:T(1,128)} %get-tuple-element.55), calls=%async_computation.1 | async-start | bytes 262144 | tf_op jit(solution)/shard_map/all_to_all | solution.py:391
  40.4 203.6 %reduce-scatter.3.cloned.1.call-start = ((), (), s32[]{:S(2)}) async-start(), calls=%async_computation.18 | async-start | bytes 2621440 | tf_op jit(solution)/shard_map/reduce_scatter | solution.py:455
  40.6 33.7 %copy-start = (bf16[2,1024,512]{2,1,0:T(8,128)(2,1)S(1)}, bf16[2,1024,512]{2,1,0:T(8,128)(2,1)}, u32[]{:S(2)}) copy-start(bf16[2,1024,512]{2,1,0:T(8,128)(2,1)} %refs_6_.5) | copy-start | bytes 6291460
  40.6 33.7 %copy-start.2 = (bf16[2,64,1024]{2,1,0:T(8,128)(2,1)S(1)}, bf16[2,64,1024]{2,1,0:T(8,128)(2,1)}, u32[]{:S(2)}) copy-start(bf16[2,64,1024]{2,1,0:T(8,128)(2,1)} %param.10) | copy-start | bytes 786436
  40.6 33.6 %copy-start.12 = (f32[2,512]{1,0:T(2,128)S(1)}, f32[2,512]{1,0:T(2,128)}, u32[]{:S(2)}) copy-start(f32[2,512]{1,0:T(2,128)} %refs_7_.7) | copy-start | bytes 12292
  40.6 33.6 %copy-start.16 = (f32[2,512]{1,0:T(2,128)S(1)}, f32[2,512]{1,0:T(2,128)}, u32[]{:S(2)}) copy-start(f32[2,512]{1,0:T(2,128)} %refs_3_.3) | copy-start | bytes 12292
  63.5 42.9 %copy-start.11 = (f32[2,1024]{1,0:T(2,128)S(1)}, f32[2,1024]{1,0:T(2,128)}, u32[]{:S(2)}) copy-start(f32[2,1024]{1,0:T(2,128)} %refs_4_.7) | copy-start | bytes 24580
  63.5 42.9 %copy-start.13 = (f32[2,1024]{1,0:T(2,128)S(1)}, f32[2,1024]{1,0:T(2,128)}, u32[]{:S(2)}) copy-start(f32[2,1024]{1,0:T(2,128)} %refs_7_.5) | copy-start | bytes 24580
  76.2 15.5 %collective-permute-start.2 = (bf16[128,1024]{1,0:T(8,128)(2,1)S(1)}, bf16[128,1024]{1,0:T(8,128)(2,1)S(1)}, u32[]{:S(2)}, u32[]{:S(2)}) collective-permute-start(bf16[128,1024]{1,0:T(8,128)(2,1)S(1)} %get-tuple-element.60.refs_1_), channel_id=1, source_target_pairs={{0,8},{1,9},{2,10},{3,11},{4,12},{5,13},{6,14},{7,15},{8,16},{9,17... | collective-permute-start | bytes 786440 | tf_op jit(solution)/shard_map/ppermute | solution.py:410
  78.7 13.0 %collective-permute-start.3 = (bf16[128,1024]{1,0:T(8,128)(2,1)S(1)}, bf16[128,1024]{1,0:T(8,128)(2,1)S(1)}, u32[]{:S(2)}, u32[]{:S(2)}) collective-permute-start(bf16[128,1024]{1,0:T(8,128)(2,1)S(1)} %get-tuple-element.60.refs_1_), channel_id=1, source_target_pairs={{8,0},{9,1},{10,2},{11,3},{12,4},{13,5},{14,6},{15,7},{16,8},{17,9... | collective-permute-start | bytes 786440 | tf_op jit(solution)/shard_map/ppermute | solution.py:410
  106.4 24.4 %copy-start.3 = (bf16[2,64,1024]{2,1,0:T(8,128)(2,1)S(1)}, bf16[2,64,1024]{2,1,0:T(8,128)(2,1)}, u32[]{:S(2)}) copy-start(bf16[2,64,1024]{2,1,0:T(8,128)(2,1)} %param.19) | copy-start | bytes 786436
  106.4 24.4 %copy-start.6 = (bf16[128,1024]{1,0:T(8,128)(2,1)S(1)}, bf16[128,1024]{1,0:T(8,128)(2,1)}, u32[]{:S(2)}) copy-start(bf16[128,1024]{1,0:T(8,128)(2,1)} %get-tuple-element.63.refs_5_.refs_10_.refs_2_) | copy-start | bytes 786436
  119.8 41.2 %copy-start.9 = (f32[128,1024]{1,0:T(8,128)S(1)}, f32[128,1024]{1,0:T(8,128)}, u32[]{:S(2)}) copy-start(f32[128,1024]{1,0:T(8,128)} %get-tuple-element.70.refs_9_) | copy-start | bytes 1572868
  119.8 41.2 %copy-start.15 = (f32[2,1024]{1,0:T(2,128)S(1)}, f32[2,1024]{1,0:T(2,128)}, u32[]{:S(2)}) copy-start(f32[2,1024]{1,0:T(2,128)} %get-tuple-element.71.refs_11_.refs_3_) | copy-start | bytes 24580
  132.5 14.3 %collective-permute-start.4 = (bf16[128,1024]{1,0:T(8,128)(2,1)S(1)}, bf16[128,1024]{1,0:T(8,128)(2,1)S(1)}, u32[]{:S(2)}, u32[]{:S(2)}) collective-permute-start(bf16[128,1024]{1,0:T(8,128)(2,1)S(1)} %get-tuple-element.66), channel_id=1, source_target_pairs={{0,8},{1,9},{2,10},{3,11},{4,12},{5,13},{6,14},{7,15},{8,16},{9,17... | collective-permute-start | bytes 786440 | tf_op jit(solution)/shard_map/ppermute | solution.py:410
  135.0 11.8 %collective-permute-start.5 = (bf16[128,1024]{1,0:T(8,128)(2,1)S(1)}, bf16[128,1024]{1,0:T(8,128)(2,1)S(1)}, u32[]{:S(2)}, u32[]{:S(2)}) collective-permute-start(bf16[128,1024]{1,0:T(8,128)(2,1)S(1)} %get-tuple-element.66), channel_id=1, source_target_pairs={{8,0},{9,1},{10,2},{11,3},{12,4},{13,5},{14,6},{15,7},{16,8},{17,9... | collective-permute-start | bytes 786440 | tf_op jit(solution)/shard_map/ppermute | solution.py:410
  165.1 25.5 %copy-start.4 = (bf16[2,64,1024]{2,1,0:T(8,128)(2,1)S(1)}, bf16[2,64,1024]{2,1,0:T(8,128)(2,1)}, u32[]{:S(2)}) copy-start(bf16[2,64,1024]{2,1,0:T(8,128)(2,1)} %param.19) | copy-start | bytes 786436
  165.1 25.5 %copy-start.7 = (f32[128,512]{1,0:T(8,128)S(1)}, f32[128,512]{1,0:T(8,128)}, u32[]{:S(2)}) copy-start(f32[128,512]{1,0:T(8,128)} %get-tuple-element.75.refs_8_.refs_2_) | copy-start | bytes 786436
  165.1 25.5 %copy-start.10 = (f32[128,512]{1,0:T(8,128)S(1)}, f32[128,512]{1,0:T(8,128)}, u32[]{:S(2)}) copy-start(f32[128,512]{1,0:T(8,128)} %get-tuple-element.74.refs_7_) | copy-start | bytes 786436
  179.3 30.2 %collective-permute-start.17 = (bf16[1024,1024]{1,0:T(8,128)(2,1)S(1)}, bf16[1024,1024]{1,0:T(8,128)(2,1)S(1)}, u32[]{:S(2)}, u32[]{:S(2)}) collective-permute-start(bf16[1024,1024]{1,0:T(8,128)(2,1)S(1)} %give.3), channel_id=1, source_target_pairs={{0,128},{128,0},{1,129},{129,1},{2,130},{130,2},{3,131},{131,3},{4... | collective-permute-start | bytes 6291464 | tf_op jit(solution)/shard_map/ppermute | solution.py:451
  191.8 17.6 %collective-permute-start.6 = (bf16[128,1024]{1,0:T(8,128)(2,1)S(1)}, bf16[128,1024]{1,0:T(8,128)(2,1)S(1)}, u32[]{:S(2)}, u32[]{:S(2)}) collective-permute-start(bf16[128,1024]{1,0:T(8,128)(2,1)S(1)} %get-tuple-element.77), channel_id=1, source_target_pairs={{0,1},{1,2},{2,3},{3,4},{4,5},{5,6},{6,7},{7,8},{8,9},{9,10},{10,1... | collective-permute-start | bytes 786440 | tf_op jit(solution)/shard_map/ppermute | solution.py:410
  194.7 14.8 %collective-permute-start.7 = (bf16[128,1024]{1,0:T(8,128)(2,1)S(1)}, bf16[128,1024]{1,0:T(8,128)(2,1)S(1)}, u32[]{:S(2)}, u32[]{:S(2)}) collective-permute-start(bf16[128,1024]{1,0:T(8,128)(2,1)S(1)} %get-tuple-element.77), channel_id=1, source_target_pairs={{1,0},{2,1},{3,2},{4,3},{5,4},{6,5},{7,6},{8,7},{9,8},{10,9},{11,1... | collective-permute-start | bytes 786440 | tf_op jit(solution)/shard_map/ppermute | solution.py:410
  213.2 12.6 %copy-start.8 = (f32[128,1024]{1,0:T(8,128)S(1)}, f32[128,1024]{1,0:T(8,128)}, u32[]{:S(2)}) copy-start(f32[128,1024]{1,0:T(8,128)} %get-tuple-element.80.refs_9_) | copy-start | bytes 1572868
  213.2 12.6 %copy-start.14 = (f32[2,1024]{1,0:T(2,128)S(1)}, f32[2,1024]{1,0:T(2,128)}, u32[]{:S(2)}) copy-start(f32[2,1024]{1,0:T(2,128)} %get-tuple-element.81.refs_11_.refs_3_) | copy-start | bytes 24580
  213.2 12.6 %copy-start.19 = (f32[1,512]{1,0:T(1,128)S(1)}, f32[1,512]{1,0:T(1,128)}, u32[]{:S(2)}) copy-start(f32[1,512]{1,0:T(1,128)} %get-tuple-element.79.refs_3_) | copy-start | bytes 6148
  213.2 12.6 %copy-start.20 = (f32[1,512]{1,0:T(1,128)S(1)}, f32[1,512]{1,0:T(1,128)}, u32[]{:S(2)}) copy-start(f32[1,512]{1,0:T(1,128)} %get-tuple-element.82.refs_12_) | copy-start | bytes 6148
  213.2 12.6 %copy-start.21 = (f32[1,512]{1,0:T(1,128)S(1)}, f32[1,512]{1,0:T(1,128)}, u32[]{:S(2)}) copy-start(f32[1,512]{1,0:T(1,128)} %get-tuple-element.83.refs_13_) | copy-start | bytes 6148
  232.2 4.2 %collective-permute-start.8 = (bf16[1024,1024]{1,0:T(8,128)(2,1)S(1)}, bf16[1024,1024]{1,0:T(8,128)(2,1)S(1)}, u32[]{:S(2)}, u32[]{:S(2)}) collective-permute-start(bf16[1024,1024]{1,0:T(8,128)(2,1)S(1)} %give.2), channel_id=1, source_target_pairs={{0,128},{128,0},{1,129},{129,1},{2,130},{130,2},{3,131},{131,3},{4... | collective-permute-start | bytes 6291464 | tf_op jit(solution)/shard_map/ppermute | solution.py:451
  240.2 38.2 %all-to-all-start.14 = ((bf16[16,64,1024]{2,1,0:T(8,128)(2,1)}), bf16[16,64,1024]{2,1,0:T(8,128)(2,1)S(1)}, u32[]{:S(2)}, u32[]{:S(2)}) async-start(bf16[16,64,1024]{2,1,0:T(8,128)(2,1)} %bitcast.23), calls=%async_computation.14 | async-start | bytes 4194304 | tf_op jit(solution)/shard_map/all_to_all | solution.py:391
  243.9 34.5 %reduce-scatter.5.cloned.1.call-start = ((), (), s32[]{:S(2)}) async-start(), calls=%async_computation.19 | async-start | bytes 655360 | tf_op jit(solution)/shard_map/reduce_scatter | solution.py:455
  245.9 57.4 %copy-start.5 = (bf16[128,1024]{1,0:T(8,128)(2,1)S(1)}, bf16[128,1024]{1,0:T(8,128)(2,1)}, u32[]{:S(2)}) copy-start(bf16[128,1024]{1,0:T(8,128)(2,1)} %get-tuple-element.87.refs_2_.refs_3_.refs_5_) | copy-start | bytes 786436
  246.0 57.4 %copy-start.17 = (f32[1,1024]{1,0:T(1,128)S(1)}, f32[1,1024]{1,0:T(1,128)}, u32[]{:S(2)}) copy-start(f32[1,1024]{1,0:T(1,128)} %get-tuple-element.90.refs_6_) | copy-start | bytes 12292
  246.0 57.4 %copy-start.18 = (f32[1,1024]{1,0:T(1,128)S(1)}, f32[1,1024]{1,0:T(1,128)}, u32[]{:S(2)}) copy-start(f32[1,1024]{1,0:T(1,128)} %get-tuple-element.91.refs_7_) | copy-start | bytes 12292
  246.0 1.3 collective-permute-start.9
  247.3 3.7 %collective-permute-start.10 = (f32[1,1,2048]{2,1,0:T(1,128)S(1)}, f32[1,1,2048]{2,1,0:T(1,128)S(1)}, u32[]{:S(2)}, u32[]{:S(2)}) collective-permute-start(f32[1,1,2048]{2,1,0:T(1,128)S(1)} %add.88), channel_id=1, source_target_pairs={{0,1},{1,0},{2,3},{3,2},{4,5},{5,4},{6,7},{7,6},{8,9},{9,8},{10,11... | collective-permute-start | bytes 24584 | tf_op jit(solution)/shard_map/ppermute | solution.py:451
  251.0 4.6 %collective-permute-start.11 = (f32[1,1,2048]{2,1,0:T(1,128)S(1)}, f32[1,1,2048]{2,1,0:T(1,128)S(1)}, u32[]{:S(2)}, u32[]{:S(2)}) collective-permute-start(f32[1,1,2048]{2,1,0:T(1,128)S(1)} %add.89), channel_id=1, source_target_pairs={{0,2},{1,3},{2,0},{3,1},{4,6},{5,7},{6,4},{7,5},{8,10},{9,11},{10,... | collective-permute-start | bytes 24584 | tf_op jit(solution)/shard_map/ppermute | solution.py:451
  255.7 7.6 %collective-permute-start.12 = (f32[1,1,2048]{2,1,0:T(1,128)S(1)}, f32[1,1,2048]{2,1,0:T(1,128)S(1)}, u32[]{:S(2)}, u32[]{:S(2)}) collective-permute-start(f32[1,1,2048]{2,1,0:T(1,128)S(1)} %add.90), channel_id=1, source_target_pairs={{0,4},{1,5},{2,6},{3,7},{4,0},{5,1},{6,2},{7,3},{8,12},{9,13},{10,... | collective-permute-start | bytes 24584 | tf_op jit(solution)/shard_map/ppermute | solution.py:451
  280.4 24.1 %all-to-all-start.15 = ((bf16[16,8,2048]{2,1,0:T(8,128)(2,1)}), bf16[16,8,2048]{2,1,0:T(8,128)(2,1)S(1)}, u32[]{:S(2)}, u32[]{:S(2)}) async-start(bf16[16,8,2048]{2,1,0:T(8,128)(2,1)} %gather_rows.1), calls=%async_computation.17 | async-start | bytes 1048576 | tf_op jit(solution)/shard_map/all_to_all | solution.py:391
  285.4 3.7 %collective-permute-start.13 = (f32[1,1,2048]{2,1,0:T(1,128)S(1)}, f32[1,1,2048]{2,1,0:T(1,128)S(1)}, u32[]{:S(2)}, u32[]{:S(2)}) collective-permute-start(f32[1,1,2048]{2,1,0:T(1,128)S(1)} %add.91.refs_2_), channel_id=1, source_target_pairs={{0,8},{8,0},{16,24},{24,16},{1,9},{9,1},{17,25},{25,17},{2,10},{10... | collective-permute-start | bytes 24584 | tf_op jit(solution)/shard_map/ppermute | solution.py:451
  289.1 5.2 %collective-permute-start.14 = (f32[1,1,2048]{2,1,0:T(1,128)S(1)}, f32[1,1,2048]{2,1,0:T(1,128)S(1)}, u32[]{:S(2)}, u32[]{:S(2)}) collective-permute-start(f32[1,1,2048]{2,1,0:T(1,128)S(1)} %add.92), channel_id=1, source_target_pairs={{0,16},{8,24},{16,0},{24,8},{1,17},{9,25},{17,1},{25,9},{2,18},{10... | collective-permute-start | bytes 24584 | tf_op jit(solution)/shard_map/ppermute | solution.py:451
  294.3 3.7 %collective-permute-start.15 = (f32[1,1,2048]{2,1,0:T(1,128)S(1)}, f32[1,1,2048]{2,1,0:T(1,128)S(1)}, u32[]{:S(2)}, u32[]{:S(2)}) collective-permute-start(f32[1,1,2048]{2,1,0:T(1,128)S(1)} %add.93), channel_id=1, source_target_pairs={{0,32},{32,0},{64,96},{96,64},{1,33},{33,1},{65,97},{97,65},{2,34}... | collective-permute-start | bytes 24584 | tf_op jit(solution)/shard_map/ppermute | solution.py:451
  298.1 5.2 %collective-permute-start.16 = (f32[1,1,2048]{2,1,0:T(1,128)S(1)}, f32[1,1,2048]{2,1,0:T(1,128)S(1)}, u32[]{:S(2)}, u32[]{:S(2)}) collective-permute-start(f32[1,1,2048]{2,1,0:T(1,128)S(1)} %add.94), channel_id=1, source_target_pairs={{0,64},{32,96},{64,0},{96,32},{1,65},{33,97},{65,1},{97,33},{2,66}... | collective-permute-start | bytes 24584 | tf_op jit(solution)/shard_map/ppermute | solution.py:451
Sparse Core Ops, SparseCore 0:
  213.4 28.4 reduce-scatter.2
  247.5 24.3 reduce-scatter.4

commit v8 on v7

--- a/solution.py
+++ b/solution.py
@@ -19,6 +19,7 @@
 BF16 = jnp.bfloat16
 ROWS, CH, HALF = 128, 1024, 512
 VMEM_LIMIT = 32 << 20
+PIECES = 4
 TOTAL = 32768.0
 TANH_SCALE = 0.7978845608028654
 CUBE = 0.044715
@@ -234,14 +235,18 @@
 
 
 def k_keep(pairs, arrived, *refs):
-    out, first = refs[-1], 0
-    for i in range(pairs):
-        left, right = refs[2 * i], refs[2 * i + 1]
-        width = right.shape[1] // 2
-        other = arrived[:, first : first + width].astype(F32)
-        mine = product_tn(left[...], half_of(right, False))
-        out[:, first : first + width] = (mine + other).astype(BF16)
-        first += width
+    out = refs[-1]
+    count = CH // PIECES
+    for piece in range(PIECES):
+        rows, first = slice(piece * count, (piece + 1) * count), 0
+        for i in range(pairs):
+            left, right = refs[2 * i], refs[2 * i + 1]
+            width = right.shape[1] // 2
+            other = arrived[rows, first : first + width].astype(F32)
+            mine = product_tn(left[:, rows], half_of(right, False))
+            out[rows, first : first + width] = (mine + other).astype(BF16)
+            first += width
+        out.send_rows(rows)
 
 
 def k_gather(parts, other, out):
@@ -267,11 +272,6 @@
             project_out[layer, :, d * width : (d + 1) * width] = total[:, first + cut : first + CH]
 
 
-def k_merge_first(parts, x, out, sent):
-    sent[...] = x[...]
-    spread_out(out, *merged_moments(parts))
-
-
 def k_pass(value, out):
     out[...] = value[...]
 
@@ -301,13 +301,20 @@
 
 
 class Stored:
-    def __init__(self, copy, ref):
-        self.copy, self.ref, self.shape, self.started = copy, ref, ref.shape, False
+    def __init__(self, ref, target, sems):
+        self.ref, self.target, self.sems, self.shape = ref, target, sems, ref.shape
+        self.copies = []
+
+    def send(self, source, target):
+        self.copies.append(pltpu.make_async_copy(source, target, self.sems[len(self.copies)]))
+        self.copies[-1].start()
+
+    def send_rows(self, rows):
+        self.send(self.ref.at[rows], self.target.at[rows])
 
     def start(self):
-        if not self.started:
-            self.copy.start()
-            self.started = True
+        if not self.copies:
+            self.send(self.ref, self.target)
 
     def __getitem__(self, place):
         return self.ref[place]
@@ -330,9 +337,10 @@
             buffer = scratch.pop(0)
             ins[i] = Loaded(pltpu.make_async_copy(source, buffer, sems.at[place]), buffer)
             late.append(ins[i])
-        for place, i in enumerate(stored, len(loaded)):
-            buffer = scratch.pop(0)
-            outs[i] = Stored(pltpu.make_async_copy(buffer, outs[i], sems.at[place]), buffer)
+        for place, i in enumerate(stored):
+            first = len(loaded) + PIECES * place
+            own = [sems.at[first + piece] for piece in range(PIECES)]
+            outs[i] = Stored(scratch.pop(0), outs[i], own)
             results.append(outs[i])
         kernel(*ins, *outs)
         for value in late:
@@ -340,7 +348,8 @@
         for value in results:
             value.start()
         for value in results:
-            value.copy.wait()
+            for copy in value.copies:
+                copy.wait()
 
     return body
 
@@ -360,7 +369,7 @@
         shape = operands[i].shape
         scratch.append(pltpu.VMEM(shape[1:] if i in layers else shape, operands[i].dtype))
     scratch += [pltpu.VMEM(*outs[i]) for i in stored]
-    scratch.append(pltpu.SemaphoreType.DMA((max(1, len(loaded) + len(stored)),)))
+    scratch.append(pltpu.SemaphoreType.DMA((max(1, len(loaded) + PIECES * len(stored)),)))
     body = staged(
         kernel,
         (len(operands), len(waits) + len(held), len(outs)),
@@ -504,17 +513,8 @@
         )
 
     (payload,) = call(k_first, [(wide, F32)], stream_0, loaded=(0,), name="first")
-    merged, sent = call(
-        k_merge_first,
-        [(wide, F32), ((ROWS, CH), BF16)],
-        exchange(payload, FIRST_STAGE),
-        stream_0,
-        loaded=(1,),
-        free=(1,),
-        name="merge_moments",
-    )
-    sides = neighbours(sent, FIRST_DILATION)
-    parts = exchange(merged, SECOND_STAGE)
+    sides = neighbours(stream_0, FIRST_DILATION)
+    parts, _ = over_all(payload, "moments", sides)
     taps_0, slope_0, conv_0, stat_0, payload = entry(0, stream_0, parts, sides)
     parts, _ = over_all(payload, "moments")
     hidden_0, stream_1, kept_1, slope_mid_0, normed_0, factor_0, payload = call(

time: 314 us -> 312 us (level)
  no operation moved by 1% of the time
where the time goes in v8:
time: 312 us; the launch traced here: 310 us
  blocking collectives  140 us (45%)
  waiting for transfers between devices  61.2 us (20%)
  starting transfers between devices  52.2 us (17%)
  Pallas kernels  39.3 us (13%)
  between operations  14.7 us (5%)
    all_to_all x12, blocking collectives, exchange(): return lax.all_to_all(value, axes, 0, 0, tiled=True)  140 us
    pallas_call x24, Pallas kernels, call(): pl.pallas_call(body, grid=(1,), in_specs=specs, out_specs=[in_hbm if i in...  39.3 us
    ppermute x10, waiting for transfers between devices, swapped(): return lax.ppermute(value, axis, pairs)  32.4 us
    all_to_all x4, waiting for transfers between devices, exchange(): return lax.all_to_all(value, axes, 0, 0, tiled=True)  28.7 us
    all_to_all x4, starting transfers between devices, exchange(): return lax.all_to_all(value, axes, 0, 0, tiled=True)  25.8 us
    ppermute x8, starting transfers between devices, passed_along(): lax.ppermute(value, SEQ, [(source, source + steps) for source in range(le...  19.3 us
    ppermute x10, starting transfers between devices, swapped(): return lax.ppermute(value, axis, pairs)  7.09 us
  transfers between devices with their start and end apart: 24, of which 12 were waited for; matrix products, arithmetic and copies ran while one was open for 1% of the time, Pallas kernels for 5%

profile of v8, /device:TPU:32, one launch (start us, length us, event | category | flops | bytes accessed | tf_op | source)
XLA Modules:
  0.0 310.2 jit_solution(9712909901053093820)
XLA Ops:
  7.2 3.8 %collective-permute-start = (bf16[128,1024]{1,0:T(8,128)(2,1)}, bf16[128,1024]{1,0:T(8,128)(2,1)S(1)}, u32[]{:S(2)}, u32[]{:S(2)}) collective-permute-start(bf16[128,1024]{1,0:T(8,128)(2,1)} %bitcast.13), channel_id=1, source_target_pairs={{0,1},{1,2},{2,3},{3,4},{4,5},{5,6},{6,7},{7,8},{8,9},{9,10},{10,1... | collective-permute-start | bytes 786440 | tf_op jit(solution)/shard_map/ppermute | solution.py:419
  11.0 2.0 collective-permute-start.1
  13.0 1.8 first.1
  14.8 9.8 %all-to-all-start = ((f32[16,1,2048]{2,1,0:T(1,128)}), f32[16,1,2048]{2,1,0:T(1,128)S(1)}, u32[]{:S(2)}, u32[]{:S(2)}) async-start(f32[16,1,2048]{2,1,0:T(1,128)} %first.1), calls=%async_computation | async-start | bytes 262144 | tf_op jit(solution)/shard_map/all_to_all | solution.py:400
  24.6 0.8 fusion.4
  25.5 0.8 select_reduce_fusion.1
  26.8 6.1 %all-to-all-done.refs_0_ = f32[16,1,2048]{2,1,0:T(1,128)S(1)} async-done(((f32[16,1,2048]{2,1,0:T(1,128)}), f32[16,1,2048]{2,1,0:T(1,128)S(1)}, u32[]{:S(2)}, u32[]{:S(2)}) %all-to-all-start) | async-done | bytes 131104 | tf_op jit(solution)/shard_map/all_to_all | solution.py:400
  32.8 0.7 merge_moments.4
  33.6 7.0 %all-to-all-start.1 = ((f32[16,1,2048]{2,1,0:T(1,128)}), f32[16,1,2048]{2,1,0:T(1,128)S(1)}, u32[]{:S(2)}, u32[]{:S(2)}) async-start(f32[16,1,2048]{2,1,0:T(1,128)} %merge_moments.4), calls=%async_computation.1 | async-start | bytes 262144 | tf_op jit(solution)/shard_map/all_to_all | solution.py:400
  40.7 0.1 copy.27
  40.9 7.7 %all-to-all-done.1.refs_0_ = f32[16,1,2048]{2,1,0:T(1,128)S(1)} async-done(((f32[16,1,2048]{2,1,0:T(1,128)}), f32[16,1,2048]{2,1,0:T(1,128)S(1)}, u32[]{:S(2)}, u32[]{:S(2)}) %all-to-all-start.1) | async-done | bytes 131104 | tf_op jit(solution)/shard_map/all_to_all | solution.py:400
  48.6 3.2 %entry.2 = (bf16[128,1024]{1,0:T(8,128)(2,1)}, f32[128,1024]{1,0:T(8,128)}, f32[128,512]{1,0:T(8,128)S(1)}, f32[2,1024]{1,0:T(2,128)}, f32[16,1,1024]{2,1,0:T(1,128)S(1)}) custom-call(f32[16,1,2048]{2,1,0:T(1,128)S(1)} %all-to-all-done.1.refs_0_, bf16[128,1024]{1,0:T(8,128)(2,1)} %bitcast.16, bf16[128,1024]{1,0:T(8,128)(2,1)S(1)} %collective-permute-done.refs_1_.refs_2_, ...), custom_call_target="tpu_custom_call" | custom-call | flops 402653184 | bytes 8349696 | tf_op jit(solution)/shard_map/entry/pallas_call | solution.py:379
  51.9 10.4 %all_to_all.80.refs_0_ = f32[16,1,1024]{2,1,0:T(1,128)S(1)} all-to-all(f32[16,1,1024]{2,1,0:T(1,128)S(1)} %get-tuple-element.53), channel_id=1, replica_groups=mesh['dp'=2,'y'=4,'x'=4,'z'=8] {'dp','z'}, dimensions={0} | all-to-all | bytes 131072 | tf_op jit(solution)/shard_map/all_to_all | solution.py:400
  62.3 10.7 %all_to_all.81.refs_0_ = f32[16,1,1024]{2,1,0:T(1,128)S(1)} all-to-all(f32[16,1,1024]{2,1,0:T(1,128)S(1)} %merge_moments.5), channel_id=1, replica_groups=mesh['dp'=2,'y'=4,'x'=4,'z'=8] {'y','x'}, dimensions={0} | all-to-all | bytes 131072 | tf_op jit(solution)/shard_map/all_to_all | solution.py:400
  73.1 2.1 middle.1
  75.2 2.5 collective-permute-start.2
  77.7 1.3 collective-permute-start.3
  79.0 11.7 %all_to_all.82.refs_0_ = f32[16,1,2048]{2,1,0:T(1,128)S(1)} all-to-all(f32[16,1,2048]{2,1,0:T(1,128)S(1)} %get-tuple-element.55), channel_id=1, replica_groups=mesh['dp'=2,'y'=4,'x'=4,'z'=8] {'dp','z'}, dimensions={0} | all-to-all | bytes 262144 | tf_op jit(solution)/shard_map/all_to_all | solution.py:400
  90.8 14.5 %all_to_all.83.refs_0_ = f32[16,1,2048]{2,1,0:T(1,128)S(1)} all-to-all(f32[16,1,2048]{2,1,0:T(1,128)S(1)} %merge_moments.6), channel_id=1, replica_groups=mesh['dp'=2,'y'=4,'x'=4,'z'=8] {'y','x'}, dimensions={0} | all-to-all | bytes 262144 | tf_op jit(solution)/shard_map/all_to_all | solution.py:400
  105.3 3.2 %entry.3 = (bf16[128,1024]{1,0:T(8,128)(2,1)}, f32[128,1024]{1,0:T(8,128)}, f32[128,512]{1,0:T(8,128)S(1)}, f32[2,1024]{1,0:T(2,128)}, f32[16,1,1024]{2,1,0:T(1,128)S(1)}) custom-call(f32[16,1,2048]{2,1,0:T(1,128)S(1)} %all_to_all.83.refs_0_, bf16[128,1024]{1,0:T(8,128)(2,1)S(1)} %get-tuple-element.56.refs_1_, ...), custom_call_target="tpu_custom_call" | custom-call | flops 402653184 | bytes 8349696 | tf_op jit(solution)/shard_map/entry/pallas_call | solution.py:379
  108.5 10.4 %all_to_all.84.refs_0_ = f32[16,1,1024]{2,1,0:T(1,128)S(1)} all-to-all(f32[16,1,1024]{2,1,0:T(1,128)S(1)} %get-tuple-element.57), channel_id=1, replica_groups=mesh['dp'=2,'y'=4,'x'=4,'z'=8] {'dp','z'}, dimensions={0} | all-to-all | bytes 131072 | tf_op jit(solution)/shard_map/all_to_all | solution.py:400
  118.9 10.9 %all_to_all.85.refs_0_ = f32[16,1,1024]{2,1,0:T(1,128)S(1)} all-to-all(f32[16,1,1024]{2,1,0:T(1,128)S(1)} %merge_moments.7), channel_id=1, replica_groups=mesh['dp'=2,'y'=4,'x'=4,'z'=8] {'y','x'}, dimensions={0} | all-to-all | bytes 131072 | tf_op jit(solution)/shard_map/all_to_all | solution.py:400
  129.8 1.8 turn.1
  131.6 2.5 collective-permute-start.4
  134.1 1.3 collective-permute-start.5
  135.4 10.5 %all_to_all.86.refs_0_ = f32[16,1,1024]{2,1,0:T(1,128)S(1)} all-to-all(f32[16,1,1024]{2,1,0:T(1,128)S(1)} %get-tuple-element.61), channel_id=1, replica_groups=mesh['dp'=2,'y'=4,'x'=4,'z'=8] {'dp','z'}, dimensions={0} | all-to-all | bytes 131072 | tf_op jit(solution)/shard_map/all_to_all | solution.py:400
  146.0 14.2 %all_to_all.87.refs_0_ = f32[16,1,1024]{2,1,0:T(1,128)S(1)} all-to-all(f32[16,1,1024]{2,1,0:T(1,128)S(1)} %merge_sums.3), channel_id=1, replica_groups=mesh['dp'=2,'y'=4,'x'=4,'z'=8] {'y','x'}, dimensions={0} | all-to-all | bytes 131072 | tf_op jit(solution)/shard_map/all_to_all | solution.py:400
  160.2 4.1 %back_middle.2 = (bf16[128,1536]{1,0:T(8,128)(2,1)}, f32[128,1024]{1,0:T(8,128)S(1)}, f32[1,512]{1,0:T(1,128)}, f32[1,512]{1,0:T(1,128)}, f32[16,1,2048]{2,1,0:T(1,128)S(1)}) custom-call(f32[16,1,1024]{2,1,0:T(1,128)S(1)} %all_to_all.87.refs_0_, f32[128,512]{1,0:T(8,128)S(1)} %get-tuple-element.63.refs_1_, f32[128,512]{1,0:T(8,128)S(1)} %get-tuple-element.64.refs_2_, ...), custom_call_target="tpu_custom_call" | custom-call | flops 402653184 | bytes 9261056 | tf_op jit(solution)/shard_map/back_middle/pallas_call | solution.py:379
  164.2 11.9 %all_to_all.88.refs_0_ = f32[16,1,2048]{2,1,0:T(1,128)S(1)} all-to-all(f32[16,1,2048]{2,1,0:T(1,128)S(1)} %get-tuple-element.68), channel_id=1, replica_groups=mesh['dp'=2,'y'=4,'x'=4,'z'=8] {'dp','z'}, dimensions={0} | all-to-all | bytes 262144 | tf_op jit(solution)/shard_map/all_to_all | solution.py:400
  176.2 2.3 give.3
  178.5 0.1 collective-permute-start.17
  178.6 11.1 %all_to_all.89.refs_0_ = f32[16,1,2048]{2,1,0:T(1,128)S(1)} all-to-all(f32[16,1,2048]{2,1,0:T(1,128)S(1)} %merge_sums.4.refs_4_), channel_id=1, replica_groups=mesh['dp'=2,'y'=4,'x'=4,'z'=8] {'y','x'}, dimensions={0} | all-to-all | bytes 262144 | tf_op jit(solution)/shard_map/all_to_all | solution.py:400
  189.7 1.4 back_entry.1
  191.1 2.7 collective-permute-start.6
  193.8 3.2 %collective-permute-start.7 = (bf16[128,1024]{1,0:T(8,128)(2,1)S(1)}, bf16[128,1024]{1,0:T(8,128)(2,1)S(1)}, u32[]{:S(2)}, u32[]{:S(2)}) collective-permute-start(bf16[128,1024]{1,0:T(8,128)(2,1)S(1)} %get-tuple-element.73), channel_id=1, source_target_pairs={{1,0},{2,1},{3,2},{4,3},{5,4},{6,5},{7,6},{8,7},{9,8},{10,9},{11,1... | collective-permute-start | bytes 786440 | tf_op jit(solution)/shard_map/ppermute | solution.py:419
  197.0 11.6 %all_to_all.90.refs_0_ = f32[16,1,1024]{2,1,0:T(1,128)S(1)} all-to-all(f32[16,1,1024]{2,1,0:T(1,128)S(1)} %get-tuple-element.72), channel_id=1, replica_groups=mesh['dp'=2,'y'=4,'x'=4,'z'=8] {'dp','z'}, dimensions={0} | all-to-all | bytes 131072 | tf_op jit(solution)/shard_map/all_to_all | solution.py:400
  208.6 3.1 keep.3
  211.8 12.5 %all_to_all.91.refs_0_ = f32[16,1,1024]{2,1,0:T(1,128)S(1)} all-to-all(f32[16,1,1024]{2,1,0:T(1,128)S(1)} %merge_sums.5.refs_5_), channel_id=1, replica_groups=mesh['dp'=2,'y'=4,'x'=4,'z'=8] {'y','x'}, dimensions={0} | all-to-all | bytes 131072 | tf_op jit(solution)/shard_map/all_to_all | solution.py:400
  224.3 4.2 %back_middle.3 = (bf16[128,1536]{1,0:T(8,128)(2,1)}, f32[128,1024]{1,0:T(8,128)S(1)}, f32[2,512]{1,0:T(2,128)}, f32[2,512]{1,0:T(2,128)}, f32[1,1,2048]{2,1,0:T(1,128)S(1)}) custom-call(f32[16,1,1024]{2,1,0:T(1,128)S(1)} %all_to_all.91.refs_0_, f32[128,512]{1,0:T(8,128)S(1)} %get-tuple-element.74.refs_1_, f32[128,512]{1,0:T(8,128)S(1)} %copy-done.6, ...), custom_call_target="tpu_custom_call" | custom-call | flops 402653184 | bytes 9146368 | tf_op jit(solution)/shard_map/back_middle/pallas_call | solution.py:379
  228.5 2.3 give.2
  230.9 4.1 %collective-permute-done.8.refs_0_ = bf16[1024,1024]{1,0:T(8,128)(2,1)S(1)} collective-permute-done((bf16[1024,1024]{1,0:T(8,128)(2,1)S(1)}, bf16[1024,1024]{1,0:T(8,128)(2,1)S(1)}, u32[]{:S(2)}, u32[]{:S(2)}) %collective-permute-start.8) | collective-permute-done | bytes 2097184 | tf_op jit(solution)/shard_map/ppermute | solution.py:460
  235.1 3.1 keep.2.refs_1_
  238.1 3.7 %all-to-all-start.14 = ((bf16[16,64,1024]{2,1,0:T(8,128)(2,1)}), bf16[16,64,1024]{2,1,0:T(8,128)(2,1)S(1)}, u32[]{:S(2)}, u32[]{:S(2)}) async-start(bf16[16,64,1024]{2,1,0:T(8,128)(2,1)} %bitcast.24), calls=%async_computation.14 | async-start | bytes 4194304 | tf_op jit(solution)/shard_map/all_to_all | solution.py:400
  242.0 1.9 pass.1
  244.0 0.2 collective-permute-start.9
  244.2 1.0 collective-permute-done.9
  245.3 1.1 collective-permute-start.10
  246.4 2.6 collective-permute-done.10
  249.0 0.8 collective-permute-start.11
  249.8 3.9 %collective-permute-done.11 = f32[1,1,2048]{2,1,0:T(1,128)S(1)} collective-permute-done((f32[1,1,2048]{2,1,0:T(1,128)S(1)}, f32[1,1,2048]{2,1,0:T(1,128)S(1)}, u32[]{:S(2)}, u32[]{:S(2)}) %collective-permute-start.11) | collective-permute-done | bytes 8224 | tf_op jit(solution)/shard_map/ppermute | solution.py:460
  253.7 2.9 collective-permute-start.12
  256.6 4.7 %collective-permute-done.12 = f32[1,1,2048]{2,1,0:T(1,128)S(1)} collective-permute-done((f32[1,1,2048]{2,1,0:T(1,128)S(1)}, f32[1,1,2048]{2,1,0:T(1,128)S(1)}, u32[]{:S(2)}, u32[]{:S(2)}) %collective-permute-start.12) | collective-permute-done | bytes 8224 | tf_op jit(solution)/shard_map/ppermute | solution.py:460
  261.3 14.9 %all-to-all-done.14.refs_0_ = bf16[16,64,1024]{2,1,0:T(8,128)(2,1)S(1)} async-done(((bf16[16,64,1024]{2,1,0:T(8,128)(2,1)}), bf16[16,64,1024]{2,1,0:T(8,128)(2,1)S(1)}, u32[]{:S(2)}, u32[]{:S(2)}) %all-to-all-start.14) | async-done | bytes 2097184 | tf_op jit(solution)/shard_map/all_to_all | solution.py:400
  276.3 2.0 gather_rows.1
  278.2 5.2 %all-to-all-start.15 = ((bf16[16,8,2048]{2,1,0:T(8,128)(2,1)}), bf16[16,8,2048]{2,1,0:T(8,128)(2,1)S(1)}, u32[]{:S(2)}, u32[]{:S(2)}) async-start(bf16[16,8,2048]{2,1,0:T(8,128)(2,1)} %gather_rows.1), calls=%async_computation.17 | async-start | bytes 1048576 | tf_op jit(solution)/shard_map/all_to_all | solution.py:400
  283.4 3.6 %collective-permute-done.13 = f32[1,1,2048]{2,1,0:T(1,128)S(1)} collective-permute-done((f32[1,1,2048]{2,1,0:T(1,128)S(1)}, f32[1,1,2048]{2,1,0:T(1,128)S(1)}, u32[]{:S(2)}, u32[]{:S(2)}) %collective-permute-start.13) | collective-permute-done | bytes 8224 | tf_op jit(solution)/shard_map/ppermute | solution.py:460
  287.1 0.1 collective-permute-start.14
  287.2 5.1 %collective-permute-done.14 = f32[1,1,2048]{2,1,0:T(1,128)S(1)} collective-permute-done((f32[1,1,2048]{2,1,0:T(1,128)S(1)}, f32[1,1,2048]{2,1,0:T(1,128)S(1)}, u32[]{:S(2)}, u32[]{:S(2)}) %collective-permute-start.14) | collective-permute-done | bytes 8224 | tf_op jit(solution)/shard_map/ppermute | solution.py:460
  292.3 0.6 collective-permute-start.15
  292.9 3.1 %collective-permute-done.15 = f32[1,1,2048]{2,1,0:T(1,128)S(1)} collective-permute-done((f32[1,1,2048]{2,1,0:T(1,128)S(1)}, f32[1,1,2048]{2,1,0:T(1,128)S(1)}, u32[]{:S(2)}, u32[]{:S(2)}) %collective-permute-start.15) | collective-permute-done | bytes 8224 | tf_op jit(solution)/shard_map/ppermute | solution.py:460
  296.1 1.2 collective-permute-start.16
  297.2 4.1 %collective-permute-done.16 = f32[1,1,2048]{2,1,0:T(1,128)S(1)} collective-permute-done((f32[1,1,2048]{2,1,0:T(1,128)S(1)}, f32[1,1,2048]{2,1,0:T(1,128)S(1)}, u32[]{:S(2)}, u32[]{:S(2)}) %collective-permute-start.16) | collective-permute-done | bytes 8224 | tf_op jit(solution)/shard_map/ppermute | solution.py:460
  301.4 1.2 last.1
  302.6 0.8 rows.1
  (91 shorter events, 1.3 us)
Async XLA Ops:
  7.2 25.7 %collective-permute-start = (bf16[128,1024]{1,0:T(8,128)(2,1)}, bf16[128,1024]{1,0:T(8,128)(2,1)S(1)}, u32[]{:S(2)}, u32[]{:S(2)}) collective-permute-start(bf16[128,1024]{1,0:T(8,128)(2,1)} %bitcast.13), channel_id=1, source_target_pairs={{0,1},{1,2},{2,3},{3,4},{4,5},{5,6},{6,7},{7,8},{8,9},{9,10},{10,1... | collective-permute-start | bytes 786440 | tf_op jit(solution)/shard_map/ppermute | solution.py:419
  11.0 21.8 %collective-permute-start.1 = (bf16[128,1024]{1,0:T(8,128)(2,1)}, bf16[128,1024]{1,0:T(8,128)(2,1)S(1)}, u32[]{:S(2)}, u32[]{:S(2)}) collective-permute-start(bf16[128,1024]{1,0:T(8,128)(2,1)} %bitcast.14), channel_id=1, source_target_pairs={{1,0},{2,1},{3,2},{4,3},{5,4},{6,5},{7,6},{8,7},{9,8},{10,9},{11,1... | collective-permute-start | bytes 786440 | tf_op jit(solution)/shard_map/ppermute | solution.py:419
  14.8 18.0 %all-to-all-start = ((f32[16,1,2048]{2,1,0:T(1,128)}), f32[16,1,2048]{2,1,0:T(1,128)S(1)}, u32[]{:S(2)}, u32[]{:S(2)}) async-start(f32[16,1,2048]{2,1,0:T(1,128)} %first.1), calls=%async_computation | async-start | bytes 262144 | tf_op jit(solution)/shard_map/all_to_all | solution.py:400
  33.6 15.0 %all-to-all-start.1 = ((f32[16,1,2048]{2,1,0:T(1,128)}), f32[16,1,2048]{2,1,0:T(1,128)S(1)}, u32[]{:S(2)}, u32[]{:S(2)}) async-start(f32[16,1,2048]{2,1,0:T(1,128)} %merge_moments.4), calls=%async_computation.1 | async-start | bytes 262144 | tf_op jit(solution)/shard_map/all_to_all | solution.py:400
  40.6 201.3 %reduce-scatter.3.cloned.1.call-start = ((), (), s32[]{:S(2)}) async-start(), calls=%async_computation.18 | async-start | bytes 2621440 | tf_op jit(solution)/shard_map/reduce_scatter | solution.py:464
  40.9 32.2 %copy-start = (bf16[2,1024,512]{2,1,0:T(8,128)(2,1)S(1)}, bf16[2,1024,512]{2,1,0:T(8,128)(2,1)}, u32[]{:S(2)}) copy-start(bf16[2,1024,512]{2,1,0:T(8,128)(2,1)} %refs_6_.5) | copy-start | bytes 6291460
  40.9 32.2 %copy-start.1 = (bf16[2,64,1024]{2,1,0:T(8,128)(2,1)S(1)}, bf16[2,64,1024]{2,1,0:T(8,128)(2,1)}, u32[]{:S(2)}) copy-start(bf16[2,64,1024]{2,1,0:T(8,128)(2,1)} %param.10) | copy-start | bytes 786436
  40.9 32.2 %copy-start.11 = (f32[2,512]{1,0:T(2,128)S(1)}, f32[2,512]{1,0:T(2,128)}, u32[]{:S(2)}) copy-start(f32[2,512]{1,0:T(2,128)} %refs_7_.7) | copy-start | bytes 12292
  40.9 32.2 %copy-start.15 = (f32[2,512]{1,0:T(2,128)S(1)}, f32[2,512]{1,0:T(2,128)}, u32[]{:S(2)}) copy-start(f32[2,512]{1,0:T(2,128)} %refs_3_.3) | copy-start | bytes 12292
  62.3 43.0 %copy-start.10 = (f32[2,1024]{1,0:T(2,128)S(1)}, f32[2,1024]{1,0:T(2,128)}, u32[]{:S(2)}) copy-start(f32[2,1024]{1,0:T(2,128)} %refs_4_.7) | copy-start | bytes 24580
  62.3 43.0 %copy-start.12 = (f32[2,1024]{1,0:T(2,128)S(1)}, f32[2,1024]{1,0:T(2,128)}, u32[]{:S(2)}) copy-start(f32[2,1024]{1,0:T(2,128)} %refs_7_.5) | copy-start | bytes 24580
  75.2 15.5 %collective-permute-start.2 = (bf16[128,1024]{1,0:T(8,128)(2,1)S(1)}, bf16[128,1024]{1,0:T(8,128)(2,1)S(1)}, u32[]{:S(2)}, u32[]{:S(2)}) collective-permute-start(bf16[128,1024]{1,0:T(8,128)(2,1)S(1)} %get-tuple-element.56.refs_1_), channel_id=1, source_target_pairs={{0,8},{1,9},{2,10},{3,11},{4,12},{5,13},{6,14},{7,15},{8,16},{9,17... | collective-permute-start | bytes 786440 | tf_op jit(solution)/shard_map/ppermute | solution.py:419
  77.7 13.0 %collective-permute-start.3 = (bf16[128,1024]{1,0:T(8,128)(2,1)S(1)}, bf16[128,1024]{1,0:T(8,128)(2,1)S(1)}, u32[]{:S(2)}, u32[]{:S(2)}) collective-permute-start(bf16[128,1024]{1,0:T(8,128)(2,1)S(1)} %get-tuple-element.56.refs_1_), channel_id=1, source_target_pairs={{8,0},{9,1},{10,2},{11,3},{12,4},{13,5},{14,6},{15,7},{16,8},{17,9... | collective-permute-start | bytes 786440 | tf_op jit(solution)/shard_map/ppermute | solution.py:419
  105.3 24.5 %copy-start.2 = (bf16[2,64,1024]{2,1,0:T(8,128)(2,1)S(1)}, bf16[2,64,1024]{2,1,0:T(8,128)(2,1)}, u32[]{:S(2)}) copy-start(bf16[2,64,1024]{2,1,0:T(8,128)(2,1)} %param.19) | copy-start | bytes 786436
  105.3 24.5 %copy-start.5 = (bf16[128,1024]{1,0:T(8,128)(2,1)S(1)}, bf16[128,1024]{1,0:T(8,128)(2,1)}, u32[]{:S(2)}) copy-start(bf16[128,1024]{1,0:T(8,128)(2,1)} %get-tuple-element.59.refs_5_.refs_10_.refs_2_) | copy-start | bytes 786436
  118.9 41.3 %copy-start.8 = (f32[128,1024]{1,0:T(8,128)S(1)}, f32[128,1024]{1,0:T(8,128)}, u32[]{:S(2)}) copy-start(f32[128,1024]{1,0:T(8,128)} %get-tuple-element.66.refs_9_) | copy-start | bytes 1572868
  118.9 41.3 %copy-start.14 = (f32[2,1024]{1,0:T(2,128)S(1)}, f32[2,1024]{1,0:T(2,128)}, u32[]{:S(2)}) copy-start(f32[2,1024]{1,0:T(2,128)} %get-tuple-element.67.refs_11_.refs_3_) | copy-start | bytes 24580
  131.6 14.3 %collective-permute-start.4 = (bf16[128,1024]{1,0:T(8,128)(2,1)S(1)}, bf16[128,1024]{1,0:T(8,128)(2,1)S(1)}, u32[]{:S(2)}, u32[]{:S(2)}) collective-permute-start(bf16[128,1024]{1,0:T(8,128)(2,1)S(1)} %get-tuple-element.62), channel_id=1, source_target_pairs={{0,8},{1,9},{2,10},{3,11},{4,12},{5,13},{6,14},{7,15},{8,16},{9,17... | collective-permute-start | bytes 786440 | tf_op jit(solution)/shard_map/ppermute | solution.py:419
  134.1 11.8 %collective-permute-start.5 = (bf16[128,1024]{1,0:T(8,128)(2,1)S(1)}, bf16[128,1024]{1,0:T(8,128)(2,1)S(1)}, u32[]{:S(2)}, u32[]{:S(2)}) collective-permute-start(bf16[128,1024]{1,0:T(8,128)(2,1)S(1)} %get-tuple-element.62), channel_id=1, source_target_pairs={{8,0},{9,1},{10,2},{11,3},{12,4},{13,5},{14,6},{15,7},{16,8},{17,9... | collective-permute-start | bytes 786440 | tf_op jit(solution)/shard_map/ppermute | solution.py:419
  164.2 25.5 %copy-start.3 = (bf16[2,64,1024]{2,1,0:T(8,128)(2,1)S(1)}, bf16[2,64,1024]{2,1,0:T(8,128)(2,1)}, u32[]{:S(2)}) copy-start(bf16[2,64,1024]{2,1,0:T(8,128)(2,1)} %param.19) | copy-start | bytes 786436
  164.2 25.5 %copy-start.6 = (f32[128,512]{1,0:T(8,128)S(1)}, f32[128,512]{1,0:T(8,128)}, u32[]{:S(2)}) copy-start(f32[128,512]{1,0:T(8,128)} %get-tuple-element.71.refs_8_.refs_2_) | copy-start | bytes 786436
  164.2 25.5 %copy-start.9 = (f32[128,512]{1,0:T(8,128)S(1)}, f32[128,512]{1,0:T(8,128)}, u32[]{:S(2)}) copy-start(f32[128,512]{1,0:T(8,128)} %get-tuple-element.70.refs_7_) | copy-start | bytes 786436
  178.5 30.1 %collective-permute-start.17 = (bf16[1024,1024]{1,0:T(8,128)(2,1)S(1)}, bf16[1024,1024]{1,0:T(8,128)(2,1)S(1)}, u32[]{:S(2)}, u32[]{:S(2)}) collective-permute-start(bf16[1024,1024]{1,0:T(8,128)(2,1)S(1)} %give.3), channel_id=1, source_target_pairs={{0,128},{128,0},{1,129},{129,1},{2,130},{130,2},{3,131},{131,3},{4... | collective-permute-start | bytes 6291464 | tf_op jit(solution)/shard_map/ppermute | solution.py:460
  191.1 17.4 %collective-permute-start.6 = (bf16[128,1024]{1,0:T(8,128)(2,1)S(1)}, bf16[128,1024]{1,0:T(8,128)(2,1)S(1)}, u32[]{:S(2)}, u32[]{:S(2)}) collective-permute-start(bf16[128,1024]{1,0:T(8,128)(2,1)S(1)} %get-tuple-element.73), channel_id=1, source_target_pairs={{0,1},{1,2},{2,3},{3,4},{4,5},{5,6},{6,7},{7,8},{8,9},{9,10},{10,1... | collective-permute-start | bytes 786440 | tf_op jit(solution)/shard_map/ppermute | solution.py:419
  193.8 14.8 %collective-permute-start.7 = (bf16[128,1024]{1,0:T(8,128)(2,1)S(1)}, bf16[128,1024]{1,0:T(8,128)(2,1)S(1)}, u32[]{:S(2)}, u32[]{:S(2)}) collective-permute-start(bf16[128,1024]{1,0:T(8,128)(2,1)S(1)} %get-tuple-element.73), channel_id=1, source_target_pairs={{1,0},{2,1},{3,2},{4,3},{5,4},{6,5},{7,6},{8,7},{9,8},{10,9},{11,1... | collective-permute-start | bytes 786440 | tf_op jit(solution)/shard_map/ppermute | solution.py:419
  211.7 12.6 %copy-start.7 = (f32[128,1024]{1,0:T(8,128)S(1)}, f32[128,1024]{1,0:T(8,128)}, u32[]{:S(2)}) copy-start(f32[128,1024]{1,0:T(8,128)} %get-tuple-element.76.refs_9_) | copy-start | bytes 1572868
  211.7 12.6 %copy-start.13 = (f32[2,1024]{1,0:T(2,128)S(1)}, f32[2,1024]{1,0:T(2,128)}, u32[]{:S(2)}) copy-start(f32[2,1024]{1,0:T(2,128)} %get-tuple-element.77.refs_11_.refs_3_) | copy-start | bytes 24580
  211.7 12.6 %copy-start.18 = (f32[1,512]{1,0:T(1,128)S(1)}, f32[1,512]{1,0:T(1,128)}, u32[]{:S(2)}) copy-start(f32[1,512]{1,0:T(1,128)} %get-tuple-element.75.refs_3_) | copy-start | bytes 6148
  211.7 12.6 %copy-start.19 = (f32[1,512]{1,0:T(1,128)S(1)}, f32[1,512]{1,0:T(1,128)}, u32[]{:S(2)}) copy-start(f32[1,512]{1,0:T(1,128)} %get-tuple-element.78.refs_12_) | copy-start | bytes 6148
  211.7 12.6 %copy-start.20 = (f32[1,512]{1,0:T(1,128)S(1)}, f32[1,512]{1,0:T(1,128)}, u32[]{:S(2)}) copy-start(f32[1,512]{1,0:T(1,128)} %get-tuple-element.79.refs_13_) | copy-start | bytes 6148
  230.8 4.2 %collective-permute-start.8 = (bf16[1024,1024]{1,0:T(8,128)(2,1)S(1)}, bf16[1024,1024]{1,0:T(8,128)(2,1)S(1)}, u32[]{:S(2)}, u32[]{:S(2)}) collective-permute-start(bf16[1024,1024]{1,0:T(8,128)(2,1)S(1)} %give.2), channel_id=1, source_target_pairs={{0,128},{128,0},{1,129},{129,1},{2,130},{130,2},{3,131},{131,3},{4... | collective-permute-start | bytes 6291464 | tf_op jit(solution)/shard_map/ppermute | solution.py:460
  238.1 38.1 %all-to-all-start.14 = ((bf16[16,64,1024]{2,1,0:T(8,128)(2,1)}), bf16[16,64,1024]{2,1,0:T(8,128)(2,1)S(1)}, u32[]{:S(2)}, u32[]{:S(2)}) async-start(bf16[16,64,1024]{2,1,0:T(8,128)(2,1)} %bitcast.24), calls=%async_computation.14 | async-start | bytes 4194304 | tf_op jit(solution)/shard_map/all_to_all | solution.py:400
  241.9 34.4 %reduce-scatter.5.cloned.1.call-start = ((), (), s32[]{:S(2)}) async-start(), calls=%async_computation.19 | async-start | bytes 655360 | tf_op jit(solution)/shard_map/reduce_scatter | solution.py:464
  243.9 57.4 %copy-start.4 = (bf16[128,1024]{1,0:T(8,128)(2,1)S(1)}, bf16[128,1024]{1,0:T(8,128)(2,1)}, u32[]{:S(2)}) copy-start(bf16[128,1024]{1,0:T(8,128)(2,1)} %get-tuple-element.83.refs_2_.refs_3_.refs_5_) | copy-start | bytes 786436
  244.0 57.4 %copy-start.16 = (f32[1,1024]{1,0:T(1,128)S(1)}, f32[1,1024]{1,0:T(1,128)}, u32[]{:S(2)}) copy-start(f32[1,1024]{1,0:T(1,128)} %get-tuple-element.86.refs_6_) | copy-start | bytes 12292
  244.0 57.4 %copy-start.17 = (f32[1,1024]{1,0:T(1,128)S(1)}, f32[1,1024]{1,0:T(1,128)}, u32[]{:S(2)}) copy-start(f32[1,1024]{1,0:T(1,128)} %get-tuple-element.87.refs_7_) | copy-start | bytes 12292
  244.0 1.3 collective-permute-start.9
  245.3 3.7 %collective-permute-start.10 = (f32[1,1,2048]{2,1,0:T(1,128)S(1)}, f32[1,1,2048]{2,1,0:T(1,128)S(1)}, u32[]{:S(2)}, u32[]{:S(2)}) collective-permute-start(f32[1,1,2048]{2,1,0:T(1,128)S(1)} %add.88), channel_id=1, source_target_pairs={{0,1},{1,0},{2,3},{3,2},{4,5},{5,4},{6,7},{7,6},{8,9},{9,8},{10,11... | collective-permute-start | bytes 24584 | tf_op jit(solution)/shard_map/ppermute | solution.py:460
  249.0 4.6 %collective-permute-start.11 = (f32[1,1,2048]{2,1,0:T(1,128)S(1)}, f32[1,1,2048]{2,1,0:T(1,128)S(1)}, u32[]{:S(2)}, u32[]{:S(2)}) collective-permute-start(f32[1,1,2048]{2,1,0:T(1,128)S(1)} %add.89), channel_id=1, source_target_pairs={{0,2},{1,3},{2,0},{3,1},{4,6},{5,7},{6,4},{7,5},{8,10},{9,11},{10,... | collective-permute-start | bytes 24584 | tf_op jit(solution)/shard_map/ppermute | solution.py:460
  253.7 7.6 %collective-permute-start.12 = (f32[1,1,2048]{2,1,0:T(1,128)S(1)}, f32[1,1,2048]{2,1,0:T(1,128)S(1)}, u32[]{:S(2)}, u32[]{:S(2)}) collective-permute-start(f32[1,1,2048]{2,1,0:T(1,128)S(1)} %add.90), channel_id=1, source_target_pairs={{0,4},{1,5},{2,6},{3,7},{4,0},{5,1},{6,2},{7,3},{8,12},{9,13},{10,... | collective-permute-start | bytes 24584 | tf_op jit(solution)/shard_map/ppermute | solution.py:460
  278.2 24.4 %all-to-all-start.15 = ((bf16[16,8,2048]{2,1,0:T(8,128)(2,1)}), bf16[16,8,2048]{2,1,0:T(8,128)(2,1)S(1)}, u32[]{:S(2)}, u32[]{:S(2)}) async-start(bf16[16,8,2048]{2,1,0:T(8,128)(2,1)} %gather_rows.1), calls=%async_computation.17 | async-start | bytes 1048576 | tf_op jit(solution)/shard_map/all_to_all | solution.py:400
  283.4 3.7 %collective-permute-start.13 = (f32[1,1,2048]{2,1,0:T(1,128)S(1)}, f32[1,1,2048]{2,1,0:T(1,128)S(1)}, u32[]{:S(2)}, u32[]{:S(2)}) collective-permute-start(f32[1,1,2048]{2,1,0:T(1,128)S(1)} %add.91.refs_2_), channel_id=1, source_target_pairs={{0,8},{8,0},{16,24},{24,16},{1,9},{9,1},{17,25},{25,17},{2,10},{10... | collective-permute-start | bytes 24584 | tf_op jit(solution)/shard_map/ppermute | solution.py:460
  287.1 5.2 %collective-permute-start.14 = (f32[1,1,2048]{2,1,0:T(1,128)S(1)}, f32[1,1,2048]{2,1,0:T(1,128)S(1)}, u32[]{:S(2)}, u32[]{:S(2)}) collective-permute-start(f32[1,1,2048]{2,1,0:T(1,128)S(1)} %add.92), channel_id=1, source_target_pairs={{0,16},{8,24},{16,0},{24,8},{1,17},{9,25},{17,1},{25,9},{2,18},{10... | collective-permute-start | bytes 24584 | tf_op jit(solution)/shard_map/ppermute | solution.py:460
  292.3 3.7 %collective-permute-start.15 = (f32[1,1,2048]{2,1,0:T(1,128)S(1)}, f32[1,1,2048]{2,1,0:T(1,128)S(1)}, u32[]{:S(2)}, u32[]{:S(2)}) collective-permute-start(f32[1,1,2048]{2,1,0:T(1,128)S(1)} %add.93), channel_id=1, source_target_pairs={{0,32},{32,0},{64,96},{96,64},{1,33},{33,1},{65,97},{97,65},{2,34}... | collective-permute-start | bytes 24584 | tf_op jit(solution)/shard_map/ppermute | solution.py:460
  296.1 5.2 %collective-permute-start.16 = (f32[1,1,2048]{2,1,0:T(1,128)S(1)}, f32[1,1,2048]{2,1,0:T(1,128)S(1)}, u32[]{:S(2)}, u32[]{:S(2)}) collective-permute-start(f32[1,1,2048]{2,1,0:T(1,128)S(1)} %add.94), channel_id=1, source_target_pairs={{0,64},{32,96},{64,0},{96,32},{1,65},{33,97},{65,1},{97,33},{2,66}... | collective-permute-start | bytes 24584 | tf_op jit(solution)/shard_map/ppermute | solution.py:460
Sparse Core Ops, SparseCore 0:
  211.9 28.4 reduce-scatter.2
  245.4 24.3 reduce-scatter.4
